TPU v7x, 256 devices: a whole 4x4x8 slice. The times are simulated.
256 devices in a mesh: ctx: 4 (over z_lo), att: 2 (over core), exp: 32 (over z_hi, x, y).
Axes of the slice: x: 4, y: 4, z: 8 (z_hi: 2, z_lo: 4; z = z_hi * 4 + z_lo), core: 2. Of those that a mesh axis runs over, the one named last changes fastest.
Arguments:
- query_latent: bfloat16 [64, 128, 512], P(('att', 'exp')), may hold values from -8 to 8
- query_rope: bfloat16 [64, 128, 64], P(('att', 'exp')), may hold values from -8 to 8
- latent_cache: bfloat16 [64, 4096, 512], P(('att', 'exp'), 'ctx'), may hold values from -4 to 4
- rope_keys: bfloat16 [64, 64, 4096], P(('att', 'exp'), None, 'ctx'), may hold values from -4 to 4
- lengths: int32 [64], P(('att', 'exp')), may hold values from 256 to 4096, as said below
- moe_rows: bfloat16 [1024, 7168], P(('ctx', 'att', 'exp'))
- route_ids: int32 [1024, 8], P(('ctx', 'att', 'exp')), may hold values from 0 to 31, all different within a row; in each aligned block of 4 rows (0 to 3, 4 to 7, ...) at most 2 rows name the same one
- route_gates: float32 [1024, 8], P(('ctx', 'att', 'exp')), may hold values from 0.05 to 0.5
- norm_gain: bfloat16 [7168], replicated, may hold values from 0.099609375 to 1.8984375
- expert_in: bfloat16 [32, 2, 7168, 2048], P('exp', None, None, ('ctx', 'att')), may hold values from -0.0625 to 0.0625
- expert_out: bfloat16 [32, 2048, 7168], P('exp', None, ('ctx', 'att')), may hold values from -0.125 to 0.125
Outputs:
- attended: bfloat16 [64, 128, 512], P(('att', 'exp'), 'ctx')
- routed_sum: bfloat16 [1024, 7168], P(('ctx', 'att', 'exp'))
Inputs may be any that keep to these rules, and one draw needn't show every extreme that they name: `route_ids`: each row names 8 different experts; among the 4 rows of one device no expert is named by more than 2 rows, a bound that some block reaches. `lengths`: some sequence has all 4096 positions live.
All inputs are finite; a program needn't handle non-finite values.
Results may differ from a plain program's by a relative error of at most 0.007.
Values may be sent and summed in bfloat16 or wider, within the bound.
No kernel may reach another device: no remote copies, remote signals or barrier semaphores. Data moves between devices by JAX's collectives and lax.ppermute only.
A program may use at most 64 MiB of HBM per device.

v0:
```python
import jax
import jax.numpy as jnp
from jax import lax
from jax.sharding import PartitionSpec as P

softmax_scale = 192.0 ** (-0.5)
epsilon = 1e-06


def attend(query_latent, query_rope, latent_cache, rope_keys, lengths):
    shard_length = latent_cache.shape[1]
    first_position = lax.axis_index("ctx") * shard_length
    scores = jnp.einsum(
        "shr,str->sht", query_latent, latent_cache, preferred_element_type=jnp.float32
    )
    scores = scores + jnp.einsum(
        "shp,spt->sht", query_rope, rope_keys, preferred_element_type=jnp.float32
    )
    position = first_position + jnp.arange(shard_length, dtype=jnp.int32)
    live_mask = position[None, :] < lengths[:, None]
    weights = jnp.where(live_mask[:, None, :], jnp.exp(softmax_scale * scores), jnp.float32(0.0))
    mass = jnp.sum(weights, axis=2)
    numerator = jnp.einsum(
        "sht,str->shr",
        weights.astype(jnp.bfloat16),
        latent_cache,
        preferred_element_type=jnp.float32,
    )
    numerator, mass = (
        lax.psum_scatter(numerator, "ctx", scatter_dimension=1, tiled=True),
        lax.psum_scatter(mass, "ctx", scatter_dimension=1, tiled=True),
    )
    return (numerator / mass[:, :, None]).astype(jnp.bfloat16)


def route_tables(route_ids, route_gates, experts, capacity):
    picks = route_ids[:, :, None] == jnp.arange(experts, dtype=jnp.int32)[None, None, :]
    chosen = jnp.any(picks, axis=1).astype(jnp.int32)
    gate_share = jnp.sum(jnp.where(picks, route_gates[:, :, None], jnp.float32(0.0)), axis=1)
    slot_index = jnp.cumsum(chosen, axis=0) - chosen
    placed = (chosen[:, :, None] == 1) & (
        slot_index[:, :, None] == jnp.arange(capacity, dtype=jnp.int32)[None, None, :]
    )
    return (placed, gate_share)


def shards(
    query_latent,
    query_rope,
    latent_cache,
    rope_keys,
    lengths,
    moe_rows,
    route_ids,
    route_gates,
    norm_gain,
    expert_in,
    expert_out,
):
    attended = attend(query_latent, query_rope, latent_cache, rope_keys, lengths)
    experts = lax.axis_size("exp")
    group = lax.axis_size(("ctx", "att"))
    token_count, model_width = moe_rows.shape
    picked = route_ids.shape[1]
    capacity = max(2, (token_count * picked + experts - 1) // experts)
    widened = moe_rows.astype(jnp.float32)
    normed = (
        widened
        * lax.rsqrt(jnp.mean(widened * widened, axis=1, keepdims=True) + epsilon)
        * norm_gain.astype(jnp.float32)
    ).astype(jnp.bfloat16)
    placed, gate_share = route_tables(route_ids, route_gates, experts, capacity)
    selector = placed.reshape(token_count, experts * capacity).T.astype(jnp.bfloat16)
    outgoing = jnp.dot(selector, normed, preferred_element_type=jnp.float32).astype(jnp.bfloat16)
    outgoing = outgoing.reshape(experts, capacity, model_width)
    gate_weight = expert_in[0, 0]
    up_weight = expert_in[0, 1]
    down_weight = expert_out[0]
    column_width = down_weight.shape[1]
    arrived = lax.all_to_all(outgoing, "exp", split_axis=0, concat_axis=0, tiled=True)
    arrived = arrived.reshape(experts * capacity, model_width)
    portion = lax.all_gather(arrived, ("ctx", "att"), axis=0, tiled=True)
    gate_part = jnp.dot(portion, gate_weight, preferred_element_type=jnp.float32)
    up_part = jnp.dot(portion, up_weight, preferred_element_type=jnp.float32)
    hidden_all = (jax.nn.silu(gate_part) * up_part).astype(jnp.bfloat16)
    column_sum = jnp.dot(
        lax.all_gather(hidden_all, ("ctx", "att"), axis=1, tiled=True),
        down_weight,
        preferred_element_type=jnp.float32,
    )
    column_sum = column_sum.astype(jnp.bfloat16)
    blocks = column_sum.reshape(group, experts * capacity, column_width)
    finished = lax.all_to_all(blocks, ("ctx", "att"), split_axis=0, concat_axis=2, tiled=True)
    returned = lax.all_to_all(
        finished.reshape(experts, capacity, model_width),
        "exp",
        split_axis=0,
        concat_axis=0,
        tiled=True,
    )
    mixing = (gate_share[:, :, None] * placed.astype(jnp.float32)).reshape(
        token_count, experts * capacity
    )
    routed_sum = jnp.dot(
        mixing,
        returned.reshape(experts * capacity, model_width).astype(jnp.float32),
        precision=lax.Precision.HIGHEST,
    )
    return (attended, routed_sum.astype(jnp.bfloat16))


def solution(mesh):
    placed = (
        P(("att", "exp"), None, None),
        P(("att", "exp"), None, None),
        P(("att", "exp"), "ctx", None),
        P(("att", "exp"), None, "ctx"),
        P(("att", "exp")),
        P(("ctx", "att", "exp"), None),
        P(("ctx", "att", "exp"), None),
        P(("ctx", "att", "exp"), None),
        P(),
        P("exp", None, None, ("ctx", "att")),
        P("exp", None, ("ctx", "att")),
    )
    return jax.shard_map(
        shards,
        mesh=mesh,
        in_specs=placed,
        out_specs=(P(("att", "exp"), "ctx", None), P(("ctx", "att", "exp"), None)),
        check_vma=False,
    )
```

profile of v0, /device:TPU:32, one launch (start us, length us, event | category | flops | bytes accessed | tf_op | source)
XLA Modules:
  0.0 291.2 jit_solution(8261702553317550294)
XLA Ops:
  8.1 0.8 fusion.36
  9.0 0.1 copy.24
  9.1 0.1 copy.27
  9.1 0.1 copy.23
  9.3 0.1 copy.31
  9.4 0.7 convert_element_type.49
  10.1 0.1 eq.58
  10.2 1.0 fusion.28
  11.2 1.3 convolution_convert_fusion
  12.5 0.3 reshape.94
  12.9 41.7 %all_to_all.25 = bf16[32,2,7168]{2,1,0:T(2,128)(2,1)S(1)} all-to-all(bf16[32,2,7168]{2,1,0:T(2,128)(2,1)S(1)} %reshape.94), channel_id=1, replica_groups=mesh['ctx'=4,'att'=2,'exp'=32] {'exp'}, dimensions={0} | all-to-all | bytes 1835008 | tf_op jit(solution)/shard_map/all_to_all | solution.py:80
  54.5 1.3 reshape.95
  55.9 75.3 %all-gather.3.cloned.1.call-done = bf16[512,7168]{1,0:T(8,128)(2,1)} async-done(((bf16[64,7168]{1,0:T(8,128)(2,1)}), bf16[512,7168]{1,0:T(8,128)(2,1)}) %all-gather.3.cloned.1.call-update) | async-done | bytes 7340048 | tf_op jit(solution)/shard_map/all_gather | solution.py:82
  131.2 6.3 %fusion.5 = f32[512,256]{1,0:T(8,128)S(1)} fusion(bf16[512,7168]{1,0:T(8,128)(2,1)} %all-gather.3.cloned.1.call-done, bf16[1,2,7168,256]{3,2,1,0:T(8,128)(2,1)} %param.20), kind=kOutput, calls=%fused_computation.7 | convolution fusion | flops 1879048192 | bytes 11534336 | tf_op jit(solution)/shard_map/dot_general | solution.py:83
  137.6 4.9 %fusion.18 = bf16[512,256]{1,0:T(8,128)(2,1)} fusion(bf16[512,7168]{1,0:T(8,128)(2,1)S(1)} %copy-done.6, bf16[1,2,7168,256]{3,2,1,0:T(8,128)(2,1)} %param.20, f32[512,256]{1,0:T(8,128)S(1)} %fusion.5), kind=kOutput, calls=%fused_computation.17 | convolution fusion | flops 1879834624 | bytes 11796480 | tf_op jit(solution)/shard_map/dot_general | solution.py:84
  142.5 39.9 %all-gather.5.cloned.1.call-done = bf16[512,2048]{1,0:T(8,128)(2,1)} async-done(((bf16[512,256]{1,0:T(8,128)(2,1)}), bf16[512,2048]{1,0:T(8,128)(2,1)}) %all-gather.5.cloned.1.call-update) | async-done | bytes 2097168 | tf_op jit(solution)/shard_map/all_gather | solution.py:87
  182.4 5.0 %fusion.9 = bf16[512,896]{1,0:T(8,128)(2,1)S(1)} fusion(bf16[512,2048]{1,0:T(8,128)(2,1)} %all-gather.5.cloned.1.call-done, bf16[1,2048,896]{2,1,0:T(8,128)(2,1)} %param.21), kind=kOutput, calls=%fused_computation.11 | convolution fusion | flops 1879506944 | bytes 6684672 | tf_op jit(solution)/shard_map/dot_general | solution.py:86
  187.4 26.8 %all_to_all.26 = bf16[8,64,896]{2,1,0:T(8,128)(2,1)S(1)} all-to-all(bf16[8,64,896]{2,1,0:T(8,128)(2,1)S(1)} %bitcast.59), channel_id=1, replica_groups=mesh['ctx'=4,'att'=2,'exp'=32] {'ctx','att'}, dimensions={0} | all-to-all | bytes 1835008 | tf_op jit(solution)/shard_map/all_to_all | solution.py:93
  214.3 0.5 copy.28
  214.8 1.1 reshape.97
  215.9 9.8 %all-to-all-start.2 = ((bf16[32,2,7168]{2,1,0:T(2,128)(2,1)}), bf16[32,2,7168]{2,1,0:T(2,128)(2,1)S(1)}, u32[]{:S(2)}, u32[]{:S(2)}) async-start(bf16[32,2,7168]{2,1,0:T(2,128)(2,1)} %reshape.97), calls=%async_computation.3 | async-start | bytes 1835008 | tf_op jit(solution)/shard_map/all_to_all | solution.py:94
  226.4 0.2 fusion.25
  226.7 0.6 fusion.41
  227.3 0.7 copy.32
  228.1 1.0 convolution_bitcast_fusion.1
  229.2 0.1 select_reduce_fusion
  229.3 0.1 copy.25
  229.4 25.4 %reduce-scatter.7.cloned.1.call-done = f32[32,1]{1,0:T(8,128)} async-done(((f32[128,1]{1,0:T(8,128)}), f32[32,1]{1,0:T(8,128)}) %reduce-scatter.7.cloned.1.call-update) | async-done | bytes 144
  254.8 0.8 copy.33
  255.6 25.4 %reduce-scatter.5.cloned.1.call-done = f32[1,32,512]{2,1,0:T(8,128)} async-done(((f32[1,128,512]{2,1,0:T(8,128)}), f32[1,32,512]{2,1,0:T(8,128)}) %reduce-scatter.5.cloned.1.call-update) | async-done | bytes 65552 | tf_op jit(solution)/shard_map/reduce_scatter | solution.py:30
  281.0 1.5 divide_convert_fusion
  282.6 1.2 fusion
  (33 shorter events, 0.5 us)
Async XLA Ops:
  8.0 218.7 %copy-start = (bf16[1,1024,512]{2,1,0:T(8,128)(2,1)S(1)}, bf16[1,1024,512]{2,1,0:T(8,128)(2,1)}, u32[]{:S(2)}) copy-start(bf16[1,1024,512]{2,1,0:T(8,128)(2,1)} %param.13) | copy-start | bytes 3145732
  8.0 123.2 %all-gather.3.cloned.1.call-start = ((), (), s32[]{:S(2)}) async-start(), calls=%async_computation.6 | async-start | bytes 8257536 | tf_op jit(solution)/shard_map/all_gather | solution.py:82
  55.8 126.5 %all-gather.5.cloned.1.call-start = ((), (), s32[]{:S(2)}) async-start(), calls=%async_computation.7 | async-start | bytes 2359296 | tf_op jit(solution)/shard_map/all_gather | solution.py:87
  131.2 6.3 %copy-start.6 = (bf16[512,7168]{1,0:T(8,128)(2,1)S(1)}, bf16[512,7168]{1,0:T(8,128)(2,1)}, u32[]{:S(2)}) copy-start(bf16[512,7168]{1,0:T(8,128)(2,1)} %all-gather.3.cloned.1.call-done) | copy-start | bytes 22020100
  187.4 39.1 %copy-start.2 = (bf16[1,64,1024]{2,1,0:T(8,128)(2,1)S(1)}, bf16[1,64,1024]{2,1,0:T(8,128)(2,1)}, u32[]{:S(2)}) copy-start(bf16[1,64,1024]{2,1,0:T(8,128)(2,1)} %param.14) | copy-start | bytes 393220
  187.4 39.1 %copy-start.3 = (bf16[1,128,64]{1,2,0:T(8,128)(2,1)S(1)}, bf16[1,128,64]{1,2,0:T(8,128)(2,1)}, u32[]{:S(2)}) copy-start(bf16[1,128,64]{1,2,0:T(8,128)(2,1)} %param.12) | copy-start | bytes 49156
  187.4 39.3 %copy-start.1 = (bf16[1,128,512]{2,1,0:T(8,128)(2,1)S(1)}, bf16[1,128,512]{2,1,0:T(8,128)(2,1)}, u32[]{:S(2)}) copy-start(bf16[1,128,512]{2,1,0:T(8,128)(2,1)} %param.11) | copy-start | bytes 393220
  215.9 13.3 %copy-start.4 = (s32[4,8]{1,0:T(4,128)S(1)}, s32[4,8]{1,0:T(4,128)}, u32[]{:S(2)}) copy-start(s32[4,8]{1,0:T(4,128)} %param.17) | copy-start | bytes 388
  215.9 13.3 %copy-start.5 = (f32[4,8]{1,0:T(4,128)S(1)}, f32[4,8]{1,0:T(4,128)}, u32[]{:S(2)}) copy-start(f32[4,8]{1,0:T(4,128)} %param.18) | copy-start | bytes 388
  215.9 66.7 %all-to-all-start.2 = ((bf16[32,2,7168]{2,1,0:T(2,128)(2,1)}), bf16[32,2,7168]{2,1,0:T(2,128)(2,1)S(1)}, u32[]{:S(2)}, u32[]{:S(2)}) async-start(bf16[32,2,7168]{2,1,0:T(2,128)(2,1)} %reshape.97), calls=%async_computation.3 | async-start | bytes 1835008 | tf_op jit(solution)/shard_map/all_to_all | solution.py:94
  225.7 29.1 %reduce-scatter.7.cloned.1.call-start = ((), (), s32[]{:S(2)}) async-start(), calls=%async_computation.8 | async-start | bytes 81920
  228.1 53.0 %reduce-scatter.5.cloned.1.call-start = ((), (), s32[]{:S(2)}) async-start(), calls=%async_computation.5 | async-start | bytes 327680 | tf_op jit(solution)/shard_map/reduce_scatter | solution.py:30
Sparse Core Ops, SparseCore 0:
  56.0 75.2 all-gather.2
  142.6 39.7 all-gather.4
Sparse Core Ops, SparseCore 1:
  228.7 26.1 reduce-scatter.6
  257.4 23.6 reduce-scatter.4
where the time goes:
time: 295 us; the launch traced here: 291 us
  waiting for transfers between devices  166 us (56%)
  blocking collectives  68.5 us (23%)
  matrix products  20.5 us (7%)
  between operations  16.3 us (6%)
  starting transfers between devices  9.96 us (3%)
  local copies, waits for them, and re-layouts  5.45 us (2%)
  other arithmetic  4.3 us (1%)
    all_gather x1, waiting for transfers between devices, shards(): portion = lax.all_gather(arrived, ('ctx', 'att'), axis=0, tiled=True)  75.3 us
    all_to_all x1, blocking collectives, shards(): lax.all_to_all(outgoing, 'exp', split_axis=0, concat_axis=0, tiled=True)  41.7 us
    all_gather x1, waiting for transfers between devices, shards(): lax.all_gather(hidden_all, ('ctx', 'att'), axis=1, tiled=True)  39.9 us
    all_to_all x1, blocking collectives, shards(): lax.all_to_all(blocks, ('ctx', 'att'), split_axis=0, concat_axis=2, tiled...  26.8 us
    unnamed x5, waiting for transfers between devices  25.5 us
    reduce_scatter x1, waiting for transfers between devices, attend(): lax.psum_scatter(numerator, 'ctx', scatter_dimension=1, tiled=True)  25.4 us
    all_to_all x1, starting transfers between devices, shards(): lax.all_to_all(finished.reshape(experts, capacity, model_width), 'exp', s...  9.79 us
    dot_general x1, matrix products, shards(): jnp.dot(portion, gate_weight, preferred_element_type=jnp.float32)  6.33 us
  transfers between devices with their start and end apart: 5, of which 4 were waited for; matrix products, arithmetic and copies ran while one was open for 2% of the time, Pallas kernels for 0%

commit v1 on v0

v1 whole, which is shorter than its diff:
```python
import jax
import jax.numpy as jnp
from jax import lax
from jax.sharding import Mesh, PartitionSpec as P

softmax_scale = 192.0 ** (-0.5)
epsilon = 1e-06
bf16 = jnp.bfloat16
f32 = jnp.float32
INFO = 128
TOK = 4
SLOTS = 2


def attend(query_latent, query_rope, latent_cache, rope_keys, lengths):
    shard_length = latent_cache.shape[1]
    first_position = lax.axis_index("ctx") * shard_length
    scores = jnp.einsum("hr,tr->ht", query_latent[0], latent_cache[0], preferred_element_type=f32)
    scores = scores + jnp.einsum("hp,pt->ht", query_rope[0], rope_keys[0], preferred_element_type=f32)
    position = first_position + jnp.arange(shard_length, dtype=jnp.int32)
    live_mask = position < lengths[0]
    weights = jnp.where(live_mask[None, :], jnp.exp(softmax_scale * scores), f32(0.0))
    mass = jnp.sum(weights, axis=1, keepdims=True)
    numerator = jnp.dot(weights.astype(bf16), latent_cache[0], preferred_element_type=f32)
    return jnp.concatenate([numerator, jnp.broadcast_to(mass, (mass.shape[0], 128))], axis=1)


def finish_attention(summed):
    return (summed[:, :512] / summed[:, 512:513]).astype(bf16)[None]


def split3(values):
    high = lax.reduce_precision(values, 8, 7)
    rest = values - high
    middle = lax.reduce_precision(rest, 8, 7)
    low = rest - middle
    return [high.astype(bf16), middle.astype(bf16), low.astype(bf16)]


def slot_table(ids, z_half):
    experts = (z_half * 16 + jnp.arange(16, dtype=jnp.int32)).astype(f32)
    picks = ids[None] == experts[:, None, None, None]
    chosen = jnp.any(picks, axis=3).astype(f32)
    before = [jnp.zeros_like(chosen[:, :, 0])]
    for t in range(TOK - 1):
        before.append(before[-1] + chosen[:, :, t])
    before = jnp.stack(before, axis=2)
    slot = jnp.arange(SLOTS, dtype=jnp.int32).astype(f32)
    placed = (chosen[..., None] == 1) & (before[..., None] == slot)
    return placed, picks


def shards(
    query_latent,
    query_rope,
    latent_cache,
    rope_keys,
    lengths,
    moe_rows,
    route_ids,
    route_gates,
    norm_gain,
    expert_in,
    expert_out,
):
    c = lax.axis_index("ctx")
    a = lax.axis_index("att")
    h = lax.axis_index("zhi")
    width = moe_rows.shape[1]
    swap_core = [(0, 1), (1, 0)]

    widened = moe_rows.astype(f32)
    normed = (
        widened
        * lax.rsqrt(jnp.mean(widened * widened, axis=1, keepdims=True) + epsilon)
        * norm_gain.astype(f32)
    ).astype(bf16)
    info = jnp.concatenate(
        [route_ids.astype(bf16)] + split3(route_gates) + [jnp.zeros((TOK, INFO - 32), bf16)], axis=1
    )
    payload = jnp.concatenate([normed, info], axis=1)

    def hop(value, k, flip):
        pairs = [
            (i * 2 + j, (i + k) % 4 * 2 + (j ^ flip)) for i in range(4) for j in range(2)
        ]
        return lax.ppermute(value, ("ctx", "zhi"), pairs)

    own_half = [payload] + [hop(payload, k, 0) for k in (1, 2, 3)]
    other_half = [hop(payload, k, 1) for k in (0, 1, 2, 3)]
    origin = (c - jnp.arange(4, dtype=jnp.int32)) % 4
    absolute = origin[None, :] == jnp.arange(4, dtype=jnp.int32)[:, None]

    part = attend(query_latent, query_rope, latent_cache, rope_keys, lengths)
    summed = lax.psum_scatter(part, "ctx", scatter_dimension=0, tiled=True)

    down = expert_out[0].reshape(4, 2, 256, 896)
    down_rel = jnp.concatenate(
        [
            lax.dynamic_slice(down, ((c - k) % 4, jnp.where(r == 0, a, 1 - a), 0, 0), (1, 1, 256, 896)).reshape(256, 896)
            for r in (0, 1)
            for k in range(4)
        ],
        axis=0,
    )

    def dispatch(half):
        tokens = jnp.concatenate(half, axis=0)
        ids = tokens[:, width : width + 8].astype(f32).reshape(4, TOK, 8)
        placed, _ = slot_table(ids, h)
        selector = placed.transpose(0, 3, 1, 2)[:, None] & absolute[None, :, None, :, None]
        selector = selector.astype(bf16).reshape(16 * 4 * SLOTS, 4 * TOK)
        rows = jnp.dot(selector, tokens[:, :width], preferred_element_type=f32).astype(bf16)
        rows = rows.reshape(16, 4 * SLOTS, width)
        got = lax.all_to_all(rows, ("x", "y"), split_axis=0, concat_axis=0, tiled=True)
        return got.reshape(128, width)

    def experts_of(got):
        other = lax.ppermute(got, "att", swap_core)
        rows = jnp.concatenate([got, other], axis=0)
        gate = jnp.dot(rows, expert_in[0, 0], preferred_element_type=f32)
        up = jnp.dot(rows, expert_in[0, 1], preferred_element_type=f32)
        hidden = (jax.nn.silu(gate) * up).astype(bf16)
        pieces = [hidden] + [hop(hidden, k, 0) for k in (1, 2, 3)]
        mine = jnp.concatenate(pieces, axis=1)
        theirs = lax.ppermute(mine, "att", swap_core)
        theirs = jnp.concatenate([theirs[128:], theirs[:128]], axis=0)
        result = jnp.dot(
            jnp.concatenate([mine, theirs], axis=1), down_rel, preferred_element_type=f32
        ).astype(bf16)
        result = result.reshape(2, 16, 8, 896).transpose(1, 0, 2, 3)
        return lax.all_to_all(result, ("x", "y"), split_axis=0, concat_axis=0, tiled=True)

    def mix(half, back):
        mine = jnp.concatenate([v[:, width:] for v in half], axis=0)
        theirs = lax.ppermute(mine, "att", swap_core)
        total = []
        for r, facts in enumerate((mine, theirs)):
            facts = facts.astype(f32).reshape(4, TOK, INFO)
            facts = jnp.sum(jnp.where(absolute[:, :, None, None], facts[None], f32(0.0)), axis=1)
            placed, picks = slot_table(facts[:, :, :8], h)
            gates = facts[:, :, 8:16] + facts[:, :, 16:24] + facts[:, :, 24:32]
            share = jnp.sum(jnp.where(picks, gates[None], f32(0.0)), axis=3)
            weight = jnp.where(placed, share[..., None], f32(0.0)).transpose(1, 2, 0, 3)
            same = jnp.eye(4, dtype=jnp.bool_)
            matrix = jnp.where(same[:, None, None, :, None], weight[:, :, :, None, :], f32(0.0))
            matrix = matrix.reshape(4 * TOK, 16 * 4 * SLOTS)
            total.append(
                jnp.dot(
                    matrix,
                    back[:, r].reshape(16 * 8, 896).astype(f32),
                    precision=lax.Precision.HIGHEST,
                ).reshape(4, TOK, 896)
            )
        first = jnp.where(a == 0, total[0], total[1])
        second = jnp.where(a == 0, total[1], total[0])
        return jnp.stack([first, second], axis=1)

    got_own = dispatch(own_half)
    got_other = dispatch(other_half)
    mixed_own = mix(own_half, experts_of(got_own))
    mixed_other = mix(other_half, experts_of(got_other))
    first = jnp.where(h == 0, mixed_own, mixed_other)
    second = jnp.where(h == 0, mixed_other, mixed_own)
    outgoing = jnp.stack([first, second], axis=2).astype(bf16)
    final = lax.all_to_all(
        outgoing.reshape(16, TOK, 896), ("ctx", "att", "zhi"), split_axis=0, concat_axis=0, tiled=True
    )
    final = final.reshape(8, 2, TOK, 896).astype(f32)
    routed = (final[:, 0] + final[:, 1]).transpose(1, 0, 2).reshape(TOK, 8 * 896)
    return (finish_attention(summed), routed.astype(bf16))


def solution(mesh):
    fine = Mesh(mesh.devices.reshape(4, 2, 2, 4, 4), ("ctx", "att", "zhi", "x", "y"))
    exp = ("zhi", "x", "y")
    sequences = ("att",) + exp
    every = ("ctx", "att") + exp
    placed = (
        P(sequences, None, None),
        P(sequences, None, None),
        P(sequences, "ctx", None),
        P(sequences, None, "ctx"),
        P(sequences),
        P(every, None),
        P(every, None),
        P(every, None),
        P(),
        P(exp, None, None, ("ctx", "att")),
        P(exp, None, ("ctx", "att")),
    )
    return jax.shard_map(
        shards,
        mesh=fine,
        in_specs=placed,
        out_specs=(P(sequences, "ctx", None), P(every, None)),
        check_vma=False,
    )
```

time: 295 us -> 211 us (0.72)
  waiting for transfers between devices: 166 us -> 81.8 us
  blocking collectives: 68.5 us -> 0 us
  starting transfers between devices: 9.96 us -> 46.1 us
  local copies, waits for them, and re-layouts: 5.45 us -> 21.7 us
  other arithmetic: 4.3 us -> 13.3 us
  matrix products: 20.5 us -> 29.2 us
    all_gather x2 -> x0, waiting for transfers between devices: 115 us -> none  [the longest x1 75.3 us: shards(): portion = lax.all_gather(arrived, ('ctx', 'att'), axis=0, tiled=True)]
    all_to_all x2 -> x0, blocking collectives: 68.5 us -> none  [the longest x1 41.7 us: shards(): lax.all_to_all(outgoing, 'exp', split_axis=0, concat_axis=0, tiled=True)]
    all_to_all x1 -> x5, waiting for transfers between devices: 0.01 us -> 61.8 us  [the longest x2 40.5 us: dispatch(): lax.all_to_all(rows, ('x', 'y'), split_axis=0, concat_axis=0, tiled=True)]
    unnamed x5 -> x1, waiting for transfers between devices: 25.5 us -> 0.02 us
    reduce_scatter x1, waiting for transfers between devices: 25.4 us -> 0.02 us  [shards(): summed = lax.psum_scatter(part, 'ctx', scatter_dimension=0, tiled=True)]
    ppermute x0 -> x19, starting transfers between devices: none -> 22.3 us  [the longest x13 21.5 us: hop(): return lax.ppermute(value, ('ctx', 'zhi'), pairs)]
    ppermute x0 -> x19, waiting for transfers between devices: none -> 19.9 us  [the longest x13 18.8 us: hop(): return lax.ppermute(value, ('ctx', 'zhi'), pairs)]
    all_to_all x1 -> x5, starting transfers between devices: 9.79 us -> 23.8 us  [the longest x2 10.7 us: dispatch(): lax.all_to_all(rows, ('x', 'y'), split_axis=0, concat_axis=0, tiled=True)]
  transfers between devices with their start and end apart: 5 -> 25, of which waited for: 4 -> 15; matrix products, arithmetic and copies ran while one was open for 2% -> 24% of each run, Pallas kernels for 0% -> 0%
where the time goes in v1:
time: 211 us; the launch traced here: 208 us
  waiting for transfers between devices  81.8 us (39%)
  starting transfers between devices  46.1 us (22%)
  matrix products  29.2 us (14%)
  local copies, waits for them, and re-layouts  21.7 us (10%)
  between operations  15.5 us (7%)
  other arithmetic  13.3 us (6%)
    all_to_all x2, waiting for transfers between devices, dispatch(): lax.all_to_all(rows, ('x', 'y'), split_axis=0, concat_axis=0, tiled=True)  40.5 us
    ppermute x13, starting transfers between devices, hop(): return lax.ppermute(value, ('ctx', 'zhi'), pairs)  21.5 us
    ppermute x13, waiting for transfers between devices, hop(): return lax.ppermute(value, ('ctx', 'zhi'), pairs)  18.8 us
    all_to_all x2, waiting for transfers between devices, experts_of(): lax.all_to_all(result, ('x', 'y'), split_axis=0, concat_axis=0, tiled=True)  14.8 us
    unnamed x51, local copies, waits for them, and re-layouts  14.3 us
    all_to_all x2, starting transfers between devices, dispatch(): lax.all_to_all(rows, ('x', 'y'), split_axis=0, concat_axis=0, tiled=True)  10.7 us
    dot_general x2, matrix products, experts_of(): gate = jnp.dot(rows, expert_in[0, 0], preferred_element_type=f32)  7.95 us
    dot_general x2, matrix products, experts_of(): up = jnp.dot(rows, expert_in[0, 1], preferred_element_type=f32)  7.51 us
  transfers between devices with their start and end apart: 25, of which 15 were waited for; matrix products, arithmetic and copies ran while one was open for 24% of the time, Pallas kernels for 0%

profile of v1, /device:TPU:32, one launch (start us, length us, event | category | flops | bytes accessed | tf_op | source)
XLA Modules:
  0.0 207.5 jit_solution(4903145626607829006)
XLA Ops:
  11.4 6.4 %collective-permute-start.9 = (bf16[4,7296]{1,0:T(4,128)(2,1)S(1)}, bf16[4,7296]{1,0:T(4,128)(2,1)S(1)}, u32[]{:S(2)}, u32[]{:S(2)}) collective-permute-start(bf16[4,7296]{1,0:T(4,128)(2,1)S(1)} %concatenate.81), channel_id=1, source_target_pairs={{0,16},{16,0},{64,80},{80,64},{128,144},{144,128},{192,208},{208,1... | collective-permute-start | bytes 175112 | tf_op jit(solution)/shard_map/ppermute | solution.py:87
  17.8 3.6 %collective-permute-start.11 = (bf16[4,7296]{1,0:T(4,128)(2,1)S(1)}, bf16[4,7296]{1,0:T(4,128)(2,1)S(1)}, u32[]{:S(2)}, u32[]{:S(2)}) collective-permute-start(bf16[4,7296]{1,0:T(4,128)(2,1)S(1)} %concatenate.81), channel_id=1, source_target_pairs={{0,144},{16,128},{64,208},{80,192},{128,16},{144,0},{192,80},{208,... | collective-permute-start | bytes 175112 | tf_op jit(solution)/shard_map/ppermute | solution.py:87
  21.4 1.9 collective-permute-start.12
  24.0 2.0 collective-permute-start.1
  26.0 2.6 %collective-permute-done.10 = bf16[4,7296]{1,0:T(4,128)(2,1)S(1)} collective-permute-done((bf16[4,7296]{1,0:T(4,128)(2,1)S(1)}, bf16[4,7296]{1,0:T(4,128)(2,1)S(1)}, u32[]{:S(2)}, u32[]{:S(2)}) %collective-permute-start.10) | collective-permute-done | bytes 58400 | tf_op jit(solution)/shard_map/ppermute | solution.py:87
  38.6 1.9 fusion
  40.5 7.0 %all-to-all-start = ((bf16[16,8,7168]{2,1,0:T(8,128)(2,1)}), bf16[16,8,7168]{2,1,0:T(8,128)(2,1)S(1)}, u32[]{:S(2)}, u32[]{:S(2)}) async-start(bf16[16,8,7168]{2,1,0:T(8,128)(2,1)} %fusion), calls=%async_computation.1 | async-start | bytes 3670016 | tf_op jit(solution)/shard_map/all_to_all | solution.py:115
  47.7 2.0 fusion.1
  49.6 25.6 %all-to-all-done = bf16[16,8,7168]{2,1,0:T(8,128)(2,1)S(1)} async-done(((bf16[16,8,7168]{2,1,0:T(8,128)(2,1)}), bf16[16,8,7168]{2,1,0:T(8,128)(2,1)S(1)}, u32[]{:S(2)}, u32[]{:S(2)}) %all-to-all-start) | async-done | bytes 1835040 | tf_op jit(solution)/shard_map/all_to_all | solution.py:115
  76.5 3.7 %all-to-all-start.2 = ((bf16[16,8,7168]{2,1,0:T(8,128)(2,1)}), bf16[16,8,7168]{2,1,0:T(8,128)(2,1)S(1)}, u32[]{:S(2)}, u32[]{:S(2)}) async-start(bf16[16,8,7168]{2,1,0:T(8,128)(2,1)} %fusion.1), calls=%async_computation.3 | async-start | bytes 3670016 | tf_op jit(solution)/shard_map/all_to_all | solution.py:115
  85.0 1.8 bitcast_dynamic-update-slice_fusion.6
  86.9 1.8 bitcast_dynamic-update-slice_fusion.5
  90.5 14.9 %all-to-all-done.2 = bf16[16,8,7168]{2,1,0:T(8,128)(2,1)S(1)} async-done(((bf16[16,8,7168]{2,1,0:T(8,128)(2,1)}), bf16[16,8,7168]{2,1,0:T(8,128)(2,1)S(1)}, u32[]{:S(2)}, u32[]{:S(2)}) %all-to-all-start.2) | async-done | bytes 1835040 | tf_op jit(solution)/shard_map/all_to_all | solution.py:115
  107.3 1.8 bitcast_dynamic-update-slice_fusion.2
  111.0 1.9 bitcast_dynamic-update-slice_fusion
  114.4 4.8 %fusion.8 = f32[256,256]{0,1:T(8,128)S(1)} fusion(bf16[1,2,7168,256]{3,2,1,0:T(8,128)(2,1)} %param.20, bf16[128,7168]{1,0:T(8,128)(2,1)} %collective-permute-done.3, bf16[128,7168]{1,0:T(8,128)(2,1)} %bitcast.171), kind=kOutput, calls=%fused_computation.12 | convolution fusion | flops 946864128 | bytes 7602176 | tf_op jit(solution)/shard_map/dot_general | solution.py:121
  119.2 4.4 %constant_dynamic-update-slice_fusion.3 = (bf16[256,2048]{0,1:T(8,128)(2,1)S(1)}, bf16[256,256]{0,1:T(8,128)(2,1)S(1)}) fusion(bf16[1,2,7168,256]{3,2,1,0:T(8,128)(2,1)} %param.20, bf16[128,7168]{1,0:T(8,128)(2,1)} %collective-permute-done.3, bf16[128,7168]{1,0:T(8,128)(2,1)S(1)} %bitcast.172, f32[256,256]{0,1:T(8,128)S(1)} %fusion.8), kind=kOutput, calls=%fused_computation.111 | convolution fusion | flops 947257344 | bytes 7864320 | tf_op jit(solution)/shard_map/dot_general | solution.py:122
  123.7 2.4 %collective-permute-start.5 = (bf16[256,256]{0,1:T(8,128)(2,1)S(1)}, bf16[256,256]{0,1:T(8,128)(2,1)S(1)}, u32[]{:S(2)}, u32[]{:S(2)}) collective-permute-start(bf16[256,256]{0,1:T(8,128)(2,1)S(1)} %get-tuple-element.90), channel_id=1, source_target_pairs={{0,128},{16,144},{64,192},{80,208},{128,0},{144,16},{192,64},{208,... | collective-permute-start | bytes 393224 | tf_op jit(solution)/shard_map/ppermute | solution.py:87
  127.0 3.1 %fusion.6 = f32[256,256]{0,1:T(8,128)S(1)} fusion(bf16[1,2,7168,256]{3,2,1,0:T(8,128)(2,1)S(1)} %bitcast.192, bf16[128,7168]{1,0:T(8,128)(2,1)} %collective-permute-done.13, bf16[128,7168]{1,0:T(8,128)(2,1)S(1)} %bitcast.168), kind=kOutput, calls=%fused_computation.10 | convolution fusion | flops 946864128 | bytes 7602176 | tf_op jit(solution)/shard_map/dot_general | solution.py:121
  130.1 3.2 %constant_dynamic-update-slice_fusion.7 = (bf16[256,2048]{0,1:T(8,128)(2,1)S(1)}, bf16[256,256]{0,1:T(8,128)(2,1)S(1)}) fusion(bf16[1,2,7168,256]{3,2,1,0:T(8,128)(2,1)S(1)} %bitcast.192, bf16[128,7168]{1,0:T(8,128)(2,1)} %collective-permute-done.13, bf16[128,7168]{1,0:T(8,128)(2,1)S(1)} %bitcast.169, f32[256,256]{0,1:T(8,128)S(1)} %fusion.6), kind=kOutput, calls=%fused_computation.115 | convolution fusion | flops 947257344 | bytes 7864320 | tf_op jit(solution)/shard_map/dot_general | solution.py:122
  134.5 2.4 %collective-permute-start.15 = (bf16[256,256]{0,1:T(8,128)(2,1)S(1)}, bf16[256,256]{0,1:T(8,128)(2,1)S(1)}, u32[]{:S(2)}, u32[]{:S(2)}) collective-permute-start(bf16[256,256]{0,1:T(8,128)(2,1)S(1)} %get-tuple-element.88), channel_id=1, source_target_pairs={{0,128},{16,144},{64,192},{80,208},{128,0},{144,16},{192,64},{208,... | collective-permute-start | bytes 393224 | tf_op jit(solution)/shard_map/ppermute | solution.py:87
  137.4 6.7 %collective-permute-done.6 = bf16[256,256]{0,1:T(8,128)(2,1)S(1)} collective-permute-done((bf16[256,256]{0,1:T(8,128)(2,1)S(1)}, bf16[256,256]{0,1:T(8,128)(2,1)S(1)}, u32[]{:S(2)}, u32[]{:S(2)}) %collective-permute-start.6) | collective-permute-done | bytes 131104 | tf_op jit(solution)/shard_map/ppermute | solution.py:87
  144.4 2.6 %collective-permute-done.15 = bf16[256,256]{0,1:T(8,128)(2,1)S(1)} collective-permute-done((bf16[256,256]{0,1:T(8,128)(2,1)S(1)}, bf16[256,256]{0,1:T(8,128)(2,1)S(1)}, u32[]{:S(2)}, u32[]{:S(2)}) %collective-permute-start.15) | collective-permute-done | bytes 131104 | tf_op jit(solution)/shard_map/ppermute | solution.py:87
  147.1 2.6 %collective-permute-done.16 = bf16[256,256]{0,1:T(8,128)(2,1)S(1)} collective-permute-done((bf16[256,256]{0,1:T(8,128)(2,1)S(1)}, bf16[256,256]{0,1:T(8,128)(2,1)S(1)}, u32[]{:S(2)}, u32[]{:S(2)}) %collective-permute-start.16) | collective-permute-done | bytes 131104 | tf_op jit(solution)/shard_map/ppermute | solution.py:87
  150.3 3.6 %convolution_convert_fusion.3 = bf16[256,896]{1,0:T(8,128)(2,1)S(1)} fusion(bf16[256,2048]{0,1:T(8,128)(2,1)S(1)} %maximum_dynamic-update-slice_fusion, bf16[2048,896]{1,0:T(8,128)(2,1)} %bitcast_dynamic-update-slice_fusion), kind=kOutput, calls=%fused_computation.19 | convolution fusion | flops 939753472 | bytes 5177344 | tf_op jit(solution)/shard_map/dot_general | solution.py:128
  154.7 3.6 %all-to-all-start.1 = ((bf16[16,2,8,896]{3,2,1,0:T(8,128)(2,1)}), bf16[16,2,8,896]{3,2,1,0:T(8,128)(2,1)S(1)}, u32[]{:S(2)}, u32[]{:S(2)}) async-start(bf16[16,2,8,896]{3,2,1,0:T(8,128)(2,1)} %bitcast.157), calls=%async_computation.2 | async-start | bytes 917504 | tf_op jit(solution)/shard_map/all_to_all | solution.py:132
  159.2 3.6 %convolution_convert_fusion.2 = bf16[256,896]{1,0:T(8,128)(2,1)S(1)} fusion(bf16[256,2048]{0,1:T(8,128)(2,1)} %maximum_dynamic-update-slice_fusion.1, bf16[2048,896]{1,0:T(8,128)(2,1)} %bitcast_dynamic-update-slice_fusion), kind=kOutput, calls=%fused_computation.18 | convolution fusion | flops 939753472 | bytes 5177344 | tf_op jit(solution)/shard_map/dot_general | solution.py:128
  163.7 6.3 %all-to-all-done.1 = bf16[16,2,8,896]{3,2,1,0:T(8,128)(2,1)S(1)} async-done(((bf16[16,2,8,896]{3,2,1,0:T(8,128)(2,1)}), bf16[16,2,8,896]{3,2,1,0:T(8,128)(2,1)S(1)}, u32[]{:S(2)}, u32[]{:S(2)}) %all-to-all-start.1) | async-done | bytes 458784 | tf_op jit(solution)/shard_map/all_to_all | solution.py:132
  169.9 3.6 %all-to-all-start.3 = ((bf16[16,2,8,896]{3,2,1,0:T(8,128)(2,1)}), bf16[16,2,8,896]{3,2,1,0:T(8,128)(2,1)S(1)}, u32[]{:S(2)}, u32[]{:S(2)}) async-start(bf16[16,2,8,896]{3,2,1,0:T(8,128)(2,1)} %bitcast.156), calls=%async_computation.4 | async-start | bytes 917504 | tf_op jit(solution)/shard_map/all_to_all | solution.py:132
  175.4 8.5 %all-to-all-done.3 = bf16[16,2,8,896]{3,2,1,0:T(8,128)(2,1)S(1)} async-done(((bf16[16,2,8,896]{3,2,1,0:T(8,128)(2,1)}), bf16[16,2,8,896]{3,2,1,0:T(8,128)(2,1)S(1)}, u32[]{:S(2)}, u32[]{:S(2)}) %all-to-all-start.3) | async-done | bytes 458784 | tf_op jit(solution)/shard_map/all_to_all | solution.py:132
  185.9 6.0 %all-to-all-start.4 = ((bf16[16,4,896]{2,1,0:T(4,128)(2,1)}), bf16[16,4,896]{2,1,0:T(4,128)(2,1)S(1)}, u32[]{:S(2)}, u32[]{:S(2)}) async-start(bf16[16,4,896]{2,1,0:T(4,128)(2,1)} %bitcast.59), calls=%async_computation.5 | async-start | bytes 229376 | tf_op jit(solution)/shard_map/all_to_all | solution.py:166
  193.4 6.6 %all-to-all-done.4 = bf16[16,4,896]{2,1,0:T(4,128)(2,1)S(1)} async-done(((bf16[16,4,896]{2,1,0:T(4,128)(2,1)}), bf16[16,4,896]{2,1,0:T(4,128)(2,1)S(1)}, u32[]{:S(2)}, u32[]{:S(2)}) %all-to-all-start.4) | async-done | bytes 114720 | tf_op jit(solution)/shard_map/all_to_all | solution.py:166
  (177 shorter events, 39.2 us)
Async XLA Ops:
  7.2 74.1 %copy-start = (bf16[1,1024,512]{2,1,0:T(8,128)(2,1)S(1)}, bf16[1,1024,512]{2,1,0:T(8,128)(2,1)}, u32[]{:S(2)}) copy-start(bf16[1,1024,512]{2,1,0:T(8,128)(2,1)} %param.13) | copy-start | bytes 3145732
  11.4 12.6 %collective-permute-start.9 = (bf16[4,7296]{1,0:T(4,128)(2,1)S(1)}, bf16[4,7296]{1,0:T(4,128)(2,1)S(1)}, u32[]{:S(2)}, u32[]{:S(2)}) collective-permute-start(bf16[4,7296]{1,0:T(4,128)(2,1)S(1)} %concatenate.81), channel_id=1, source_target_pairs={{0,16},{16,0},{64,80},{80,64},{128,144},{144,128},{192,208},{208,1... | collective-permute-start | bytes 175112 | tf_op jit(solution)/shard_map/ppermute | solution.py:87
  17.7 10.9 %collective-permute-start.10 = (bf16[4,7296]{1,0:T(4,128)(2,1)S(1)}, bf16[4,7296]{1,0:T(4,128)(2,1)S(1)}, u32[]{:S(2)}, u32[]{:S(2)}) collective-permute-start(bf16[4,7296]{1,0:T(4,128)(2,1)S(1)} %concatenate.81), channel_id=1, source_target_pairs={{0,80},{16,64},{64,144},{80,128},{128,208},{144,192},{192,16},{208... | collective-permute-start | bytes 175112 | tf_op jit(solution)/shard_map/ppermute | solution.py:87
  17.8 10.8 %collective-permute-start.11 = (bf16[4,7296]{1,0:T(4,128)(2,1)S(1)}, bf16[4,7296]{1,0:T(4,128)(2,1)S(1)}, u32[]{:S(2)}, u32[]{:S(2)}) collective-permute-start(bf16[4,7296]{1,0:T(4,128)(2,1)S(1)} %concatenate.81), channel_id=1, source_target_pairs={{0,144},{16,128},{64,208},{80,192},{128,16},{144,0},{192,80},{208,... | collective-permute-start | bytes 175112 | tf_op jit(solution)/shard_map/ppermute | solution.py:87
  21.4 7.9 %collective-permute-start.12 = (bf16[4,7296]{1,0:T(4,128)(2,1)S(1)}, bf16[4,7296]{1,0:T(4,128)(2,1)S(1)}, u32[]{:S(2)}, u32[]{:S(2)}) collective-permute-start(bf16[4,7296]{1,0:T(4,128)(2,1)S(1)} %concatenate.81), channel_id=1, source_target_pairs={{0,208},{16,192},{64,16},{80,0},{128,80},{144,64},{192,144},{208,1... | collective-permute-start | bytes 175112 | tf_op jit(solution)/shard_map/ppermute | solution.py:87
  23.3 6.5 %collective-permute-start = (bf16[4,7296]{1,0:T(4,128)(2,1)S(1)}, bf16[4,7296]{1,0:T(4,128)(2,1)S(1)}, u32[]{:S(2)}, u32[]{:S(2)}) collective-permute-start(bf16[4,7296]{1,0:T(4,128)(2,1)S(1)} %concatenate.81), channel_id=1, source_target_pairs={{0,64},{16,80},{64,128},{80,144},{128,192},{144,208},{192,0},{208,... | collective-permute-start | bytes 175112 | tf_op jit(solution)/shard_map/ppermute | solution.py:87
  24.0 7.1 %collective-permute-start.1 = (bf16[4,7296]{1,0:T(4,128)(2,1)S(1)}, bf16[4,7296]{1,0:T(4,128)(2,1)S(1)}, u32[]{:S(2)}, u32[]{:S(2)}) collective-permute-start(bf16[4,7296]{1,0:T(4,128)(2,1)S(1)} %concatenate.81), channel_id=1, source_target_pairs={{0,128},{16,144},{64,192},{80,208},{128,0},{144,16},{192,64},{208,... | collective-permute-start | bytes 175112 | tf_op jit(solution)/shard_map/ppermute | solution.py:87
  28.6 4.2 %collective-permute-start.2 = (bf16[4,7296]{1,0:T(4,128)(2,1)S(1)}, bf16[4,7296]{1,0:T(4,128)(2,1)S(1)}, u32[]{:S(2)}, u32[]{:S(2)}) collective-permute-start(bf16[4,7296]{1,0:T(4,128)(2,1)S(1)} %concatenate.81), channel_id=1, source_target_pairs={{0,192},{16,208},{64,0},{80,16},{128,64},{144,80},{192,128},{208,1... | collective-permute-start | bytes 175112 | tf_op jit(solution)/shard_map/ppermute | solution.py:87
  29.4 3.6 %collective-permute-start.18 = (bf16[16,128]{1,0:T(8,128)(2,1)S(1)}, bf16[16,128]{1,0:T(8,128)(2,1)S(1)}, u32[]{:S(2)}, u32[]{:S(2)}) collective-permute-start(bf16[16,128]{1,0:T(8,128)(2,1)S(1)} %pad_maximum_fusion.29), channel_id=1, source_target_pairs={{0,32},{32,0},{1,33},{33,1},{2,34},{34,2},{3,35},{35,3},{4,36},{36... | collective-permute-start | bytes 12296 | tf_op jit(solution)/shard_map/ppermute | solution.py:136
  32.8 1.3 collective-permute-start.8
  40.5 34.7 %all-to-all-start = ((bf16[16,8,7168]{2,1,0:T(8,128)(2,1)}), bf16[16,8,7168]{2,1,0:T(8,128)(2,1)S(1)}, u32[]{:S(2)}, u32[]{:S(2)}) async-start(bf16[16,8,7168]{2,1,0:T(8,128)(2,1)} %fusion), calls=%async_computation.1 | async-start | bytes 3670016 | tf_op jit(solution)/shard_map/all_to_all | solution.py:115
  47.5 33.4 %copy-start.4 = (bf16[1,64,1024]{2,1,0:T(8,128)(2,1)S(1)}, bf16[1,64,1024]{2,1,0:T(8,128)(2,1)}, u32[]{:S(2)}) copy-start(bf16[1,64,1024]{2,1,0:T(8,128)(2,1)} %param.14) | copy-start | bytes 393220
  47.5 33.8 %copy-start.3 = (bf16[1,128,512]{2,1,0:T(8,128)(2,1)S(1)}, bf16[1,128,512]{2,1,0:T(8,128)(2,1)}, u32[]{:S(2)}) copy-start(bf16[1,128,512]{2,1,0:T(8,128)(2,1)} %param.11) | copy-start | bytes 393220
  47.7 33.2 %copy-start.7 = (bf16[1,128,64]{1,2,0:T(8,128)(2,1)S(1)}, bf16[1,128,64]{1,2,0:T(8,128)(2,1)}, u32[]{:S(2)}) copy-start(bf16[1,128,64]{1,2,0:T(8,128)(2,1)} %param.12) | copy-start | bytes 49156
  76.5 29.0 %all-to-all-start.2 = ((bf16[16,8,7168]{2,1,0:T(8,128)(2,1)}), bf16[16,8,7168]{2,1,0:T(8,128)(2,1)S(1)}, u32[]{:S(2)}, u32[]{:S(2)}) async-start(bf16[16,8,7168]{2,1,0:T(8,128)(2,1)} %fusion.1), calls=%async_computation.3 | async-start | bytes 3670016 | tf_op jit(solution)/shard_map/all_to_all | solution.py:115
  80.2 94.0 %reduce-scatter.2.cloned.1.call-start = ((), (), s32[]{:S(2)}) async-start(), calls=%async_computation.6 | async-start | bytes 409600 | tf_op jit(solution)/shard_map/reduce_scatter | solution.py:95
  81.2 33.2 %collective-permute-start.3 = (bf16[128,7168]{1,0:T(8,128)(2,1)}, bf16[128,7168]{1,0:T(8,128)(2,1)}, u32[]{:S(2)}, u32[]{:S(2)}) collective-permute-start(bf16[128,7168]{1,0:T(8,128)(2,1)} %bitcast.170), channel_id=1, source_target_pairs={{0,32},{32,0},{1,33},{33,1},{2,34},{34,2},{3,35},{35,3},{4,36},{36... | collective-permute-start | bytes 5505032 | tf_op jit(solution)/shard_map/ppermute | solution.py:119
  83.1 29.7 %copy-start.6 = (f32[4,4,16]{2,1,0:T(4,128)S(1)}, f32[4,4,16]{2,1,0:T(4,128)}, u32[]{:S(2)}) copy-start(f32[4,4,16]{2,1,0:T(4,128)} %get-tuple-element.75) | copy-start | bytes 3076
  83.1 29.8 %copy-start.5 = (f32[4,4,16]{2,1,0:T(4,128)S(1)}, f32[4,4,16]{2,1,0:T(4,128)}, u32[]{:S(2)}) copy-start(f32[4,4,16]{2,1,0:T(4,128)} %get-tuple-element.77) | copy-start | bytes 3076
  83.2 30.1 %copy-start.15 = (f32[16]{0:T(128)S(1)}, f32[16]{0:T(128)}, u32[]{:S(2)}) copy-start(f32[16]{0:T(128)} %copy-done.14) | copy-start | bytes 196
  105.5 21.5 %collective-permute-start.13 = (bf16[128,7168]{1,0:T(8,128)(2,1)S(1)}, bf16[128,7168]{1,0:T(8,128)(2,1)}, u32[]{:S(2)}, u32[]{:S(2)}) collective-permute-start(bf16[128,7168]{1,0:T(8,128)(2,1)S(1)} %bitcast.167), channel_id=1, source_target_pairs={{0,32},{32,0},{1,33},{33,1},{2,34},{34,2},{3,35},{35,3},{4,36},{36... | collective-permute-start | bytes 5505032 | tf_op jit(solution)/shard_map/ppermute | solution.py:119
  123.6 13.3 %collective-permute-start.4 = (bf16[256,256]{0,1:T(8,128)(2,1)S(1)}, bf16[256,256]{0,1:T(8,128)(2,1)S(1)}, u32[]{:S(2)}, u32[]{:S(2)}) collective-permute-start(bf16[256,256]{0,1:T(8,128)(2,1)S(1)} %get-tuple-element.90), channel_id=1, source_target_pairs={{0,64},{16,80},{64,128},{80,144},{128,192},{144,208},{192,0},{208,... | collective-permute-start | bytes 393224 | tf_op jit(solution)/shard_map/ppermute | solution.py:87
  123.7 13.7 %collective-permute-start.5 = (bf16[256,256]{0,1:T(8,128)(2,1)S(1)}, bf16[256,256]{0,1:T(8,128)(2,1)S(1)}, u32[]{:S(2)}, u32[]{:S(2)}) collective-permute-start(bf16[256,256]{0,1:T(8,128)(2,1)S(1)} %get-tuple-element.90), channel_id=1, source_target_pairs={{0,128},{16,144},{64,192},{80,208},{128,0},{144,16},{192,64},{208,... | collective-permute-start | bytes 393224 | tf_op jit(solution)/shard_map/ppermute | solution.py:87
  126.1 18.0 %collective-permute-start.6 = (bf16[256,256]{0,1:T(8,128)(2,1)S(1)}, bf16[256,256]{0,1:T(8,128)(2,1)S(1)}, u32[]{:S(2)}, u32[]{:S(2)}) collective-permute-start(bf16[256,256]{0,1:T(8,128)(2,1)S(1)} %get-tuple-element.90), channel_id=1, source_target_pairs={{0,192},{16,208},{64,0},{80,16},{128,64},{144,80},{192,128},{208,1... | collective-permute-start | bytes 393224 | tf_op jit(solution)/shard_map/ppermute | solution.py:87
  133.3 11.1 %collective-permute-start.14 = (bf16[256,256]{0,1:T(8,128)(2,1)S(1)}, bf16[256,256]{0,1:T(8,128)(2,1)S(1)}, u32[]{:S(2)}, u32[]{:S(2)}) collective-permute-start(bf16[256,256]{0,1:T(8,128)(2,1)S(1)} %get-tuple-element.88), channel_id=1, source_target_pairs={{0,64},{16,80},{64,128},{80,144},{128,192},{144,208},{192,0},{208,... | collective-permute-start | bytes 393224 | tf_op jit(solution)/shard_map/ppermute | solution.py:87
  134.5 12.5 %collective-permute-start.15 = (bf16[256,256]{0,1:T(8,128)(2,1)S(1)}, bf16[256,256]{0,1:T(8,128)(2,1)S(1)}, u32[]{:S(2)}, u32[]{:S(2)}) collective-permute-start(bf16[256,256]{0,1:T(8,128)(2,1)S(1)} %get-tuple-element.88), channel_id=1, source_target_pairs={{0,128},{16,144},{64,192},{80,208},{128,0},{144,16},{192,64},{208,... | collective-permute-start | bytes 393224 | tf_op jit(solution)/shard_map/ppermute | solution.py:87
  136.9 12.7 %collective-permute-start.16 = (bf16[256,256]{0,1:T(8,128)(2,1)S(1)}, bf16[256,256]{0,1:T(8,128)(2,1)S(1)}, u32[]{:S(2)}, u32[]{:S(2)}) collective-permute-start(bf16[256,256]{0,1:T(8,128)(2,1)S(1)} %get-tuple-element.88), channel_id=1, source_target_pairs={{0,192},{16,208},{64,0},{80,16},{128,64},{144,80},{192,128},{208,1... | collective-permute-start | bytes 393224 | tf_op jit(solution)/shard_map/ppermute | solution.py:87
  144.1 6.0 %collective-permute-start.7 = (bf16[256,1024]{0,1:T(8,128)(2,1)S(1)}, bf16[256,1024]{0,1:T(8,128)(2,1)S(1)}, u32[]{:S(2)}, u32[]{:S(2)}) collective-permute-start(bf16[256,1024]{0,1:T(8,128)(2,1)S(1)} %pad_maximum_fusion.6), channel_id=1, source_target_pairs={{0,32},{32,0},{1,33},{33,1},{2,34},{34,2},{3,35},{35,3},{4,36},{36... | collective-permute-start | bytes 1572872 | tf_op jit(solution)/shard_map/ppermute | solution.py:126
  149.7 8.6 %collective-permute-start.17 = (bf16[256,1024]{0,1:T(8,128)(2,1)S(1)}, bf16[256,1024]{0,1:T(8,128)(2,1)S(1)}, u32[]{:S(2)}, u32[]{:S(2)}) collective-permute-start(bf16[256,1024]{0,1:T(8,128)(2,1)S(1)} %pad_maximum_fusion.7), channel_id=1, source_target_pairs={{0,32},{32,0},{1,33},{33,1},{2,34},{34,2},{3,35},{35,3},{4,36},{36... | collective-permute-start | bytes 1572872 | tf_op jit(solution)/shard_map/ppermute | solution.py:126
  154.7 15.2 %all-to-all-start.1 = ((bf16[16,2,8,896]{3,2,1,0:T(8,128)(2,1)}), bf16[16,2,8,896]{3,2,1,0:T(8,128)(2,1)S(1)}, u32[]{:S(2)}, u32[]{:S(2)}) async-start(bf16[16,2,8,896]{3,2,1,0:T(8,128)(2,1)} %bitcast.157), calls=%async_computation.2 | async-start | bytes 917504 | tf_op jit(solution)/shard_map/all_to_all | solution.py:132
  169.9 13.9 %all-to-all-start.3 = ((bf16[16,2,8,896]{3,2,1,0:T(8,128)(2,1)}), bf16[16,2,8,896]{3,2,1,0:T(8,128)(2,1)S(1)}, u32[]{:S(2)}, u32[]{:S(2)}) async-start(bf16[16,2,8,896]{3,2,1,0:T(8,128)(2,1)} %bitcast.156), calls=%async_computation.4 | async-start | bytes 917504 | tf_op jit(solution)/shard_map/all_to_all | solution.py:132
  185.9 14.1 %all-to-all-start.4 = ((bf16[16,4,896]{2,1,0:T(4,128)(2,1)}), bf16[16,4,896]{2,1,0:T(4,128)(2,1)S(1)}, u32[]{:S(2)}, u32[]{:S(2)}) async-start(bf16[16,4,896]{2,1,0:T(4,128)(2,1)} %bitcast.59), calls=%async_computation.5 | async-start | bytes 229376 | tf_op jit(solution)/shard_map/all_to_all | solution.py:166
  (12 other events, 181.1 us)
Sparse Core Ops, SparseCore 0:
  83.5 21.8 reduce-scatter.1

commit v2 on v1

v2 whole, which is shorter than its diff:
```python
import jax
import jax.numpy as jnp
from jax import lax
from jax.experimental import pallas as pl
from jax.experimental.pallas import tpu as pltpu
from jax.sharding import Mesh, PartitionSpec as P

softmax_scale = 192.0 ** (-0.5)
epsilon = 1e-06
bf16 = jnp.bfloat16
f32 = jnp.float32
INFO = 128
TOK = 4
SLOTS = 2


def attend(query_latent, query_rope, latent_cache, rope_keys, lengths):
    shard_length = latent_cache.shape[1]
    first_position = lax.axis_index("ctx") * shard_length
    scores = jnp.einsum("hr,tr->ht", query_latent[0], latent_cache[0], preferred_element_type=f32)
    scores = scores + jnp.einsum("hp,pt->ht", query_rope[0], rope_keys[0], preferred_element_type=f32)
    position = first_position + jnp.arange(shard_length, dtype=jnp.int32)
    live_mask = position < lengths[0]
    weights = jnp.where(live_mask[None, :], jnp.exp(softmax_scale * scores), f32(0.0))
    mass = jnp.sum(weights, axis=1, keepdims=True)
    numerator = jnp.dot(weights.astype(bf16), latent_cache[0], preferred_element_type=f32)
    return jnp.concatenate([numerator, jnp.broadcast_to(mass, (mass.shape[0], 128))], axis=1)


def finish_attention(summed):
    return (summed[:, :512] / summed[:, 512:513]).astype(bf16)[None]


VMEM = pl.BlockSpec(memory_space=pltpu.VMEM)
SMEM = pl.BlockSpec(memory_space=pltpu.SMEM)
ROOM = pltpu.CompilerParams(vmem_limit_bytes=40 * 1024 * 1024)


def prepare_kernel(ids_ref, gates_ref, rows_ref, gain_ref, out_ref):
    width = rows_ref.shape[1]
    rows = rows_ref[...].astype(f32)
    mean = jnp.mean(rows * rows, axis=1, keepdims=True)
    gain = gain_ref[...].astype(f32).reshape(1, width)
    out_ref[:, :width] = (rows * lax.rsqrt(mean + epsilon) * gain).astype(bf16)
    lane = lax.broadcasted_iota(jnp.int32, (1, 128), 1)
    expert, slot = lane // SLOTS, lane % SLOTS
    count = jnp.zeros((1, 128), jnp.int32)
    token = jnp.full((1, 128), -1.0, f32)
    gate = jnp.zeros((1, 128), f32)
    for t in range(TOK):
        picked = jnp.zeros((1, 128), jnp.int32)
        share = jnp.zeros((1, 128), f32)
        for j in range(8):
            hit = expert == ids_ref[t, j]
            picked = jnp.where(hit, 1, picked)
            share = share + jnp.where(hit, gates_ref[t, j], f32(0.0))
        here = (picked == 1) & (count == slot)
        token = jnp.where(here, f32(t), token)
        gate = jnp.where(here, share, gate)
        count = count + picked
    high = gate.astype(bf16).astype(f32)
    middle = (gate - high).astype(bf16).astype(f32)
    low = gate - high - middle
    row = lax.broadcasted_iota(jnp.int32, (TOK, 128), 0)
    facts = jnp.where(row == 0, token, jnp.where(row == 1, high, jnp.where(row == 2, middle, low)))
    out_ref[:, width:] = facts.astype(bf16)


def prepare(moe_rows, route_ids, route_gates, norm_gain):
    return pl.pallas_call(
        prepare_kernel,
        out_shape=jax.ShapeDtypeStruct((TOK, moe_rows.shape[1] + INFO), bf16),
        in_specs=[SMEM, SMEM, VMEM, VMEM],
        out_specs=VMEM,
    )(route_ids, route_gates, moe_rows, norm_gain)


def gate_up_kernel(place_ref, own_ref, other_ref, weight_ref, out_ref):
    rows = jnp.concatenate([own_ref[...], other_ref[...]], axis=0)
    gate = jnp.dot(rows, weight_ref[0], preferred_element_type=f32)
    up = jnp.dot(rows, weight_ref[1], preferred_element_type=f32)
    hidden = gate / (1.0 + jnp.exp(-gate)) * up
    own, other = hidden[:128], hidden[128:]
    core = place_ref[1]
    first = jnp.where(core == 0, own, other).reshape(16, 8, 256)
    second = jnp.where(core == 0, other, own).reshape(16, 8, 256)
    out_ref[...] = jnp.concatenate([first, second], axis=1).reshape(256, 256).astype(bf16)


def gate_up(place, own, other, weight):
    width = own.shape[1]
    return pl.pallas_call(
        gate_up_kernel,
        out_shape=jax.ShapeDtypeStruct((256, 256), bf16),
        in_specs=[SMEM, VMEM, VMEM, VMEM],
        out_specs=VMEM,
        compiler_params=ROOM,
        cost_estimate=pl.CostEstimate(
            flops=2 * 256 * width * 512, bytes_accessed=2 * width * (512 + 256), transcendentals=65536
        ),
    )(place, own, other, weight)


def down_kernel(place_ref, p0, p1, p2, p3, theirs_ref, weight_ref, out_ref):
    ctx, core = place_ref[0], place_ref[1]
    total = jnp.zeros(out_ref.shape, f32)
    for k, piece in enumerate((p0, p1, p2, p3)):
        source = (ctx - k + 4) % 4
        total += jnp.dot(piece[...], weight_ref[source, core], preferred_element_type=f32)
        theirs = theirs_ref[:, k * 256 : (k + 1) * 256]
        total += jnp.dot(theirs, weight_ref[source, 1 - core], preferred_element_type=f32)
    out_ref[...] = total.astype(bf16)


def down(place, pieces, theirs, weight):
    return pl.pallas_call(
        down_kernel,
        out_shape=jax.ShapeDtypeStruct((256, 896), bf16),
        in_specs=[SMEM] + [VMEM] * 6,
        out_specs=VMEM,
        compiler_params=ROOM,
        cost_estimate=pl.CostEstimate(
            flops=2 * 256 * 2048 * 896, bytes_accessed=2 * 2048 * 896 + 2 * 256 * 2048, transcendentals=0
        ),
    )(place, *pieces, theirs, weight)


def mix_kernel(place_ref, back0, back1, mine0, mine1, theirs0, theirs1, out_ref):
    ctx, core, half = place_ref[0], place_ref[1], place_ref[2]

    def grid(rows, columns, dim):
        return lax.broadcasted_iota(jnp.int32, (rows, columns), dim)

    def lanes(rows):
        at = grid(rows, 256, 1)
        return at // 16, at // 8 % 2, at // 2 % 4, at % 2

    expert, _, _, slot = lanes(128)
    spread = (grid(128, 256, 0) == half * 32 + expert * SLOTS + slot).astype(f32).astype(bf16)
    total = jnp.zeros(out_ref.shape, f32)
    for q, (back, mine, theirs) in enumerate(((back0, mine0, theirs0), (back1, mine1, theirs1))):
        facts = jnp.concatenate([mine[...], theirs[...]], axis=0)
        facts = jnp.dot(facts, spread, preferred_element_type=f32)
        at = grid(32, 256, 0)
        _, lane_core, lane_ctx, _ = lanes(32)
        source_core = jnp.where(at // 16 == 0, core, 1 - core)
        here = (source_core == lane_core) & ((ctx - at // 4 % 4 + 4) % 4 == lane_ctx)
        token, high, middle, low = (
            jnp.sum(jnp.where(here & (at % 4 == i), facts, 0.0), axis=0, keepdims=True) for i in range(4)
        )
        _, lane_core, lane_ctx, _ = lanes(64)
        at = grid(64, 256, 0)
        fits = (at // 16 == lane_ctx) & (at // 8 % 2 == lane_core)
        fits = fits & (at // 4 % 2 == (half if q == 0 else 1 - half))
        fits = fits & ((at % 4).astype(f32) == token)
        for part in (high, middle, low):
            matrix = jnp.where(fits, part, 0.0).astype(bf16)
            total += jnp.dot(matrix, back[...], preferred_element_type=f32)
    out_ref[...] = total.astype(bf16)


def mix(place, back0, back1, mine0, mine1, theirs0, theirs1):
    return pl.pallas_call(
        mix_kernel,
        out_shape=jax.ShapeDtypeStruct((64, 896), bf16),
        in_specs=[SMEM] + [VMEM] * 6,
        out_specs=VMEM,
        cost_estimate=pl.CostEstimate(flops=2 * 64 * 512 * 896 * 3, bytes_accessed=1 << 20, transcendentals=0),
    )(place, back0, back1, mine0, mine1, theirs0, theirs1)


def shards(
    query_latent,
    query_rope,
    latent_cache,
    rope_keys,
    lengths,
    moe_rows,
    route_ids,
    route_gates,
    norm_gain,
    expert_in,
    expert_out,
):
    c = lax.axis_index("ctx")
    a = lax.axis_index("att")
    h = lax.axis_index("zhi")
    width = moe_rows.shape[1]
    swap_core = [(0, 1), (1, 0)]

    place = jnp.stack([c, a, h]).astype(jnp.int32)
    payload = prepare(moe_rows, route_ids, route_gates, norm_gain)

    def hop(value, k, flip):
        pairs = [
            (i * 2 + j, (i + k) % 4 * 2 + (j ^ flip)) for i in range(4) for j in range(2)
        ]
        return lax.ppermute(value, ("ctx", "zhi"), pairs)

    origin = (c - jnp.arange(4, dtype=jnp.int32)) % 4
    absolute = origin[None, :] == jnp.arange(4, dtype=jnp.int32)[:, None]
    gate_up_weight = expert_in[0]
    down_weight = expert_out[0].reshape(4, 2, 256, 896)

    def choose(half):
        tokens = jnp.concatenate(half, axis=0)
        facts = tokens[:, width:]
        wanted = facts.reshape(4, TOK, INFO)[:, 0].astype(f32)
        wanted = jnp.where(h == 0, wanted[:, :32], wanted[:, 32:64]).reshape(4, 16, SLOTS)
        number = jnp.arange(TOK, dtype=jnp.int32).astype(f32)
        hit = wanted.transpose(1, 2, 0)[:, None, :, :, None] == number
        selector = (hit & absolute[None, :, None, :, None]).astype(bf16).reshape(128, 4 * TOK)
        rows = jnp.dot(selector, tokens[:, :width], preferred_element_type=f32).astype(bf16)
        return rows.reshape(16, 4 * SLOTS, width), facts

    def across(value):
        return lax.all_to_all(value, ("x", "y"), split_axis=0, concat_axis=0, tiled=True)

    def hidden_of(got):
        got = got.reshape(128, width)
        hidden = gate_up(place, got, lax.ppermute(got, "att", swap_core), gate_up_weight)
        return [hidden] + [hop(hidden, k, 0) for k in (1, 2, 3)]

    def down_of(pieces, joined):
        theirs = lax.ppermute(joined, "att", swap_core)
        return down(place, pieces, theirs, down_weight).reshape(16, 16, 896)

    rows0, facts0 = choose([payload] + [hop(payload, k, 0) for k in (1, 2, 3)])
    rows0, facts0, payload = lax.optimization_barrier((rows0, facts0, payload))
    got0 = across(rows0)
    rows1, facts1 = choose([hop(payload, k, 1) for k in (0, 1, 2, 3)])
    rows1, facts1, got0 = lax.optimization_barrier((rows1, facts1, got0))
    got1 = across(rows1)

    pieces0 = hidden_of(got0)
    theirs0 = lax.ppermute(facts0, "att", swap_core)
    theirs1 = lax.ppermute(facts1, "att", swap_core)
    part = attend(query_latent, query_rope, latent_cache, rope_keys, lengths)
    result0 = down_of(pieces0, jnp.concatenate(pieces0, axis=1))
    got1, result0, part, theirs0, theirs1 = lax.optimization_barrier((got1, result0, part, theirs0, theirs1))
    summed = lax.psum_scatter(part, "ctx", scatter_dimension=0, tiled=True)
    back0 = across(result0)
    pieces1 = hidden_of(got1)
    joined1, back0 = lax.optimization_barrier((jnp.concatenate(pieces1, axis=1), back0))
    result1 = down_of(pieces1, joined1)
    back1 = across(result1)

    outgoing = mix(place, back0.reshape(256, 896), back1.reshape(256, 896), facts0, facts1, theirs0, theirs1)
    final = lax.all_to_all(
        outgoing.reshape(16, TOK, 896), ("ctx", "att", "zhi"), split_axis=0, concat_axis=0, tiled=True
    )
    final = final.reshape(8, 2, TOK, 896).astype(f32)
    routed = (final[:, 0] + final[:, 1]).transpose(1, 0, 2).reshape(TOK, 8 * 896)
    return (finish_attention(summed), routed.astype(bf16))


def solution(mesh):
    fine = Mesh(mesh.devices.reshape(4, 2, 2, 4, 4), ("ctx", "att", "zhi", "x", "y"))
    exp = ("zhi", "x", "y")
    sequences = ("att",) + exp
    every = ("ctx", "att") + exp
    placed = (
        P(sequences, None, None),
        P(sequences, None, None),
        P(sequences, "ctx", None),
        P(sequences, None, "ctx"),
        P(sequences),
        P(every, None),
        P(every, None),
        P(every, None),
        P(),
        P(exp, None, None, ("ctx", "att")),
        P(exp, None, ("ctx", "att")),
    )
    return jax.shard_map(
        shards,
        mesh=fine,
        in_specs=placed,
        out_specs=(P(sequences, "ctx", None), P(every, None)),
        check_vma=False,
    )
```

time: 211 us -> 177 us (0.84)
  waiting for transfers between devices: 81.8 us -> 54.8 us
  matrix products: 29.2 us -> 7.57 us
  Pallas kernels: 0 us -> 17.9 us
  starting transfers between devices: 46.1 us -> 59.5 us
  other arithmetic: 13.3 us -> 4.49 us
  local copies, waits for them, and re-layouts: 21.7 us -> 14.8 us
    all_to_all x4, waiting for transfers between devices: 55.2 us -> 8.37 us  [across(): lax.all_to_all(value, ('x', 'y'), split_axis=0, concat_axis=0, tiled=True)]
    dot_general x12 -> x2, matrix products: 28.1 us -> 4.59 us  [choose(): jnp.dot(selector, tokens[:, :width], preferred_element_type=f32)]
    pallas_call x0 -> x6, Pallas kernels: none -> 17.9 us  [the longest x2 7.8 us: gate_up(): pl.pallas_call(gate_up_kernel, out_shape=jax.ShapeDtypeStruct((256, 256),...]
    reduce_scatter x1, waiting for transfers between devices: 0.02 us -> 10.7 us  [shards(): summed = lax.psum_scatter(part, 'ctx', scatter_dimension=0, tiled=True)]
    ppermute x13, waiting for transfers between devices: 18.8 us -> 26.9 us  [hop(): return lax.ppermute(value, ('ctx', 'zhi'), pairs)]
    all_to_all x4, starting transfers between devices: 17.9 us -> 24.8 us  [across(): lax.all_to_all(value, ('x', 'y'), split_axis=0, concat_axis=0, tiled=True)]
    convert_element_type x14 -> x3, other arithmetic: 6.01 us -> 0.02 us  [the longest x2 0.02 us: choose(): wanted = facts.reshape(4, TOK, INFO)[:, 0].astype(f32)]
    ppermute x13, starting transfers between devices: 21.5 us -> 25.7 us  [hop(): return lax.ppermute(value, ('ctx', 'zhi'), pairs)]
  transfers between devices with their start and end apart: 25 -> 25, of which waited for: 15 -> 14; matrix products, arithmetic and copies ran while one was open for 24% -> 6% of each run, Pallas kernels for 0% -> 8%
where the time goes in v2:
time: 177 us; the launch traced here: 174 us
  starting transfers between devices  59.5 us (34%)
  waiting for transfers between devices  54.8 us (31%)
  Pallas kernels  17.9 us (10%)
  between operations  15 us (8%)
  local copies, waits for them, and re-layouts  14.8 us (8%)
  matrix products  7.57 us (4%)
  other arithmetic  4.49 us (3%)
    ppermute x13, waiting for transfers between devices, hop(): return lax.ppermute(value, ('ctx', 'zhi'), pairs)  26.9 us
    ppermute x13, starting transfers between devices, hop(): return lax.ppermute(value, ('ctx', 'zhi'), pairs)  25.7 us
    all_to_all x4, starting transfers between devices, across(): lax.all_to_all(value, ('x', 'y'), split_axis=0, concat_axis=0, tiled=True)  24.8 us
    unnamed x35, local copies, waits for them, and re-layouts  12 us
    reduce_scatter x1, waiting for transfers between devices, shards(): summed = lax.psum_scatter(part, 'ctx', scatter_dimension=0, tiled=True)  10.7 us
    all_to_all x4, waiting for transfers between devices, across(): lax.all_to_all(value, ('x', 'y'), split_axis=0, concat_axis=0, tiled=True)  8.37 us
    all_to_all x1, starting transfers between devices, shards(): lax.all_to_all(outgoing.reshape(16, TOK, 896), ('ctx', 'att', 'zhi'), spl...  7.82 us
    pallas_call x2, Pallas kernels, gate_up(): pl.pallas_call(gate_up_kernel, out_shape=jax.ShapeDtypeStruct((256, 256),...  7.8 us
  transfers between devices with their start and end apart: 25, of which 14 were waited for; matrix products, arithmetic and copies ran while one was open for 6% of the time, Pallas kernels for 8%

profile of v2, /device:TPU:32, one launch (start us, length us, event | category | flops | bytes accessed | tf_op | source)
XLA Modules:
  0.0 174.0 jit_solution(4529627575638302413)
XLA Ops:
  8.9 1.9 %collective-permute-start = (bf16[4,7296]{1,0:T(4,128)(2,1)}, bf16[4,7296]{1,0:T(4,128)(2,1)S(1)}, u32[]{:S(2)}, u32[]{:S(2)}) collective-permute-start(bf16[4,7296]{1,0:T(4,128)(2,1)} %shard_map.122), channel_id=1, source_target_pairs={{0,64},{16,80},{64,128},{80,144},{128,192},{144,208},{192,0},{208,... | collective-permute-start | bytes 175112 | tf_op jit(solution)/shard_map/ppermute | solution.py:198
  10.8 2.3 %collective-permute-start.1 = (bf16[4,7296]{1,0:T(4,128)(2,1)}, bf16[4,7296]{1,0:T(4,128)(2,1)S(1)}, u32[]{:S(2)}, u32[]{:S(2)}) collective-permute-start(bf16[4,7296]{1,0:T(4,128)(2,1)} %shard_map.122), channel_id=1, source_target_pairs={{0,128},{16,144},{64,192},{80,208},{128,0},{144,16},{192,64},{208,... | collective-permute-start | bytes 175112 | tf_op jit(solution)/shard_map/ppermute | solution.py:198
  14.2 2.3 %collective-permute-done.1 = bf16[4,7296]{1,0:T(4,128)(2,1)S(1)} collective-permute-done((bf16[4,7296]{1,0:T(4,128)(2,1)}, bf16[4,7296]{1,0:T(4,128)(2,1)S(1)}, u32[]{:S(2)}, u32[]{:S(2)}) %collective-permute-start.1) | collective-permute-done | bytes 58400 | tf_op jit(solution)/shard_map/ppermute | solution.py:198
  19.3 2.7 %fusion = bf16[16,8,7168]{2,1,0:T(8,128)(2,1)} fusion(pred[128,16]{1,0:T(32,128)(4,1)S(1)} %and.51, bf16[4,7296]{1,0:T(4,128)(2,1)S(1)} %collective-permute-done.2, bf16[4,7296]{1,0:T(4,128)(2,1)S(1)} %collective-permute-done.1, bf16[4,7296]{1,0:T(4,128)(2,1)S(1)} %collective-permute-done, bf16[4,7296]{1,0:T(4,128)(2,1)} %shard_map.122), kind=kOutput, calls=%fused_computation.2 | convolution fusion | flops 31195136 | bytes 2070528 | tf_op jit(solution)/shard_map/dot_general | solution.py:213
  22.0 7.2 %all-to-all-start = ((bf16[16,8,7168]{2,1,0:T(8,128)(2,1)}), bf16[16,8,7168]{2,1,0:T(8,128)(2,1)}, u32[]{:S(2)}, u32[]{:S(2)}) async-start(bf16[16,8,7168]{2,1,0:T(8,128)(2,1)} %fusion), calls=%async_computation | async-start | bytes 3670016 | tf_op jit(solution)/shard_map/all_to_all | solution.py:217
  29.3 6.0 %collective-permute-start.3 = (bf16[4,7296]{1,0:T(4,128)(2,1)S(1)}, bf16[4,7296]{1,0:T(4,128)(2,1)S(1)}, u32[]{:S(2)}, u32[]{:S(2)}) collective-permute-start(bf16[4,7296]{1,0:T(4,128)(2,1)S(1)} %copy-done.8), channel_id=1, source_target_pairs={{0,16},{16,0},{64,80},{80,64},{128,144},{144,128},{192,208},{208,1... | collective-permute-start | bytes 175112 | tf_op jit(solution)/shard_map/ppermute | solution.py:198
  35.3 3.1 %collective-permute-start.5 = (bf16[4,7296]{1,0:T(4,128)(2,1)S(1)}, bf16[4,7296]{1,0:T(4,128)(2,1)S(1)}, u32[]{:S(2)}, u32[]{:S(2)}) collective-permute-start(bf16[4,7296]{1,0:T(4,128)(2,1)S(1)} %copy-done.8), channel_id=1, source_target_pairs={{0,144},{16,128},{64,208},{80,192},{128,16},{144,0},{192,80},{208,... | collective-permute-start | bytes 175112 | tf_op jit(solution)/shard_map/ppermute | solution.py:198
  38.4 1.9 %collective-permute-start.6 = (bf16[4,7296]{1,0:T(4,128)(2,1)S(1)}, bf16[4,7296]{1,0:T(4,128)(2,1)S(1)}, u32[]{:S(2)}, u32[]{:S(2)}) collective-permute-start(bf16[4,7296]{1,0:T(4,128)(2,1)S(1)} %copy-done.8), channel_id=1, source_target_pairs={{0,208},{16,192},{64,16},{80,0},{128,80},{144,64},{192,144},{208,1... | collective-permute-start | bytes 175112 | tf_op jit(solution)/shard_map/ppermute | solution.py:198
  40.3 4.0 %collective-permute-done.4 = bf16[4,7296]{1,0:T(4,128)(2,1)S(1)} collective-permute-done((bf16[4,7296]{1,0:T(4,128)(2,1)S(1)}, bf16[4,7296]{1,0:T(4,128)(2,1)S(1)}, u32[]{:S(2)}, u32[]{:S(2)}) %collective-permute-start.4) | collective-permute-done | bytes 58400 | tf_op jit(solution)/shard_map/ppermute | solution.py:198
  46.2 1.9 %fusion.1 = bf16[16,8,7168]{2,1,0:T(8,128)(2,1)} fusion(pred[128,16]{1,0:T(32,128)(4,1)S(1)} %and.54, bf16[4,7296]{1,0:T(4,128)(2,1)S(1)} %collective-permute-done.6, bf16[4,7296]{1,0:T(4,128)(2,1)S(1)} %collective-permute-done.5, bf16[4,7296]{1,0:T(4,128)(2,1)S(1)} %collective-permute-done.4, bf16[4,7296]{1,0:T(4,128)(2,1)S(1)} %collective-permute-done.3), kind=kOutput, calls=%fused_computation.3 | convolution fusion | flops 31195136 | bytes 2070528 | tf_op jit(solution)/shard_map/dot_general | solution.py:213
  48.1 8.4 %all-to-all-done = bf16[16,8,7168]{2,1,0:T(8,128)(2,1)} async-done(((bf16[16,8,7168]{2,1,0:T(8,128)(2,1)}), bf16[16,8,7168]{2,1,0:T(8,128)(2,1)}, u32[]{:S(2)}, u32[]{:S(2)}) %all-to-all-start) | async-done | bytes 1835040 | tf_op jit(solution)/shard_map/all_to_all | solution.py:217
  56.5 3.7 %all-to-all-start.1 = ((bf16[16,8,7168]{2,1,0:T(8,128)(2,1)}), bf16[16,8,7168]{2,1,0:T(8,128)(2,1)S(1)}, u32[]{:S(2)}, u32[]{:S(2)}) async-start(bf16[16,8,7168]{2,1,0:T(8,128)(2,1)} %fusion.1), calls=%async_computation.1 | async-start | bytes 3670016 | tf_op jit(solution)/shard_map/all_to_all | solution.py:217
  60.6 3.1 %copy-done.1 = bf16[1,2,7168,256]{3,2,1,0:T(8,128)(2,1)S(1)} copy-done((bf16[1,2,7168,256]{3,2,1,0:T(8,128)(2,1)S(1)}, bf16[1,2,7168,256]{3,2,1,0:T(8,128)(2,1)}, u32[]{:S(2)}) %copy-start.1) | copy-done | bytes 7340056
  63.7 4.2 %shard_map.123.p0 = bf16[256,256]{1,0:T(8,128)(2,1)S(1)} custom-call(s32[3]{0:T(128)S(1)} %pad_add_fusion.place_ref, bf16[128,7168]{1,0:T(8,128)(2,1)} %bitcast.15.own_ref, bf16[128,7168]{1,0:T(8,128)(2,1)} %collective-permute-done.7.other_ref, bf16[2,7168,256]{2,1,0:T(8,128)(2,1)S(1)} %bitcast.62), custom_call_target="tpu_custom_call" | custom-call | flops 1879048192 | bytes 11010048 | tf_op jit(solution)/shard_map/pallas_call | solution.py:92
  68.0 2.0 %collective-permute-start.8 = (bf16[256,256]{1,0:T(8,128)(2,1)S(1)}, bf16[256,256]{1,0:T(8,128)(2,1)S(1)}, u32[]{:S(2)}, u32[]{:S(2)}) collective-permute-start(bf16[256,256]{1,0:T(8,128)(2,1)S(1)} %shard_map.123.p0), channel_id=1, source_target_pairs={{0,64},{16,80},{64,128},{80,144},{128,192},{144,208},{192,0},{208,... | collective-permute-start | bytes 393224 | tf_op jit(solution)/shard_map/ppermute | solution.py:198
  73.2 6.7 %collective-permute-done.10.p3 = bf16[256,256]{1,0:T(8,128)(2,1)S(1)} collective-permute-done((bf16[256,256]{1,0:T(8,128)(2,1)S(1)}, bf16[256,256]{1,0:T(8,128)(2,1)S(1)}, u32[]{:S(2)}, u32[]{:S(2)}) %collective-permute-start.10) | collective-permute-done | bytes 131104 | tf_op jit(solution)/shard_map/ppermute | solution.py:198
  84.4 2.0 %copy-done.3 = bf16[1,2048,896]{2,1,0:T(8,128)(2,1)S(1)} copy-done((bf16[1,2048,896]{2,1,0:T(8,128)(2,1)S(1)}, bf16[1,2048,896]{2,1,0:T(8,128)(2,1)}, u32[]{:S(2)}) %copy-start.3) | copy-done | bytes 3670040
  86.4 3.1 %shard_map.124 = bf16[256,896]{1,0:T(8,128)(2,1)} custom-call(s32[3]{0:T(128)S(1)} %pad_add_fusion.place_ref, bf16[256,256]{1,0:T(8,128)(2,1)S(1)} %shard_map.123.p0, bf16[256,256]{1,0:T(8,128)(2,1)S(1)} %collective-permute-done.8.p1, bf16[256,256]{1,0:T(8,128)(2,1)S(1)} %collective-permute-done.9.p2, bf16[256,256]{1,0:T(8,128)(2,1)S(1)} %collective-permute-done.10.p3, ...), custom_call_target="tpu_custom_call" | custom-call | flops 939524096 | bytes 4718592 | tf_op jit(solution)/shard_map/pallas_call | solution.py:116
  90.1 6.9 %all-to-all-start.2 = ((bf16[16,16,896]{2,1,0:T(8,128)(2,1)}), bf16[16,16,896]{2,1,0:T(8,128)(2,1)S(1)}, u32[]{:S(2)}, u32[]{:S(2)}) async-start(bf16[16,16,896]{2,1,0:T(8,128)(2,1)} %bitcast.18), calls=%async_computation.3 | async-start | bytes 917504 | tf_op jit(solution)/shard_map/all_to_all | solution.py:217
  97.0 3.1 %copy-done.2 = bf16[1,2,7168,256]{3,2,1,0:T(8,128)(2,1)S(1)} copy-done((bf16[1,2,7168,256]{3,2,1,0:T(8,128)(2,1)S(1)}, bf16[1,2,7168,256]{3,2,1,0:T(8,128)(2,1)}, u32[]{:S(2)}) %copy-start.2) | copy-done | bytes 7340056
  100.1 3.6 %shard_map.125.p0 = bf16[256,256]{1,0:T(8,128)(2,1)S(1)} custom-call(s32[3]{0:T(128)S(1)} %pad_add_fusion.place_ref, bf16[128,7168]{1,0:T(8,128)(2,1)S(1)} %bitcast.67, bf16[128,7168]{1,0:T(8,128)(2,1)} %collective-permute-done.14.other_ref, bf16[2,7168,256]{2,1,0:T(8,128)(2,1)S(1)} %bitcast.63), custom_call_target="tpu_custom_call" | custom-call | flops 1879048192 | bytes 11010048 | tf_op jit(solution)/shard_map/pallas_call | solution.py:92
  105.2 4.3 %collective-permute-start.16 = (bf16[256,256]{1,0:T(8,128)(2,1)S(1)}, bf16[256,256]{1,0:T(8,128)(2,1)S(1)}, u32[]{:S(2)}, u32[]{:S(2)}) collective-permute-start(bf16[256,256]{1,0:T(8,128)(2,1)S(1)} %shard_map.125.p0), channel_id=1, source_target_pairs={{0,128},{16,144},{64,192},{80,208},{128,0},{144,16},{192,64},{208,... | collective-permute-start | bytes 393224 | tf_op jit(solution)/shard_map/ppermute | solution.py:198
  109.5 2.0 %collective-permute-done.15.p1 = bf16[256,256]{1,0:T(8,128)(2,1)S(1)} collective-permute-done((bf16[256,256]{1,0:T(8,128)(2,1)S(1)}, bf16[256,256]{1,0:T(8,128)(2,1)S(1)}, u32[]{:S(2)}, u32[]{:S(2)}) %collective-permute-start.15) | collective-permute-done | bytes 131104 | tf_op jit(solution)/shard_map/ppermute | solution.py:198
  111.4 5.9 %collective-permute-done.16.p2 = bf16[256,256]{1,0:T(8,128)(2,1)S(1)} collective-permute-done((bf16[256,256]{1,0:T(8,128)(2,1)S(1)}, bf16[256,256]{1,0:T(8,128)(2,1)S(1)}, u32[]{:S(2)}, u32[]{:S(2)}) %collective-permute-start.16) | collective-permute-done | bytes 131104 | tf_op jit(solution)/shard_map/ppermute | solution.py:198
  117.3 2.9 %collective-permute-done.17.p3 = bf16[256,256]{1,0:T(8,128)(2,1)S(1)} collective-permute-done((bf16[256,256]{1,0:T(8,128)(2,1)S(1)}, bf16[256,256]{1,0:T(8,128)(2,1)S(1)}, u32[]{:S(2)}, u32[]{:S(2)}) %collective-permute-start.17) | collective-permute-done | bytes 131104 | tf_op jit(solution)/shard_map/ppermute | solution.py:198
  122.4 2.0 %copy-done.4 = bf16[1,2048,896]{2,1,0:T(8,128)(2,1)S(1)} copy-done((bf16[1,2048,896]{2,1,0:T(8,128)(2,1)S(1)}, bf16[1,2048,896]{2,1,0:T(8,128)(2,1)}, u32[]{:S(2)}) %copy-start.4) | copy-done | bytes 3670040
  124.4 2.6 %shard_map.126 = bf16[256,896]{1,0:T(8,128)(2,1)} custom-call(s32[3]{0:T(128)S(1)} %pad_add_fusion.place_ref, bf16[256,256]{1,0:T(8,128)(2,1)S(1)} %shard_map.125.p0, bf16[256,256]{1,0:T(8,128)(2,1)S(1)} %collective-permute-done.15.p1, bf16[256,256]{1,0:T(8,128)(2,1)S(1)} %collective-permute-done.16.p2, bf16[256,256]{1,0:T(8,128)(2,1)S(1)} %collective-permute-done.17.p3, ...), custom_call_target="tpu_custom_call" | custom-call | flops 939524096 | bytes 4718592 | tf_op jit(solution)/shard_map/pallas_call | solution.py:116
  127.0 6.9 %all-to-all-start.3 = ((bf16[16,16,896]{2,1,0:T(8,128)(2,1)}), bf16[16,16,896]{2,1,0:T(8,128)(2,1)S(1)}, u32[]{:S(2)}, u32[]{:S(2)}) async-start(bf16[16,16,896]{2,1,0:T(8,128)(2,1)} %bitcast.27), calls=%async_computation.4 | async-start | bytes 917504 | tf_op jit(solution)/shard_map/all_to_all | solution.py:217
  133.9 10.7 %reduce-scatter.2.cloned.1.call-done = f32[32,640]{1,0:T(8,128)} async-done(((f32[128,640]{1,0:T(8,128)}), f32[32,640]{1,0:T(8,128)}) %reduce-scatter.2.cloned.1.call-update) | async-done | bytes 81936 | tf_op jit(solution)/shard_map/reduce_scatter | solution.py:241
  146.3 2.7 %shard_map.127 = bf16[64,896]{1,0:T(8,128)(2,1)} custom-call(s32[3]{0:T(128)} %copy-done.5, bf16[256,896]{1,0:T(8,128)(2,1)} %bitcast.68, bf16[256,896]{1,0:T(8,128)(2,1)} %bitcast.69, bf16[16,128]{1,0:T(8,128)(2,1)} %copy-done.11, bf16[16,128]{1,0:T(8,128)(2,1)} %copy-done.12, bf16[16,128]{1,0:T(8,128)(2,1)} %copy-done.14, bf16[16,128]{1,0:T(8,128)(2,1)} %copy-done.15), custom_call_target="tpu_custom_call" | custom-call | flops 176160768 | bytes 1048576 | tf_op jit(solution)/shard_map/pallas_call | solution.py:163
  150.5 7.8 %all-to-all-start.4 = ((bf16[16,4,896]{2,1,0:T(4,128)(2,1)}), bf16[16,4,896]{2,1,0:T(4,128)(2,1)S(1)}, u32[]{:S(2)}, u32[]{:S(2)}) async-start(bf16[16,4,896]{2,1,0:T(4,128)(2,1)} %reshape.134), calls=%async_computation.5 | async-start | bytes 229376 | tf_op jit(solution)/shard_map/all_to_all | solution.py:249
  159.9 6.6 %all-to-all-done.4 = bf16[16,4,896]{2,1,0:T(4,128)(2,1)S(1)} async-done(((bf16[16,4,896]{2,1,0:T(4,128)(2,1)}), bf16[16,4,896]{2,1,0:T(4,128)(2,1)S(1)}, u32[]{:S(2)}, u32[]{:S(2)}) %all-to-all-start.4) | async-done | bytes 114720 | tf_op jit(solution)/shard_map/all_to_all | solution.py:249
  (93 shorter events, 24.3 us)
Async XLA Ops:
  7.2 73.9 %copy-start = (bf16[1,1024,512]{2,1,0:T(8,128)(2,1)S(1)}, bf16[1,1024,512]{2,1,0:T(8,128)(2,1)}, u32[]{:S(2)}) copy-start(bf16[1,1024,512]{2,1,0:T(8,128)(2,1)} %param.13) | copy-start | bytes 3145732
  8.9 5.3 %collective-permute-start = (bf16[4,7296]{1,0:T(4,128)(2,1)}, bf16[4,7296]{1,0:T(4,128)(2,1)S(1)}, u32[]{:S(2)}, u32[]{:S(2)}) collective-permute-start(bf16[4,7296]{1,0:T(4,128)(2,1)} %shard_map.122), channel_id=1, source_target_pairs={{0,64},{16,80},{64,128},{80,144},{128,192},{144,208},{192,0},{208,... | collective-permute-start | bytes 175112 | tf_op jit(solution)/shard_map/ppermute | solution.py:198
  10.8 5.8 %collective-permute-start.1 = (bf16[4,7296]{1,0:T(4,128)(2,1)}, bf16[4,7296]{1,0:T(4,128)(2,1)S(1)}, u32[]{:S(2)}, u32[]{:S(2)}) collective-permute-start(bf16[4,7296]{1,0:T(4,128)(2,1)} %shard_map.122), channel_id=1, source_target_pairs={{0,128},{16,144},{64,192},{80,208},{128,0},{144,16},{192,64},{208,... | collective-permute-start | bytes 175112 | tf_op jit(solution)/shard_map/ppermute | solution.py:198
  13.1 5.0 %collective-permute-start.2 = (bf16[4,7296]{1,0:T(4,128)(2,1)}, bf16[4,7296]{1,0:T(4,128)(2,1)S(1)}, u32[]{:S(2)}, u32[]{:S(2)}) collective-permute-start(bf16[4,7296]{1,0:T(4,128)(2,1)} %shard_map.122), channel_id=1, source_target_pairs={{0,192},{16,208},{64,0},{80,16},{128,64},{144,80},{192,128},{208,1... | collective-permute-start | bytes 175112 | tf_op jit(solution)/shard_map/ppermute | solution.py:198
  18.8 65.0 %copy-start.11 = (bf16[16,128]{1,0:T(8,128)(2,1)}, bf16[16,128]{1,0:T(8,128)(2,1)S(1)}, u32[]{:S(2)}) copy-start(bf16[16,128]{1,0:T(8,128)(2,1)S(1)} %pad_maximum_fusion.16.mine0) | copy-start | bytes 12292
  22.0 34.4 %all-to-all-start = ((bf16[16,8,7168]{2,1,0:T(8,128)(2,1)}), bf16[16,8,7168]{2,1,0:T(8,128)(2,1)}, u32[]{:S(2)}, u32[]{:S(2)}) async-start(bf16[16,8,7168]{2,1,0:T(8,128)(2,1)} %fusion), calls=%async_computation | async-start | bytes 3670016 | tf_op jit(solution)/shard_map/all_to_all | solution.py:217
  29.3 11.1 %collective-permute-start.3 = (bf16[4,7296]{1,0:T(4,128)(2,1)S(1)}, bf16[4,7296]{1,0:T(4,128)(2,1)S(1)}, u32[]{:S(2)}, u32[]{:S(2)}) collective-permute-start(bf16[4,7296]{1,0:T(4,128)(2,1)S(1)} %copy-done.8), channel_id=1, source_target_pairs={{0,16},{16,0},{64,80},{80,64},{128,144},{144,128},{192,208},{208,1... | collective-permute-start | bytes 175112 | tf_op jit(solution)/shard_map/ppermute | solution.py:198
  35.3 9.1 %collective-permute-start.4 = (bf16[4,7296]{1,0:T(4,128)(2,1)S(1)}, bf16[4,7296]{1,0:T(4,128)(2,1)S(1)}, u32[]{:S(2)}, u32[]{:S(2)}) collective-permute-start(bf16[4,7296]{1,0:T(4,128)(2,1)S(1)} %copy-done.8), channel_id=1, source_target_pairs={{0,80},{16,64},{64,144},{80,128},{128,208},{144,192},{192,16},{208... | collective-permute-start | bytes 175112 | tf_op jit(solution)/shard_map/ppermute | solution.py:198
  35.3 9.1 %collective-permute-start.5 = (bf16[4,7296]{1,0:T(4,128)(2,1)S(1)}, bf16[4,7296]{1,0:T(4,128)(2,1)S(1)}, u32[]{:S(2)}, u32[]{:S(2)}) collective-permute-start(bf16[4,7296]{1,0:T(4,128)(2,1)S(1)} %copy-done.8), channel_id=1, source_target_pairs={{0,144},{16,128},{64,208},{80,192},{128,16},{144,0},{192,80},{208,... | collective-permute-start | bytes 175112 | tf_op jit(solution)/shard_map/ppermute | solution.py:198
  38.4 7.2 %collective-permute-start.6 = (bf16[4,7296]{1,0:T(4,128)(2,1)S(1)}, bf16[4,7296]{1,0:T(4,128)(2,1)S(1)}, u32[]{:S(2)}, u32[]{:S(2)}) collective-permute-start(bf16[4,7296]{1,0:T(4,128)(2,1)S(1)} %copy-done.8), channel_id=1, source_target_pairs={{0,208},{16,192},{64,16},{80,0},{128,80},{144,64},{192,144},{208,1... | collective-permute-start | bytes 175112 | tf_op jit(solution)/shard_map/ppermute | solution.py:198
  45.6 38.6 %copy-start.12 = (bf16[16,128]{1,0:T(8,128)(2,1)}, bf16[16,128]{1,0:T(8,128)(2,1)S(1)}, u32[]{:S(2)}) copy-start(bf16[16,128]{1,0:T(8,128)(2,1)S(1)} %pad_maximum_fusion.15.mine1) | copy-start | bytes 12292
  56.5 4.1 %collective-permute-start.7 = (bf16[128,7168]{1,0:T(8,128)(2,1)}, bf16[128,7168]{1,0:T(8,128)(2,1)}, u32[]{:S(2)}, u32[]{:S(2)}) collective-permute-start(bf16[128,7168]{1,0:T(8,128)(2,1)} %bitcast.15.own_ref), channel_id=1, source_target_pairs={{0,32},{32,0},{1,33},{33,1},{2,34},{34,2},{3,35},{35,3},{4,36},{36... | collective-permute-start | bytes 5505032 | tf_op jit(solution)/shard_map/ppermute | solution.py:221
  56.5 33.1 %all-to-all-start.1 = ((bf16[16,8,7168]{2,1,0:T(8,128)(2,1)}), bf16[16,8,7168]{2,1,0:T(8,128)(2,1)S(1)}, u32[]{:S(2)}, u32[]{:S(2)}) async-start(bf16[16,8,7168]{2,1,0:T(8,128)(2,1)} %fusion.1), calls=%async_computation.1 | async-start | bytes 3670016 | tf_op jit(solution)/shard_map/all_to_all | solution.py:217
  60.3 62.1 %copy-start.5 = (s32[3]{0:T(128)}, s32[3]{0:T(128)S(1)}, u32[]{:S(2)}) copy-start(s32[3]{0:T(128)S(1)} %pad_add_fusion.place_ref) | copy-start | bytes 40
  63.7 17.3 %copy-start.9 = (bf16[1,128,512]{2,1,0:T(8,128)(2,1)S(1)}, bf16[1,128,512]{2,1,0:T(8,128)(2,1)}, u32[]{:S(2)}) copy-start(bf16[1,128,512]{2,1,0:T(8,128)(2,1)} %param.11) | copy-start | bytes 393220
  67.9 12.0 %collective-permute-start.10 = (bf16[256,256]{1,0:T(8,128)(2,1)S(1)}, bf16[256,256]{1,0:T(8,128)(2,1)S(1)}, u32[]{:S(2)}, u32[]{:S(2)}) collective-permute-start(bf16[256,256]{1,0:T(8,128)(2,1)S(1)} %shard_map.123.p0), channel_id=1, source_target_pairs={{0,192},{16,208},{64,0},{80,16},{128,64},{144,80},{192,128},{208,1... | collective-permute-start | bytes 393224 | tf_op jit(solution)/shard_map/ppermute | solution.py:198
  68.0 11.9 %collective-permute-start.8 = (bf16[256,256]{1,0:T(8,128)(2,1)S(1)}, bf16[256,256]{1,0:T(8,128)(2,1)S(1)}, u32[]{:S(2)}, u32[]{:S(2)}) collective-permute-start(bf16[256,256]{1,0:T(8,128)(2,1)S(1)} %shard_map.123.p0), channel_id=1, source_target_pairs={{0,64},{16,80},{64,128},{80,144},{128,192},{144,208},{192,0},{208,... | collective-permute-start | bytes 393224 | tf_op jit(solution)/shard_map/ppermute | solution.py:198
  70.0 10.2 %collective-permute-start.9 = (bf16[256,256]{1,0:T(8,128)(2,1)S(1)}, bf16[256,256]{1,0:T(8,128)(2,1)S(1)}, u32[]{:S(2)}, u32[]{:S(2)}) collective-permute-start(bf16[256,256]{1,0:T(8,128)(2,1)S(1)} %shard_map.123.p0), channel_id=1, source_target_pairs={{0,128},{16,144},{64,192},{80,208},{128,0},{144,16},{192,64},{208,... | collective-permute-start | bytes 393224 | tf_op jit(solution)/shard_map/ppermute | solution.py:198
  81.0 3.4 %collective-permute-start.11 = (bf16[256,1024]{1,0:T(8,128)(2,1)}, bf16[256,1024]{1,0:T(8,128)(2,1)}, u32[]{:S(2)}, u32[]{:S(2)}) collective-permute-start(bf16[256,1024]{1,0:T(8,128)(2,1)} %pad_maximum_fusion), channel_id=1, source_target_pairs={{0,32},{32,0},{1,33},{33,1},{2,34},{34,2},{3,35},{35,3},{4,36},{36... | collective-permute-start | bytes 1572872 | tf_op jit(solution)/shard_map/ppermute | solution.py:225
  83.8 5.7 %collective-permute-start.12 = (bf16[16,128]{1,0:T(8,128)(2,1)S(1)}, bf16[16,128]{1,0:T(8,128)(2,1)S(1)}, u32[]{:S(2)}, u32[]{:S(2)}) collective-permute-start(bf16[16,128]{1,0:T(8,128)(2,1)S(1)} %pad_maximum_fusion.16.mine0), channel_id=1, source_target_pairs={{0,32},{32,0},{1,33},{33,1},{2,34},{34,2},{3,35},{35,3},{4,36},{36... | collective-permute-start | bytes 12296 | tf_op jit(solution)/shard_map/ppermute | solution.py:236
  84.3 5.2 %collective-permute-start.13 = (bf16[16,128]{1,0:T(8,128)(2,1)S(1)}, bf16[16,128]{1,0:T(8,128)(2,1)S(1)}, u32[]{:S(2)}, u32[]{:S(2)}) collective-permute-start(bf16[16,128]{1,0:T(8,128)(2,1)S(1)} %pad_maximum_fusion.15.mine1), channel_id=1, source_target_pairs={{0,32},{32,0},{1,33},{33,1},{2,34},{34,2},{3,35},{35,3},{4,36},{36... | collective-permute-start | bytes 12296 | tf_op jit(solution)/shard_map/ppermute | solution.py:237
  89.5 14.2 %copy-start.14 = (bf16[16,128]{1,0:T(8,128)(2,1)}, bf16[16,128]{1,0:T(8,128)(2,1)S(1)}, u32[]{:S(2)}) copy-start(bf16[16,128]{1,0:T(8,128)(2,1)S(1)} %collective-permute-done.12.theirs0) | copy-start | bytes 12292
  89.5 14.2 %copy-start.15 = (bf16[16,128]{1,0:T(8,128)(2,1)}, bf16[16,128]{1,0:T(8,128)(2,1)S(1)}, u32[]{:S(2)}) copy-start(bf16[16,128]{1,0:T(8,128)(2,1)S(1)} %collective-permute-done.13.theirs1) | copy-start | bytes 12292
  89.5 7.5 %collective-permute-start.14 = (bf16[128,7168]{1,0:T(8,128)(2,1)S(1)}, bf16[128,7168]{1,0:T(8,128)(2,1)}, u32[]{:S(2)}, u32[]{:S(2)}) collective-permute-start(bf16[128,7168]{1,0:T(8,128)(2,1)S(1)} %bitcast.66), channel_id=1, source_target_pairs={{0,32},{32,0},{1,33},{33,1},{2,34},{34,2},{3,35},{35,3},{4,36},{36... | collective-permute-start | bytes 5505032 | tf_op jit(solution)/shard_map/ppermute | solution.py:221
  90.1 30.3 %all-to-all-start.2 = ((bf16[16,16,896]{2,1,0:T(8,128)(2,1)}), bf16[16,16,896]{2,1,0:T(8,128)(2,1)S(1)}, u32[]{:S(2)}, u32[]{:S(2)}) async-start(bf16[16,16,896]{2,1,0:T(8,128)(2,1)} %bitcast.18), calls=%async_computation.3 | async-start | bytes 917504 | tf_op jit(solution)/shard_map/all_to_all | solution.py:217
  96.9 47.7 %reduce-scatter.2.cloned.1.call-start = ((), (), s32[]{:S(2)}) async-start(), calls=%async_computation.6 | async-start | bytes 409600 | tf_op jit(solution)/shard_map/reduce_scatter | solution.py:241
  103.7 7.7 %collective-permute-start.15 = (bf16[256,256]{1,0:T(8,128)(2,1)S(1)}, bf16[256,256]{1,0:T(8,128)(2,1)S(1)}, u32[]{:S(2)}, u32[]{:S(2)}) collective-permute-start(bf16[256,256]{1,0:T(8,128)(2,1)S(1)} %shard_map.125.p0), channel_id=1, source_target_pairs={{0,64},{16,80},{64,128},{80,144},{128,192},{144,208},{192,0},{208,... | collective-permute-start | bytes 393224 | tf_op jit(solution)/shard_map/ppermute | solution.py:198
  105.2 12.2 %collective-permute-start.16 = (bf16[256,256]{1,0:T(8,128)(2,1)S(1)}, bf16[256,256]{1,0:T(8,128)(2,1)S(1)}, u32[]{:S(2)}, u32[]{:S(2)}) collective-permute-start(bf16[256,256]{1,0:T(8,128)(2,1)S(1)} %shard_map.125.p0), channel_id=1, source_target_pairs={{0,128},{16,144},{64,192},{80,208},{128,0},{144,16},{192,64},{208,... | collective-permute-start | bytes 393224 | tf_op jit(solution)/shard_map/ppermute | solution.py:198
  109.5 10.8 %collective-permute-start.17 = (bf16[256,256]{1,0:T(8,128)(2,1)S(1)}, bf16[256,256]{1,0:T(8,128)(2,1)S(1)}, u32[]{:S(2)}, u32[]{:S(2)}) collective-permute-start(bf16[256,256]{1,0:T(8,128)(2,1)S(1)} %shard_map.125.p0), channel_id=1, source_target_pairs={{0,192},{16,208},{64,0},{80,16},{128,64},{144,80},{192,128},{208,1... | collective-permute-start | bytes 393224 | tf_op jit(solution)/shard_map/ppermute | solution.py:198
  120.4 2.0 %collective-permute-start.18 = (bf16[256,1024]{1,0:T(8,128)(2,1)S(1)}, bf16[256,1024]{1,0:T(8,128)(2,1)S(1)}, u32[]{:S(2)}, u32[]{:S(2)}) collective-permute-start(bf16[256,1024]{1,0:T(8,128)(2,1)S(1)} %pad_maximum_fusion.1), channel_id=1, source_target_pairs={{0,32},{32,0},{1,33},{33,1},{2,34},{34,2},{3,35},{35,3},{4,36},{36... | collective-permute-start | bytes 1572872 | tf_op jit(solution)/shard_map/ppermute | solution.py:225
  127.0 18.5 %all-to-all-start.3 = ((bf16[16,16,896]{2,1,0:T(8,128)(2,1)}), bf16[16,16,896]{2,1,0:T(8,128)(2,1)S(1)}, u32[]{:S(2)}, u32[]{:S(2)}) async-start(bf16[16,16,896]{2,1,0:T(8,128)(2,1)} %bitcast.27), calls=%async_computation.4 | async-start | bytes 917504 | tf_op jit(solution)/shard_map/all_to_all | solution.py:217
  150.5 15.9 %all-to-all-start.4 = ((bf16[16,4,896]{2,1,0:T(4,128)(2,1)}), bf16[16,4,896]{2,1,0:T(4,128)(2,1)S(1)}, u32[]{:S(2)}, u32[]{:S(2)}) async-start(bf16[16,4,896]{2,1,0:T(4,128)(2,1)} %reshape.134), calls=%async_computation.5 | async-start | bytes 229376 | tf_op jit(solution)/shard_map/all_to_all | solution.py:249
  (9 other events, 40.6 us)
Sparse Core Ops, SparseCore 0:
  120.6 23.9 reduce-scatter.1

commit v3 on v2

--- a/solution.py
+++ b/solution.py
@@ -33,7 +33,12 @@
 
 VMEM = pl.BlockSpec(memory_space=pltpu.VMEM)
 SMEM = pl.BlockSpec(memory_space=pltpu.SMEM)
-ROOM = pltpu.CompilerParams(vmem_limit_bytes=40 * 1024 * 1024)
+ANY = pl.BlockSpec(memory_space=pl.ANY)
+CUTS = (0, 1024, 3072, 7168)
+
+
+def room(mib):
+    return pltpu.CompilerParams(vmem_limit_bytes=mib * 1024 * 1024)
 
 
 def prepare_kernel(ids_ref, gates_ref, rows_ref, gain_ref, out_ref):
@@ -72,13 +77,67 @@
         out_shape=jax.ShapeDtypeStruct((TOK, moe_rows.shape[1] + INFO), bf16),
         in_specs=[SMEM, SMEM, VMEM, VMEM],
         out_specs=VMEM,
+        compiler_params=room(4),
     )(route_ids, route_gates, moe_rows, norm_gain)
 
 
-def gate_up_kernel(place_ref, own_ref, other_ref, weight_ref, out_ref):
-    rows = jnp.concatenate([own_ref[...], other_ref[...]], axis=0)
-    gate = jnp.dot(rows, weight_ref[0], preferred_element_type=f32)
-    up = jnp.dot(rows, weight_ref[1], preferred_element_type=f32)
+def choose_kernel(place_ref, facts_ref, tokens_ref, out_ref, selector_ref):
+    @pl.when(pl.program_id(0) == 0)
+    def _():
+        ctx, half = place_ref[0], place_ref[2]
+
+        def grid(rows, columns, dim):
+            return lax.broadcasted_iota(jnp.int32, (rows, columns), dim)
+
+        first = grid(16, 16, 1) == grid(16, 16, 0) // TOK * TOK
+        tokens = jnp.dot(first.astype(f32).astype(bf16), facts_ref[...], preferred_element_type=f32)
+        row = grid(128, 128, 0)
+        lane = half * 32 + row // 8 * SLOTS + row % SLOTS
+        pick = (grid(128, 128, 1) == lane).astype(f32).astype(bf16)
+        wanted = lax.dot_general(
+            pick, tokens.astype(bf16), (((1,), (1,)), ((), ())), preferred_element_type=f32
+        )
+        row, column = grid(128, 16, 0), grid(128, 16, 1)
+        hit = wanted == (column % TOK).astype(f32)
+        hit = hit & ((ctx - column // TOK + 4) % 4 == row // SLOTS % 4)
+        selector_ref[...] = hit.astype(f32).astype(bf16)
+
+    out_ref[...] = jnp.dot(
+        selector_ref[...], tokens_ref[...], preferred_element_type=f32
+    ).astype(bf16)
+
+
+def choose(place, tokens, width):
+    block = 1024
+    return pl.pallas_call(
+        choose_kernel,
+        out_shape=jax.ShapeDtypeStruct((128, width), bf16),
+        grid=(width // block,),
+        in_specs=[
+            SMEM,
+            pl.BlockSpec((4 * TOK, INFO), lambda k: (0, width // INFO)),
+            pl.BlockSpec((4 * TOK, block), lambda k: (0, k)),
+        ],
+        out_specs=pl.BlockSpec((128, block), lambda k: (0, k)),
+        scratch_shapes=[pltpu.VMEM((128, 4 * TOK), bf16)],
+        compiler_params=room(6),
+        cost_estimate=pl.CostEstimate(flops=2 * 128 * 16 * width, bytes_accessed=2 * 144 * width, transcendentals=0),
+    )(place, tokens, tokens)
+
+
+def gate_up_kernel(place_ref, own_ref, other_ref, weight_ref, out_ref, held_ref, sems):
+    copies = []
+    for i, (low, high) in enumerate(zip(CUTS[:-1], CUTS[1:])):
+        part = pl.ds(low, high - low)
+        copies.append(pltpu.make_async_copy(weight_ref.at[:, part], held_ref.at[:, part], sems.at[i]))
+        copies[-1].start()
+    gate = jnp.zeros((256, 256), f32)
+    up = jnp.zeros((256, 256), f32)
+    for copy, low, high in zip(copies, CUTS[:-1], CUTS[1:]):
+        rows = jnp.concatenate([own_ref[:, low:high], other_ref[:, low:high]], axis=0)
+        copy.wait()
+        gate += jnp.dot(rows, held_ref[0, low:high], preferred_element_type=f32)
+        up += jnp.dot(rows, held_ref[1, low:high], preferred_element_type=f32)
     hidden = gate / (1.0 + jnp.exp(-gate)) * up
     own, other = hidden[:128], hidden[128:]
     core = place_ref[1]
@@ -92,23 +151,29 @@
     return pl.pallas_call(
         gate_up_kernel,
         out_shape=jax.ShapeDtypeStruct((256, 256), bf16),
-        in_specs=[SMEM, VMEM, VMEM, VMEM],
+        in_specs=[SMEM, VMEM, VMEM, ANY],
         out_specs=VMEM,
-        compiler_params=ROOM,
+        scratch_shapes=[pltpu.VMEM((2, width, 256), bf16), pltpu.SemaphoreType.DMA((len(CUTS) - 1,))],
+        compiler_params=room(16),
         cost_estimate=pl.CostEstimate(
             flops=2 * 256 * width * 512, bytes_accessed=2 * width * (512 + 256), transcendentals=65536
         ),
     )(place, own, other, weight)
 
 
-def down_kernel(place_ref, p0, p1, p2, p3, theirs_ref, weight_ref, out_ref):
+def down_kernel(place_ref, p0, p1, p2, p3, theirs_ref, weight_ref, out_ref, held_ref, sems):
     ctx, core = place_ref[0], place_ref[1]
+    copies = []
+    for k in range(4):
+        source = (ctx - k + 4) % 4
+        copies.append(pltpu.make_async_copy(weight_ref.at[source], held_ref.at[k], sems.at[k]))
+        copies[-1].start()
     total = jnp.zeros(out_ref.shape, f32)
     for k, piece in enumerate((p0, p1, p2, p3)):
-        source = (ctx - k + 4) % 4
-        total += jnp.dot(piece[...], weight_ref[source, core], preferred_element_type=f32)
+        copies[k].wait()
+        total += jnp.dot(piece[...], held_ref[k, core], preferred_element_type=f32)
         theirs = theirs_ref[:, k * 256 : (k + 1) * 256]
-        total += jnp.dot(theirs, weight_ref[source, 1 - core], preferred_element_type=f32)
+        total += jnp.dot(theirs, held_ref[k, 1 - core], preferred_element_type=f32)
     out_ref[...] = total.astype(bf16)
 
 
@@ -116,9 +181,10 @@
     return pl.pallas_call(
         down_kernel,
         out_shape=jax.ShapeDtypeStruct((256, 896), bf16),
-        in_specs=[SMEM] + [VMEM] * 6,
+        in_specs=[SMEM] + [VMEM] * 5 + [ANY],
         out_specs=VMEM,
-        compiler_params=ROOM,
+        scratch_shapes=[pltpu.VMEM((4, 2, 256, 896), bf16), pltpu.SemaphoreType.DMA((4,))],
+        compiler_params=room(10),
         cost_estimate=pl.CostEstimate(
             flops=2 * 256 * 2048 * 896, bytes_accessed=2 * 2048 * 896 + 2 * 256 * 2048, transcendentals=0
         ),
@@ -137,7 +203,7 @@
 
     expert, _, _, slot = lanes(128)
     spread = (grid(128, 256, 0) == half * 32 + expert * SLOTS + slot).astype(f32).astype(bf16)
-    total = jnp.zeros(out_ref.shape, f32)
+    total = jnp.zeros((64, 896), f32)
     for q, (back, mine, theirs) in enumerate(((back0, mine0, theirs0), (back1, mine1, theirs1))):
         facts = jnp.concatenate([mine[...], theirs[...]], axis=0)
         facts = jnp.dot(facts, spread, preferred_element_type=f32)
@@ -156,15 +222,16 @@
         for part in (high, middle, low):
             matrix = jnp.where(fits, part, 0.0).astype(bf16)
             total += jnp.dot(matrix, back[...], preferred_element_type=f32)
-    out_ref[...] = total.astype(bf16)
+    out_ref[...] = total.reshape(16, TOK, 896).astype(bf16)
 
 
 def mix(place, back0, back1, mine0, mine1, theirs0, theirs1):
     return pl.pallas_call(
         mix_kernel,
-        out_shape=jax.ShapeDtypeStruct((64, 896), bf16),
+        out_shape=jax.ShapeDtypeStruct((16, TOK, 896), bf16),
         in_specs=[SMEM] + [VMEM] * 6,
         out_specs=VMEM,
+        compiler_params=room(6),
         cost_estimate=pl.CostEstimate(flops=2 * 64 * 512 * 896 * 3, bytes_accessed=1 << 20, transcendentals=0),
     )(place, back0, back1, mine0, mine1, theirs0, theirs1)
 
@@ -197,21 +264,13 @@
         ]
         return lax.ppermute(value, ("ctx", "zhi"), pairs)
 
-    origin = (c - jnp.arange(4, dtype=jnp.int32)) % 4
-    absolute = origin[None, :] == jnp.arange(4, dtype=jnp.int32)[:, None]
     gate_up_weight = expert_in[0]
     down_weight = expert_out[0].reshape(4, 2, 256, 896)
 
-    def choose(half):
+    def rows_of(half):
         tokens = jnp.concatenate(half, axis=0)
-        facts = tokens[:, width:]
-        wanted = facts.reshape(4, TOK, INFO)[:, 0].astype(f32)
-        wanted = jnp.where(h == 0, wanted[:, :32], wanted[:, 32:64]).reshape(4, 16, SLOTS)
-        number = jnp.arange(TOK, dtype=jnp.int32).astype(f32)
-        hit = wanted.transpose(1, 2, 0)[:, None, :, :, None] == number
-        selector = (hit & absolute[None, :, None, :, None]).astype(bf16).reshape(128, 4 * TOK)
-        rows = jnp.dot(selector, tokens[:, :width], preferred_element_type=f32).astype(bf16)
-        return rows.reshape(16, 4 * SLOTS, width), facts
+        rows = choose(place, tokens, width)
+        return rows.reshape(16, 4 * SLOTS, width), tokens[:, width:]
 
     def across(value):
         return lax.all_to_all(value, ("x", "y"), split_axis=0, concat_axis=0, tiled=True)
@@ -225,20 +284,20 @@
         theirs = lax.ppermute(joined, "att", swap_core)
         return down(place, pieces, theirs, down_weight).reshape(16, 16, 896)
 
-    rows0, facts0 = choose([payload] + [hop(payload, k, 0) for k in (1, 2, 3)])
+    rows0, facts0 = rows_of([payload] + [hop(payload, k, 0) for k in (1, 2, 3)])
     rows0, facts0, payload = lax.optimization_barrier((rows0, facts0, payload))
     got0 = across(rows0)
-    rows1, facts1 = choose([hop(payload, k, 1) for k in (0, 1, 2, 3)])
-    rows1, facts1, got0 = lax.optimization_barrier((rows1, facts1, got0))
+    rows1, facts1 = rows_of([hop(payload, k, 1) for k in (0, 1, 2, 3)])
+    part = attend(query_latent, query_rope, latent_cache, rope_keys, lengths)
+    rows1, facts1, got0, part = lax.optimization_barrier((rows1, facts1, got0, part))
+    summed = lax.psum_scatter(part, "ctx", scatter_dimension=0, tiled=True)
     got1 = across(rows1)
 
     pieces0 = hidden_of(got0)
     theirs0 = lax.ppermute(facts0, "att", swap_core)
     theirs1 = lax.ppermute(facts1, "att", swap_core)
-    part = attend(query_latent, query_rope, latent_cache, rope_keys, lengths)
     result0 = down_of(pieces0, jnp.concatenate(pieces0, axis=1))
-    got1, result0, part, theirs0, theirs1 = lax.optimization_barrier((got1, result0, part, theirs0, theirs1))
-    summed = lax.psum_scatter(part, "ctx", scatter_dimension=0, tiled=True)
+    got1, result0, theirs0, theirs1 = lax.optimization_barrier((got1, result0, theirs0, theirs1))
     back0 = across(result0)
     pieces1 = hidden_of(got1)
     joined1, back0 = lax.optimization_barrier((jnp.concatenate(pieces1, axis=1), back0))
@@ -246,8 +305,9 @@
     back1 = across(result1)
 
     outgoing = mix(place, back0.reshape(256, 896), back1.reshape(256, 896), facts0, facts1, theirs0, theirs1)
+    outgoing, summed = lax.optimization_barrier((outgoing, summed))
     final = lax.all_to_all(
-        outgoing.reshape(16, TOK, 896), ("ctx", "att", "zhi"), split_axis=0, concat_axis=0, tiled=True
+        outgoing, ("ctx", "att", "zhi"), split_axis=0, concat_axis=0, tiled=True
     )
     final = final.reshape(8, 2, TOK, 896).astype(f32)
     routed = (final[:, 0] + final[:, 1]).transpose(1, 0, 2).reshape(TOK, 8 * 896)

time: 177 us -> 175 us (0.989)
  blocking collectives: 0 us -> 17.8 us
  waiting for transfers between devices: 54.8 us -> 38.9 us
  Pallas kernels: 17.9 us -> 28.3 us
  starting transfers between devices: 59.5 us -> 53.8 us
  matrix products: 7.57 us -> 2.95 us
  local copies, waits for them, and re-layouts: 14.8 us -> 12.1 us
    all_to_all x0 -> x1, blocking collectives: none -> 17.8 us  [across(): lax.all_to_all(value, ('x', 'y'), split_axis=0, concat_axis=0, tiled=True)]
    reduce_scatter x1, waiting for transfers between devices: 10.7 us -> 0.01 us  [shards(): summed = lax.psum_scatter(part, 'ctx', scatter_dimension=0, tiled=True)]
    pallas_call x1 -> x3, Pallas kernels: 2.67 us -> 11.2 us  [the longest x2 9.18 us: choose(): pl.pallas_call(choose_kernel, out_shape=jax.ShapeDtypeStruct((128, width)...]
    all_to_all x4 -> x3, waiting for transfers between devices: 8.37 us -> 0.87 us  [across(): lax.all_to_all(value, ('x', 'y'), split_axis=0, concat_axis=0, tiled=True)]
    dot_general x2 -> x0, matrix products: 4.59 us -> none  [choose(): jnp.dot(selector, tokens[:, :width], preferred_element_type=f32)]
    all_to_all x4 -> x3, starting transfers between devices: 24.8 us -> 20.3 us  [across(): lax.all_to_all(value, ('x', 'y'), split_axis=0, concat_axis=0, tiled=True)]
    unnamed x35 -> x20, local copies, waits for them, and re-layouts: 12 us -> 11.2 us
  transfers between devices with their start and end apart: 25 -> 24, of which waited for: 14 -> 14; matrix products, arithmetic and copies ran while one was open for 6% -> 3% of each run, Pallas kernels for 8% -> 13%
where the time goes in v3:
time: 175 us; the launch traced here: 172 us
  starting transfers between devices  53.8 us (31%)
  waiting for transfers between devices  38.9 us (22%)
  Pallas kernels  28.3 us (16%)
  blocking collectives  17.8 us (10%)
  between operations  14.9 us (9%)
  local copies, waits for them, and re-layouts  12.1 us (7%)
  other arithmetic  3.43 us (2%)
  matrix products  2.95 us (2%)
    ppermute x13, waiting for transfers between devices, hop(): return lax.ppermute(value, ('ctx', 'zhi'), pairs)  28.4 us
    ppermute x13, starting transfers between devices, hop(): return lax.ppermute(value, ('ctx', 'zhi'), pairs)  24.6 us
    all_to_all x3, starting transfers between devices, across(): lax.all_to_all(value, ('x', 'y'), split_axis=0, concat_axis=0, tiled=True)  20.3 us
    all_to_all x1, blocking collectives, across(): lax.all_to_all(value, ('x', 'y'), split_axis=0, concat_axis=0, tiled=True)  17.8 us
    unnamed x20, local copies, waits for them, and re-layouts  11.2 us
    pallas_call x2, Pallas kernels, choose(): pl.pallas_call(choose_kernel, out_shape=jax.ShapeDtypeStruct((128, width)...  9.18 us
    pallas_call x2, Pallas kernels, gate_up(): pl.pallas_call(gate_up_kernel, out_shape=jax.ShapeDtypeStruct((256, 256),...  9.08 us
    all_to_all x1, starting transfers between devices, shards(): lax.all_to_all(outgoing, ('ctx', 'att', 'zhi'), split_axis=0, concat_axis...  7.76 us
  transfers between devices with their start and end apart: 24, of which 14 were waited for; matrix products, arithmetic and copies ran while one was open for 3% of the time, Pallas kernels for 13%

profile of v3, /device:TPU:32, one launch (start us, length us, event | category | flops | bytes accessed | tf_op | source)
XLA Modules:
  0.0 172.2 jit_solution(8387284422703756527)
XLA Ops:
  10.9 1.9 %collective-permute-start.2 = (bf16[4,7296]{1,0:T(4,128)(2,1)S(1)}, bf16[4,7296]{1,0:T(4,128)(2,1)S(1)}, u32[]{:S(2)}, u32[]{:S(2)}) collective-permute-start(bf16[4,7296]{1,0:T(4,128)(2,1)S(1)} %shard_map.122), channel_id=1, source_target_pairs={{0,192},{16,208},{64,0},{80,16},{128,64},{144,80},{192,128},{208,1... | collective-permute-start | bytes 175112 | tf_op jit(solution)/shard_map/ppermute | solution.py:265
  14.4 2.8 %collective-permute-start = (bf16[4,7296]{1,0:T(4,128)(2,1)S(1)}, bf16[4,7296]{1,0:T(4,128)(2,1)S(1)}, u32[]{:S(2)}, u32[]{:S(2)}) collective-permute-start(bf16[4,7296]{1,0:T(4,128)(2,1)S(1)} %shard_map.122), channel_id=1, source_target_pairs={{0,64},{16,80},{64,128},{80,144},{128,192},{144,208},{192,0},{208,... | collective-permute-start | bytes 175112 | tf_op jit(solution)/shard_map/ppermute | solution.py:265
  20.1 4.5 %shard_map.123 = bf16[128,7168]{1,0:T(8,128)(2,1)} custom-call(s32[3]{0:T(128)S(1)} %pad_add_fusion.place_ref, bf16[16,7296]{1,0:T(8,128)(2,1)S(1)} %pad_maximum_fusion.3.facts_ref.tokens_ref, bf16[16,7296]{1,0:T(8,128)(2,1)S(1)} %pad_maximum_fusion.3.facts_ref.tokens_ref), custom_call_target="tpu_custom_call" | custom-call | flops 29360128 | bytes 2064384 | tf_op jit(solution)/shard_map/pallas_call | solution.py:112
  24.6 7.2 %all-to-all-start = ((bf16[16,8,7168]{2,1,0:T(8,128)(2,1)}), bf16[16,8,7168]{2,1,0:T(8,128)(2,1)S(1)}, u32[]{:S(2)}, u32[]{:S(2)}) async-start(bf16[16,8,7168]{2,1,0:T(8,128)(2,1)} %bitcast.3), calls=%async_computation | async-start | bytes 3670016 | tf_op jit(solution)/shard_map/all_to_all | solution.py:276
  35.4 5.5 %collective-permute-start.6 = (bf16[4,7296]{1,0:T(4,128)(2,1)S(1)}, bf16[4,7296]{1,0:T(4,128)(2,1)S(1)}, u32[]{:S(2)}, u32[]{:S(2)}) collective-permute-start(bf16[4,7296]{1,0:T(4,128)(2,1)S(1)} %shard_map.122), channel_id=1, source_target_pairs={{0,208},{16,192},{64,16},{80,0},{128,80},{144,64},{192,144},{208,1... | collective-permute-start | bytes 175112 | tf_op jit(solution)/shard_map/ppermute | solution.py:265
  41.2 3.1 %collective-permute-start.4 = (bf16[4,7296]{1,0:T(4,128)(2,1)S(1)}, bf16[4,7296]{1,0:T(4,128)(2,1)S(1)}, u32[]{:S(2)}, u32[]{:S(2)}) collective-permute-start(bf16[4,7296]{1,0:T(4,128)(2,1)S(1)} %shard_map.122), channel_id=1, source_target_pairs={{0,80},{16,64},{64,144},{80,128},{128,208},{144,192},{192,16},{208... | collective-permute-start | bytes 175112 | tf_op jit(solution)/shard_map/ppermute | solution.py:265
  44.2 1.9 %collective-permute-start.3 = (bf16[4,7296]{1,0:T(4,128)(2,1)S(1)}, bf16[4,7296]{1,0:T(4,128)(2,1)S(1)}, u32[]{:S(2)}, u32[]{:S(2)}) collective-permute-start(bf16[4,7296]{1,0:T(4,128)(2,1)S(1)} %shard_map.122), channel_id=1, source_target_pairs={{0,16},{16,0},{64,80},{80,64},{128,144},{144,128},{192,208},{208,1... | collective-permute-start | bytes 175112 | tf_op jit(solution)/shard_map/ppermute | solution.py:265
  47.7 5.9 %collective-permute-done.4 = bf16[4,7296]{1,0:T(4,128)(2,1)S(1)} collective-permute-done((bf16[4,7296]{1,0:T(4,128)(2,1)S(1)}, bf16[4,7296]{1,0:T(4,128)(2,1)S(1)}, u32[]{:S(2)}, u32[]{:S(2)}) %collective-permute-start.4) | collective-permute-done | bytes 58400 | tf_op jit(solution)/shard_map/ppermute | solution.py:265
  53.8 4.6 %shard_map.124 = bf16[128,7168]{1,0:T(8,128)(2,1)} custom-call(s32[3]{0:T(128)S(1)} %pad_add_fusion.place_ref, bf16[16,7296]{1,0:T(8,128)(2,1)S(1)} %pad_maximum_fusion.4.facts_ref.tokens_ref, bf16[16,7296]{1,0:T(8,128)(2,1)S(1)} %pad_maximum_fusion.4.facts_ref.tokens_ref), custom_call_target="tpu_custom_call" | custom-call | flops 29360128 | bytes 2064384 | tf_op jit(solution)/shard_map/pallas_call | solution.py:112
  58.5 6.9 %all-to-all-start.1 = ((bf16[16,8,7168]{2,1,0:T(8,128)(2,1)}), bf16[16,8,7168]{2,1,0:T(8,128)(2,1)}, u32[]{:S(2)}, u32[]{:S(2)}) async-start(bf16[16,8,7168]{2,1,0:T(8,128)(2,1)} %bitcast.4), calls=%async_computation.1 | async-start | bytes 3670016 | tf_op jit(solution)/shard_map/all_to_all | solution.py:276
  65.4 3.1 %copy-done.1 = bf16[1,2,7168,256]{3,2,1,0:T(8,128)(2,1)S(1)} copy-done((bf16[1,2,7168,256]{3,2,1,0:T(8,128)(2,1)S(1)}, bf16[1,2,7168,256]{3,2,1,0:T(8,128)(2,1)}, u32[]{:S(2)}) %copy-start.1) | copy-done | bytes 7340056
  68.5 4.6 %shard_map.125.p0 = bf16[256,256]{1,0:T(8,128)(2,1)S(1)} custom-call(s32[3]{0:T(128)S(1)} %pad_add_fusion.place_ref, bf16[128,7168]{1,0:T(8,128)(2,1)S(1)} %bitcast.48, bf16[128,7168]{1,0:T(8,128)(2,1)} %collective-permute-done.7.other_ref, bf16[2,7168,256]{2,1,0:T(8,128)(2,1)S(1)} %bitcast.43), custom_call_target="tpu_custom_call" | custom-call | flops 1879048192 | bytes 11010048 | tf_op jit(solution)/shard_map/pallas_call | solution.py:151
  73.1 1.7 collective-permute-start.10
  76.7 3.3 %collective-permute-done.10.p3 = bf16[256,256]{1,0:T(8,128)(2,1)S(1)} collective-permute-done((bf16[256,256]{1,0:T(8,128)(2,1)S(1)}, bf16[256,256]{1,0:T(8,128)(2,1)S(1)}, u32[]{:S(2)}, u32[]{:S(2)}) %collective-permute-start.10) | collective-permute-done | bytes 131104 | tf_op jit(solution)/shard_map/ppermute | solution.py:265
  80.1 3.5 %collective-permute-done.9.p2 = bf16[256,256]{1,0:T(8,128)(2,1)S(1)} collective-permute-done((bf16[256,256]{1,0:T(8,128)(2,1)S(1)}, bf16[256,256]{1,0:T(8,128)(2,1)S(1)}, u32[]{:S(2)}, u32[]{:S(2)}) %collective-permute-start.9) | collective-permute-done | bytes 131104 | tf_op jit(solution)/shard_map/ppermute | solution.py:265
  83.6 2.7 %collective-permute-done.8.p1 = bf16[256,256]{1,0:T(8,128)(2,1)S(1)} collective-permute-done((bf16[256,256]{1,0:T(8,128)(2,1)S(1)}, bf16[256,256]{1,0:T(8,128)(2,1)S(1)}, u32[]{:S(2)}, u32[]{:S(2)}) %collective-permute-start.8) | collective-permute-done | bytes 131104 | tf_op jit(solution)/shard_map/ppermute | solution.py:265
  88.3 4.0 %shard_map.126 = bf16[256,896]{1,0:T(8,128)(2,1)} custom-call(s32[3]{0:T(128)S(1)} %pad_add_fusion.place_ref, bf16[256,256]{1,0:T(8,128)(2,1)S(1)} %shard_map.125.p0, bf16[256,256]{1,0:T(8,128)(2,1)S(1)} %collective-permute-done.8.p1, bf16[256,256]{1,0:T(8,128)(2,1)S(1)} %collective-permute-done.9.p2, bf16[256,256]{1,0:T(8,128)(2,1)S(1)} %collective-permute-done.10.p3, ...), custom_call_target="tpu_custom_call" | custom-call | flops 939524096 | bytes 4718592 | tf_op jit(solution)/shard_map/pallas_call | solution.py:181
  93.2 6.3 %all-to-all-start.2 = ((bf16[16,16,896]{2,1,0:T(8,128)(2,1)}), bf16[16,16,896]{2,1,0:T(8,128)(2,1)S(1)}, u32[]{:S(2)}, u32[]{:S(2)}) async-start(bf16[16,16,896]{2,1,0:T(8,128)(2,1)} %bitcast.13), calls=%async_computation.2 | async-start | bytes 917504 | tf_op jit(solution)/shard_map/all_to_all | solution.py:276
  99.6 3.1 %copy-done.2 = bf16[1,2,7168,256]{3,2,1,0:T(8,128)(2,1)S(1)} copy-done((bf16[1,2,7168,256]{3,2,1,0:T(8,128)(2,1)S(1)}, bf16[1,2,7168,256]{3,2,1,0:T(8,128)(2,1)}, u32[]{:S(2)}) %copy-start.2) | copy-done | bytes 7340056
  102.7 4.5 %shard_map.127.p0 = bf16[256,256]{1,0:T(8,128)(2,1)S(1)} custom-call(s32[3]{0:T(128)S(1)} %pad_add_fusion.place_ref, bf16[128,7168]{1,0:T(8,128)(2,1)} %bitcast.14.own_ref, bf16[128,7168]{1,0:T(8,128)(2,1)S(1)} %collective-permute-done.14.other_ref, bf16[2,7168,256]{2,1,0:T(8,128)(2,1)S(1)} %bitcast.44), custom_call_target="tpu_custom_call" | custom-call | flops 1879048192 | bytes 11010048 | tf_op jit(solution)/shard_map/pallas_call | solution.py:151
  107.1 2.5 %collective-permute-start.17 = (bf16[256,256]{1,0:T(8,128)(2,1)S(1)}, bf16[256,256]{1,0:T(8,128)(2,1)S(1)}, u32[]{:S(2)}, u32[]{:S(2)}) collective-permute-start(bf16[256,256]{1,0:T(8,128)(2,1)S(1)} %shard_map.127.p0), channel_id=1, source_target_pairs={{0,192},{16,208},{64,0},{80,16},{128,64},{144,80},{192,128},{208,1... | collective-permute-start | bytes 393224 | tf_op jit(solution)/shard_map/ppermute | solution.py:265
  109.6 1.5 collective-permute-start.16
  111.2 3.1 %collective-permute-done.17.p3 = bf16[256,256]{1,0:T(8,128)(2,1)S(1)} collective-permute-done((bf16[256,256]{1,0:T(8,128)(2,1)S(1)}, bf16[256,256]{1,0:T(8,128)(2,1)S(1)}, u32[]{:S(2)}, u32[]{:S(2)}) %collective-permute-start.17) | collective-permute-done | bytes 131104 | tf_op jit(solution)/shard_map/ppermute | solution.py:265
  114.2 4.2 %collective-permute-done.16.p2 = bf16[256,256]{1,0:T(8,128)(2,1)S(1)} collective-permute-done((bf16[256,256]{1,0:T(8,128)(2,1)S(1)}, bf16[256,256]{1,0:T(8,128)(2,1)S(1)}, u32[]{:S(2)}, u32[]{:S(2)}) %collective-permute-start.16) | collective-permute-done | bytes 131104 | tf_op jit(solution)/shard_map/ppermute | solution.py:265
  118.4 2.4 %collective-permute-done.15.p1 = bf16[256,256]{1,0:T(8,128)(2,1)S(1)} collective-permute-done((bf16[256,256]{1,0:T(8,128)(2,1)S(1)}, bf16[256,256]{1,0:T(8,128)(2,1)S(1)}, u32[]{:S(2)}, u32[]{:S(2)}) %collective-permute-start.15) | collective-permute-done | bytes 131104 | tf_op jit(solution)/shard_map/ppermute | solution.py:265
  121.0 1.9 %collective-permute-done.18.theirs_ref = bf16[256,1024]{1,0:T(8,128)(2,1)S(1)} collective-permute-done((bf16[256,1024]{1,0:T(8,128)(2,1)S(1)}, bf16[256,1024]{1,0:T(8,128)(2,1)S(1)}, u32[]{:S(2)}, u32[]{:S(2)}) %collective-permute-start.18) | collective-permute-done | bytes 524320 | tf_op jit(solution)/shard_map/ppermute | solution.py:284
  122.8 2.0 %copy-done.4 = bf16[1,2048,896]{2,1,0:T(8,128)(2,1)S(1)} copy-done((bf16[1,2048,896]{2,1,0:T(8,128)(2,1)S(1)}, bf16[1,2048,896]{2,1,0:T(8,128)(2,1)}, u32[]{:S(2)}) %copy-start.4) | copy-done | bytes 3670040
  124.9 3.2 %shard_map.128 = bf16[256,896]{1,0:T(8,128)(2,1)S(1)} custom-call(s32[3]{0:T(128)S(1)} %pad_add_fusion.place_ref, bf16[256,256]{1,0:T(8,128)(2,1)S(1)} %shard_map.127.p0, bf16[256,256]{1,0:T(8,128)(2,1)S(1)} %collective-permute-done.15.p1, bf16[256,256]{1,0:T(8,128)(2,1)S(1)} %collective-permute-done.16.p2, bf16[256,256]{1,0:T(8,128)(2,1)S(1)} %collective-permute-done.17.p3, ...), custom_call_target="tpu_custom_call" | custom-call | flops 939524096 | bytes 4718592 | tf_op jit(solution)/shard_map/pallas_call | solution.py:181
  128.1 17.8 %all_to_all.25 = bf16[16,16,896]{2,1,0:T(8,128)(2,1)S(1)} all-to-all(bf16[16,16,896]{2,1,0:T(8,128)(2,1)S(1)} %bitcast.51), channel_id=1, replica_groups=mesh['ctx'=4,'att'=2,'zhi'=2,'x'=4,'y'=4] {'x','y'}, dimensions={0} | all-to-all | bytes 917504 | tf_op jit(solution)/shard_map/all_to_all | solution.py:276
  145.9 2.0 %shard_map.129 = bf16[16,4,896]{2,1,0:T(4,128)(2,1)} custom-call(s32[3]{0:T(128)S(1)} %pad_add_fusion.place_ref, bf16[256,896]{1,0:T(8,128)(2,1)S(1)} %bitcast.49, bf16[256,896]{1,0:T(8,128)(2,1)S(1)} %bitcast.50, bf16[16,128]{1,0:T(8,128)(2,1)S(1)} %slice.24.mine0, bf16[16,128]{1,0:T(8,128)(2,1)S(1)} %slice.25.mine1, ...), custom_call_target="tpu_custom_call" | custom-call | flops 176160768 | bytes 1048576 | tf_op jit(solution)/shard_map/pallas_call | solution.py:229
  148.8 7.8 %all-to-all-start.4 = ((bf16[16,4,896]{2,1,0:T(4,128)(2,1)}), bf16[16,4,896]{2,1,0:T(4,128)(2,1)S(1)}, u32[]{:S(2)}, u32[]{:S(2)}) async-start(bf16[16,4,896]{2,1,0:T(4,128)(2,1)} %shard_map.129), calls=%async_computation.5 | async-start | bytes 229376 | tf_op jit(solution)/shard_map/all_to_all | solution.py:309
  158.1 6.6 %all-to-all-done.4 = bf16[16,4,896]{2,1,0:T(4,128)(2,1)S(1)} async-done(((bf16[16,4,896]{2,1,0:T(4,128)(2,1)}), bf16[16,4,896]{2,1,0:T(4,128)(2,1)S(1)}, u32[]{:S(2)}, u32[]{:S(2)}) %all-to-all-start.4) | async-done | bytes 114720 | tf_op jit(solution)/shard_map/all_to_all | solution.py:309
  (63 shorter events, 21.2 us)
Async XLA Ops:
  7.2 26.5 %copy-start = (bf16[1,1024,512]{2,1,0:T(8,128)(2,1)S(1)}, bf16[1,1024,512]{2,1,0:T(8,128)(2,1)}, u32[]{:S(2)}) copy-start(bf16[1,1024,512]{2,1,0:T(8,128)(2,1)} %param.13) | copy-start | bytes 3145732
  7.2 0.9 copy-start.5
  8.1 0.7 copy-start.6
  10.9 6.4 %collective-permute-start.2 = (bf16[4,7296]{1,0:T(4,128)(2,1)S(1)}, bf16[4,7296]{1,0:T(4,128)(2,1)S(1)}, u32[]{:S(2)}, u32[]{:S(2)}) collective-permute-start(bf16[4,7296]{1,0:T(4,128)(2,1)S(1)} %shard_map.122), channel_id=1, source_target_pairs={{0,192},{16,208},{64,0},{80,16},{128,64},{144,80},{192,128},{208,1... | collective-permute-start | bytes 175112 | tf_op jit(solution)/shard_map/ppermute | solution.py:265
  12.9 5.8 %collective-permute-start.1 = (bf16[4,7296]{1,0:T(4,128)(2,1)S(1)}, bf16[4,7296]{1,0:T(4,128)(2,1)S(1)}, u32[]{:S(2)}, u32[]{:S(2)}) collective-permute-start(bf16[4,7296]{1,0:T(4,128)(2,1)S(1)} %shard_map.122), channel_id=1, source_target_pairs={{0,128},{16,144},{64,192},{80,208},{128,0},{144,16},{192,64},{208,... | collective-permute-start | bytes 175112 | tf_op jit(solution)/shard_map/ppermute | solution.py:265
  14.4 5.5 %collective-permute-start = (bf16[4,7296]{1,0:T(4,128)(2,1)S(1)}, bf16[4,7296]{1,0:T(4,128)(2,1)S(1)}, u32[]{:S(2)}, u32[]{:S(2)}) collective-permute-start(bf16[4,7296]{1,0:T(4,128)(2,1)S(1)} %shard_map.122), channel_id=1, source_target_pairs={{0,64},{16,80},{64,128},{80,144},{128,192},{144,208},{192,0},{208,... | collective-permute-start | bytes 175112 | tf_op jit(solution)/shard_map/ppermute | solution.py:265
  24.6 7.2 %copy-start.9 = (bf16[1,128,64]{1,2,0:T(8,128)(2,1)S(1)}, bf16[1,128,64]{1,2,0:T(8,128)(2,1)}, u32[]{:S(2)}) copy-start(bf16[1,128,64]{1,2,0:T(8,128)(2,1)} %param.12) | copy-start | bytes 49156
  24.6 33.9 %all-to-all-start = ((bf16[16,8,7168]{2,1,0:T(8,128)(2,1)}), bf16[16,8,7168]{2,1,0:T(8,128)(2,1)S(1)}, u32[]{:S(2)}, u32[]{:S(2)}) async-start(bf16[16,8,7168]{2,1,0:T(8,128)(2,1)} %bitcast.3), calls=%async_computation | async-start | bytes 3670016 | tf_op jit(solution)/shard_map/all_to_all | solution.py:276
  35.4 11.5 %collective-permute-start.6 = (bf16[4,7296]{1,0:T(4,128)(2,1)S(1)}, bf16[4,7296]{1,0:T(4,128)(2,1)S(1)}, u32[]{:S(2)}, u32[]{:S(2)}) collective-permute-start(bf16[4,7296]{1,0:T(4,128)(2,1)S(1)} %shard_map.122), channel_id=1, source_target_pairs={{0,208},{16,192},{64,16},{80,0},{128,80},{144,64},{192,144},{208,1... | collective-permute-start | bytes 175112 | tf_op jit(solution)/shard_map/ppermute | solution.py:265
  40.9 6.8 %collective-permute-start.5 = (bf16[4,7296]{1,0:T(4,128)(2,1)S(1)}, bf16[4,7296]{1,0:T(4,128)(2,1)S(1)}, u32[]{:S(2)}, u32[]{:S(2)}) collective-permute-start(bf16[4,7296]{1,0:T(4,128)(2,1)S(1)} %shard_map.122), channel_id=1, source_target_pairs={{0,144},{16,128},{64,208},{80,192},{128,16},{144,0},{192,80},{208,... | collective-permute-start | bytes 175112 | tf_op jit(solution)/shard_map/ppermute | solution.py:265
  41.2 12.5 %collective-permute-start.4 = (bf16[4,7296]{1,0:T(4,128)(2,1)S(1)}, bf16[4,7296]{1,0:T(4,128)(2,1)S(1)}, u32[]{:S(2)}, u32[]{:S(2)}) collective-permute-start(bf16[4,7296]{1,0:T(4,128)(2,1)S(1)} %shard_map.122), channel_id=1, source_target_pairs={{0,80},{16,64},{64,144},{80,128},{128,208},{144,192},{192,16},{208... | collective-permute-start | bytes 175112 | tf_op jit(solution)/shard_map/ppermute | solution.py:265
  44.2 9.4 %collective-permute-start.3 = (bf16[4,7296]{1,0:T(4,128)(2,1)S(1)}, bf16[4,7296]{1,0:T(4,128)(2,1)S(1)}, u32[]{:S(2)}, u32[]{:S(2)}) collective-permute-start(bf16[4,7296]{1,0:T(4,128)(2,1)S(1)} %shard_map.122), channel_id=1, source_target_pairs={{0,16},{16,0},{64,80},{80,64},{128,144},{144,128},{192,208},{208,1... | collective-permute-start | bytes 175112 | tf_op jit(solution)/shard_map/ppermute | solution.py:265
  58.5 6.9 %collective-permute-start.7 = (bf16[128,7168]{1,0:T(8,128)(2,1)S(1)}, bf16[128,7168]{1,0:T(8,128)(2,1)}, u32[]{:S(2)}, u32[]{:S(2)}) collective-permute-start(bf16[128,7168]{1,0:T(8,128)(2,1)S(1)} %bitcast.47), channel_id=1, source_target_pairs={{0,32},{32,0},{1,33},{33,1},{2,34},{34,2},{3,35},{35,3},{4,36},{36... | collective-permute-start | bytes 5505032 | tf_op jit(solution)/shard_map/ppermute | solution.py:280
  58.5 34.8 %all-to-all-start.1 = ((bf16[16,8,7168]{2,1,0:T(8,128)(2,1)}), bf16[16,8,7168]{2,1,0:T(8,128)(2,1)}, u32[]{:S(2)}, u32[]{:S(2)}) async-start(bf16[16,8,7168]{2,1,0:T(8,128)(2,1)} %bitcast.4), calls=%async_computation.1 | async-start | bytes 3670016 | tf_op jit(solution)/shard_map/all_to_all | solution.py:276
  65.4 3.1 %copy-start.1 = (bf16[1,2,7168,256]{3,2,1,0:T(8,128)(2,1)S(1)}, bf16[1,2,7168,256]{3,2,1,0:T(8,128)(2,1)}, u32[]{:S(2)}) copy-start(bf16[1,2,7168,256]{3,2,1,0:T(8,128)(2,1)} %param.20) | copy-start | bytes 22020100
  68.5 19.9 %copy-start.3 = (bf16[1,2048,896]{2,1,0:T(8,128)(2,1)S(1)}, bf16[1,2048,896]{2,1,0:T(8,128)(2,1)}, u32[]{:S(2)}) copy-start(bf16[1,2048,896]{2,1,0:T(8,128)(2,1)} %param.21) | copy-start | bytes 11010052
  73.1 7.0 %collective-permute-start.10 = (bf16[256,256]{1,0:T(8,128)(2,1)S(1)}, bf16[256,256]{1,0:T(8,128)(2,1)S(1)}, u32[]{:S(2)}, u32[]{:S(2)}) collective-permute-start(bf16[256,256]{1,0:T(8,128)(2,1)S(1)} %shard_map.125.p0), channel_id=1, source_target_pairs={{0,192},{16,208},{64,0},{80,16},{128,64},{144,80},{192,128},{208,1... | collective-permute-start | bytes 393224 | tf_op jit(solution)/shard_map/ppermute | solution.py:265
  74.8 8.8 %collective-permute-start.9 = (bf16[256,256]{1,0:T(8,128)(2,1)S(1)}, bf16[256,256]{1,0:T(8,128)(2,1)S(1)}, u32[]{:S(2)}, u32[]{:S(2)}) collective-permute-start(bf16[256,256]{1,0:T(8,128)(2,1)S(1)} %shard_map.125.p0), channel_id=1, source_target_pairs={{0,128},{16,144},{64,192},{80,208},{128,0},{144,16},{192,64},{208,... | collective-permute-start | bytes 393224 | tf_op jit(solution)/shard_map/ppermute | solution.py:265
  76.0 10.3 %collective-permute-start.8 = (bf16[256,256]{1,0:T(8,128)(2,1)S(1)}, bf16[256,256]{1,0:T(8,128)(2,1)S(1)}, u32[]{:S(2)}, u32[]{:S(2)}) collective-permute-start(bf16[256,256]{1,0:T(8,128)(2,1)S(1)} %shard_map.125.p0), channel_id=1, source_target_pairs={{0,64},{16,80},{64,128},{80,144},{128,192},{144,208},{192,0},{208,... | collective-permute-start | bytes 393224 | tf_op jit(solution)/shard_map/ppermute | solution.py:265
  86.3 2.0 %collective-permute-start.11 = (bf16[256,1024]{1,0:T(8,128)(2,1)S(1)}, bf16[256,1024]{1,0:T(8,128)(2,1)S(1)}, u32[]{:S(2)}, u32[]{:S(2)}) collective-permute-start(bf16[256,1024]{1,0:T(8,128)(2,1)S(1)} %pad_maximum_fusion), channel_id=1, source_target_pairs={{0,32},{32,0},{1,33},{33,1},{2,34},{34,2},{3,35},{35,3},{4,36},{36... | collective-permute-start | bytes 1572872 | tf_op jit(solution)/shard_map/ppermute | solution.py:284
  86.5 5.9 %collective-permute-start.12 = (bf16[16,128]{1,0:T(8,128)(2,1)S(1)}, bf16[16,128]{1,0:T(8,128)(2,1)S(1)}, u32[]{:S(2)}, u32[]{:S(2)}) collective-permute-start(bf16[16,128]{1,0:T(8,128)(2,1)S(1)} %slice.24.mine0), channel_id=1, source_target_pairs={{0,32},{32,0},{1,33},{33,1},{2,34},{34,2},{3,35},{35,3},{4,36},{36... | collective-permute-start | bytes 12296 | tf_op jit(solution)/shard_map/ppermute | solution.py:297
  86.9 5.4 %collective-permute-start.13 = (bf16[16,128]{1,0:T(8,128)(2,1)S(1)}, bf16[16,128]{1,0:T(8,128)(2,1)S(1)}, u32[]{:S(2)}, u32[]{:S(2)}) collective-permute-start(bf16[16,128]{1,0:T(8,128)(2,1)S(1)} %slice.25.mine1), channel_id=1, source_target_pairs={{0,32},{32,0},{1,33},{33,1},{2,34},{34,2},{3,35},{35,3},{4,36},{36... | collective-permute-start | bytes 12296 | tf_op jit(solution)/shard_map/ppermute | solution.py:298
  93.2 6.3 %collective-permute-start.14 = (bf16[128,7168]{1,0:T(8,128)(2,1)}, bf16[128,7168]{1,0:T(8,128)(2,1)S(1)}, u32[]{:S(2)}, u32[]{:S(2)}) collective-permute-start(bf16[128,7168]{1,0:T(8,128)(2,1)} %bitcast.14.own_ref), channel_id=1, source_target_pairs={{0,32},{32,0},{1,33},{33,1},{2,34},{34,2},{3,35},{35,3},{4,36},{36... | collective-permute-start | bytes 5505032 | tf_op jit(solution)/shard_map/ppermute | solution.py:280
  93.2 27.6 %all-to-all-start.2 = ((bf16[16,16,896]{2,1,0:T(8,128)(2,1)}), bf16[16,16,896]{2,1,0:T(8,128)(2,1)S(1)}, u32[]{:S(2)}, u32[]{:S(2)}) async-start(bf16[16,16,896]{2,1,0:T(8,128)(2,1)} %bitcast.13), calls=%async_computation.2 | async-start | bytes 917504 | tf_op jit(solution)/shard_map/all_to_all | solution.py:276
  99.5 48.5 %reduce-scatter.2.cloned.1.call-start = ((), (), s32[]{:S(2)}) async-start(), calls=%async_computation.6 | async-start | bytes 409600 | tf_op jit(solution)/shard_map/reduce_scatter | solution.py:293
  99.6 3.1 %copy-start.2 = (bf16[1,2,7168,256]{3,2,1,0:T(8,128)(2,1)S(1)}, bf16[1,2,7168,256]{3,2,1,0:T(8,128)(2,1)}, u32[]{:S(2)}) copy-start(bf16[1,2,7168,256]{3,2,1,0:T(8,128)(2,1)} %param.20) | copy-start | bytes 22020100
  107.1 7.1 %collective-permute-start.17 = (bf16[256,256]{1,0:T(8,128)(2,1)S(1)}, bf16[256,256]{1,0:T(8,128)(2,1)S(1)}, u32[]{:S(2)}, u32[]{:S(2)}) collective-permute-start(bf16[256,256]{1,0:T(8,128)(2,1)S(1)} %shard_map.127.p0), channel_id=1, source_target_pairs={{0,192},{16,208},{64,0},{80,16},{128,64},{144,80},{192,128},{208,1... | collective-permute-start | bytes 393224 | tf_op jit(solution)/shard_map/ppermute | solution.py:265
  109.6 8.8 %collective-permute-start.16 = (bf16[256,256]{1,0:T(8,128)(2,1)S(1)}, bf16[256,256]{1,0:T(8,128)(2,1)S(1)}, u32[]{:S(2)}, u32[]{:S(2)}) collective-permute-start(bf16[256,256]{1,0:T(8,128)(2,1)S(1)} %shard_map.127.p0), channel_id=1, source_target_pairs={{0,128},{16,144},{64,192},{80,208},{128,0},{144,16},{192,64},{208,... | collective-permute-start | bytes 393224 | tf_op jit(solution)/shard_map/ppermute | solution.py:265
  111.2 9.6 %collective-permute-start.15 = (bf16[256,256]{1,0:T(8,128)(2,1)S(1)}, bf16[256,256]{1,0:T(8,128)(2,1)S(1)}, u32[]{:S(2)}, u32[]{:S(2)}) collective-permute-start(bf16[256,256]{1,0:T(8,128)(2,1)S(1)} %shard_map.127.p0), channel_id=1, source_target_pairs={{0,64},{16,80},{64,128},{80,144},{128,192},{144,208},{192,0},{208,... | collective-permute-start | bytes 393224 | tf_op jit(solution)/shard_map/ppermute | solution.py:265
  120.8 2.0 %collective-permute-start.18 = (bf16[256,1024]{1,0:T(8,128)(2,1)S(1)}, bf16[256,1024]{1,0:T(8,128)(2,1)S(1)}, u32[]{:S(2)}, u32[]{:S(2)}) collective-permute-start(bf16[256,1024]{1,0:T(8,128)(2,1)S(1)} %pad_maximum_fusion.1), channel_id=1, source_target_pairs={{0,32},{32,0},{1,33},{33,1},{2,34},{34,2},{3,35},{35,3},{4,36},{36... | collective-permute-start | bytes 1572872 | tf_op jit(solution)/shard_map/ppermute | solution.py:284
  122.8 2.0 %copy-start.4 = (bf16[1,2048,896]{2,1,0:T(8,128)(2,1)S(1)}, bf16[1,2048,896]{2,1,0:T(8,128)(2,1)}, u32[]{:S(2)}) copy-start(bf16[1,2048,896]{2,1,0:T(8,128)(2,1)} %param.21) | copy-start | bytes 11010052
  148.8 15.9 %all-to-all-start.4 = ((bf16[16,4,896]{2,1,0:T(4,128)(2,1)}), bf16[16,4,896]{2,1,0:T(4,128)(2,1)S(1)}, u32[]{:S(2)}, u32[]{:S(2)}) async-start(bf16[16,4,896]{2,1,0:T(4,128)(2,1)} %shard_map.129), calls=%async_computation.5 | async-start | bytes 229376 | tf_op jit(solution)/shard_map/all_to_all | solution.py:309
  (2 other events, 1.4 us)
Sparse Core Ops, SparseCore 0:
  121.1 24.0 reduce-scatter.1

commit v4 on v2

v4 whole, which is shorter than its diff:
```python
import jax
import jax.numpy as jnp
from jax import lax
from jax.experimental import pallas as pl
from jax.experimental.pallas import tpu as pltpu
from jax.sharding import Mesh, PartitionSpec as P

softmax_scale = 192.0 ** (-0.5)
epsilon = 1e-06
bf16 = jnp.bfloat16
f32 = jnp.float32
INFO = 128
TOK = 4
SLOTS = 2


def attend(query_latent, query_rope, latent_cache, rope_keys, lengths):
    shard_length = latent_cache.shape[1]
    first_position = lax.axis_index("ctx") * shard_length
    scores = jnp.einsum("hr,tr->ht", query_latent[0], latent_cache[0], preferred_element_type=f32)
    scores = scores + jnp.einsum("hp,pt->ht", query_rope[0], rope_keys[0], preferred_element_type=f32)
    position = first_position + jnp.arange(shard_length, dtype=jnp.int32)
    live_mask = position < lengths[0]
    weights = jnp.where(live_mask[None, :], jnp.exp(softmax_scale * scores), f32(0.0))
    mass = jnp.sum(weights, axis=1, keepdims=True)
    numerator = jnp.dot(weights.astype(bf16), latent_cache[0], preferred_element_type=f32)
    return jnp.concatenate([numerator, jnp.broadcast_to(mass, (mass.shape[0], 128))], axis=1)


def finish_attention(summed):
    return (summed[:, :512] / summed[:, 512:513]).astype(bf16)[None]


VMEM = pl.BlockSpec(memory_space=pltpu.VMEM)
SMEM = pl.BlockSpec(memory_space=pltpu.SMEM)
HBM = pl.BlockSpec(memory_space=pltpu.HBM)
STEP = 1024


def room(mib):
    return pltpu.CompilerParams(vmem_limit_bytes=mib * 1024 * 1024)


def prepare_kernel(ids_ref, gates_ref, rows_ref, gain_ref, out_ref):
    width = rows_ref.shape[1]
    rows = rows_ref[...].astype(f32)
    mean = jnp.mean(rows * rows, axis=1, keepdims=True)
    gain = gain_ref[...].astype(f32).reshape(1, width)
    out_ref[:, :width] = (rows * lax.rsqrt(mean + epsilon) * gain).astype(bf16)
    lane = lax.broadcasted_iota(jnp.int32, (1, 128), 1)
    expert, slot = lane // SLOTS, lane % SLOTS
    count = jnp.zeros((1, 128), jnp.int32)
    token = jnp.full((1, 128), -1.0, f32)
    gate = jnp.zeros((1, 128), f32)
    for t in range(TOK):
        picked = jnp.zeros((1, 128), jnp.int32)
        share = jnp.zeros((1, 128), f32)
        for j in range(8):
            hit = expert == ids_ref[t, j]
            picked = jnp.where(hit, 1, picked)
            share = share + jnp.where(hit, gates_ref[t, j], f32(0.0))
        here = (picked == 1) & (count == slot)
        token = jnp.where(here, f32(t), token)
        gate = jnp.where(here, share, gate)
        count = count + picked
    high = gate.astype(bf16).astype(f32)
    middle = (gate - high).astype(bf16).astype(f32)
    low = gate - high - middle
    row = lax.broadcasted_iota(jnp.int32, (TOK, 128), 0)
    facts = jnp.where(row == 0, token, jnp.where(row == 1, high, jnp.where(row == 2, middle, low)))
    out_ref[:, width:] = facts.astype(bf16)


def prepare(moe_rows, route_ids, route_gates, norm_gain):
    return pl.pallas_call(
        prepare_kernel,
        out_shape=jax.ShapeDtypeStruct((TOK, moe_rows.shape[1] + INFO), bf16),
        in_specs=[SMEM, SMEM, VMEM, VMEM],
        out_specs=VMEM,
        compiler_params=room(4),
    )(route_ids, route_gates, moe_rows, norm_gain)


def grid(rows, columns, dim):
    return lax.broadcasted_iota(jnp.int32, (rows, columns), dim)


def choose_kernel(place_ref, tokens_ref, out_ref):
    ctx, half = place_ref[0], place_ref[2]
    width = out_ref.shape[1]
    first = grid(16, 16, 1) == grid(16, 16, 0) // TOK * TOK
    tokens = jnp.dot(
        first.astype(f32).astype(bf16), tokens_ref[:, width:], preferred_element_type=f32
    )
    row = grid(128, 128, 0)
    lane = half * 32 + row // 8 * SLOTS + row % SLOTS
    pick = (grid(128, 128, 1) == lane).astype(f32).astype(bf16)
    wanted = lax.dot_general(
        pick, tokens.astype(bf16), (((1,), (1,)), ((), ())), preferred_element_type=f32
    )
    row, column = grid(128, 16, 0), grid(128, 16, 1)
    hit = wanted == (column % TOK).astype(f32)
    hit = hit & ((ctx - column // TOK + 4) % 4 == row // SLOTS % 4)
    selector = hit.astype(f32).astype(bf16)
    for low in range(0, width, STEP):
        part = jnp.dot(selector, tokens_ref[:, low : low + STEP], preferred_element_type=f32)
        out_ref[:, low : low + STEP] = part.astype(bf16)


def choose(place, tokens, width):
    return pl.pallas_call(
        choose_kernel,
        out_shape=jax.ShapeDtypeStruct((128, width), bf16),
        in_specs=[SMEM, VMEM],
        out_specs=VMEM,
        compiler_params=room(6),
        cost_estimate=pl.CostEstimate(flops=2 * 128 * 16 * width, bytes_accessed=2 * 144 * width, transcendentals=0),
    )(place, tokens)


def gate_up_kernel(rows_ref, own_ref, other_ref, out_ref, held_ref, sems):
    width = rows_ref.shape[1]
    copies = []
    for i in range(width // STEP):
        part = pl.ds(i * STEP, STEP)
        for j, weight_ref in enumerate((own_ref, other_ref)):
            copies.append(
                pltpu.make_async_copy(weight_ref.at[:, part], held_ref.at[j, :, part], sems.at[i, j])
            )
            copies[-1].start()
    sums = [jnp.zeros((128, 256), f32) for _ in range(4)]
    for i in range(width // STEP):
        low, high = i * STEP, (i + 1) * STEP
        rows = rows_ref[:, low:high]
        for j in range(2):
            copies[2 * i + j].wait()
            for k in range(2):
                sums[2 * j + k] += jnp.dot(rows, held_ref[j, k, low:high], preferred_element_type=f32)
    for j in range(2):
        gate, up = sums[2 * j], sums[2 * j + 1]
        out_ref[:, j * 256 : (j + 1) * 256] = (gate / (1.0 + jnp.exp(-gate)) * up).astype(bf16)


def gate_up(rows, own, other):
    width = rows.shape[1]
    return pl.pallas_call(
        gate_up_kernel,
        out_shape=jax.ShapeDtypeStruct((128, 512), bf16),
        in_specs=[VMEM, HBM, HBM],
        out_specs=VMEM,
        scratch_shapes=[
            pltpu.VMEM((2, 2, width, 256), bf16),
            pltpu.SemaphoreType.DMA((width // STEP, 2)),
        ],
        compiler_params=room(24),
        cost_estimate=pl.CostEstimate(
            flops=2 * 128 * width * 1024, bytes_accessed=2 * width * (1024 + 128), transcendentals=65536
        ),
    )(rows, own, other)


def down_kernel(place_ref, p0, p1, p2, p3, own_ref, other_ref, out_ref, held_ref, sems):
    ctx, core = place_ref[0], place_ref[1]
    copies = []
    for k in range(4):
        source = (ctx - k + 4) % 4
        for j, weight_ref in enumerate((own_ref, other_ref)):
            copies.append(
                pltpu.make_async_copy(weight_ref.at[source], held_ref.at[j, k], sems.at[j, k])
            )
            copies[-1].start()
    totals = [jnp.zeros((128, 896), f32) for _ in range(2)]
    for k, piece in enumerate((p0, p1, p2, p3)):
        for j in range(2):
            copies[2 * k + j].wait()
            totals[j] += jnp.dot(piece[:, :256], held_ref[j, k, core], preferred_element_type=f32)
            totals[j] += jnp.dot(piece[:, 256:], held_ref[j, k, 1 - core], preferred_element_type=f32)
    out_ref[:, :896] = jnp.where(core == 0, totals[0], totals[1]).astype(bf16)
    out_ref[:, 896:] = jnp.where(core == 0, totals[1], totals[0]).astype(bf16)


def down(place, pieces, own, other):
    return pl.pallas_call(
        down_kernel,
        out_shape=jax.ShapeDtypeStruct((128, 1792), bf16),
        in_specs=[SMEM] + [VMEM] * 4 + [HBM] * 2,
        out_specs=VMEM,
        scratch_shapes=[pltpu.VMEM((2, 4, 2, 256, 896), bf16), pltpu.SemaphoreType.DMA((2, 4))],
        compiler_params=room(16),
        cost_estimate=pl.CostEstimate(
            flops=2 * 128 * 2048 * 1792, bytes_accessed=2 * 2048 * 1792 + 2 * 128 * 2048, transcendentals=0
        ),
    )(place, *pieces, own, other)


def mix_kernel(place_ref, back0, back1, facts0, facts1, out_ref):
    ctx, half = place_ref[0], place_ref[2]
    lane = grid(128, 128, 1)
    spread = grid(128, 128, 0) == half * 32 + lane // 8 * SLOTS + lane % SLOTS
    spread = spread.astype(f32).astype(bf16)
    total = jnp.zeros((32, 1792), f32)
    for q, (back, facts) in enumerate(((back0, facts0), (back1, facts1))):
        facts = jnp.dot(facts[...], spread, preferred_element_type=f32)
        at, lane_ctx = grid(16, 128, 0), grid(16, 128, 1) // SLOTS % 4
        here = (ctx - at // TOK + 4) % 4 == lane_ctx
        token, high, middle, low = (
            jnp.sum(jnp.where(here & (at % TOK == i), facts, 0.0), axis=0, keepdims=True) for i in range(4)
        )
        at, lane_ctx = grid(32, 128, 0), grid(32, 128, 1) // SLOTS % 4
        fits = (at // 8 == lane_ctx) & (at // 4 % 2 == (half if q == 0 else 1 - half))
        fits = fits & ((at % TOK).astype(f32) == token)
        for part in (high, middle, low):
            matrix = jnp.where(fits, part, 0.0).astype(bf16)
            total += jnp.dot(matrix, back[...], preferred_element_type=f32)
    out_ref[...] = total.reshape(8, TOK, 1792).astype(bf16)


def mix(place, back0, back1, facts0, facts1):
    return pl.pallas_call(
        mix_kernel,
        out_shape=jax.ShapeDtypeStruct((8, TOK, 1792), bf16),
        in_specs=[SMEM] + [VMEM] * 4,
        out_specs=VMEM,
        compiler_params=room(6),
        cost_estimate=pl.CostEstimate(flops=2 * 32 * 256 * 1792 * 3, bytes_accessed=1 << 20, transcendentals=0),
    )(place, back0, back1, facts0, facts1)


def shards(
    query_latent,
    query_rope,
    latent_cache,
    rope_keys,
    lengths,
    moe_rows,
    route_ids,
    route_gates,
    norm_gain,
    expert_in,
    expert_out,
):
    c = lax.axis_index("ctx")
    a = lax.axis_index("att")
    h = lax.axis_index("zhi")
    width = moe_rows.shape[1]
    swap_core = [(0, 1), (1, 0)]

    place = jnp.stack([c, a, h]).astype(jnp.int32)
    payload = prepare(moe_rows, route_ids, route_gates, norm_gain)

    def hop(value, k, flip):
        pairs = [
            (i * 2 + j, (i + k) % 4 * 2 + (j ^ flip)) for i in range(4) for j in range(2)
        ]
        return lax.ppermute(value, ("ctx", "zhi"), pairs)

    def rows_of(half):
        tokens = jnp.concatenate(half, axis=0)
        return choose(place, tokens, width), tokens[:, width:]

    def across(value):
        value = value.reshape(16, 8, value.shape[1])
        moved = lax.all_to_all(value, ("x", "y"), split_axis=0, concat_axis=0, tiled=True)
        return moved.reshape(128, moved.shape[2])

    def hidden_of(got):
        hidden = gate_up(got, weight_in, other_in)
        return [hidden] + [hop(hidden, k, 0) for k in (1, 2, 3)]

    rows0, facts0 = rows_of([payload] + [hop(payload, k, 0) for k in (1, 2, 3)])
    weight_in, weight_out = expert_in[0], expert_out[0].reshape(4, 2, 256, 896)
    rows0, facts0, payload, moving_in, moving_out = lax.optimization_barrier(
        (rows0, facts0, payload, weight_in, weight_out)
    )
    got0 = across(rows0)
    other_in = lax.ppermute(moving_in, "att", swap_core)
    other_out = lax.ppermute(moving_out, "att", swap_core)
    rows1, facts1 = rows_of([hop(payload, k, 1) for k in (0, 1, 2, 3)])
    part = attend(query_latent, query_rope, latent_cache, rope_keys, lengths)
    rows1, facts1, got0, part = lax.optimization_barrier((rows1, facts1, got0, part))
    got1 = across(rows1)

    pieces0 = hidden_of(got0)
    part = part.reshape(4, 32, 640)
    summed = lax.dynamic_index_in_dim(part, c, 0, keepdims=False)
    for k in (1, 2, 3):
        sent = lax.dynamic_index_in_dim(part, (c + k) % 4, 0, keepdims=False)
        summed = summed + lax.ppermute(sent, "ctx", [(i, (i + k) % 4) for i in range(4)])
    attended = finish_attention(summed)
    result0 = down(place, pieces0, weight_out, other_out)
    got1, result0, attended = lax.optimization_barrier((got1, result0, attended))
    back0 = across(result0)
    pieces1 = hidden_of(got1)
    pieces1[0], back0 = lax.optimization_barrier((pieces1[0], back0))
    result1 = down(place, pieces1, weight_out, other_out)
    back1 = across(result1)

    outgoing = mix(place, back0, back1, facts0, facts1)
    final = lax.all_to_all(outgoing, ("ctx", "zhi"), split_axis=0, concat_axis=0, tiled=True)
    final = final.reshape(4, 2, TOK, 1792).astype(f32)
    routed = (final[:, 0] + final[:, 1]).transpose(1, 0, 2).reshape(TOK, 4 * 1792)
    return (attended, routed.astype(bf16))


def solution(mesh):
    fine = Mesh(mesh.devices.reshape(4, 2, 2, 4, 4), ("ctx", "att", "zhi", "x", "y"))
    exp = ("zhi", "x", "y")
    sequences = ("att",) + exp
    every = ("ctx", "att") + exp
    placed = (
        P(sequences, None, None),
        P(sequences, None, None),
        P(sequences, "ctx", None),
        P(sequences, None, "ctx"),
        P(sequences),
        P(every, None),
        P(every, None),
        P(every, None),
        P(),
        P(exp, None, None, ("ctx", "att")),
        P(exp, None, ("ctx", "att")),
    )
    return jax.shard_map(
        shards,
        mesh=fine,
        in_specs=placed,
        out_specs=(P(sequences, "ctx", None), P(every, None)),
        check_vma=False,
    )
```

time: 177 us -> 156 us (0.88); the launches traced: 174 us -> 156 us
  blocking collectives: 0 us -> 28.5 us
  waiting for transfers between devices: 54.8 us -> 30.2 us
  between operations: 15 us -> 1.56 us
  Pallas kernels: 17.9 us -> 27 us
  starting transfers between devices: 59.5 us -> 50.8 us
  matrix products: 7.57 us -> 2.94 us
  local copies, waits for them, and re-layouts: 14.8 us -> 12 us
  other arithmetic: 4.49 us -> 2.71 us
    all_to_all x0 -> x2, blocking collectives: none -> 28.5 us  [the longest x1 16.6 us: across(): lax.all_to_all(value, ('x', 'y'), split_axis=0, concat_axis=0, tiled=True)]
    reduce_scatter x1 -> x0, waiting for transfers between devices: 10.7 us -> none  [shards(): summed = lax.psum_scatter(part, 'ctx', scatter_dimension=0, tiled=True)]
    pallas_call x5 -> x7, Pallas kernels: 16.2 us -> 26.2 us  [the longest x2 10.6 us: gate_up(): pl.pallas_call(gate_up_kernel, out_shape=jax.ShapeDtypeStruct((128, 512),...]
    all_to_all x1 -> x0, starting transfers between devices: 7.82 us -> none  [shards(): lax.all_to_all(outgoing.reshape(16, TOK, 896), ('ctx', 'att', 'zhi'), spl...]
    all_to_all x4 -> x3, starting transfers between devices: 24.8 us -> 17.9 us  [across(): lax.all_to_all(value, ('x', 'y'), split_axis=0, concat_axis=0, tiled=True)]
    all_to_all x1 -> x0, waiting for transfers between devices: 6.6 us -> none  [shards(): lax.all_to_all(outgoing.reshape(16, TOK, 896), ('ctx', 'att', 'zhi'), spl...]
    all_to_all x4 -> x3, waiting for transfers between devices: 8.37 us -> 3.08 us  [across(): lax.all_to_all(value, ('x', 'y'), split_axis=0, concat_axis=0, tiled=True)]
    dot_general x2 -> x0, matrix products: 4.59 us -> none  [choose(): jnp.dot(selector, tokens[:, :width], preferred_element_type=f32)]
  transfers between devices with their start and end apart: 25 -> 21, of which waited for: 14 -> 12; matrix products, arithmetic and copies ran while one was open for 6% -> 4% of each run, Pallas kernels for 8% -> 12%
where the time goes in v4:
time: 156 us
  starting transfers between devices  50.8 us (33%)
  waiting for transfers between devices  30.2 us (19%)
  blocking collectives  28.5 us (18%)
  Pallas kernels  27 us (17%)
  local copies, waits for them, and re-layouts  12 us (8%)
  matrix products  2.94 us (2%)
  other arithmetic  2.71 us (2%)
  between operations  1.56 us (1%)
    ppermute x13, starting transfers between devices, hop(): return lax.ppermute(value, ('ctx', 'zhi'), pairs)  27.1 us
    ppermute x13, waiting for transfers between devices, hop(): return lax.ppermute(value, ('ctx', 'zhi'), pairs)  24 us
    all_to_all x3, starting transfers between devices, across(): lax.all_to_all(value, ('x', 'y'), split_axis=0, concat_axis=0, tiled=True)  17.9 us
    all_to_all x1, blocking collectives, across(): lax.all_to_all(value, ('x', 'y'), split_axis=0, concat_axis=0, tiled=True)  16.6 us
    all_to_all x1, blocking collectives, shards(): lax.all_to_all(outgoing, ('ctx', 'zhi'), split_axis=0, concat_axis=0, til...  11.9 us
    unnamed x20, local copies, waits for them, and re-layouts  11.2 us
    pallas_call x2, Pallas kernels, gate_up(): pl.pallas_call(gate_up_kernel, out_shape=jax.ShapeDtypeStruct((128, 512),...  10.6 us
    pallas_call x2, Pallas kernels, down(): pl.pallas_call(down_kernel, out_shape=jax.ShapeDtypeStruct((128, 1792), b...  8.99 us
  transfers between devices with their start and end apart: 21, of which 12 were waited for; matrix products, arithmetic and copies ran while one was open for 4% of the time, Pallas kernels for 12%

profile of v4, /device:TPU:32, one launch (start us, length us, event | category | flops | bytes accessed | tf_op | source)
XLA Modules:
  0.0 155.7 jit_solution(10041217499708010473)
XLA Ops:
  4.4 1.9 %collective-permute-start.2 = (bf16[4,7296]{1,0:T(4,128)(2,1)S(1)}, bf16[4,7296]{1,0:T(4,128)(2,1)S(1)}, u32[]{:S(2)}, u32[]{:S(2)}) collective-permute-start(bf16[4,7296]{1,0:T(4,128)(2,1)S(1)} %shard_map.122), channel_id=1, source_target_pairs={{0,192},{16,208},{64,0},{80,16},{128,64},{144,80},{192,128},{208,1... | collective-permute-start | bytes 175112 | tf_op jit(solution)/shard_map/ppermute | solution.py:255
  7.9 2.8 %collective-permute-start = (bf16[4,7296]{1,0:T(4,128)(2,1)S(1)}, bf16[4,7296]{1,0:T(4,128)(2,1)S(1)}, u32[]{:S(2)}, u32[]{:S(2)}) collective-permute-start(bf16[4,7296]{1,0:T(4,128)(2,1)S(1)} %shard_map.122), channel_id=1, source_target_pairs={{0,64},{16,80},{64,128},{80,144},{128,192},{144,208},{192,0},{208,... | collective-permute-start | bytes 175112 | tf_op jit(solution)/shard_map/ppermute | solution.py:255
  13.5 2.7 %shard_map.123 = bf16[128,7168]{1,0:T(8,128)(2,1)} custom-call(s32[3]{0:T(128)S(1)} %pad_add_fusion.place_ref, bf16[16,7296]{1,0:T(8,128)(2,1)S(1)} %pad_maximum_fusion.1.tokens_ref), custom_call_target="tpu_custom_call" | custom-call | flops 29360128 | bytes 2064384 | tf_op jit(solution)/shard_map/pallas_call | solution.py:111
  16.7 7.0 %all-to-all-start = ((bf16[16,8,7168]{2,1,0:T(8,128)(2,1)}), bf16[16,8,7168]{2,1,0:T(8,128)(2,1)S(1)}, u32[]{:S(2)}, u32[]{:S(2)}) async-start(bf16[16,8,7168]{2,1,0:T(8,128)(2,1)} %bitcast.5), calls=%async_computation | async-start | bytes 3670016 | tf_op jit(solution)/shard_map/all_to_all | solution.py:263
  27.1 5.5 %collective-permute-start.6 = (bf16[4,7296]{1,0:T(4,128)(2,1)S(1)}, bf16[4,7296]{1,0:T(4,128)(2,1)S(1)}, u32[]{:S(2)}, u32[]{:S(2)}) collective-permute-start(bf16[4,7296]{1,0:T(4,128)(2,1)S(1)} %shard_map.122), channel_id=1, source_target_pairs={{0,208},{16,192},{64,16},{80,0},{128,80},{144,64},{192,144},{208,1... | collective-permute-start | bytes 175112 | tf_op jit(solution)/shard_map/ppermute | solution.py:255
  33.3 3.0 %collective-permute-start.4 = (bf16[4,7296]{1,0:T(4,128)(2,1)S(1)}, bf16[4,7296]{1,0:T(4,128)(2,1)S(1)}, u32[]{:S(2)}, u32[]{:S(2)}) collective-permute-start(bf16[4,7296]{1,0:T(4,128)(2,1)S(1)} %shard_map.122), channel_id=1, source_target_pairs={{0,80},{16,64},{64,144},{80,128},{128,208},{144,192},{192,16},{208... | collective-permute-start | bytes 175112 | tf_op jit(solution)/shard_map/ppermute | solution.py:255
  36.3 3.9 %collective-permute-start.3 = (bf16[4,7296]{1,0:T(4,128)(2,1)S(1)}, bf16[4,7296]{1,0:T(4,128)(2,1)S(1)}, u32[]{:S(2)}, u32[]{:S(2)}) collective-permute-start(bf16[4,7296]{1,0:T(4,128)(2,1)S(1)} %shard_map.122), channel_id=1, source_target_pairs={{0,16},{16,0},{64,80},{80,64},{128,144},{144,128},{192,208},{208,1... | collective-permute-start | bytes 175112 | tf_op jit(solution)/shard_map/ppermute | solution.py:255
  40.4 5.0 %collective-permute-done.4 = bf16[4,7296]{1,0:T(4,128)(2,1)S(1)} collective-permute-done((bf16[4,7296]{1,0:T(4,128)(2,1)S(1)}, bf16[4,7296]{1,0:T(4,128)(2,1)S(1)}, u32[]{:S(2)}, u32[]{:S(2)}) %collective-permute-start.4) | collective-permute-done | bytes 58400 | tf_op jit(solution)/shard_map/ppermute | solution.py:255
  45.5 2.6 %shard_map.124 = bf16[128,7168]{1,0:T(8,128)(2,1)} custom-call(s32[3]{0:T(128)S(1)} %pad_add_fusion.place_ref, bf16[16,7296]{1,0:T(8,128)(2,1)S(1)} %pad_maximum_fusion.2.tokens_ref), custom_call_target="tpu_custom_call" | custom-call | flops 29360128 | bytes 2064384 | tf_op jit(solution)/shard_map/pallas_call | solution.py:111
  48.1 3.1 %all-to-all-done = bf16[16,8,7168]{2,1,0:T(8,128)(2,1)S(1)} async-done(((bf16[16,8,7168]{2,1,0:T(8,128)(2,1)}), bf16[16,8,7168]{2,1,0:T(8,128)(2,1)S(1)}, u32[]{:S(2)}, u32[]{:S(2)}) %all-to-all-start) | async-done | bytes 1835040 | tf_op jit(solution)/shard_map/all_to_all | solution.py:263
  51.2 4.4 %all-to-all-start.1 = ((bf16[16,8,7168]{2,1,0:T(8,128)(2,1)}), bf16[16,8,7168]{2,1,0:T(8,128)(2,1)}, u32[]{:S(2)}, u32[]{:S(2)}) async-start(bf16[16,8,7168]{2,1,0:T(8,128)(2,1)} %bitcast.12), calls=%async_computation.1 | async-start | bytes 3670016 | tf_op jit(solution)/shard_map/all_to_all | solution.py:263
  56.3 1.8 %collective-permute-start.14 = (f32[32,640]{1,0:T(8,128)}, f32[32,640]{1,0:T(8,128)S(1)}, u32[]{:S(2)}, u32[]{:S(2)}) collective-permute-start(f32[32,640]{1,0:T(8,128)} %get-tuple-element.31), channel_id=1, source_target_pairs={{0,192},{64,0},{128,64},{192,128},{1,193},{65,1},{129,65},{193,129... | collective-permute-start | bytes 245768 | tf_op jit(solution)/shard_map/ppermute | solution.py:288
  58.1 1.7 %collective-permute-start.13 = (f32[32,640]{1,0:T(8,128)S(1)}, f32[32,640]{1,0:T(8,128)}, u32[]{:S(2)}, u32[]{:S(2)}) collective-permute-start(f32[32,640]{1,0:T(8,128)S(1)} %get-tuple-element.32), channel_id=1, source_target_pairs={{0,128},{64,192},{128,0},{192,64},{1,129},{65,193},{129,1},{193,65... | collective-permute-start | bytes 245768 | tf_op jit(solution)/shard_map/ppermute | solution.py:288
  61.5 2.1 %collective-permute-done.14 = f32[32,640]{1,0:T(8,128)S(1)} collective-permute-done((f32[32,640]{1,0:T(8,128)}, f32[32,640]{1,0:T(8,128)S(1)}, u32[]{:S(2)}, u32[]{:S(2)}) %collective-permute-start.14) | collective-permute-done | bytes 81952 | tf_op jit(solution)/shard_map/ppermute | solution.py:288
  65.6 3.1 %copy-done.1 = bf16[1,2,7168,256]{3,2,1,0:T(8,128)(2,1)S(1)} copy-done((bf16[1,2,7168,256]{3,2,1,0:T(8,128)(2,1)S(1)}, bf16[1,2,7168,256]{3,2,1,0:T(8,128)(2,1)}, u32[]{:S(2)}) %copy-start.1) | copy-done | bytes 7340056
  68.7 4.6 %shard_map.125.p0 = bf16[128,512]{1,0:T(8,128)(2,1)S(1)} custom-call(bf16[128,7168]{1,0:T(8,128)(2,1)S(1)} %bitcast.62, bf16[2,7168,256]{2,1,0:T(8,128)(2,1)S(1)} %bitcast.57, bf16[2,7168,256]{2,1,0:T(8,128)(2,1)} %collective-permute-done.7.other_ref), custom_call_target="tpu_custom_call" | custom-call | flops 1879048192 | bytes 16515072 | tf_op jit(solution)/shard_map/pallas_call | solution.py:146
  73.3 2.4 %collective-permute-start.8 = (bf16[128,512]{1,0:T(8,128)(2,1)S(1)}, bf16[128,512]{1,0:T(8,128)(2,1)S(1)}, u32[]{:S(2)}, u32[]{:S(2)}) collective-permute-start(bf16[128,512]{1,0:T(8,128)(2,1)S(1)} %shard_map.125.p0), channel_id=1, source_target_pairs={{0,64},{16,80},{64,128},{80,144},{128,192},{144,208},{192,0},{208,... | collective-permute-start | bytes 393224 | tf_op jit(solution)/shard_map/ppermute | solution.py:255
  75.7 2.5 %collective-permute-start.9 = (bf16[128,512]{1,0:T(8,128)(2,1)S(1)}, bf16[128,512]{1,0:T(8,128)(2,1)S(1)}, u32[]{:S(2)}, u32[]{:S(2)}) collective-permute-start(bf16[128,512]{1,0:T(8,128)(2,1)S(1)} %shard_map.125.p0), channel_id=1, source_target_pairs={{0,128},{16,144},{64,192},{80,208},{128,0},{144,16},{192,64},{208,... | collective-permute-start | bytes 393224 | tf_op jit(solution)/shard_map/ppermute | solution.py:255
  78.9 3.8 %collective-permute-done.8.p1 = bf16[128,512]{1,0:T(8,128)(2,1)S(1)} collective-permute-done((bf16[128,512]{1,0:T(8,128)(2,1)S(1)}, bf16[128,512]{1,0:T(8,128)(2,1)S(1)}, u32[]{:S(2)}, u32[]{:S(2)}) %collective-permute-start.8) | collective-permute-done | bytes 131104 | tf_op jit(solution)/shard_map/ppermute | solution.py:255
  84.1 2.3 %collective-permute-done.10.p3 = bf16[128,512]{1,0:T(8,128)(2,1)S(1)} collective-permute-done((bf16[128,512]{1,0:T(8,128)(2,1)S(1)}, bf16[128,512]{1,0:T(8,128)(2,1)S(1)}, u32[]{:S(2)}, u32[]{:S(2)}) %collective-permute-start.10) | collective-permute-done | bytes 131104 | tf_op jit(solution)/shard_map/ppermute | solution.py:255
  86.4 4.9 %shard_map.126 = bf16[128,1792]{1,0:T(8,128)(2,1)} custom-call(s32[3]{0:T(128)S(1)} %pad_add_fusion.place_ref, bf16[128,512]{1,0:T(8,128)(2,1)S(1)} %shard_map.125.p0, bf16[128,512]{1,0:T(8,128)(2,1)S(1)} %collective-permute-done.8.p1, bf16[128,512]{1,0:T(8,128)(2,1)S(1)} %collective-permute-done.9.p2, bf16[128,512]{1,0:T(8,128)(2,1)S(1)} %collective-permute-done.10.p3, ...), custom_call_target="tpu_custom_call" | custom-call | flops 939524096 | bytes 7864320 | tf_op jit(solution)/shard_map/pallas_call | solution.py:183
  91.3 6.5 %all-to-all-start.2 = ((bf16[16,8,1792]{2,1,0:T(8,128)(2,1)}), bf16[16,8,1792]{2,1,0:T(8,128)(2,1)S(1)}, u32[]{:S(2)}, u32[]{:S(2)}) async-start(bf16[16,8,1792]{2,1,0:T(8,128)(2,1)} %bitcast.20), calls=%async_computation.2 | async-start | bytes 917504 | tf_op jit(solution)/shard_map/all_to_all | solution.py:263
  97.8 3.1 %copy-done.2 = bf16[1,2,7168,256]{3,2,1,0:T(8,128)(2,1)S(1)} copy-done((bf16[1,2,7168,256]{3,2,1,0:T(8,128)(2,1)S(1)}, bf16[1,2,7168,256]{3,2,1,0:T(8,128)(2,1)}, u32[]{:S(2)}) %copy-start.2) | copy-done | bytes 7340056
  100.9 6.0 %shard_map.127.p0 = bf16[128,512]{1,0:T(8,128)(2,1)S(1)} custom-call(bf16[128,7168]{1,0:T(8,128)(2,1)} %bitcast.13.rows_ref, bf16[2,7168,256]{2,1,0:T(8,128)(2,1)S(1)} %bitcast.58, bf16[2,7168,256]{2,1,0:T(8,128)(2,1)} %collective-permute-done.7.other_ref), custom_call_target="tpu_custom_call" | custom-call | flops 1879048192 | bytes 16515072 | tf_op jit(solution)/shard_map/pallas_call | solution.py:146
  106.9 2.3 %collective-permute-start.16 = (bf16[128,512]{1,0:T(8,128)(2,1)S(1)}, bf16[128,512]{1,0:T(8,128)(2,1)S(1)}, u32[]{:S(2)}, u32[]{:S(2)}) collective-permute-start(bf16[128,512]{1,0:T(8,128)(2,1)S(1)} %shard_map.127.p0), channel_id=1, source_target_pairs={{0,128},{16,144},{64,192},{80,208},{128,0},{144,16},{192,64},{208,... | collective-permute-start | bytes 393224 | tf_op jit(solution)/shard_map/ppermute | solution.py:255
  110.0 3.4 %collective-permute-done.15.p1 = bf16[128,512]{1,0:T(8,128)(2,1)S(1)} collective-permute-done((bf16[128,512]{1,0:T(8,128)(2,1)S(1)}, bf16[128,512]{1,0:T(8,128)(2,1)S(1)}, u32[]{:S(2)}, u32[]{:S(2)}) %collective-permute-start.15) | collective-permute-done | bytes 131104 | tf_op jit(solution)/shard_map/ppermute | solution.py:255
  113.4 3.8 %collective-permute-done.16.p2 = bf16[128,512]{1,0:T(8,128)(2,1)S(1)} collective-permute-done((bf16[128,512]{1,0:T(8,128)(2,1)S(1)}, bf16[128,512]{1,0:T(8,128)(2,1)S(1)}, u32[]{:S(2)}, u32[]{:S(2)}) %collective-permute-start.16) | collective-permute-done | bytes 131104 | tf_op jit(solution)/shard_map/ppermute | solution.py:255
  117.2 1.8 %collective-permute-done.17.p3 = bf16[128,512]{1,0:T(8,128)(2,1)S(1)} collective-permute-done((bf16[128,512]{1,0:T(8,128)(2,1)S(1)}, bf16[128,512]{1,0:T(8,128)(2,1)S(1)}, u32[]{:S(2)}, u32[]{:S(2)}) %collective-permute-start.17) | collective-permute-done | bytes 131104 | tf_op jit(solution)/shard_map/ppermute | solution.py:255
  119.0 2.0 %copy-done.4 = bf16[1,2048,896]{2,1,0:T(8,128)(2,1)S(1)} copy-done((bf16[1,2048,896]{2,1,0:T(8,128)(2,1)S(1)}, bf16[1,2048,896]{2,1,0:T(8,128)(2,1)}, u32[]{:S(2)}) %copy-start.4) | copy-done | bytes 3670040
  121.0 4.1 %shard_map.128 = bf16[128,1792]{1,0:T(8,128)(2,1)S(1)} custom-call(s32[3]{0:T(128)S(1)} %pad_add_fusion.place_ref, bf16[128,512]{1,0:T(8,128)(2,1)S(1)} %shard_map.127.p0, bf16[128,512]{1,0:T(8,128)(2,1)S(1)} %collective-permute-done.15.p1, bf16[128,512]{1,0:T(8,128)(2,1)S(1)} %collective-permute-done.16.p2, ...), custom_call_target="tpu_custom_call" | custom-call | flops 939524096 | bytes 7864320 | tf_op jit(solution)/shard_map/pallas_call | solution.py:183
  125.1 16.6 %all_to_all.25 = bf16[16,8,1792]{2,1,0:T(8,128)(2,1)S(1)} all-to-all(bf16[16,8,1792]{2,1,0:T(8,128)(2,1)S(1)} %bitcast.65), channel_id=1, replica_groups=mesh['ctx'=4,'att'=2,'zhi'=2,'x'=4,'y'=4] {'x','y'}, dimensions={0} | all-to-all | bytes 917504 | tf_op jit(solution)/shard_map/all_to_all | solution.py:263
  143.1 11.9 %all_to_all.26 = bf16[8,4,1792]{2,1,0:T(4,128)(2,1)S(1)} all-to-all(bf16[8,4,1792]{2,1,0:T(4,128)(2,1)S(1)} %shard_map.129), channel_id=1, replica_groups=mesh['ctx'=4,'att'=2,'zhi'=2,'x'=4,'y'=4] {'ctx','zhi'}, dimensions={0} | all-to-all | bytes 229376 | tf_op jit(solution)/shard_map/all_to_all | solution.py:299
  (57 shorter events, 21.4 us)
Async XLA Ops:
  0.6 25.0 %copy-start = (bf16[1,1024,512]{2,1,0:T(8,128)(2,1)S(1)}, bf16[1,1024,512]{2,1,0:T(8,128)(2,1)}, u32[]{:S(2)}) copy-start(bf16[1,1024,512]{2,1,0:T(8,128)(2,1)} %param.13) | copy-start | bytes 3145732
  0.6 0.9 copy-start.5
  1.6 0.7 copy-start.6
  2.3 0.7 copy-start.7
  2.9 0.7 copy-start.8
  3.6 20.1 %copy-start.9 = (bf16[1,128,64]{1,2,0:T(8,128)(2,1)S(1)}, bf16[1,128,64]{1,2,0:T(8,128)(2,1)}, u32[]{:S(2)}) copy-start(bf16[1,128,64]{1,2,0:T(8,128)(2,1)} %param.12) | copy-start | bytes 49156
  4.4 6.4 %collective-permute-start.2 = (bf16[4,7296]{1,0:T(4,128)(2,1)S(1)}, bf16[4,7296]{1,0:T(4,128)(2,1)S(1)}, u32[]{:S(2)}, u32[]{:S(2)}) collective-permute-start(bf16[4,7296]{1,0:T(4,128)(2,1)S(1)} %shard_map.122), channel_id=1, source_target_pairs={{0,192},{16,208},{64,0},{80,16},{128,64},{144,80},{192,128},{208,1... | collective-permute-start | bytes 175112 | tf_op jit(solution)/shard_map/ppermute | solution.py:255
  6.3 5.8 %collective-permute-start.1 = (bf16[4,7296]{1,0:T(4,128)(2,1)S(1)}, bf16[4,7296]{1,0:T(4,128)(2,1)S(1)}, u32[]{:S(2)}, u32[]{:S(2)}) collective-permute-start(bf16[4,7296]{1,0:T(4,128)(2,1)S(1)} %shard_map.122), channel_id=1, source_target_pairs={{0,128},{16,144},{64,192},{80,208},{128,0},{144,16},{192,64},{208,... | collective-permute-start | bytes 175112 | tf_op jit(solution)/shard_map/ppermute | solution.py:255
  7.9 5.5 %collective-permute-start = (bf16[4,7296]{1,0:T(4,128)(2,1)S(1)}, bf16[4,7296]{1,0:T(4,128)(2,1)S(1)}, u32[]{:S(2)}, u32[]{:S(2)}) collective-permute-start(bf16[4,7296]{1,0:T(4,128)(2,1)S(1)} %shard_map.122), channel_id=1, source_target_pairs={{0,64},{16,80},{64,128},{80,144},{128,192},{144,208},{192,0},{208,... | collective-permute-start | bytes 175112 | tf_op jit(solution)/shard_map/ppermute | solution.py:255
  16.2 49.4 %collective-permute-start.7 = (bf16[2,7168,256]{2,1,0:T(8,128)(2,1)}, bf16[2,7168,256]{2,1,0:T(8,128)(2,1)}, u32[]{:S(2)}, u32[]{:S(2)}) collective-permute-start(bf16[2,7168,256]{2,1,0:T(8,128)(2,1)} %bitcast.56), channel_id=1, source_target_pairs={{0,32},{32,0},{1,33},{33,1},{2,34},{34,2},{3,35},{35,3},{4,36},{36... | collective-permute-start | bytes 22020104 | tf_op jit(solution)/shard_map/ppermute | solution.py:276
  16.2 62.7 %collective-permute-start.11 = (bf16[4,2,256,896]{3,2,1,0:T(8,128)(2,1)}, bf16[4,2,256,896]{3,2,1,0:T(8,128)(2,1)}, u32[]{:S(2)}, u32[]{:S(2)}) collective-permute-start(bf16[4,2,256,896]{3,2,1,0:T(8,128)(2,1)} %bitcast.59), channel_id=1, source_target_pairs={{0,32},{32,0},{1,33},{33,1},{2,34},{34,2},{3,35},{35,3},{4,36},{36... | collective-permute-start | bytes 11010056 | tf_op jit(solution)/shard_map/ppermute | solution.py:277
  16.7 34.4 %all-to-all-start = ((bf16[16,8,7168]{2,1,0:T(8,128)(2,1)}), bf16[16,8,7168]{2,1,0:T(8,128)(2,1)S(1)}, u32[]{:S(2)}, u32[]{:S(2)}) async-start(bf16[16,8,7168]{2,1,0:T(8,128)(2,1)} %bitcast.5), calls=%async_computation | async-start | bytes 3670016 | tf_op jit(solution)/shard_map/all_to_all | solution.py:263
  27.1 9.2 %collective-permute-start.6 = (bf16[4,7296]{1,0:T(4,128)(2,1)S(1)}, bf16[4,7296]{1,0:T(4,128)(2,1)S(1)}, u32[]{:S(2)}, u32[]{:S(2)}) collective-permute-start(bf16[4,7296]{1,0:T(4,128)(2,1)S(1)} %shard_map.122), channel_id=1, source_target_pairs={{0,208},{16,192},{64,16},{80,0},{128,80},{144,64},{192,144},{208,1... | collective-permute-start | bytes 175112 | tf_op jit(solution)/shard_map/ppermute | solution.py:255
  32.9 7.4 %collective-permute-start.5 = (bf16[4,7296]{1,0:T(4,128)(2,1)S(1)}, bf16[4,7296]{1,0:T(4,128)(2,1)S(1)}, u32[]{:S(2)}, u32[]{:S(2)}) collective-permute-start(bf16[4,7296]{1,0:T(4,128)(2,1)S(1)} %shard_map.122), channel_id=1, source_target_pairs={{0,144},{16,128},{64,208},{80,192},{128,16},{144,0},{192,80},{208,... | collective-permute-start | bytes 175112 | tf_op jit(solution)/shard_map/ppermute | solution.py:255
  33.3 12.1 %collective-permute-start.4 = (bf16[4,7296]{1,0:T(4,128)(2,1)S(1)}, bf16[4,7296]{1,0:T(4,128)(2,1)S(1)}, u32[]{:S(2)}, u32[]{:S(2)}) collective-permute-start(bf16[4,7296]{1,0:T(4,128)(2,1)S(1)} %shard_map.122), channel_id=1, source_target_pairs={{0,80},{16,64},{64,144},{80,128},{128,208},{144,192},{192,16},{208... | collective-permute-start | bytes 175112 | tf_op jit(solution)/shard_map/ppermute | solution.py:255
  36.3 9.0 %collective-permute-start.3 = (bf16[4,7296]{1,0:T(4,128)(2,1)S(1)}, bf16[4,7296]{1,0:T(4,128)(2,1)S(1)}, u32[]{:S(2)}, u32[]{:S(2)}) collective-permute-start(bf16[4,7296]{1,0:T(4,128)(2,1)S(1)} %shard_map.122), channel_id=1, source_target_pairs={{0,16},{16,0},{64,80},{80,64},{128,144},{144,128},{192,208},{208,1... | collective-permute-start | bytes 175112 | tf_op jit(solution)/shard_map/ppermute | solution.py:255
  51.2 40.1 %all-to-all-start.1 = ((bf16[16,8,7168]{2,1,0:T(8,128)(2,1)}), bf16[16,8,7168]{2,1,0:T(8,128)(2,1)}, u32[]{:S(2)}, u32[]{:S(2)}) async-start(bf16[16,8,7168]{2,1,0:T(8,128)(2,1)} %bitcast.12), calls=%async_computation.1 | async-start | bytes 3670016 | tf_op jit(solution)/shard_map/all_to_all | solution.py:263
  56.3 7.3 %collective-permute-start.14 = (f32[32,640]{1,0:T(8,128)}, f32[32,640]{1,0:T(8,128)S(1)}, u32[]{:S(2)}, u32[]{:S(2)}) collective-permute-start(f32[32,640]{1,0:T(8,128)} %get-tuple-element.31), channel_id=1, source_target_pairs={{0,192},{64,0},{128,64},{192,128},{1,193},{65,1},{129,65},{193,129... | collective-permute-start | bytes 245768 | tf_op jit(solution)/shard_map/ppermute | solution.py:288
  58.1 5.6 %collective-permute-start.13 = (f32[32,640]{1,0:T(8,128)S(1)}, f32[32,640]{1,0:T(8,128)}, u32[]{:S(2)}, u32[]{:S(2)}) collective-permute-start(f32[32,640]{1,0:T(8,128)S(1)} %get-tuple-element.32), channel_id=1, source_target_pairs={{0,128},{64,192},{128,0},{192,64},{1,129},{65,193},{129,1},{193,65... | collective-permute-start | bytes 245768 | tf_op jit(solution)/shard_map/ppermute | solution.py:288
  59.9 4.7 %collective-permute-start.12 = (f32[32,640]{1,0:T(8,128)S(1)}, f32[32,640]{1,0:T(8,128)}, u32[]{:S(2)}, u32[]{:S(2)}) collective-permute-start(f32[32,640]{1,0:T(8,128)S(1)} %get-tuple-element.30), channel_id=1, source_target_pairs={{0,64},{64,128},{128,192},{192,0},{1,65},{65,129},{129,193},{193,1... | collective-permute-start | bytes 245768 | tf_op jit(solution)/shard_map/ppermute | solution.py:288
  65.6 3.1 %copy-start.1 = (bf16[1,2,7168,256]{3,2,1,0:T(8,128)(2,1)S(1)}, bf16[1,2,7168,256]{3,2,1,0:T(8,128)(2,1)}, u32[]{:S(2)}) copy-start(bf16[1,2,7168,256]{3,2,1,0:T(8,128)(2,1)} %param.20) | copy-start | bytes 22020100
  68.7 17.7 %copy-start.3 = (bf16[1,2048,896]{2,1,0:T(8,128)(2,1)S(1)}, bf16[1,2048,896]{2,1,0:T(8,128)(2,1)}, u32[]{:S(2)}) copy-start(bf16[1,2048,896]{2,1,0:T(8,128)(2,1)} %param.21) | copy-start | bytes 11010052
  73.3 9.4 %collective-permute-start.8 = (bf16[128,512]{1,0:T(8,128)(2,1)S(1)}, bf16[128,512]{1,0:T(8,128)(2,1)S(1)}, u32[]{:S(2)}, u32[]{:S(2)}) collective-permute-start(bf16[128,512]{1,0:T(8,128)(2,1)S(1)} %shard_map.125.p0), channel_id=1, source_target_pairs={{0,64},{16,80},{64,128},{80,144},{128,192},{144,208},{192,0},{208,... | collective-permute-start | bytes 393224 | tf_op jit(solution)/shard_map/ppermute | solution.py:255
  75.7 8.4 %collective-permute-start.9 = (bf16[128,512]{1,0:T(8,128)(2,1)S(1)}, bf16[128,512]{1,0:T(8,128)(2,1)S(1)}, u32[]{:S(2)}, u32[]{:S(2)}) collective-permute-start(bf16[128,512]{1,0:T(8,128)(2,1)S(1)} %shard_map.125.p0), channel_id=1, source_target_pairs={{0,128},{16,144},{64,192},{80,208},{128,0},{144,16},{192,64},{208,... | collective-permute-start | bytes 393224 | tf_op jit(solution)/shard_map/ppermute | solution.py:255
  78.2 8.2 %collective-permute-start.10 = (bf16[128,512]{1,0:T(8,128)(2,1)S(1)}, bf16[128,512]{1,0:T(8,128)(2,1)S(1)}, u32[]{:S(2)}, u32[]{:S(2)}) collective-permute-start(bf16[128,512]{1,0:T(8,128)(2,1)S(1)} %shard_map.125.p0), channel_id=1, source_target_pairs={{0,192},{16,208},{64,0},{80,16},{128,64},{144,80},{192,128},{208,1... | collective-permute-start | bytes 393224 | tf_op jit(solution)/shard_map/ppermute | solution.py:255
  91.3 18.7 %all-to-all-start.2 = ((bf16[16,8,1792]{2,1,0:T(8,128)(2,1)}), bf16[16,8,1792]{2,1,0:T(8,128)(2,1)S(1)}, u32[]{:S(2)}, u32[]{:S(2)}) async-start(bf16[16,8,1792]{2,1,0:T(8,128)(2,1)} %bitcast.20), calls=%async_computation.2 | async-start | bytes 917504 | tf_op jit(solution)/shard_map/all_to_all | solution.py:263
  97.8 3.1 %copy-start.2 = (bf16[1,2,7168,256]{3,2,1,0:T(8,128)(2,1)S(1)}, bf16[1,2,7168,256]{3,2,1,0:T(8,128)(2,1)}, u32[]{:S(2)}) copy-start(bf16[1,2,7168,256]{3,2,1,0:T(8,128)(2,1)} %param.20) | copy-start | bytes 22020100
  106.8 6.6 %collective-permute-start.15 = (bf16[128,512]{1,0:T(8,128)(2,1)S(1)}, bf16[128,512]{1,0:T(8,128)(2,1)S(1)}, u32[]{:S(2)}, u32[]{:S(2)}) collective-permute-start(bf16[128,512]{1,0:T(8,128)(2,1)S(1)} %shard_map.127.p0), channel_id=1, source_target_pairs={{0,64},{16,80},{64,128},{80,144},{128,192},{144,208},{192,0},{208,... | collective-permute-start | bytes 393224 | tf_op jit(solution)/shard_map/ppermute | solution.py:255
  106.9 10.3 %collective-permute-start.16 = (bf16[128,512]{1,0:T(8,128)(2,1)S(1)}, bf16[128,512]{1,0:T(8,128)(2,1)S(1)}, u32[]{:S(2)}, u32[]{:S(2)}) collective-permute-start(bf16[128,512]{1,0:T(8,128)(2,1)S(1)} %shard_map.127.p0), channel_id=1, source_target_pairs={{0,128},{16,144},{64,192},{80,208},{128,0},{144,16},{192,64},{208,... | collective-permute-start | bytes 393224 | tf_op jit(solution)/shard_map/ppermute | solution.py:255
  109.3 9.7 %collective-permute-start.17 = (bf16[128,512]{1,0:T(8,128)(2,1)S(1)}, bf16[128,512]{1,0:T(8,128)(2,1)S(1)}, u32[]{:S(2)}, u32[]{:S(2)}) collective-permute-start(bf16[128,512]{1,0:T(8,128)(2,1)S(1)} %shard_map.127.p0), channel_id=1, source_target_pairs={{0,192},{16,208},{64,0},{80,16},{128,64},{144,80},{192,128},{208,1... | collective-permute-start | bytes 393224 | tf_op jit(solution)/shard_map/ppermute | solution.py:255
  119.0 2.0 %copy-start.4 = (bf16[1,2048,896]{2,1,0:T(8,128)(2,1)S(1)}, bf16[1,2048,896]{2,1,0:T(8,128)(2,1)}, u32[]{:S(2)}) copy-start(bf16[1,2048,896]{2,1,0:T(8,128)(2,1)} %param.21) | copy-start | bytes 11010052

commit v5 on v4

--- a/solution.py
+++ b/solution.py
@@ -24,11 +24,15 @@
     weights = jnp.where(live_mask[None, :], jnp.exp(softmax_scale * scores), f32(0.0))
     mass = jnp.sum(weights, axis=1, keepdims=True)
     numerator = jnp.dot(weights.astype(bf16), latent_cache[0], preferred_element_type=f32)
-    return jnp.concatenate([numerator, jnp.broadcast_to(mass, (mass.shape[0], 128))], axis=1)
-
-
-def finish_attention(summed):
-    return (summed[:, :512] / summed[:, 512:513]).astype(bf16)[None]
+    high = lax.reduce_precision(mass, 8, 7)
+    low = mass - high
+    tail = jnp.concatenate([jnp.broadcast_to(v, (128, 64)) for v in (high, low)], axis=1)
+    return jnp.concatenate([numerator, tail], axis=1).astype(bf16)
+
+
+def finish_attention(parts):
+    summed = sum(v.astype(f32) for v in parts)
+    return (summed[:, :512] / (summed[:, 512:513] + summed[:, 576:577])).astype(bf16)[None]
 
 
 VMEM = pl.BlockSpec(memory_space=pltpu.VMEM)
@@ -77,7 +81,6 @@
         out_shape=jax.ShapeDtypeStruct((TOK, moe_rows.shape[1] + INFO), bf16),
         in_specs=[SMEM, SMEM, VMEM, VMEM],
         out_specs=VMEM,
-        compiler_params=room(4),
     )(route_ids, route_gates, moe_rows, norm_gain)
 
 
@@ -152,7 +155,7 @@
             pltpu.VMEM((2, 2, width, 256), bf16),
             pltpu.SemaphoreType.DMA((width // STEP, 2)),
         ],
-        compiler_params=room(24),
+        compiler_params=room(57),
         cost_estimate=pl.CostEstimate(
             flops=2 * 128 * width * 1024, bytes_accessed=2 * width * (1024 + 128), transcendentals=65536
         ),
@@ -186,7 +189,7 @@
         in_specs=[SMEM] + [VMEM] * 4 + [HBM] * 2,
         out_specs=VMEM,
         scratch_shapes=[pltpu.VMEM((2, 4, 2, 256, 896), bf16), pltpu.SemaphoreType.DMA((2, 4))],
-        compiler_params=room(16),
+        compiler_params=room(58),
         cost_estimate=pl.CostEstimate(
             flops=2 * 128 * 2048 * 1792, bytes_accessed=2 * 2048 * 1792 + 2 * 128 * 2048, transcendentals=0
         ),
@@ -281,15 +284,16 @@
     got1 = across(rows1)
 
     pieces0 = hidden_of(got0)
+    pieces0[0], part = lax.optimization_barrier((pieces0[0], part))
     part = part.reshape(4, 32, 640)
-    summed = lax.dynamic_index_in_dim(part, c, 0, keepdims=False)
+    parts = [lax.dynamic_index_in_dim(part, c, 0, keepdims=False)]
     for k in (1, 2, 3):
         sent = lax.dynamic_index_in_dim(part, (c + k) % 4, 0, keepdims=False)
-        summed = summed + lax.ppermute(sent, "ctx", [(i, (i + k) % 4) for i in range(4)])
-    attended = finish_attention(summed)
+        parts.append(lax.ppermute(sent, "ctx", [(i, (i + k) % 4) for i in range(4)]))
+    attended = finish_attention(parts)
     result0 = down(place, pieces0, weight_out, other_out)
-    got1, result0, attended = lax.optimization_barrier((got1, result0, attended))
     back0 = across(result0)
+    got1, attended, _ = lax.optimization_barrier((got1, attended, result0))
     pieces1 = hidden_of(got1)
     pieces1[0], back0 = lax.optimization_barrier((pieces1[0], back0))
     result1 = down(place, pieces1, weight_out, other_out)

time: 156 us -> 158 us (1.013)
  local copies, waits for them, and re-layouts: 12 us -> 2.76 us
  Pallas kernels: 27 us -> 35.1 us
  starting transfers between devices: 50.8 us -> 53.8 us
  waiting for transfers between devices: 30.2 us -> 27.2 us
  blocking collectives: 28.5 us -> 31.1 us
    unnamed x20 -> x24, local copies, waits for them, and re-layouts: 11.2 us -> 2.57 us
    pallas_call x2, Pallas kernels: 10.6 us -> 15.6 us  [gate_up(): pl.pallas_call(gate_up_kernel, out_shape=jax.ShapeDtypeStruct((128, 512),...]
    ppermute x3, waiting for transfers between devices: 3.04 us -> 0.01 us  [shards(): lax.ppermute(sent, 'ctx', [(i, (i + k) % 4) for i in range(4)])]
    ppermute x13, starting transfers between devices: 27.1 us -> 30 us  [hop(): return lax.ppermute(value, ('ctx', 'zhi'), pairs)]
    all_to_all x3, waiting for transfers between devices: 3.08 us -> 5.33 us  [across(): lax.all_to_all(value, ('x', 'y'), split_axis=0, concat_axis=0, tiled=True)]
    ppermute x13, waiting for transfers between devices: 24 us -> 21.8 us  [hop(): return lax.ppermute(value, ('ctx', 'zhi'), pairs)]
    pallas_call x2, Pallas kernels: 8.99 us -> 11.1 us  [down(): pl.pallas_call(down_kernel, out_shape=jax.ShapeDtypeStruct((128, 1792), b...]
    all_to_all x1, blocking collectives: 11.9 us -> 13.6 us  [shards(): lax.all_to_all(outgoing, ('ctx', 'zhi'), split_axis=0, concat_axis=0, til...]
  transfers between devices with their start and end apart: 21 -> 21, of which waited for: 12 -> 10; matrix products, arithmetic and copies ran while one was open for 4% -> 3% of each run, Pallas kernels for 12% -> 15%
where the time goes in v5:
time: 158 us; the launch traced here: 157 us
  starting transfers between devices  53.8 us (34%)
  Pallas kernels  35.1 us (22%)
  blocking collectives  31.1 us (20%)
  waiting for transfers between devices  27.2 us (17%)
  matrix products  2.97 us (2%)
  other arithmetic  2.85 us (2%)
  local copies, waits for them, and re-layouts  2.76 us (2%)
  between operations  1.58 us (1%)
    ppermute x13, starting transfers between devices, hop(): return lax.ppermute(value, ('ctx', 'zhi'), pairs)  30 us
    ppermute x13, waiting for transfers between devices, hop(): return lax.ppermute(value, ('ctx', 'zhi'), pairs)  21.8 us
    all_to_all x3, starting transfers between devices, across(): lax.all_to_all(value, ('x', 'y'), split_axis=0, concat_axis=0, tiled=True)  18 us
    all_to_all x1, blocking collectives, across(): lax.all_to_all(value, ('x', 'y'), split_axis=0, concat_axis=0, tiled=True)  17.5 us
    pallas_call x2, Pallas kernels, gate_up(): pl.pallas_call(gate_up_kernel, out_shape=jax.ShapeDtypeStruct((128, 512),...  15.6 us
    all_to_all x1, blocking collectives, shards(): lax.all_to_all(outgoing, ('ctx', 'zhi'), split_axis=0, concat_axis=0, til...  13.6 us
    pallas_call x2, Pallas kernels, down(): pl.pallas_call(down_kernel, out_shape=jax.ShapeDtypeStruct((128, 1792), b...  11.1 us
    pallas_call x2, Pallas kernels, choose(): pl.pallas_call(choose_kernel, out_shape=jax.ShapeDtypeStruct((128, width)...  5.34 us
  transfers between devices with their start and end apart: 21, of which 10 were waited for; matrix products, arithmetic and copies ran while one was open for 3% of the time, Pallas kernels for 15%

profile of v5, /device:TPU:32, one launch (start us, length us, event | category | flops | bytes accessed | tf_op | source)
XLA Modules:
  0.0 157.3 jit_solution(13389280046484173631)
XLA Ops:
  0.6 1.7 %shard_map.122 = bf16[4,7296]{1,0:T(4,128)(2,1)} custom-call(s32[4,8]{1,0:T(4,128)} %ids_ref.1, f32[4,8]{1,0:T(4,128)} %gates_ref.1, bf16[4,7168]{1,0:T(4,128)(2,1)} %rows_ref.1, bf16[7168]{0:T(1024)(128)(2,1)} %gain_ref.1), custom_call_target="tpu_custom_call" | custom-call | tf_op jit(solution)/shard_map/pallas_call | solution.py:79
  2.4 1.8 %collective-permute-start.2 = (bf16[4,7296]{1,0:T(4,128)(2,1)}, bf16[4,7296]{1,0:T(4,128)(2,1)S(1)}, u32[]{:S(2)}, u32[]{:S(2)}) collective-permute-start(bf16[4,7296]{1,0:T(4,128)(2,1)} %shard_map.122), channel_id=1, source_target_pairs={{0,192},{16,208},{64,0},{80,16},{128,64},{144,80},{192,128},{208,1... | collective-permute-start | bytes 175112 | tf_op jit(solution)/shard_map/ppermute | solution.py:258
  4.2 1.5 collective-permute-start.1
  5.7 2.8 %collective-permute-start = (bf16[4,7296]{1,0:T(4,128)(2,1)}, bf16[4,7296]{1,0:T(4,128)(2,1)S(1)}, u32[]{:S(2)}, u32[]{:S(2)}) collective-permute-start(bf16[4,7296]{1,0:T(4,128)(2,1)} %shard_map.122), channel_id=1, source_target_pairs={{0,64},{16,80},{64,128},{80,144},{128,192},{144,208},{192,0},{208,... | collective-permute-start | bytes 175112 | tf_op jit(solution)/shard_map/ppermute | solution.py:258
  8.6 1.7 %collective-permute-done.1 = bf16[4,7296]{1,0:T(4,128)(2,1)S(1)} collective-permute-done((bf16[4,7296]{1,0:T(4,128)(2,1)}, bf16[4,7296]{1,0:T(4,128)(2,1)S(1)}, u32[]{:S(2)}, u32[]{:S(2)}) %collective-permute-start.1) | collective-permute-done | bytes 58400 | tf_op jit(solution)/shard_map/ppermute | solution.py:258
  12.4 2.6 %shard_map.123 = bf16[128,7168]{1,0:T(8,128)(2,1)} custom-call(s32[3]{0:T(128)S(1)} %pad_add_fusion.place_ref, bf16[16,7296]{1,0:T(8,128)(2,1)S(1)} %pad_maximum_fusion.tokens_ref), custom_call_target="tpu_custom_call" | custom-call | flops 29360128 | bytes 2064384 | tf_op jit(solution)/shard_map/pallas_call | solution.py:114
  17.5 7.2 %all-to-all-start = ((bf16[16,8,7168]{2,1,0:T(8,128)(2,1)}), bf16[16,8,7168]{2,1,0:T(8,128)(2,1)S(1)}, u32[]{:S(2)}, u32[]{:S(2)}) async-start(bf16[16,8,7168]{2,1,0:T(8,128)(2,1)} %bitcast.5), calls=%async_computation | async-start | bytes 3670016 | tf_op jit(solution)/shard_map/all_to_all | solution.py:266
  26.5 5.5 %collective-permute-start.6 = (bf16[4,7296]{1,0:T(4,128)(2,1)S(1)}, bf16[4,7296]{1,0:T(4,128)(2,1)S(1)}, u32[]{:S(2)}, u32[]{:S(2)}) collective-permute-start(bf16[4,7296]{1,0:T(4,128)(2,1)S(1)} %copy-done.5), channel_id=1, source_target_pairs={{0,208},{16,192},{64,16},{80,0},{128,80},{144,64},{192,144},{208,1... | collective-permute-start | bytes 175112 | tf_op jit(solution)/shard_map/ppermute | solution.py:258
  32.3 3.1 %collective-permute-start.4 = (bf16[4,7296]{1,0:T(4,128)(2,1)S(1)}, bf16[4,7296]{1,0:T(4,128)(2,1)S(1)}, u32[]{:S(2)}, u32[]{:S(2)}) collective-permute-start(bf16[4,7296]{1,0:T(4,128)(2,1)S(1)} %copy-done.5), channel_id=1, source_target_pairs={{0,80},{16,64},{64,144},{80,128},{128,208},{144,192},{192,16},{208... | collective-permute-start | bytes 175112 | tf_op jit(solution)/shard_map/ppermute | solution.py:258
  35.4 4.1 %collective-permute-start.3 = (bf16[4,7296]{1,0:T(4,128)(2,1)S(1)}, bf16[4,7296]{1,0:T(4,128)(2,1)S(1)}, u32[]{:S(2)}, u32[]{:S(2)}) collective-permute-start(bf16[4,7296]{1,0:T(4,128)(2,1)S(1)} %copy-done.5), channel_id=1, source_target_pairs={{0,16},{16,0},{64,80},{80,64},{128,144},{144,128},{192,208},{208,1... | collective-permute-start | bytes 175112 | tf_op jit(solution)/shard_map/ppermute | solution.py:258
  39.7 4.2 %collective-permute-done.4 = bf16[4,7296]{1,0:T(4,128)(2,1)S(1)} collective-permute-done((bf16[4,7296]{1,0:T(4,128)(2,1)S(1)}, bf16[4,7296]{1,0:T(4,128)(2,1)S(1)}, u32[]{:S(2)}, u32[]{:S(2)}) %collective-permute-start.4) | collective-permute-done | bytes 58400 | tf_op jit(solution)/shard_map/ppermute | solution.py:258
  44.1 2.7 %shard_map.124 = bf16[128,7168]{1,0:T(8,128)(2,1)} custom-call(s32[3]{0:T(128)S(1)} %pad_add_fusion.place_ref, bf16[16,7296]{1,0:T(8,128)(2,1)S(1)} %pad_maximum_fusion.1.tokens_ref), custom_call_target="tpu_custom_call" | custom-call | flops 29360128 | bytes 2064384 | tf_op jit(solution)/shard_map/pallas_call | solution.py:114
  46.8 5.3 %all-to-all-done = bf16[16,8,7168]{2,1,0:T(8,128)(2,1)S(1)} async-done(((bf16[16,8,7168]{2,1,0:T(8,128)(2,1)}), bf16[16,8,7168]{2,1,0:T(8,128)(2,1)S(1)}, u32[]{:S(2)}, u32[]{:S(2)}) %all-to-all-start) | async-done | bytes 1835040 | tf_op jit(solution)/shard_map/all_to_all | solution.py:266
  53.4 3.7 %all-to-all-start.1 = ((bf16[16,8,7168]{2,1,0:T(8,128)(2,1)}), bf16[16,8,7168]{2,1,0:T(8,128)(2,1)S(1)}, u32[]{:S(2)}, u32[]{:S(2)}) async-start(bf16[16,8,7168]{2,1,0:T(8,128)(2,1)} %bitcast.12), calls=%async_computation.1 | async-start | bytes 3670016 | tf_op jit(solution)/shard_map/all_to_all | solution.py:266
  57.1 7.8 %shard_map.125.p0 = bf16[128,512]{1,0:T(8,128)(2,1)} custom-call(bf16[128,7168]{1,0:T(8,128)(2,1)} %bitcast.62, bf16[2,7168,256]{2,1,0:T(8,128)(2,1)} %bitcast.56, bf16[2,7168,256]{2,1,0:T(8,128)(2,1)} %collective-permute-done.7.other_ref), custom_call_target="tpu_custom_call" | custom-call | flops 1879048192 | bytes 16515072 | tf_op jit(solution)/shard_map/pallas_call | solution.py:149
  65.0 1.9 %collective-permute-start.10 = (bf16[32,640]{1,0:T(8,128)(2,1)S(1)}, bf16[32,640]{1,0:T(8,128)(2,1)S(1)}, u32[]{:S(2)}, u32[]{:S(2)}) collective-permute-start(bf16[32,640]{1,0:T(8,128)(2,1)S(1)} %get-tuple-element.33), channel_id=1, source_target_pairs={{0,192},{64,0},{128,64},{192,128},{1,193},{65,1},{129,65},{193,129... | collective-permute-start | bytes 122888 | tf_op jit(solution)/shard_map/ppermute | solution.py:292
  66.9 1.7 %collective-permute-start.9 = (bf16[32,640]{1,0:T(8,128)(2,1)S(1)}, bf16[32,640]{1,0:T(8,128)(2,1)S(1)}, u32[]{:S(2)}, u32[]{:S(2)}) collective-permute-start(bf16[32,640]{1,0:T(8,128)(2,1)S(1)} %get-tuple-element.34), channel_id=1, source_target_pairs={{0,128},{64,192},{128,0},{192,64},{1,129},{65,193},{129,1},{193,65... | collective-permute-start | bytes 122888 | tf_op jit(solution)/shard_map/ppermute | solution.py:292
  68.6 1.6 %collective-permute-start.8 = (bf16[32,640]{1,0:T(8,128)(2,1)S(1)}, bf16[32,640]{1,0:T(8,128)(2,1)S(1)}, u32[]{:S(2)}, u32[]{:S(2)}) collective-permute-start(bf16[32,640]{1,0:T(8,128)(2,1)S(1)} %get-tuple-element.32), channel_id=1, source_target_pairs={{0,64},{64,128},{128,192},{192,0},{1,65},{65,129},{129,193},{193,1... | collective-permute-start | bytes 122888 | tf_op jit(solution)/shard_map/ppermute | solution.py:292
  70.4 3.1 %collective-permute-start.12 = (bf16[128,512]{1,0:T(8,128)(2,1)}, bf16[128,512]{1,0:T(8,128)(2,1)S(1)}, u32[]{:S(2)}, u32[]{:S(2)}) collective-permute-start(bf16[128,512]{1,0:T(8,128)(2,1)} %shard_map.125.p0), channel_id=1, source_target_pairs={{0,128},{16,144},{64,192},{80,208},{128,0},{144,16},{192,64},{208,... | collective-permute-start | bytes 393224 | tf_op jit(solution)/shard_map/ppermute | solution.py:258
  73.5 3.6 %collective-permute-start.13 = (bf16[128,512]{1,0:T(8,128)(2,1)}, bf16[128,512]{1,0:T(8,128)(2,1)S(1)}, u32[]{:S(2)}, u32[]{:S(2)}) collective-permute-start(bf16[128,512]{1,0:T(8,128)(2,1)} %shard_map.125.p0), channel_id=1, source_target_pairs={{0,192},{16,208},{64,0},{80,16},{128,64},{144,80},{192,128},{208,1... | collective-permute-start | bytes 393224 | tf_op jit(solution)/shard_map/ppermute | solution.py:258
  77.4 2.4 %collective-permute-done.11.p1 = bf16[128,512]{1,0:T(8,128)(2,1)S(1)} collective-permute-done((bf16[128,512]{1,0:T(8,128)(2,1)}, bf16[128,512]{1,0:T(8,128)(2,1)S(1)}, u32[]{:S(2)}, u32[]{:S(2)}) %collective-permute-start.11) | collective-permute-done | bytes 131104 | tf_op jit(solution)/shard_map/ppermute | solution.py:258
  81.1 2.0 %collective-permute-done.13.p3 = bf16[128,512]{1,0:T(8,128)(2,1)S(1)} collective-permute-done((bf16[128,512]{1,0:T(8,128)(2,1)}, bf16[128,512]{1,0:T(8,128)(2,1)S(1)}, u32[]{:S(2)}, u32[]{:S(2)}) %collective-permute-start.13) | collective-permute-done | bytes 131104 | tf_op jit(solution)/shard_map/ppermute | solution.py:258
  83.8 5.5 %shard_map.126 = bf16[128,1792]{1,0:T(8,128)(2,1)} custom-call(s32[3]{0:T(128)} %copy-done.1, bf16[128,512]{1,0:T(8,128)(2,1)} %shard_map.125.p0, bf16[128,512]{1,0:T(8,128)(2,1)} %copy-done.6, bf16[128,512]{1,0:T(8,128)(2,1)} %copy-done.7, bf16[128,512]{1,0:T(8,128)(2,1)} %copy-done.8, bf16[4,2,256,896]{3,2,1,0:T(8,128)(2,1)} %bitcast.59, ...), custom_call_target="tpu_custom_call" | custom-call | flops 939524096 | bytes 7864320 | tf_op jit(solution)/shard_map/pallas_call | solution.py:186
  89.4 7.1 %all-to-all-start.2 = ((bf16[16,8,1792]{2,1,0:T(8,128)(2,1)}), bf16[16,8,1792]{2,1,0:T(8,128)(2,1)S(1)}, u32[]{:S(2)}, u32[]{:S(2)}) async-start(bf16[16,8,1792]{2,1,0:T(8,128)(2,1)} %bitcast.63), calls=%async_computation.2 | async-start | bytes 917504 | tf_op jit(solution)/shard_map/all_to_all | solution.py:266
  97.2 7.8 %shard_map.127.p0 = bf16[128,512]{1,0:T(8,128)(2,1)} custom-call(bf16[128,7168]{1,0:T(8,128)(2,1)} %bitcast.61, bf16[2,7168,256]{2,1,0:T(8,128)(2,1)} %bitcast.57, bf16[2,7168,256]{2,1,0:T(8,128)(2,1)} %collective-permute-done.7.other_ref), custom_call_target="tpu_custom_call" | custom-call | flops 1879048192 | bytes 16515072 | tf_op jit(solution)/shard_map/pallas_call | solution.py:149
  105.1 2.4 %collective-permute-start.16 = (bf16[128,512]{1,0:T(8,128)(2,1)}, bf16[128,512]{1,0:T(8,128)(2,1)S(1)}, u32[]{:S(2)}, u32[]{:S(2)}) collective-permute-start(bf16[128,512]{1,0:T(8,128)(2,1)} %shard_map.127.p0), channel_id=1, source_target_pairs={{0,128},{16,144},{64,192},{80,208},{128,0},{144,16},{192,64},{208,... | collective-permute-start | bytes 393224 | tf_op jit(solution)/shard_map/ppermute | solution.py:258
  107.5 1.5 collective-permute-start.17
  109.0 5.9 %collective-permute-done.15.p1 = bf16[128,512]{1,0:T(8,128)(2,1)S(1)} collective-permute-done((bf16[128,512]{1,0:T(8,128)(2,1)}, bf16[128,512]{1,0:T(8,128)(2,1)S(1)}, u32[]{:S(2)}, u32[]{:S(2)}) %collective-permute-start.15) | collective-permute-done | bytes 131104 | tf_op jit(solution)/shard_map/ppermute | solution.py:258
  116.3 1.7 %collective-permute-done.17.p3 = bf16[128,512]{1,0:T(8,128)(2,1)S(1)} collective-permute-done((bf16[128,512]{1,0:T(8,128)(2,1)}, bf16[128,512]{1,0:T(8,128)(2,1)S(1)}, u32[]{:S(2)}, u32[]{:S(2)}) %collective-permute-start.17) | collective-permute-done | bytes 131104 | tf_op jit(solution)/shard_map/ppermute | solution.py:258
  118.7 5.5 %shard_map.128 = bf16[128,1792]{1,0:T(8,128)(2,1)} custom-call(s32[3]{0:T(128)} %copy-done.1, bf16[128,512]{1,0:T(8,128)(2,1)} %shard_map.127.p0, bf16[128,512]{1,0:T(8,128)(2,1)} %copy-done.9, bf16[128,512]{1,0:T(8,128)(2,1)} %copy-done.10, bf16[128,512]{1,0:T(8,128)(2,1)} %copy-done.11, bf16[4,2,256,896]{3,2,1,0:T(8,128)(2,1)} %bitcast.60, ...), custom_call_target="tpu_custom_call" | custom-call | flops 939524096 | bytes 7864320 | tf_op jit(solution)/shard_map/pallas_call | solution.py:186
  124.2 17.5 %all_to_all.25 = bf16[16,8,1792]{2,1,0:T(8,128)(2,1)S(1)} all-to-all(bf16[16,8,1792]{2,1,0:T(8,128)(2,1)} %bitcast.64), channel_id=1, replica_groups=mesh['ctx'=4,'att'=2,'zhi'=2,'x'=4,'y'=4] {'x','y'}, dimensions={0} | all-to-all | bytes 917504 | tf_op jit(solution)/shard_map/all_to_all | solution.py:266
  143.0 13.6 %all_to_all.26 = bf16[8,4,1792]{2,1,0:T(4,128)(2,1)S(1)} all-to-all(bf16[8,4,1792]{2,1,0:T(4,128)(2,1)S(1)} %shard_map.129), channel_id=1, replica_groups=mesh['ctx'=4,'att'=2,'zhi'=2,'x'=4,'y'=4] {'ctx','zhi'}, dimensions={0} | all-to-all | bytes 229376 | tf_op jit(solution)/shard_map/all_to_all | solution.py:303
  (63 shorter events, 14.9 us)
Async XLA Ops:
  0.6 24.1 %copy-start = (bf16[1,1024,512]{2,1,0:T(8,128)(2,1)S(1)}, bf16[1,1024,512]{2,1,0:T(8,128)(2,1)}, u32[]{:S(2)}) copy-start(bf16[1,1024,512]{2,1,0:T(8,128)(2,1)} %param.13) | copy-start | bytes 3145732
  2.4 6.3 %collective-permute-start.2 = (bf16[4,7296]{1,0:T(4,128)(2,1)}, bf16[4,7296]{1,0:T(4,128)(2,1)S(1)}, u32[]{:S(2)}, u32[]{:S(2)}) collective-permute-start(bf16[4,7296]{1,0:T(4,128)(2,1)} %shard_map.122), channel_id=1, source_target_pairs={{0,192},{16,208},{64,0},{80,16},{128,64},{144,80},{192,128},{208,1... | collective-permute-start | bytes 175112 | tf_op jit(solution)/shard_map/ppermute | solution.py:258
  4.2 6.1 %collective-permute-start.1 = (bf16[4,7296]{1,0:T(4,128)(2,1)}, bf16[4,7296]{1,0:T(4,128)(2,1)S(1)}, u32[]{:S(2)}, u32[]{:S(2)}) collective-permute-start(bf16[4,7296]{1,0:T(4,128)(2,1)} %shard_map.122), channel_id=1, source_target_pairs={{0,128},{16,144},{64,192},{80,208},{128,0},{144,16},{192,64},{208,... | collective-permute-start | bytes 175112 | tf_op jit(solution)/shard_map/ppermute | solution.py:258
  5.7 5.7 %collective-permute-start = (bf16[4,7296]{1,0:T(4,128)(2,1)}, bf16[4,7296]{1,0:T(4,128)(2,1)S(1)}, u32[]{:S(2)}, u32[]{:S(2)}) collective-permute-start(bf16[4,7296]{1,0:T(4,128)(2,1)} %shard_map.122), channel_id=1, source_target_pairs={{0,64},{16,80},{64,128},{80,144},{128,192},{144,208},{192,0},{208,... | collective-permute-start | bytes 175112 | tf_op jit(solution)/shard_map/ppermute | solution.py:258
  8.6 35.4 %copy-start.1 = (s32[3]{0:T(128)}, s32[3]{0:T(128)S(1)}, u32[]{:S(2)}) copy-start(s32[3]{0:T(128)S(1)} %pad_add_fusion.place_ref) | copy-start | bytes 40
  15.1 42.1 %collective-permute-start.7 = (bf16[2,7168,256]{2,1,0:T(8,128)(2,1)}, bf16[2,7168,256]{2,1,0:T(8,128)(2,1)}, u32[]{:S(2)}, u32[]{:S(2)}) collective-permute-start(bf16[2,7168,256]{2,1,0:T(8,128)(2,1)} %bitcast.55), channel_id=1, source_target_pairs={{0,32},{32,0},{1,33},{33,1},{2,34},{34,2},{3,35},{35,3},{4,36},{36... | collective-permute-start | bytes 22020104 | tf_op jit(solution)/shard_map/ppermute | solution.py:279
  15.7 61.6 %collective-permute-start.14 = (bf16[4,2,256,896]{3,2,1,0:T(8,128)(2,1)}, bf16[4,2,256,896]{3,2,1,0:T(8,128)(2,1)}, u32[]{:S(2)}, u32[]{:S(2)}) collective-permute-start(bf16[4,2,256,896]{3,2,1,0:T(8,128)(2,1)} %bitcast.58), channel_id=1, source_target_pairs={{0,32},{32,0},{1,33},{33,1},{2,34},{34,2},{3,35},{35,3},{4,36},{36... | collective-permute-start | bytes 11010056 | tf_op jit(solution)/shard_map/ppermute | solution.py:280
  17.5 9.0 %copy-start.5 = (bf16[4,7296]{1,0:T(4,128)(2,1)S(1)}, bf16[4,7296]{1,0:T(4,128)(2,1)}, u32[]{:S(2)}) copy-start(bf16[4,7296]{1,0:T(4,128)(2,1)} %shard_map.122) | copy-start | bytes 175108
  17.5 34.6 %all-to-all-start = ((bf16[16,8,7168]{2,1,0:T(8,128)(2,1)}), bf16[16,8,7168]{2,1,0:T(8,128)(2,1)S(1)}, u32[]{:S(2)}, u32[]{:S(2)}) async-start(bf16[16,8,7168]{2,1,0:T(8,128)(2,1)} %bitcast.5), calls=%async_computation | async-start | bytes 3670016 | tf_op jit(solution)/shard_map/all_to_all | solution.py:266
  26.5 8.8 %collective-permute-start.6 = (bf16[4,7296]{1,0:T(4,128)(2,1)S(1)}, bf16[4,7296]{1,0:T(4,128)(2,1)S(1)}, u32[]{:S(2)}, u32[]{:S(2)}) collective-permute-start(bf16[4,7296]{1,0:T(4,128)(2,1)S(1)} %copy-done.5), channel_id=1, source_target_pairs={{0,208},{16,192},{64,16},{80,0},{128,80},{144,64},{192,144},{208,1... | collective-permute-start | bytes 175112 | tf_op jit(solution)/shard_map/ppermute | solution.py:258
  32.0 7.7 %collective-permute-start.5 = (bf16[4,7296]{1,0:T(4,128)(2,1)S(1)}, bf16[4,7296]{1,0:T(4,128)(2,1)S(1)}, u32[]{:S(2)}, u32[]{:S(2)}) collective-permute-start(bf16[4,7296]{1,0:T(4,128)(2,1)S(1)} %copy-done.5), channel_id=1, source_target_pairs={{0,144},{16,128},{64,208},{80,192},{128,16},{144,0},{192,80},{208,... | collective-permute-start | bytes 175112 | tf_op jit(solution)/shard_map/ppermute | solution.py:258
  32.3 11.7 %collective-permute-start.4 = (bf16[4,7296]{1,0:T(4,128)(2,1)S(1)}, bf16[4,7296]{1,0:T(4,128)(2,1)S(1)}, u32[]{:S(2)}, u32[]{:S(2)}) collective-permute-start(bf16[4,7296]{1,0:T(4,128)(2,1)S(1)} %copy-done.5), channel_id=1, source_target_pairs={{0,80},{16,64},{64,144},{80,128},{128,208},{144,192},{192,16},{208... | collective-permute-start | bytes 175112 | tf_op jit(solution)/shard_map/ppermute | solution.py:258
  35.4 8.5 %collective-permute-start.3 = (bf16[4,7296]{1,0:T(4,128)(2,1)S(1)}, bf16[4,7296]{1,0:T(4,128)(2,1)S(1)}, u32[]{:S(2)}, u32[]{:S(2)}) collective-permute-start(bf16[4,7296]{1,0:T(4,128)(2,1)S(1)} %copy-done.5), channel_id=1, source_target_pairs={{0,16},{16,0},{64,80},{80,64},{128,144},{144,128},{192,208},{208,1... | collective-permute-start | bytes 175112 | tf_op jit(solution)/shard_map/ppermute | solution.py:258
  52.1 1.2 copy-start.4
  53.4 36.0 %all-to-all-start.1 = ((bf16[16,8,7168]{2,1,0:T(8,128)(2,1)}), bf16[16,8,7168]{2,1,0:T(8,128)(2,1)S(1)}, u32[]{:S(2)}, u32[]{:S(2)}) async-start(bf16[16,8,7168]{2,1,0:T(8,128)(2,1)} %bitcast.12), calls=%async_computation.1 | async-start | bytes 3670016 | tf_op jit(solution)/shard_map/all_to_all | solution.py:266
  65.0 5.4 %collective-permute-start.10 = (bf16[32,640]{1,0:T(8,128)(2,1)S(1)}, bf16[32,640]{1,0:T(8,128)(2,1)S(1)}, u32[]{:S(2)}, u32[]{:S(2)}) collective-permute-start(bf16[32,640]{1,0:T(8,128)(2,1)S(1)} %get-tuple-element.33), channel_id=1, source_target_pairs={{0,192},{64,0},{128,64},{192,128},{1,193},{65,1},{129,65},{193,129... | collective-permute-start | bytes 122888 | tf_op jit(solution)/shard_map/ppermute | solution.py:292
  66.9 6.6 %collective-permute-start.9 = (bf16[32,640]{1,0:T(8,128)(2,1)S(1)}, bf16[32,640]{1,0:T(8,128)(2,1)S(1)}, u32[]{:S(2)}, u32[]{:S(2)}) collective-permute-start(bf16[32,640]{1,0:T(8,128)(2,1)S(1)} %get-tuple-element.34), channel_id=1, source_target_pairs={{0,128},{64,192},{128,0},{192,64},{1,129},{65,193},{129,1},{193,65... | collective-permute-start | bytes 122888 | tf_op jit(solution)/shard_map/ppermute | solution.py:292
  68.6 8.5 %collective-permute-start.8 = (bf16[32,640]{1,0:T(8,128)(2,1)S(1)}, bf16[32,640]{1,0:T(8,128)(2,1)S(1)}, u32[]{:S(2)}, u32[]{:S(2)}) collective-permute-start(bf16[32,640]{1,0:T(8,128)(2,1)S(1)} %get-tuple-element.32), channel_id=1, source_target_pairs={{0,64},{64,128},{128,192},{192,0},{1,65},{65,129},{129,193},{193,1... | collective-permute-start | bytes 122888 | tf_op jit(solution)/shard_map/ppermute | solution.py:292
  70.2 9.5 %collective-permute-start.11 = (bf16[128,512]{1,0:T(8,128)(2,1)}, bf16[128,512]{1,0:T(8,128)(2,1)S(1)}, u32[]{:S(2)}, u32[]{:S(2)}) collective-permute-start(bf16[128,512]{1,0:T(8,128)(2,1)} %shard_map.125.p0), channel_id=1, source_target_pairs={{0,64},{16,80},{64,128},{80,144},{128,192},{144,208},{192,0},{208,... | collective-permute-start | bytes 393224 | tf_op jit(solution)/shard_map/ppermute | solution.py:258
  70.4 10.8 %collective-permute-start.12 = (bf16[128,512]{1,0:T(8,128)(2,1)}, bf16[128,512]{1,0:T(8,128)(2,1)S(1)}, u32[]{:S(2)}, u32[]{:S(2)}) collective-permute-start(bf16[128,512]{1,0:T(8,128)(2,1)} %shard_map.125.p0), channel_id=1, source_target_pairs={{0,128},{16,144},{64,192},{80,208},{128,0},{144,16},{192,64},{208,... | collective-permute-start | bytes 393224 | tf_op jit(solution)/shard_map/ppermute | solution.py:258
  73.5 9.7 %collective-permute-start.13 = (bf16[128,512]{1,0:T(8,128)(2,1)}, bf16[128,512]{1,0:T(8,128)(2,1)S(1)}, u32[]{:S(2)}, u32[]{:S(2)}) collective-permute-start(bf16[128,512]{1,0:T(8,128)(2,1)} %shard_map.125.p0), channel_id=1, source_target_pairs={{0,192},{16,208},{64,0},{80,16},{128,64},{144,80},{192,128},{208,1... | collective-permute-start | bytes 393224 | tf_op jit(solution)/shard_map/ppermute | solution.py:258
  79.8 3.4 %copy-start.6 = (bf16[128,512]{1,0:T(8,128)(2,1)}, bf16[128,512]{1,0:T(8,128)(2,1)S(1)}, u32[]{:S(2)}) copy-start(bf16[128,512]{1,0:T(8,128)(2,1)S(1)} %collective-permute-done.11.p1) | copy-start | bytes 393220
  81.1 2.0 %copy-start.7 = (bf16[128,512]{1,0:T(8,128)(2,1)}, bf16[128,512]{1,0:T(8,128)(2,1)S(1)}, u32[]{:S(2)}) copy-start(bf16[128,512]{1,0:T(8,128)(2,1)S(1)} %collective-permute-done.12.p2) | copy-start | bytes 393220
  89.4 7.8 %copy-start.3 = (bf16[16,8,7168]{2,1,0:T(8,128)(2,1)}, bf16[16,8,7168]{2,1,0:T(8,128)(2,1)S(1)}, u32[]{:S(2)}) copy-start(bf16[16,8,7168]{2,1,0:T(8,128)(2,1)S(1)} %all-to-all-done.1) | copy-start | bytes 5505028
  89.4 19.6 %all-to-all-start.2 = ((bf16[16,8,1792]{2,1,0:T(8,128)(2,1)}), bf16[16,8,1792]{2,1,0:T(8,128)(2,1)S(1)}, u32[]{:S(2)}, u32[]{:S(2)}) async-start(bf16[16,8,1792]{2,1,0:T(8,128)(2,1)} %bitcast.63), calls=%async_computation.2 | async-start | bytes 917504 | tf_op jit(solution)/shard_map/all_to_all | solution.py:266
  105.0 10.0 %collective-permute-start.15 = (bf16[128,512]{1,0:T(8,128)(2,1)}, bf16[128,512]{1,0:T(8,128)(2,1)S(1)}, u32[]{:S(2)}, u32[]{:S(2)}) collective-permute-start(bf16[128,512]{1,0:T(8,128)(2,1)} %shard_map.127.p0), channel_id=1, source_target_pairs={{0,64},{16,80},{64,128},{80,144},{128,192},{144,208},{192,0},{208,... | collective-permute-start | bytes 393224 | tf_op jit(solution)/shard_map/ppermute | solution.py:258
  105.1 11.2 %collective-permute-start.16 = (bf16[128,512]{1,0:T(8,128)(2,1)}, bf16[128,512]{1,0:T(8,128)(2,1)S(1)}, u32[]{:S(2)}, u32[]{:S(2)}) collective-permute-start(bf16[128,512]{1,0:T(8,128)(2,1)} %shard_map.127.p0), channel_id=1, source_target_pairs={{0,128},{16,144},{64,192},{80,208},{128,0},{144,16},{192,64},{208,... | collective-permute-start | bytes 393224 | tf_op jit(solution)/shard_map/ppermute | solution.py:258
  107.5 10.6 %collective-permute-start.17 = (bf16[128,512]{1,0:T(8,128)(2,1)}, bf16[128,512]{1,0:T(8,128)(2,1)S(1)}, u32[]{:S(2)}, u32[]{:S(2)}) collective-permute-start(bf16[128,512]{1,0:T(8,128)(2,1)} %shard_map.127.p0), channel_id=1, source_target_pairs={{0,192},{16,208},{64,0},{80,16},{128,64},{144,80},{192,128},{208,1... | collective-permute-start | bytes 393224 | tf_op jit(solution)/shard_map/ppermute | solution.py:258
  109.0 32.7 %copy-start.2 = (s32[3]{0:T(128)S(1)}, s32[3]{0:T(128)}, u32[]{:S(2)}) copy-start(s32[3]{0:T(128)} %copy-done.1) | copy-start | bytes 40
  114.9 3.1 %copy-start.9 = (bf16[128,512]{1,0:T(8,128)(2,1)}, bf16[128,512]{1,0:T(8,128)(2,1)S(1)}, u32[]{:S(2)}) copy-start(bf16[128,512]{1,0:T(8,128)(2,1)S(1)} %collective-permute-done.15.p1) | copy-start | bytes 393220
  116.3 1.7 %copy-start.10 = (bf16[128,512]{1,0:T(8,128)(2,1)}, bf16[128,512]{1,0:T(8,128)(2,1)S(1)}, u32[]{:S(2)}) copy-start(bf16[128,512]{1,0:T(8,128)(2,1)S(1)} %collective-permute-done.16.p2) | copy-start | bytes 393220
  118.0 0.7 copy-start.11
  (1 other events, 0.6 us)

commit v6 on v5

--- a/solution.py
+++ b/solution.py
@@ -121,22 +121,27 @@
     )(place, tokens)
 
 
-def gate_up_kernel(rows_ref, own_ref, other_ref, out_ref, held_ref, sems):
+def gate_up_kernel(rows_hbm, own_hbm, other_hbm, out_ref, rows_ref, held_ref, sems):
     width = rows_ref.shape[1]
     copies = []
     for i in range(width // STEP):
         part = pl.ds(i * STEP, STEP)
-        for j, weight_ref in enumerate((own_ref, other_ref)):
-            copies.append(
-                pltpu.make_async_copy(weight_ref.at[:, part], held_ref.at[j, :, part], sems.at[i, j])
-            )
-            copies[-1].start()
+        copies.append(
+            [
+                pltpu.make_async_copy(rows_hbm.at[:, part], rows_ref.at[:, part], sems.at[i, 0]),
+                pltpu.make_async_copy(own_hbm.at[:, part], held_ref.at[0, :, part], sems.at[i, 1]),
+                pltpu.make_async_copy(other_hbm.at[:, part], held_ref.at[1, :, part], sems.at[i, 2]),
+            ]
+        )
+        for copy in copies[-1]:
+            copy.start()
     sums = [jnp.zeros((128, 256), f32) for _ in range(4)]
     for i in range(width // STEP):
         low, high = i * STEP, (i + 1) * STEP
+        for copy in copies[i]:
+            copy.wait()
         rows = rows_ref[:, low:high]
         for j in range(2):
-            copies[2 * i + j].wait()
             for k in range(2):
                 sums[2 * j + k] += jnp.dot(rows, held_ref[j, k, low:high], preferred_element_type=f32)
     for j in range(2):
@@ -149,35 +154,41 @@
     return pl.pallas_call(
         gate_up_kernel,
         out_shape=jax.ShapeDtypeStruct((128, 512), bf16),
-        in_specs=[VMEM, HBM, HBM],
+        in_specs=[HBM] * 3,
         out_specs=VMEM,
         scratch_shapes=[
+            pltpu.VMEM((128, width), bf16),
             pltpu.VMEM((2, 2, width, 256), bf16),
-            pltpu.SemaphoreType.DMA((width // STEP, 2)),
+            pltpu.SemaphoreType.DMA((width // STEP, 3)),
         ],
-        compiler_params=room(57),
+        compiler_params=room(55),
         cost_estimate=pl.CostEstimate(
             flops=2 * 128 * width * 1024, bytes_accessed=2 * width * (1024 + 128), transcendentals=65536
         ),
     )(rows, own, other)
 
 
-def down_kernel(place_ref, p0, p1, p2, p3, own_ref, other_ref, out_ref, held_ref, sems):
+def down_kernel(place_ref, p0, p1, p2, p3, own_hbm, other_hbm, out_ref, pieces_ref, held_ref, sems):
     ctx, core = place_ref[0], place_ref[1]
     copies = []
+    for k, piece in enumerate((p0, p1, p2, p3)):
+        source = (ctx - k + 4) % 4
+        copies.append(
+            [
+                pltpu.make_async_copy(piece, pieces_ref.at[k], sems.at[k, 0]),
+                pltpu.make_async_copy(own_hbm.at[source], held_ref.at[0, k], sems.at[k, 1]),
+                pltpu.make_async_copy(other_hbm.at[source], held_ref.at[1, k], sems.at[k, 2]),
+            ]
+        )
+        for copy in copies[-1]:
+            copy.start()
+    totals = [jnp.zeros((128, 896), f32) for _ in range(2)]
     for k in range(4):
-        source = (ctx - k + 4) % 4
-        for j, weight_ref in enumerate((own_ref, other_ref)):
-            copies.append(
-                pltpu.make_async_copy(weight_ref.at[source], held_ref.at[j, k], sems.at[j, k])
-            )
-            copies[-1].start()
-    totals = [jnp.zeros((128, 896), f32) for _ in range(2)]
-    for k, piece in enumerate((p0, p1, p2, p3)):
+        for copy in copies[k]:
+            copy.wait()
         for j in range(2):
-            copies[2 * k + j].wait()
-            totals[j] += jnp.dot(piece[:, :256], held_ref[j, k, core], preferred_element_type=f32)
-            totals[j] += jnp.dot(piece[:, 256:], held_ref[j, k, 1 - core], preferred_element_type=f32)
+            totals[j] += jnp.dot(pieces_ref[k, :, :256], held_ref[j, k, core], preferred_element_type=f32)
+            totals[j] += jnp.dot(pieces_ref[k, :, 256:], held_ref[j, k, 1 - core], preferred_element_type=f32)
     out_ref[:, :896] = jnp.where(core == 0, totals[0], totals[1]).astype(bf16)
     out_ref[:, 896:] = jnp.where(core == 0, totals[1], totals[0]).astype(bf16)
 
@@ -186,10 +197,14 @@
     return pl.pallas_call(
         down_kernel,
         out_shape=jax.ShapeDtypeStruct((128, 1792), bf16),
-        in_specs=[SMEM] + [VMEM] * 4 + [HBM] * 2,
-        out_specs=VMEM,
-        scratch_shapes=[pltpu.VMEM((2, 4, 2, 256, 896), bf16), pltpu.SemaphoreType.DMA((2, 4))],
-        compiler_params=room(58),
+        in_specs=[SMEM] + [HBM] * 6,
+        out_specs=VMEM,
+        scratch_shapes=[
+            pltpu.VMEM((4, 128, 512), bf16),
+            pltpu.VMEM((2, 4, 2, 256, 896), bf16),
+            pltpu.SemaphoreType.DMA((4, 3)),
+        ],
+        compiler_params=room(57),
         cost_estimate=pl.CostEstimate(
             flops=2 * 128 * 2048 * 1792, bytes_accessed=2 * 2048 * 1792 + 2 * 128 * 2048, transcendentals=0
         ),
@@ -279,25 +294,25 @@
     other_in = lax.ppermute(moving_in, "att", swap_core)
     other_out = lax.ppermute(moving_out, "att", swap_core)
     rows1, facts1 = rows_of([hop(payload, k, 1) for k in (0, 1, 2, 3)])
-    part = attend(query_latent, query_rope, latent_cache, rope_keys, lengths)
-    rows1, facts1, got0, part = lax.optimization_barrier((rows1, facts1, got0, part))
+    rows1, facts1, got0 = lax.optimization_barrier((rows1, facts1, got0))
     got1 = across(rows1)
 
     pieces0 = hidden_of(got0)
-    pieces0[0], part = lax.optimization_barrier((pieces0[0], part))
-    part = part.reshape(4, 32, 640)
+    query_latent, query_rope, pieces0[0] = lax.optimization_barrier((query_latent, query_rope, pieces0[0]))
+    part = attend(query_latent, query_rope, latent_cache, rope_keys, lengths).reshape(4, 32, 640)
+    result0 = down(place, pieces0, weight_out, other_out)
+    back0 = across(result0)
+    got1, part, _ = lax.optimization_barrier((got1, part, result0))
+    pieces1 = hidden_of(got1)
+    pieces1[2], back0 = lax.optimization_barrier((pieces1[2], back0))
+    result1 = down(place, pieces1, weight_out, other_out)
+    back1 = across(result1)
+    part, _ = lax.optimization_barrier((part, result1))
     parts = [lax.dynamic_index_in_dim(part, c, 0, keepdims=False)]
     for k in (1, 2, 3):
         sent = lax.dynamic_index_in_dim(part, (c + k) % 4, 0, keepdims=False)
         parts.append(lax.ppermute(sent, "ctx", [(i, (i + k) % 4) for i in range(4)]))
     attended = finish_attention(parts)
-    result0 = down(place, pieces0, weight_out, other_out)
-    back0 = across(result0)
-    got1, attended, _ = lax.optimization_barrier((got1, attended, result0))
-    pieces1 = hidden_of(got1)
-    pieces1[0], back0 = lax.optimization_barrier((pieces1[0], back0))
-    result1 = down(place, pieces1, weight_out, other_out)
-    back1 = across(result1)
 
     outgoing = mix(place, back0, back1, facts0, facts1)
     final = lax.all_to_all(outgoing, ("ctx", "zhi"), split_axis=0, concat_axis=0, tiled=True)

time: 158 us -> 149 us (0.943)
  blocking collectives: 31.1 us -> 0 us
  waiting for transfers between devices: 27.2 us -> 41.6 us
  starting transfers between devices: 53.8 us -> 64.1 us
    all_to_all x2 -> x0, blocking collectives: 31.1 us -> none  [the longest x1 17.5 us: across(): lax.all_to_all(value, ('x', 'y'), split_axis=0, concat_axis=0, tiled=True)]
    all_to_all x0 -> x1, starting transfers between devices: none -> 7.06 us  [shards(): lax.all_to_all(outgoing, ('ctx', 'zhi'), split_axis=0, concat_axis=0, til...]
    all_to_all x3 -> x4, starting transfers between devices: 18 us -> 24.7 us  [across(): lax.all_to_all(value, ('x', 'y'), split_axis=0, concat_axis=0, tiled=True)]
    all_to_all x0 -> x1, waiting for transfers between devices: none -> 6.6 us  [shards(): lax.all_to_all(outgoing, ('ctx', 'zhi'), split_axis=0, concat_axis=0, til...]
    all_to_all x3 -> x4, waiting for transfers between devices: 5.33 us -> 9.48 us  [across(): lax.all_to_all(value, ('x', 'y'), split_axis=0, concat_axis=0, tiled=True)]
    ppermute x3, waiting for transfers between devices: 0.01 us -> 2.98 us  [shards(): lax.ppermute(sent, 'ctx', [(i, (i + k) % 4) for i in range(4)])]
    ppermute x13, starting transfers between devices: 30 us -> 27.7 us  [hop(): return lax.ppermute(value, ('ctx', 'zhi'), pairs)]
  transfers between devices with their start and end apart: 21 -> 23, of which waited for: 10 -> 14; matrix products, arithmetic and copies ran while one was open for 3% -> 3% of each run, Pallas kernels for 15% -> 15%
where the time goes in v6:
time: 149 us
  starting transfers between devices  64.1 us (43%)
  waiting for transfers between devices  41.6 us (28%)
  Pallas kernels  33.7 us (23%)
  other arithmetic  3.75 us (3%)
  local copies, waits for them, and re-layouts  2.2 us (1%)
  matrix products  1.79 us (1%)
  between operations  1.54 us (1%)
    ppermute x13, starting transfers between devices, hop(): return lax.ppermute(value, ('ctx', 'zhi'), pairs)  27.7 us
    all_to_all x4, starting transfers between devices, across(): lax.all_to_all(value, ('x', 'y'), split_axis=0, concat_axis=0, tiled=True)  24.7 us
    ppermute x13, waiting for transfers between devices, hop(): return lax.ppermute(value, ('ctx', 'zhi'), pairs)  22.5 us
    pallas_call x2, Pallas kernels, gate_up(): pl.pallas_call(gate_up_kernel, out_shape=jax.ShapeDtypeStruct((128, 512),...  14.1 us
    pallas_call x2, Pallas kernels, down(): pl.pallas_call(down_kernel, out_shape=jax.ShapeDtypeStruct((128, 1792), b...  10.5 us
    all_to_all x4, waiting for transfers between devices, across(): lax.all_to_all(value, ('x', 'y'), split_axis=0, concat_axis=0, tiled=True)  9.48 us
    all_to_all x1, starting transfers between devices, shards(): lax.all_to_all(outgoing, ('ctx', 'zhi'), split_axis=0, concat_axis=0, til...  7.06 us
    all_to_all x1, waiting for transfers between devices, shards(): lax.all_to_all(outgoing, ('ctx', 'zhi'), split_axis=0, concat_axis=0, til...  6.6 us
  transfers between devices with their start and end apart: 23, of which 14 were waited for; matrix products, arithmetic and copies ran while one was open for 3% of the time, Pallas kernels for 15%

profile of v6, /device:TPU:32, one launch (start us, length us, event | category | flops | bytes accessed | tf_op | source)
XLA Modules:
  0.0 148.6 jit_solution(13962480659929306925)
XLA Ops:
  0.6 1.7 %shard_map.122 = bf16[4,7296]{1,0:T(4,128)(2,1)} custom-call(s32[4,8]{1,0:T(4,128)} %ids_ref.1, f32[4,8]{1,0:T(4,128)} %gates_ref.1, bf16[4,7168]{1,0:T(4,128)(2,1)} %rows_ref.1, bf16[7168]{0:T(1024)(128)(2,1)} %gain_ref.1), custom_call_target="tpu_custom_call" | custom-call | tf_op jit(solution)/shard_map/pallas_call | solution.py:79
  2.4 1.8 %collective-permute-start.2 = (bf16[4,7296]{1,0:T(4,128)(2,1)}, bf16[4,7296]{1,0:T(4,128)(2,1)S(1)}, u32[]{:S(2)}, u32[]{:S(2)}) collective-permute-start(bf16[4,7296]{1,0:T(4,128)(2,1)} %shard_map.122), channel_id=1, source_target_pairs={{0,192},{16,208},{64,0},{80,16},{128,64},{144,80},{192,128},{208,1... | collective-permute-start | bytes 175112 | tf_op jit(solution)/shard_map/ppermute | solution.py:273
  5.7 2.8 %collective-permute-start = (bf16[4,7296]{1,0:T(4,128)(2,1)}, bf16[4,7296]{1,0:T(4,128)(2,1)S(1)}, u32[]{:S(2)}, u32[]{:S(2)}) collective-permute-start(bf16[4,7296]{1,0:T(4,128)(2,1)} %shard_map.122), channel_id=1, source_target_pairs={{0,64},{16,80},{64,128},{80,144},{128,192},{144,208},{192,0},{208,... | collective-permute-start | bytes 175112 | tf_op jit(solution)/shard_map/ppermute | solution.py:273
  8.6 1.7 %collective-permute-done.1 = bf16[4,7296]{1,0:T(4,128)(2,1)S(1)} collective-permute-done((bf16[4,7296]{1,0:T(4,128)(2,1)}, bf16[4,7296]{1,0:T(4,128)(2,1)S(1)}, u32[]{:S(2)}, u32[]{:S(2)}) %collective-permute-start.1) | collective-permute-done | bytes 58400 | tf_op jit(solution)/shard_map/ppermute | solution.py:273
  12.4 2.6 %shard_map.123 = bf16[128,7168]{1,0:T(8,128)(2,1)} custom-call(s32[3]{0:T(128)S(1)} %pad_add_fusion.place_ref, bf16[16,7296]{1,0:T(8,128)(2,1)S(1)} %pad_maximum_fusion.tokens_ref), custom_call_target="tpu_custom_call" | custom-call | flops 29360128 | bytes 2064384 | tf_op jit(solution)/shard_map/pallas_call | solution.py:114
  15.6 7.0 %all-to-all-start = ((bf16[16,8,7168]{2,1,0:T(8,128)(2,1)}), bf16[16,8,7168]{2,1,0:T(8,128)(2,1)S(1)}, u32[]{:S(2)}, u32[]{:S(2)}) async-start(bf16[16,8,7168]{2,1,0:T(8,128)(2,1)} %bitcast.5), calls=%async_computation | async-start | bytes 3670016 | tf_op jit(solution)/shard_map/all_to_all | solution.py:281
  22.6 5.5 %collective-permute-start.6 = (bf16[4,7296]{1,0:T(4,128)(2,1)S(1)}, bf16[4,7296]{1,0:T(4,128)(2,1)S(1)}, u32[]{:S(2)}, u32[]{:S(2)}) collective-permute-start(bf16[4,7296]{1,0:T(4,128)(2,1)S(1)} %copy-done.5), channel_id=1, source_target_pairs={{0,208},{16,192},{64,16},{80,0},{128,80},{144,64},{192,144},{208,1... | collective-permute-start | bytes 175112 | tf_op jit(solution)/shard_map/ppermute | solution.py:273
  28.3 3.1 %collective-permute-start.4 = (bf16[4,7296]{1,0:T(4,128)(2,1)S(1)}, bf16[4,7296]{1,0:T(4,128)(2,1)S(1)}, u32[]{:S(2)}, u32[]{:S(2)}) collective-permute-start(bf16[4,7296]{1,0:T(4,128)(2,1)S(1)} %copy-done.5), channel_id=1, source_target_pairs={{0,80},{16,64},{64,144},{80,128},{128,208},{144,192},{192,16},{208... | collective-permute-start | bytes 175112 | tf_op jit(solution)/shard_map/ppermute | solution.py:273
  31.4 4.1 %collective-permute-start.3 = (bf16[4,7296]{1,0:T(4,128)(2,1)S(1)}, bf16[4,7296]{1,0:T(4,128)(2,1)S(1)}, u32[]{:S(2)}, u32[]{:S(2)}) collective-permute-start(bf16[4,7296]{1,0:T(4,128)(2,1)S(1)} %copy-done.5), channel_id=1, source_target_pairs={{0,16},{16,0},{64,80},{80,64},{128,144},{144,128},{192,208},{208,1... | collective-permute-start | bytes 175112 | tf_op jit(solution)/shard_map/ppermute | solution.py:273
  35.5 4.5 %collective-permute-done.4 = bf16[4,7296]{1,0:T(4,128)(2,1)S(1)} collective-permute-done((bf16[4,7296]{1,0:T(4,128)(2,1)S(1)}, bf16[4,7296]{1,0:T(4,128)(2,1)S(1)}, u32[]{:S(2)}, u32[]{:S(2)}) %collective-permute-start.4) | collective-permute-done | bytes 58400 | tf_op jit(solution)/shard_map/ppermute | solution.py:273
  40.2 2.7 %shard_map.124 = bf16[128,7168]{1,0:T(8,128)(2,1)} custom-call(s32[3]{0:T(128)S(1)} %pad_add_fusion.place_ref, bf16[16,7296]{1,0:T(8,128)(2,1)S(1)} %pad_maximum_fusion.1.tokens_ref), custom_call_target="tpu_custom_call" | custom-call | flops 29360128 | bytes 2064384 | tf_op jit(solution)/shard_map/pallas_call | solution.py:114
  42.9 7.1 %all-to-all-done = bf16[16,8,7168]{2,1,0:T(8,128)(2,1)S(1)} async-done(((bf16[16,8,7168]{2,1,0:T(8,128)(2,1)}), bf16[16,8,7168]{2,1,0:T(8,128)(2,1)S(1)}, u32[]{:S(2)}, u32[]{:S(2)}) %all-to-all-start) | async-done | bytes 1835040 | tf_op jit(solution)/shard_map/all_to_all | solution.py:281
  51.2 3.7 %all-to-all-start.1 = ((bf16[16,8,7168]{2,1,0:T(8,128)(2,1)}), bf16[16,8,7168]{2,1,0:T(8,128)(2,1)S(1)}, u32[]{:S(2)}, u32[]{:S(2)}) async-start(bf16[16,8,7168]{2,1,0:T(8,128)(2,1)} %bitcast.7), calls=%async_computation.1 | async-start | bytes 3670016 | tf_op jit(solution)/shard_map/all_to_all | solution.py:281
  55.7 7.1 %shard_map.125.p0 = bf16[128,512]{1,0:T(8,128)(2,1)} custom-call(bf16[128,7168]{1,0:T(8,128)(2,1)} %bitcast.63, bf16[2,7168,256]{2,1,0:T(8,128)(2,1)} %bitcast.57, bf16[2,7168,256]{2,1,0:T(8,128)(2,1)} %collective-permute-done.7.other_hbm), custom_call_target="tpu_custom_call" | custom-call | flops 1879048192 | bytes 16515072 | tf_op jit(solution)/shard_map/pallas_call | solution.py:154
  62.7 2.2 %collective-permute-start.8 = (bf16[128,512]{1,0:T(8,128)(2,1)}, bf16[128,512]{1,0:T(8,128)(2,1)S(1)}, u32[]{:S(2)}, u32[]{:S(2)}) collective-permute-start(bf16[128,512]{1,0:T(8,128)(2,1)} %shard_map.125.p0), channel_id=1, source_target_pairs={{0,64},{16,80},{64,128},{80,144},{128,192},{144,208},{192,0},{208,... | collective-permute-start | bytes 393224 | tf_op jit(solution)/shard_map/ppermute | solution.py:273
  64.9 2.1 %collective-permute-start.9 = (bf16[128,512]{1,0:T(8,128)(2,1)}, bf16[128,512]{1,0:T(8,128)(2,1)S(1)}, u32[]{:S(2)}, u32[]{:S(2)}) collective-permute-start(bf16[128,512]{1,0:T(8,128)(2,1)} %shard_map.125.p0), channel_id=1, source_target_pairs={{0,128},{16,144},{64,192},{80,208},{128,0},{144,16},{192,64},{208,... | collective-permute-start | bytes 393224 | tf_op jit(solution)/shard_map/ppermute | solution.py:273
  69.0 3.8 %collective-permute-done.8.p1 = bf16[128,512]{1,0:T(8,128)(2,1)S(1)} collective-permute-done((bf16[128,512]{1,0:T(8,128)(2,1)}, bf16[128,512]{1,0:T(8,128)(2,1)S(1)}, u32[]{:S(2)}, u32[]{:S(2)}) %collective-permute-start.8) | collective-permute-done | bytes 131104 | tf_op jit(solution)/shard_map/ppermute | solution.py:273
  74.2 1.8 %collective-permute-done.10.p3 = bf16[128,512]{1,0:T(8,128)(2,1)} collective-permute-done((bf16[128,512]{1,0:T(8,128)(2,1)}, bf16[128,512]{1,0:T(8,128)(2,1)}, u32[]{:S(2)}, u32[]{:S(2)}) %collective-permute-start.10) | collective-permute-done | bytes 131104 | tf_op jit(solution)/shard_map/ppermute | solution.py:273
  76.0 5.3 %shard_map.126 = bf16[128,1792]{1,0:T(8,128)(2,1)} custom-call(s32[3]{0:T(128)} %copy-done.1, bf16[128,512]{1,0:T(8,128)(2,1)} %shard_map.125.p0, bf16[128,512]{1,0:T(8,128)(2,1)} %copy-done.9, bf16[128,512]{1,0:T(8,128)(2,1)} %copy-done.10, bf16[128,512]{1,0:T(8,128)(2,1)} %collective-permute-done.10.p3, bf16[4,2,256,896]{3,2,1,0:T(8,128)(2,1)} %bitcast.60, ...), custom_call_target="tpu_custom_call" | custom-call | flops 939524096 | bytes 7864320 | tf_op jit(solution)/shard_map/pallas_call | solution.py:197
  81.3 7.0 %all-to-all-start.2 = ((bf16[16,8,1792]{2,1,0:T(8,128)(2,1)}), bf16[16,8,1792]{2,1,0:T(8,128)(2,1)S(1)}, u32[]{:S(2)}, u32[]{:S(2)}) async-start(bf16[16,8,1792]{2,1,0:T(8,128)(2,1)} %bitcast.64), calls=%async_computation.2 | async-start | bytes 917504 | tf_op jit(solution)/shard_map/all_to_all | solution.py:281
  89.5 7.0 %shard_map.127.p0 = bf16[128,512]{1,0:T(8,128)(2,1)} custom-call(bf16[128,7168]{1,0:T(8,128)(2,1)} %bitcast.62, bf16[2,7168,256]{2,1,0:T(8,128)(2,1)} %bitcast.58, bf16[2,7168,256]{2,1,0:T(8,128)(2,1)} %collective-permute-done.7.other_hbm), custom_call_target="tpu_custom_call" | custom-call | flops 1879048192 | bytes 16515072 | tf_op jit(solution)/shard_map/pallas_call | solution.py:154
  96.5 2.2 %collective-permute-start.13 = (bf16[128,512]{1,0:T(8,128)(2,1)}, bf16[128,512]{1,0:T(8,128)(2,1)S(1)}, u32[]{:S(2)}, u32[]{:S(2)}) collective-permute-start(bf16[128,512]{1,0:T(8,128)(2,1)} %shard_map.127.p0), channel_id=1, source_target_pairs={{0,128},{16,144},{64,192},{80,208},{128,0},{144,16},{192,64},{208,... | collective-permute-start | bytes 393224 | tf_op jit(solution)/shard_map/ppermute | solution.py:273
  98.7 2.0 %collective-permute-start.14 = (bf16[128,512]{1,0:T(8,128)(2,1)}, bf16[128,512]{1,0:T(8,128)(2,1)S(1)}, u32[]{:S(2)}, u32[]{:S(2)}) collective-permute-start(bf16[128,512]{1,0:T(8,128)(2,1)} %shard_map.127.p0), channel_id=1, source_target_pairs={{0,192},{16,208},{64,0},{80,16},{128,64},{144,80},{192,128},{208,1... | collective-permute-start | bytes 393224 | tf_op jit(solution)/shard_map/ppermute | solution.py:273
  100.8 5.4 %collective-permute-done.13.p2 = bf16[128,512]{1,0:T(8,128)(2,1)S(1)} collective-permute-done((bf16[128,512]{1,0:T(8,128)(2,1)}, bf16[128,512]{1,0:T(8,128)(2,1)S(1)}, u32[]{:S(2)}, u32[]{:S(2)}) %collective-permute-start.13) | collective-permute-done | bytes 131104 | tf_op jit(solution)/shard_map/ppermute | solution.py:273
  109.6 5.3 %shard_map.128 = bf16[128,1792]{1,0:T(8,128)(2,1)} custom-call(s32[3]{0:T(128)} %copy-done.1, bf16[128,512]{1,0:T(8,128)(2,1)} %shard_map.127.p0, bf16[128,512]{1,0:T(8,128)(2,1)} %copy-done.7, bf16[128,512]{1,0:T(8,128)(2,1)} %copy-done.6, bf16[128,512]{1,0:T(8,128)(2,1)} %copy-done.8, bf16[4,2,256,896]{3,2,1,0:T(8,128)(2,1)} %bitcast.61, ...), custom_call_target="tpu_custom_call" | custom-call | flops 939524096 | bytes 7864320 | tf_op jit(solution)/shard_map/pallas_call | solution.py:197
  114.9 7.0 %all-to-all-start.3 = ((bf16[16,8,1792]{2,1,0:T(8,128)(2,1)}), bf16[16,8,1792]{2,1,0:T(8,128)(2,1)S(1)}, u32[]{:S(2)}, u32[]{:S(2)}) async-start(bf16[16,8,1792]{2,1,0:T(8,128)(2,1)} %bitcast.65), calls=%async_computation.3 | async-start | bytes 917504 | tf_op jit(solution)/shard_map/all_to_all | solution.py:281
  122.8 2.3 %collective-permute-start.16 = (bf16[32,640]{1,0:T(8,128)(2,1)S(1)}, bf16[32,640]{1,0:T(8,128)(2,1)S(1)}, u32[]{:S(2)}, u32[]{:S(2)}) collective-permute-start(bf16[32,640]{1,0:T(8,128)(2,1)S(1)} %get-tuple-element.38), channel_id=1, source_target_pairs={{0,128},{64,192},{128,0},{192,64},{1,129},{65,193},{129,1},{193,65... | collective-permute-start | bytes 122888 | tf_op jit(solution)/shard_map/ppermute | solution.py:314
  126.1 1.6 %collective-permute-done.16 = bf16[32,640]{1,0:T(8,128)(2,1)S(1)} collective-permute-done((bf16[32,640]{1,0:T(8,128)(2,1)S(1)}, bf16[32,640]{1,0:T(8,128)(2,1)S(1)}, u32[]{:S(2)}, u32[]{:S(2)}) %collective-permute-start.16) | collective-permute-done | bytes 40992 | tf_op jit(solution)/shard_map/ppermute | solution.py:314
  129.3 2.4 %all-to-all-done.3 = bf16[16,8,1792]{2,1,0:T(8,128)(2,1)S(1)} async-done(((bf16[16,8,1792]{2,1,0:T(8,128)(2,1)}), bf16[16,8,1792]{2,1,0:T(8,128)(2,1)S(1)}, u32[]{:S(2)}, u32[]{:S(2)}) %all-to-all-start.3) | async-done | bytes 458784 | tf_op jit(solution)/shard_map/all_to_all | solution.py:281
  131.6 2.0 %shard_map.129 = bf16[8,4,1792]{2,1,0:T(4,128)(2,1)} custom-call(s32[3]{0:T(128)S(1)} %copy-done.2, bf16[128,1792]{1,0:T(8,128)(2,1)S(1)} %bitcast.54, bf16[128,1792]{1,0:T(8,128)(2,1)S(1)} %bitcast.55, bf16[16,128]{1,0:T(8,128)(2,1)S(1)} %slice.28.facts0, bf16[16,128]{1,0:T(8,128)(2,1)S(1)} %slice.29.facts1), custom_call_target="tpu_custom_call" | custom-call | flops 88080384 | bytes 1048576 | tf_op jit(solution)/shard_map/pallas_call | solution.py:237
  133.6 7.1 %all-to-all-start.4 = ((bf16[8,4,1792]{2,1,0:T(4,128)(2,1)}), bf16[8,4,1792]{2,1,0:T(4,128)(2,1)S(1)}, u32[]{:S(2)}, u32[]{:S(2)}) async-start(bf16[8,4,1792]{2,1,0:T(4,128)(2,1)} %shard_map.129), calls=%async_computation.4 | async-start | bytes 229376 | tf_op jit(solution)/shard_map/all_to_all | solution.py:318
  141.4 6.6 %all-to-all-done.4 = bf16[8,4,1792]{2,1,0:T(4,128)(2,1)S(1)} async-done(((bf16[8,4,1792]{2,1,0:T(4,128)(2,1)}), bf16[8,4,1792]{2,1,0:T(4,128)(2,1)S(1)}, u32[]{:S(2)}, u32[]{:S(2)}) %all-to-all-start.4) | async-done | bytes 114720 | tf_op jit(solution)/shard_map/all_to_all | solution.py:318
  (70 shorter events, 18.8 us)
Async XLA Ops:
  0.6 66.7 %copy-start = (bf16[1,1024,512]{2,1,0:T(8,128)(2,1)S(1)}, bf16[1,1024,512]{2,1,0:T(8,128)(2,1)}, u32[]{:S(2)}) copy-start(bf16[1,1024,512]{2,1,0:T(8,128)(2,1)} %param.13) | copy-start | bytes 3145732
  2.4 20.3 %copy-start.5 = (bf16[4,7296]{1,0:T(4,128)(2,1)S(1)}, bf16[4,7296]{1,0:T(4,128)(2,1)}, u32[]{:S(2)}) copy-start(bf16[4,7296]{1,0:T(4,128)(2,1)} %shard_map.122) | copy-start | bytes 175108
  2.4 6.3 %collective-permute-start.2 = (bf16[4,7296]{1,0:T(4,128)(2,1)}, bf16[4,7296]{1,0:T(4,128)(2,1)S(1)}, u32[]{:S(2)}, u32[]{:S(2)}) collective-permute-start(bf16[4,7296]{1,0:T(4,128)(2,1)} %shard_map.122), channel_id=1, source_target_pairs={{0,192},{16,208},{64,0},{80,16},{128,64},{144,80},{192,128},{208,1... | collective-permute-start | bytes 175112 | tf_op jit(solution)/shard_map/ppermute | solution.py:273
  4.2 6.1 %collective-permute-start.1 = (bf16[4,7296]{1,0:T(4,128)(2,1)}, bf16[4,7296]{1,0:T(4,128)(2,1)S(1)}, u32[]{:S(2)}, u32[]{:S(2)}) collective-permute-start(bf16[4,7296]{1,0:T(4,128)(2,1)} %shard_map.122), channel_id=1, source_target_pairs={{0,128},{16,144},{64,192},{80,208},{128,0},{144,16},{192,64},{208,... | collective-permute-start | bytes 175112 | tf_op jit(solution)/shard_map/ppermute | solution.py:273
  5.7 5.7 %collective-permute-start = (bf16[4,7296]{1,0:T(4,128)(2,1)}, bf16[4,7296]{1,0:T(4,128)(2,1)S(1)}, u32[]{:S(2)}, u32[]{:S(2)}) collective-permute-start(bf16[4,7296]{1,0:T(4,128)(2,1)} %shard_map.122), channel_id=1, source_target_pairs={{0,64},{16,80},{64,128},{80,144},{128,192},{144,208},{192,0},{208,... | collective-permute-start | bytes 175112 | tf_op jit(solution)/shard_map/ppermute | solution.py:273
  8.6 34.3 %copy-start.1 = (s32[3]{0:T(128)}, s32[3]{0:T(128)S(1)}, u32[]{:S(2)}) copy-start(s32[3]{0:T(128)S(1)} %pad_add_fusion.place_ref) | copy-start | bytes 40
  15.0 40.6 %collective-permute-start.7 = (bf16[2,7168,256]{2,1,0:T(8,128)(2,1)}, bf16[2,7168,256]{2,1,0:T(8,128)(2,1)}, u32[]{:S(2)}, u32[]{:S(2)}) collective-permute-start(bf16[2,7168,256]{2,1,0:T(8,128)(2,1)} %bitcast.56), channel_id=1, source_target_pairs={{0,32},{32,0},{1,33},{33,1},{2,34},{34,2},{3,35},{35,3},{4,36},{36... | collective-permute-start | bytes 22020104 | tf_op jit(solution)/shard_map/ppermute | solution.py:294
  15.0 54.0 %collective-permute-start.11 = (bf16[4,2,256,896]{3,2,1,0:T(8,128)(2,1)}, bf16[4,2,256,896]{3,2,1,0:T(8,128)(2,1)}, u32[]{:S(2)}, u32[]{:S(2)}) collective-permute-start(bf16[4,2,256,896]{3,2,1,0:T(8,128)(2,1)} %bitcast.59), channel_id=1, source_target_pairs={{0,32},{32,0},{1,33},{33,1},{2,34},{34,2},{3,35},{35,3},{4,36},{36... | collective-permute-start | bytes 11010056 | tf_op jit(solution)/shard_map/ppermute | solution.py:295
  15.6 34.4 %all-to-all-start = ((bf16[16,8,7168]{2,1,0:T(8,128)(2,1)}), bf16[16,8,7168]{2,1,0:T(8,128)(2,1)S(1)}, u32[]{:S(2)}, u32[]{:S(2)}) async-start(bf16[16,8,7168]{2,1,0:T(8,128)(2,1)} %bitcast.5), calls=%async_computation | async-start | bytes 3670016 | tf_op jit(solution)/shard_map/all_to_all | solution.py:281
  22.6 8.8 %collective-permute-start.6 = (bf16[4,7296]{1,0:T(4,128)(2,1)S(1)}, bf16[4,7296]{1,0:T(4,128)(2,1)S(1)}, u32[]{:S(2)}, u32[]{:S(2)}) collective-permute-start(bf16[4,7296]{1,0:T(4,128)(2,1)S(1)} %copy-done.5), channel_id=1, source_target_pairs={{0,208},{16,192},{64,16},{80,0},{128,80},{144,64},{192,144},{208,1... | collective-permute-start | bytes 175112 | tf_op jit(solution)/shard_map/ppermute | solution.py:273
  28.1 7.4 %collective-permute-start.5 = (bf16[4,7296]{1,0:T(4,128)(2,1)S(1)}, bf16[4,7296]{1,0:T(4,128)(2,1)S(1)}, u32[]{:S(2)}, u32[]{:S(2)}) collective-permute-start(bf16[4,7296]{1,0:T(4,128)(2,1)S(1)} %copy-done.5), channel_id=1, source_target_pairs={{0,144},{16,128},{64,208},{80,192},{128,16},{144,0},{192,80},{208,... | collective-permute-start | bytes 175112 | tf_op jit(solution)/shard_map/ppermute | solution.py:273
  28.3 11.7 %collective-permute-start.4 = (bf16[4,7296]{1,0:T(4,128)(2,1)S(1)}, bf16[4,7296]{1,0:T(4,128)(2,1)S(1)}, u32[]{:S(2)}, u32[]{:S(2)}) collective-permute-start(bf16[4,7296]{1,0:T(4,128)(2,1)S(1)} %copy-done.5), channel_id=1, source_target_pairs={{0,80},{16,64},{64,144},{80,128},{128,208},{144,192},{192,16},{208... | collective-permute-start | bytes 175112 | tf_op jit(solution)/shard_map/ppermute | solution.py:273
  31.4 8.6 %collective-permute-start.3 = (bf16[4,7296]{1,0:T(4,128)(2,1)S(1)}, bf16[4,7296]{1,0:T(4,128)(2,1)S(1)}, u32[]{:S(2)}, u32[]{:S(2)}) collective-permute-start(bf16[4,7296]{1,0:T(4,128)(2,1)S(1)} %copy-done.5), channel_id=1, source_target_pairs={{0,16},{16,0},{64,80},{80,64},{128,144},{144,128},{192,208},{208,1... | collective-permute-start | bytes 175112 | tf_op jit(solution)/shard_map/ppermute | solution.py:273
  51.2 30.1 %all-to-all-start.1 = ((bf16[16,8,7168]{2,1,0:T(8,128)(2,1)}), bf16[16,8,7168]{2,1,0:T(8,128)(2,1)S(1)}, u32[]{:S(2)}, u32[]{:S(2)}) async-start(bf16[16,8,7168]{2,1,0:T(8,128)(2,1)} %bitcast.7), calls=%async_computation.1 | async-start | bytes 3670016 | tf_op jit(solution)/shard_map/all_to_all | solution.py:281
  55.6 11.5 %copy-start.12 = (bf16[1,64,1024]{2,1,0:T(8,128)(2,1)S(1)}, bf16[1,64,1024]{2,1,0:T(8,128)(2,1)}, u32[]{:S(2)}) copy-start(bf16[1,64,1024]{2,1,0:T(8,128)(2,1)} %param.14) | copy-start | bytes 393220
  55.6 11.5 %copy-start.13 = (bf16[1,128,64]{1,2,0:T(8,128)(2,1)S(1)}, bf16[1,128,64]{1,2,0:T(8,128)(2,1)}, u32[]{:S(2)}) copy-start(bf16[1,128,64]{1,2,0:T(8,128)(2,1)} %param.12) | copy-start | bytes 49156
  55.6 11.7 %copy-start.11 = (bf16[1,128,512]{2,1,0:T(8,128)(2,1)S(1)}, bf16[1,128,512]{2,1,0:T(8,128)(2,1)}, u32[]{:S(2)}) copy-start(bf16[1,128,512]{2,1,0:T(8,128)(2,1)} %param.11) | copy-start | bytes 393220
  62.7 10.1 %collective-permute-start.8 = (bf16[128,512]{1,0:T(8,128)(2,1)}, bf16[128,512]{1,0:T(8,128)(2,1)S(1)}, u32[]{:S(2)}, u32[]{:S(2)}) collective-permute-start(bf16[128,512]{1,0:T(8,128)(2,1)} %shard_map.125.p0), channel_id=1, source_target_pairs={{0,64},{16,80},{64,128},{80,144},{128,192},{144,208},{192,0},{208,... | collective-permute-start | bytes 393224 | tf_op jit(solution)/shard_map/ppermute | solution.py:273
  64.9 9.3 %collective-permute-start.9 = (bf16[128,512]{1,0:T(8,128)(2,1)}, bf16[128,512]{1,0:T(8,128)(2,1)S(1)}, u32[]{:S(2)}, u32[]{:S(2)}) collective-permute-start(bf16[128,512]{1,0:T(8,128)(2,1)} %shard_map.125.p0), channel_id=1, source_target_pairs={{0,128},{16,144},{64,192},{80,208},{128,0},{144,16},{192,64},{208,... | collective-permute-start | bytes 393224 | tf_op jit(solution)/shard_map/ppermute | solution.py:273
  67.0 9.0 %collective-permute-start.10 = (bf16[128,512]{1,0:T(8,128)(2,1)}, bf16[128,512]{1,0:T(8,128)(2,1)}, u32[]{:S(2)}, u32[]{:S(2)}) collective-permute-start(bf16[128,512]{1,0:T(8,128)(2,1)} %shard_map.125.p0), channel_id=1, source_target_pairs={{0,192},{16,208},{64,0},{80,16},{128,64},{144,80},{192,128},{208,1... | collective-permute-start | bytes 393224 | tf_op jit(solution)/shard_map/ppermute | solution.py:273
  72.8 3.2 %copy-start.9 = (bf16[128,512]{1,0:T(8,128)(2,1)}, bf16[128,512]{1,0:T(8,128)(2,1)S(1)}, u32[]{:S(2)}) copy-start(bf16[128,512]{1,0:T(8,128)(2,1)S(1)} %collective-permute-done.8.p1) | copy-start | bytes 393220
  81.3 8.2 %copy-start.3 = (bf16[16,8,7168]{2,1,0:T(8,128)(2,1)}, bf16[16,8,7168]{2,1,0:T(8,128)(2,1)S(1)}, u32[]{:S(2)}) copy-start(bf16[16,8,7168]{2,1,0:T(8,128)(2,1)S(1)} %all-to-all-done.1) | copy-start | bytes 5505028
  81.3 24.9 %all-to-all-start.2 = ((bf16[16,8,1792]{2,1,0:T(8,128)(2,1)}), bf16[16,8,1792]{2,1,0:T(8,128)(2,1)S(1)}, u32[]{:S(2)}, u32[]{:S(2)}) async-start(bf16[16,8,1792]{2,1,0:T(8,128)(2,1)} %bitcast.64), calls=%async_computation.2 | async-start | bytes 917504 | tf_op jit(solution)/shard_map/all_to_all | solution.py:281
  96.5 9.7 %collective-permute-start.13 = (bf16[128,512]{1,0:T(8,128)(2,1)}, bf16[128,512]{1,0:T(8,128)(2,1)S(1)}, u32[]{:S(2)}, u32[]{:S(2)}) collective-permute-start(bf16[128,512]{1,0:T(8,128)(2,1)} %shard_map.127.p0), channel_id=1, source_target_pairs={{0,128},{16,144},{64,192},{80,208},{128,0},{144,16},{192,64},{208,... | collective-permute-start | bytes 393224 | tf_op jit(solution)/shard_map/ppermute | solution.py:273
  98.7 8.8 %collective-permute-start.12 = (bf16[128,512]{1,0:T(8,128)(2,1)}, bf16[128,512]{1,0:T(8,128)(2,1)S(1)}, u32[]{:S(2)}, u32[]{:S(2)}) collective-permute-start(bf16[128,512]{1,0:T(8,128)(2,1)} %shard_map.127.p0), channel_id=1, source_target_pairs={{0,64},{16,80},{64,128},{80,144},{128,192},{144,208},{192,0},{208,... | collective-permute-start | bytes 393224 | tf_op jit(solution)/shard_map/ppermute | solution.py:273
  98.7 10.2 %collective-permute-start.14 = (bf16[128,512]{1,0:T(8,128)(2,1)}, bf16[128,512]{1,0:T(8,128)(2,1)S(1)}, u32[]{:S(2)}, u32[]{:S(2)}) collective-permute-start(bf16[128,512]{1,0:T(8,128)(2,1)} %shard_map.127.p0), channel_id=1, source_target_pairs={{0,192},{16,208},{64,0},{80,16},{128,64},{144,80},{192,128},{208,1... | collective-permute-start | bytes 393224 | tf_op jit(solution)/shard_map/ppermute | solution.py:273
  106.2 25.5 %copy-start.2 = (s32[3]{0:T(128)S(1)}, s32[3]{0:T(128)}, u32[]{:S(2)}) copy-start(s32[3]{0:T(128)} %copy-done.1) | copy-start | bytes 40
  114.9 16.7 %all-to-all-start.3 = ((bf16[16,8,1792]{2,1,0:T(8,128)(2,1)}), bf16[16,8,1792]{2,1,0:T(8,128)(2,1)S(1)}, u32[]{:S(2)}, u32[]{:S(2)}) async-start(bf16[16,8,1792]{2,1,0:T(8,128)(2,1)} %bitcast.65), calls=%async_computation.3 | async-start | bytes 917504 | tf_op jit(solution)/shard_map/all_to_all | solution.py:281
  121.9 4.2 %collective-permute-start.17 = (bf16[32,640]{1,0:T(8,128)(2,1)S(1)}, bf16[32,640]{1,0:T(8,128)(2,1)S(1)}, u32[]{:S(2)}, u32[]{:S(2)}) collective-permute-start(bf16[32,640]{1,0:T(8,128)(2,1)S(1)} %get-tuple-element.37), channel_id=1, source_target_pairs={{0,192},{64,0},{128,64},{192,128},{1,193},{65,1},{129,65},{193,129... | collective-permute-start | bytes 122888 | tf_op jit(solution)/shard_map/ppermute | solution.py:314
  122.8 4.9 %collective-permute-start.16 = (bf16[32,640]{1,0:T(8,128)(2,1)S(1)}, bf16[32,640]{1,0:T(8,128)(2,1)S(1)}, u32[]{:S(2)}, u32[]{:S(2)}) collective-permute-start(bf16[32,640]{1,0:T(8,128)(2,1)S(1)} %get-tuple-element.38), channel_id=1, source_target_pairs={{0,128},{64,192},{128,0},{192,64},{1,129},{65,193},{129,1},{193,65... | collective-permute-start | bytes 122888 | tf_op jit(solution)/shard_map/ppermute | solution.py:314
  125.0 4.0 %collective-permute-start.15 = (bf16[32,640]{1,0:T(8,128)(2,1)S(1)}, bf16[32,640]{1,0:T(8,128)(2,1)S(1)}, u32[]{:S(2)}, u32[]{:S(2)}) collective-permute-start(bf16[32,640]{1,0:T(8,128)(2,1)S(1)} %get-tuple-element.36), channel_id=1, source_target_pairs={{0,64},{64,128},{128,192},{192,0},{1,65},{65,129},{129,193},{193,1... | collective-permute-start | bytes 122888 | tf_op jit(solution)/shard_map/ppermute | solution.py:314
  133.6 14.4 %all-to-all-start.4 = ((bf16[8,4,1792]{2,1,0:T(4,128)(2,1)}), bf16[8,4,1792]{2,1,0:T(4,128)(2,1)S(1)}, u32[]{:S(2)}, u32[]{:S(2)}) async-start(bf16[8,4,1792]{2,1,0:T(4,128)(2,1)} %shard_map.129), calls=%async_computation.4 | async-start | bytes 229376 | tf_op jit(solution)/shard_map/all_to_all | solution.py:318
  (5 other events, 7.9 us)

commit v7 on v6

v7 whole, which is shorter than its diff:
```python
import jax
import jax.numpy as jnp
from jax import lax
from jax.experimental import pallas as pl
from jax.experimental.pallas import tpu as pltpu
from jax.sharding import Mesh, PartitionSpec as P

softmax_scale = 192.0 ** (-0.5)
epsilon = 1e-06
bf16 = jnp.bfloat16
f32 = jnp.float32
INFO = 128
TOK = 4
SLOTS = 2


def attend(query_latent, query_rope, latent_cache, rope_keys, lengths):
    shard_length = latent_cache.shape[1]
    first_position = lax.axis_index("ctx") * shard_length
    scores = jnp.einsum("hr,tr->ht", query_latent[0], latent_cache[0], preferred_element_type=f32)
    scores = scores + jnp.einsum("hp,pt->ht", query_rope[0], rope_keys[0], preferred_element_type=f32)
    position = first_position + jnp.arange(shard_length, dtype=jnp.int32)
    live_mask = position < lengths[0]
    weights = jnp.where(live_mask[None, :], jnp.exp(softmax_scale * scores), f32(0.0))
    mass = jnp.sum(weights, axis=1, keepdims=True)
    numerator = jnp.dot(weights.astype(bf16), latent_cache[0], preferred_element_type=f32)
    high = lax.reduce_precision(mass, 8, 7)
    low = mass - high
    tail = jnp.concatenate([jnp.broadcast_to(v, (128, 64)) for v in (high, low)], axis=1)
    return jnp.concatenate([numerator, tail], axis=1).astype(bf16)


def finish_attention(parts):
    summed = sum(v.astype(f32) for v in parts)
    return (summed[:, :512] / (summed[:, 512:513] + summed[:, 576:577])).astype(bf16)[None]


VMEM = pl.BlockSpec(memory_space=pltpu.VMEM)
SMEM = pl.BlockSpec(memory_space=pltpu.SMEM)
HBM = pl.BlockSpec(memory_space=pltpu.HBM)
ANY = pl.BlockSpec(memory_space=pl.ANY)
STEP = 1024


def room(mib):
    return pltpu.CompilerParams(vmem_limit_bytes=mib * 1024 * 1024)


def prepare_kernel(ids_ref, gates_ref, rows_ref, gain_ref, out_ref):
    width = rows_ref.shape[1]
    rows = rows_ref[...].astype(f32)
    mean = jnp.mean(rows * rows, axis=1, keepdims=True)
    gain = gain_ref[...].astype(f32).reshape(1, width)
    out_ref[:, :width] = (rows * lax.rsqrt(mean + epsilon) * gain).astype(bf16)
    lane = lax.broadcasted_iota(jnp.int32, (1, 128), 1)
    expert, slot = lane // SLOTS, lane % SLOTS
    count = jnp.zeros((1, 128), jnp.int32)
    token = jnp.full((1, 128), -1.0, f32)
    gate = jnp.zeros((1, 128), f32)
    for t in range(TOK):
        picked = jnp.zeros((1, 128), jnp.int32)
        share = jnp.zeros((1, 128), f32)
        for j in range(8):
            hit = expert == ids_ref[t, j]
            picked = jnp.where(hit, 1, picked)
            share = share + jnp.where(hit, gates_ref[t, j], f32(0.0))
        here = (picked == 1) & (count == slot)
        token = jnp.where(here, f32(t), token)
        gate = jnp.where(here, share, gate)
        count = count + picked
    high = gate.astype(bf16).astype(f32)
    middle = (gate - high).astype(bf16).astype(f32)
    low = gate - high - middle
    row = lax.broadcasted_iota(jnp.int32, (TOK, 128), 0)
    facts = jnp.where(row == 0, token, jnp.where(row == 1, high, jnp.where(row == 2, middle, low)))
    out_ref[:, width:] = facts.astype(bf16)


def prepare(moe_rows, route_ids, route_gates, norm_gain):
    return pl.pallas_call(
        prepare_kernel,
        out_shape=jax.ShapeDtypeStruct((TOK, moe_rows.shape[1] + INFO), bf16),
        in_specs=[SMEM, SMEM, VMEM, VMEM],
        out_specs=VMEM,
    )(route_ids, route_gates, moe_rows, norm_gain)


def grid(rows, columns, dim):
    return lax.broadcasted_iota(jnp.int32, (rows, columns), dim)


def choose_kernel(place_ref, t0, t1, t2, t3, *out_refs):
    ctx, core, half, x, y = (place_ref[i] for i in range(5))
    width = out_refs[0].shape[1]
    refs = (t0, t1, t2, t3)
    facts = jnp.concatenate([ref[:, width:] for ref in refs], axis=0)
    first = grid(64, 64, 1) == grid(64, 64, 0) // TOK * TOK
    facts = jnp.dot(first.astype(f32).astype(bf16), facts, preferred_element_type=f32)
    row = grid(128, 128, 0)
    ahead = row // 32
    expert = jnp.where(core == 0, (x + ahead) % 4 * 4 + y, x * 4 + (y + ahead) % 4)
    lane = half * 32 + expert * SLOTS + row % SLOTS
    pick = (grid(128, 128, 1) == lane).astype(f32).astype(bf16)
    wanted = lax.dot_general(
        pick, facts.astype(bf16), (((1,), (1,)), ((), ())), preferred_element_type=f32
    )
    row, column = grid(128, 64, 0), grid(128, 64, 1)
    hit = wanted == (column % TOK).astype(f32)
    hit = hit & (column // 16 == row // 8 % 4)
    hit = hit & ((ctx - column // TOK % 4 + 4) % 4 == row // SLOTS % 4)
    selector = hit.astype(f32).astype(bf16)
    for low in range(0, width, STEP):
        tokens = jnp.concatenate([ref[:, low : low + STEP] for ref in refs], axis=0)
        part = jnp.dot(selector, tokens, preferred_element_type=f32).astype(bf16)
        for k, out_ref in enumerate(out_refs):
            out_ref[:, low : low + STEP] = part[32 * k : 32 * (k + 1)]


def choose(place, line, width):
    return pl.pallas_call(
        choose_kernel,
        out_shape=tuple(jax.ShapeDtypeStruct((32, width), bf16) for _ in range(4)),
        in_specs=[SMEM] + [VMEM] * 4,
        out_specs=(VMEM,) * 4,
        compiler_params=room(8),
        cost_estimate=pl.CostEstimate(flops=2 * 128 * 64 * width, bytes_accessed=2 * 192 * width, transcendentals=0),
    )(place, *line)


def gate_up_kernel(
    place_ref, r0, r1, r2, r3, own_hbm, other_hbm, out_ref, rows_ref, held_ref, hidden_ref, row_sems, sems
):
    core, x, y = place_ref[1], place_ref[3], place_ref[4]
    width = rows_ref.shape[1]
    moves = []
    for k, source in enumerate((r0, r1, r2, r3)):
        moves.append(pltpu.make_async_copy(source, rows_ref.at[pl.ds(32 * k, 32)], row_sems.at[k]))
        moves[k].start()
    copies = []
    for i in range(width // STEP):
        part = pl.ds(i * STEP, STEP)
        copies.append(
            [
                pltpu.make_async_copy(own_hbm.at[:, part], held_ref.at[0, :, part], sems.at[i, 0]),
                pltpu.make_async_copy(other_hbm.at[:, part], held_ref.at[1, :, part], sems.at[i, 1]),
            ]
        )
        for copy in copies[-1]:
            copy.start()
    sums = [jnp.zeros((128, 256), f32) for _ in range(4)]
    for move in moves:
        move.wait()
    for i in range(width // STEP):
        low, high = i * STEP, (i + 1) * STEP
        for copy in copies[i]:
            copy.wait()
        rows = rows_ref[:, low:high]
        for j in range(2):
            for k in range(2):
                sums[2 * j + k] += jnp.dot(rows, held_ref[j, k, low:high], preferred_element_type=f32)
    for j in range(2):
        gate, up = sums[2 * j], sums[2 * j + 1]
        hidden = gate / (1.0 + jnp.exp(-gate)) * up
        for v in range(4):
            for u in range(4):
                back_x = (x - jnp.where(core == 0, v, u) + 4) % 4
                back_y = (y - jnp.where(core == 0, u, v) + 4) % 4
                at = pl.ds(pl.multiple_of((back_x * 4 + back_y) * 8, 8), 8)
                low = 8 * (4 * v + u)
                hidden_ref[at, j * 256 : (j + 1) * 256] = hidden[low : low + 8]
    out_ref[...] = hidden_ref[...].astype(bf16)


def gate_up(place, rows, own, other):
    width = own.shape[1]
    return pl.pallas_call(
        gate_up_kernel,
        out_shape=jax.ShapeDtypeStruct((128, 512), bf16),
        in_specs=[SMEM] + [ANY] * 4 + [HBM] * 2,
        out_specs=VMEM,
        scratch_shapes=[
            pltpu.VMEM((128, width), bf16),
            pltpu.VMEM((2, 2, width, 256), bf16),
            pltpu.VMEM((128, 512), f32),
            pltpu.SemaphoreType.DMA((4,)),
            pltpu.SemaphoreType.DMA((width // STEP, 2)),
        ],
        compiler_params=room(46),
        cost_estimate=pl.CostEstimate(
            flops=2 * 128 * width * 1024, bytes_accessed=2 * width * (1024 + 128), transcendentals=65536
        ),
    )(place, *rows, own, other)


def down_kernel(place_ref, *refs):
    ctx, core = place_ref[0], place_ref[1]
    pieces, (own_hbm, other_hbm, out_ref, pieces_ref, held_ref, sems) = refs[:8], refs[8:]
    copies = []
    for k in range(4):
        source = (ctx - k + 4) % 4
        copies.append(
            [
                pltpu.make_async_copy(pieces[k], pieces_ref.at[k, pl.ds(0, 128)], sems.at[k, 0]),
                pltpu.make_async_copy(pieces[4 + k], pieces_ref.at[k, pl.ds(128, 128)], sems.at[k, 1]),
                pltpu.make_async_copy(own_hbm.at[source], held_ref.at[0, k], sems.at[k, 2]),
                pltpu.make_async_copy(other_hbm.at[source], held_ref.at[1, k], sems.at[k, 3]),
            ]
        )
        for copy in copies[-1]:
            copy.start()
    totals = [jnp.zeros((256, 896), f32) for _ in range(2)]
    for k in range(4):
        for copy in copies[k]:
            copy.wait()
        for j in range(2):
            totals[j] += jnp.dot(pieces_ref[k, :, :256], held_ref[j, k, core], preferred_element_type=f32)
            totals[j] += jnp.dot(pieces_ref[k, :, 256:], held_ref[j, k, 1 - core], preferred_element_type=f32)
    for j in range(2):
        total = jnp.where(core == j, totals[0], totals[1]).reshape(2, 16, 8, 896)
        total = jnp.concatenate([total[0], total[1]], axis=1).reshape(256, 896)
        out_ref[:, j * 896 : (j + 1) * 896] = total.astype(bf16)


def down(place, pieces, own, other):
    return pl.pallas_call(
        down_kernel,
        out_shape=jax.ShapeDtypeStruct((256, 1792), bf16),
        in_specs=[SMEM] + [ANY] * 8 + [HBM] * 2,
        out_specs=VMEM,
        scratch_shapes=[
            pltpu.VMEM((4, 256, 512), bf16),
            pltpu.VMEM((2, 4, 2, 256, 896), bf16),
            pltpu.SemaphoreType.DMA((4, 4)),
        ],
        compiler_params=room(53),
        cost_estimate=pl.CostEstimate(
            flops=2 * 256 * 2048 * 1792, bytes_accessed=2 * 2048 * 1792 + 2 * 256 * 2048, transcendentals=0
        ),
    )(place, *pieces, own, other)


def mix_kernel(place_ref, back, facts0, facts1, out_ref):
    ctx, half = place_ref[0], place_ref[2]
    lane = grid(128, 256, 1)
    spread = grid(128, 256, 0) == half * 32 + lane // 16 * SLOTS + lane % SLOTS
    spread = spread.astype(f32).astype(bf16)
    facts = jnp.concatenate([facts0[...], facts1[...]], axis=0)
    facts = jnp.dot(facts, spread, preferred_element_type=f32)
    at, lane = grid(32, 256, 0), grid(32, 256, 1)
    chunk, lane_ctx = lane // 8 % 2, lane // SLOTS % 4
    here = (at // 16 == chunk) & ((ctx - at // TOK % 4 + 4) % 4 == lane_ctx)
    token, high, middle, low = (
        jnp.sum(jnp.where(here & (at % TOK == i), facts, 0.0), axis=0, keepdims=True) for i in range(4)
    )
    fits = (at // 8 == lane_ctx) & (at // 4 % 2 == jnp.where(chunk == 0, half, 1 - half))
    fits = fits & ((at % TOK).astype(f32) == token)
    total = jnp.zeros((32, 1792), f32)
    for part in (high, middle, low):
        matrix = jnp.where(fits, part, 0.0).astype(bf16)
        total += jnp.dot(matrix, back[...], preferred_element_type=f32)
    out_ref[...] = total.reshape(8, TOK, 1792).astype(bf16)


def mix(place, back, facts0, facts1):
    return pl.pallas_call(
        mix_kernel,
        out_shape=jax.ShapeDtypeStruct((8, TOK, 1792), bf16),
        in_specs=[SMEM] + [VMEM] * 3,
        out_specs=VMEM,
        compiler_params=room(6),
        cost_estimate=pl.CostEstimate(flops=2 * 32 * 256 * 1792 * 3, bytes_accessed=1 << 20, transcendentals=0),
    )(place, back, facts0, facts1)


def shards(
    query_latent,
    query_rope,
    latent_cache,
    rope_keys,
    lengths,
    moe_rows,
    route_ids,
    route_gates,
    norm_gain,
    expert_in,
    expert_out,
):
    c = lax.axis_index("ctx")
    a = lax.axis_index("att")
    h = lax.axis_index("zhi")
    width = moe_rows.shape[1]
    swap_core = [(0, 1), (1, 0)]

    place = jnp.stack([c, a, h, lax.axis_index("x"), lax.axis_index("y")]).astype(jnp.int32)
    payload = prepare(moe_rows, route_ids, route_gates, norm_gain)

    def hop(value, k):
        return lax.ppermute(value, "ctx", [(i, (i + k) % 4) for i in range(4)])

    def along(value, k, second):
        pairs = []
        for i in range(32):
            core, x, y = i // 16, i // 4 % 4, i % 4
            if (core == 0) == second:
                x = (x + k) % 4
            else:
                y = (y + k) % 4
            pairs.append((i, core * 16 + x * 4 + y))
        return lax.ppermute(value, ("att", "x", "y"), pairs)

    def first_stage(tokens):
        return [tokens] + [along(tokens, k, False) for k in (1, 2, 3)]

    def second_stage(rows):
        return [rows[0]] + [along(rows[k], k, True) for k in (1, 2, 3)]

    def hidden_of(got):
        hidden = gate_up(place, got, weight_in, other_in)
        return [hidden] + [hop(hidden, k) for k in (1, 2, 3)]

    weight_in, weight_out = expert_in[0], expert_out[0].reshape(4, 2, 256, 896)
    payload, moving_in, moving_out = lax.optimization_barrier((payload, weight_in, weight_out))
    other_in = lax.ppermute(moving_in, "att", swap_core)
    other_out = lax.ppermute(moving_out, "att", swap_core)
    tokens0 = jnp.concatenate([payload] + [hop(payload, k) for k in (1, 2, 3)], axis=0)
    part = attend(query_latent, query_rope, latent_cache, rope_keys, lengths).reshape(4, 32, 640)
    tokens0, facts0, part = lax.optimization_barrier((tokens0, tokens0[:, width:], part))
    line0 = first_stage(tokens0)
    tokens1, line0[1] = lax.optimization_barrier((tokens0, line0[1]))
    tokens1 = lax.ppermute(tokens1, "zhi", swap_core)
    rows0 = choose(place, line0, width)
    got0 = second_stage(rows0)
    tokens1, facts1, got0[1] = lax.optimization_barrier((tokens1, tokens1[:, width:], got0[1]))
    line1 = first_stage(tokens1)
    pieces0 = hidden_of(got0)
    pieces0[0], *line1 = lax.optimization_barrier((pieces0[0], *line1))
    got1 = second_stage(choose(place, line1, width))

    pieces1 = hidden_of(got1)
    result = down(place, pieces0 + pieces1, weight_out, other_out)
    back = lax.all_to_all(result.reshape(16, 16, 1792), ("x", "y"), split_axis=0, concat_axis=0, tiled=True)
    part, _ = lax.optimization_barrier((part, result))
    parts = [lax.dynamic_index_in_dim(part, c, 0, keepdims=False)]
    for k in (1, 2, 3):
        sent = lax.dynamic_index_in_dim(part, (c + k) % 4, 0, keepdims=False)
        parts.append(hop(sent, k))
    attended = finish_attention(parts)

    outgoing = mix(place, back.reshape(256, 1792), facts0, facts1)
    final = lax.all_to_all(outgoing, ("ctx", "zhi"), split_axis=0, concat_axis=0, tiled=True)
    final = final.reshape(4, 2, TOK, 1792).astype(f32)
    routed = (final[:, 0] + final[:, 1]).transpose(1, 0, 2).reshape(TOK, 4 * 1792)
    return (attended, routed.astype(bf16))


def solution(mesh):
    fine = Mesh(mesh.devices.reshape(4, 2, 2, 4, 4), ("ctx", "att", "zhi", "x", "y"))
    exp = ("zhi", "x", "y")
    sequences = ("att",) + exp
    every = ("ctx", "att") + exp
    placed = (
        P(sequences, None, None),
        P(sequences, None, None),
        P(sequences, "ctx", None),
        P(sequences, None, "ctx"),
        P(sequences),
        P(every, None),
        P(every, None),
        P(every, None),
        P(),
        P(exp, None, None, ("ctx", "att")),
        P(exp, None, ("ctx", "att")),
    )
    return jax.shard_map(
        shards,
        mesh=fine,
        in_specs=placed,
        out_specs=(P(sequences, "ctx", None), P(every, None)),
        check_vma=False,
    )
```

time: 149 us -> 138 us (0.926)
  Pallas kernels: 33.7 us -> 27.7 us
  waiting for transfers between devices: 41.6 us -> 38.9 us
  starting transfers between devices: 64.1 us -> 62.4 us
    all_to_all x4 -> x1, starting transfers between devices: 24.7 us -> 4.55 us  [shards(): lax.all_to_all(result.reshape(16, 16, 1792), ('x', 'y'), split_axis=0, co...]
    ppermute x16 -> x25, starting transfers between devices: 31.9 us -> 48.3 us  [the longest x12 22.6 us: along(): return lax.ppermute(value, ('att', 'x', 'y'), pairs)]
    pallas_call x4 -> x3, Pallas kernels: 15.9 us -> 9.17 us  [the longest x1 6.32 us: down(): pl.pallas_call(down_kernel, out_shape=jax.ShapeDtypeStruct((256, 1792), b...]
    all_to_all x4 -> x1, waiting for transfers between devices: 9.48 us -> 5.42 us  [shards(): lax.all_to_all(result.reshape(16, 16, 1792), ('x', 'y'), split_axis=0, co...]
    all_to_all x1, starting transfers between devices: 7.06 us -> 9.63 us  [shards(): lax.all_to_all(outgoing, ('ctx', 'zhi'), split_axis=0, concat_axis=0, til...]
    ppermute x16 -> x25, waiting for transfers between devices: 25.5 us -> 26.9 us  [the longest x12 12.3 us: along(): return lax.ppermute(value, ('att', 'x', 'y'), pairs)]
  transfers between devices with their start and end apart: 23 -> 29, of which waited for: 14 -> 13; matrix products, arithmetic and copies ran while one was open for 3% -> 4% of each run, Pallas kernels for 15% -> 13%
where the time goes in v7:
time: 138 us; the launch traced here: 137 us
  starting transfers between devices  62.4 us (45%)
  waiting for transfers between devices  38.9 us (28%)
  Pallas kernels  27.7 us (20%)
  matrix products  2.98 us (2%)
  other arithmetic  2.64 us (2%)
  between operations  1.54 us (1%)
    ppermute x12, starting transfers between devices, along(): return lax.ppermute(value, ('att', 'x', 'y'), pairs)  22.6 us
    ppermute x12, starting transfers between devices, hop(): return lax.ppermute(value, 'ctx', [(i, (i + k) % 4) for i in range(4)])  20.1 us
    pallas_call x2, Pallas kernels, gate_up(): pl.pallas_call(gate_up_kernel, out_shape=jax.ShapeDtypeStruct((128, 512),...  14.9 us
    ppermute x12, waiting for transfers between devices, along(): return lax.ppermute(value, ('att', 'x', 'y'), pairs)  12.3 us
    ppermute x12, waiting for transfers between devices, hop(): return lax.ppermute(value, 'ctx', [(i, (i + k) % 4) for i in range(4)])  10.4 us
    all_to_all x1, starting transfers between devices, shards(): lax.all_to_all(outgoing, ('ctx', 'zhi'), split_axis=0, concat_axis=0, til...  9.63 us
    all_to_all x1, waiting for transfers between devices, shards(): lax.all_to_all(outgoing, ('ctx', 'zhi'), split_axis=0, concat_axis=0, til...  6.6 us
    pallas_call x1, Pallas kernels, down(): pl.pallas_call(down_kernel, out_shape=jax.ShapeDtypeStruct((256, 1792), b...  6.32 us
  transfers between devices with their start and end apart: 29, of which 13 were waited for; matrix products, arithmetic and copies ran while one was open for 4% of the time, Pallas kernels for 13%

profile of v7, /device:TPU:32, one launch (start us, length us, event | category | flops | bytes accessed | tf_op | source)
XLA Modules:
  0.0 137.2 jit_solution(3230610787753184821)
XLA Ops:
  0.6 1.7 %shard_map.122 = bf16[4,7296]{1,0:T(4,128)(2,1)} custom-call(s32[4,8]{1,0:T(4,128)} %ids_ref.1, f32[4,8]{1,0:T(4,128)} %gates_ref.1, bf16[4,7168]{1,0:T(4,128)(2,1)} %rows_ref.1, bf16[7168]{0:T(1024)(128)(2,1)} %gain_ref.1), custom_call_target="tpu_custom_call" | custom-call | tf_op jit(solution)/shard_map/pallas_call | solution.py:80
  2.4 1.9 %collective-permute-start = (bf16[4,7296]{1,0:T(4,128)(2,1)}, bf16[4,7296]{1,0:T(4,128)(2,1)S(1)}, u32[]{:S(2)}, u32[]{:S(2)}) collective-permute-start(bf16[4,7296]{1,0:T(4,128)(2,1)} %shard_map.122), channel_id=1, source_target_pairs={{0,64},{64,128},{128,192},{192,0},{1,65},{65,129},{129,193},{193,1... | collective-permute-start | bytes 175112 | tf_op jit(solution)/shard_map/ppermute | solution.py:298
  4.3 2.3 %collective-permute-start.1 = (bf16[4,7296]{1,0:T(4,128)(2,1)}, bf16[4,7296]{1,0:T(4,128)(2,1)S(1)}, u32[]{:S(2)}, u32[]{:S(2)}) collective-permute-start(bf16[4,7296]{1,0:T(4,128)(2,1)} %shard_map.122), channel_id=1, source_target_pairs={{0,128},{64,192},{128,0},{192,64},{1,129},{65,193},{129,1},{193,65... | collective-permute-start | bytes 175112 | tf_op jit(solution)/shard_map/ppermute | solution.py:298
  9.5 1.5 %fusion.16 = (bf16[128,1024]{1,0:T(8,128)(2,1)S(1)}, f32[128]{0:T(128)S(1)}) fusion(f32[128,1024]{1,0:T(8,128)S(1)} %fusion.5, bf16[1,1024,512]{2,1,0:T(8,128)(2,1)S(1)} %copy-done, bf16[1,128,512]{2,1,0:T(8,128)(2,1)} %param.11, pred[1024]{0:T(1024)(128)(4,1)S(1)} %add_compare_fusion), kind=kOutput, calls=%fused_computation.30 | convolution fusion | flops 134872960 | bytes 1967616 | tf_op jit(solution)/shard_map/hr,tr->ht/dot_general | solution.py:20
  14.8 2.9 %collective-permute-start.4 = (bf16[16,7296]{1,0:T(8,128)(2,1)S(1)}, bf16[16,7296]{1,0:T(8,128)(2,1)S(1)}, u32[]{:S(2)}, u32[]{:S(2)}) collective-permute-start(bf16[16,7296]{1,0:T(8,128)(2,1)S(1)} %pad_maximum_fusion.t0), channel_id=1, source_target_pairs={{0,2},{1,3},{2,0},{3,1},{4,6},{5,7},{6,4},{7,5},{8,10},{9,11},{10,... | collective-permute-start | bytes 700424 | tf_op jit(solution)/shard_map/ppermute | solution.py:309
  19.1 1.8 %collective-permute-done.3.t1 = bf16[16,7296]{1,0:T(8,128)(2,1)S(1)} collective-permute-done((bf16[16,7296]{1,0:T(8,128)(2,1)S(1)}, bf16[16,7296]{1,0:T(8,128)(2,1)S(1)}, u32[]{:S(2)}, u32[]{:S(2)}) %collective-permute-start.3) | collective-permute-done | bytes 233504 | tf_op jit(solution)/shard_map/ppermute | solution.py:309
  20.9 5.6 %collective-permute-start.6 = (bf16[16,7296]{1,0:T(8,128)(2,1)S(1)}, bf16[16,7296]{1,0:T(8,128)(2,1)S(1)}, u32[]{:S(2)}, u32[]{:S(2)}) collective-permute-start(bf16[16,7296]{1,0:T(8,128)(2,1)S(1)} %pad_maximum_fusion.t0), channel_id=1, source_target_pairs={{0,16},{16,0},{1,17},{17,1},{2,18},{18,2},{3,19},{19,3},{4,20},{20... | collective-permute-start | bytes 700424 | tf_op jit(solution)/shard_map/ppermute | solution.py:330
  28.0 1.6 %collective-permute-start.7 = (bf16[32,7168]{1,0:T(8,128)(2,1)S(1)}, bf16[32,7168]{1,0:T(8,128)(2,1)S(1)}, u32[]{:S(2)}, u32[]{:S(2)}) collective-permute-start(bf16[32,7168]{1,0:T(8,128)(2,1)S(1)} %get-tuple-element.33), channel_id=1, source_target_pairs={{0,4},{1,5},{2,6},{3,7},{4,8},{5,9},{6,10},{7,11},{8,12},{9,13},{1... | collective-permute-start | bytes 1376264 | tf_op jit(solution)/shard_map/ppermute | solution.py:309
  29.6 2.7 %collective-permute-start.8 = (bf16[32,7168]{1,0:T(8,128)(2,1)S(1)}, bf16[32,7168]{1,0:T(8,128)(2,1)S(1)}, u32[]{:S(2)}, u32[]{:S(2)}) collective-permute-start(bf16[32,7168]{1,0:T(8,128)(2,1)S(1)} %get-tuple-element.35), channel_id=1, source_target_pairs={{0,8},{1,9},{2,10},{3,11},{4,12},{5,13},{6,14},{7,15},{8,0},{9,1},... | collective-permute-start | bytes 1376264 | tf_op jit(solution)/shard_map/ppermute | solution.py:309
  32.3 4.2 %collective-permute-done.6.t0 = bf16[16,7296]{1,0:T(8,128)(2,1)S(1)} collective-permute-done((bf16[16,7296]{1,0:T(8,128)(2,1)S(1)}, bf16[16,7296]{1,0:T(8,128)(2,1)S(1)}, u32[]{:S(2)}, u32[]{:S(2)}) %collective-permute-start.6) | collective-permute-done | bytes 233504 | tf_op jit(solution)/shard_map/ppermute | solution.py:330
  36.5 1.5 %collective-permute-start.9 = (bf16[32,7168]{1,0:T(8,128)(2,1)S(1)}, bf16[32,7168]{1,0:T(8,128)(2,1)S(1)}, u32[]{:S(2)}, u32[]{:S(2)}) collective-permute-start(bf16[32,7168]{1,0:T(8,128)(2,1)S(1)} %get-tuple-element.36), channel_id=1, source_target_pairs={{0,12},{1,13},{2,14},{3,15},{4,0},{5,1},{6,2},{7,3},{8,4},{9,5},{1... | collective-permute-start | bytes 1376264 | tf_op jit(solution)/shard_map/ppermute | solution.py:309
  38.0 1.6 %collective-permute-start.11 = (bf16[16,7296]{1,0:T(8,128)(2,1)S(1)}, bf16[16,7296]{1,0:T(8,128)(2,1)S(1)}, u32[]{:S(2)}, u32[]{:S(2)}) collective-permute-start(bf16[16,7296]{1,0:T(8,128)(2,1)S(1)} %collective-permute-done.6.t0), channel_id=1, source_target_pairs={{0,1},{1,2},{2,3},{3,0},{4,5},{5,6},{6,7},{7,4},{8,9},{9,10},{10,1... | collective-permute-start | bytes 700424 | tf_op jit(solution)/shard_map/ppermute | solution.py:309
  39.6 5.8 %collective-permute-done.8.r2 = bf16[32,7168]{1,0:T(8,128)(2,1)S(1)} collective-permute-done((bf16[32,7168]{1,0:T(8,128)(2,1)S(1)}, bf16[32,7168]{1,0:T(8,128)(2,1)S(1)}, u32[]{:S(2)}, u32[]{:S(2)}) %collective-permute-start.8) | collective-permute-done | bytes 458784 | tf_op jit(solution)/shard_map/ppermute | solution.py:309
  45.7 4.8 %collective-permute-start.13 = (bf16[16,7296]{1,0:T(8,128)(2,1)S(1)}, bf16[16,7296]{1,0:T(8,128)(2,1)S(1)}, u32[]{:S(2)}, u32[]{:S(2)}) collective-permute-start(bf16[16,7296]{1,0:T(8,128)(2,1)S(1)} %collective-permute-done.6.t0), channel_id=1, source_target_pairs={{0,3},{1,0},{2,1},{3,2},{4,7},{5,4},{6,5},{7,6},{8,11},{9,8},{10,9... | collective-permute-start | bytes 700424 | tf_op jit(solution)/shard_map/ppermute | solution.py:309
  50.5 7.5 %shard_map.124.refs_0_ = bf16[128,512]{1,0:T(8,128)(2,1)S(1)} custom-call(s32[5]{0:T(128)S(1)} %stack.23.place_ref, bf16[32,7168]{1,0:T(8,128)(2,1)S(1)} %get-tuple-element.31.r0, bf16[32,7168]{1,0:T(8,128)(2,1)S(1)} %collective-permute-done.7.r1, bf16[32,7168]{1,0:T(8,128)(2,1)S(1)} %collective-permute-done.8.r2, ...), custom_call_target="tpu_custom_call" | custom-call | flops 1879048192 | bytes 16515072 | tf_op jit(solution)/shard_map/pallas_call | solution.py:176
  58.0 1.4 %shard_map.125 = (bf16[32,7168]{1,0:T(8,128)(2,1)S(1)}, bf16[32,7168]{1,0:T(8,128)(2,1)S(1)}, bf16[32,7168]{1,0:T(8,128)(2,1)S(1)}, bf16[32,7168]{1,0:T(8,128)(2,1)S(1)}) custom-call(s32[5]{0:T(128)S(1)} %stack.23.place_ref, bf16[16,7296]{1,0:T(8,128)(2,1)S(1)} %collective-permute-done.6.t0, bf16[16,7296]{1,0:T(8,128)(2,1)S(1)} %collective-permute-done.11.t1, ...), custom_call_target="tpu_custom_call" | custom-call | flops 117440512 | bytes 2752512 | tf_op jit(solution)/shard_map/pallas_call | solution.py:120
  60.5 3.2 %collective-permute-start.18 = (bf16[32,7168]{1,0:T(8,128)(2,1)S(1)}, bf16[32,7168]{1,0:T(8,128)(2,1)S(1)}, u32[]{:S(2)}, u32[]{:S(2)}) collective-permute-start(bf16[32,7168]{1,0:T(8,128)(2,1)S(1)} %get-tuple-element.46), channel_id=1, source_target_pairs={{0,8},{1,9},{2,10},{3,11},{4,12},{5,13},{6,14},{7,15},{8,0},{9,1},... | collective-permute-start | bytes 1376264 | tf_op jit(solution)/shard_map/ppermute | solution.py:309
  64.5 4.7 %collective-permute-done.17.r1 = bf16[32,7168]{1,0:T(8,128)(2,1)S(1)} collective-permute-done((bf16[32,7168]{1,0:T(8,128)(2,1)S(1)}, bf16[32,7168]{1,0:T(8,128)(2,1)S(1)}, u32[]{:S(2)}, u32[]{:S(2)}) %collective-permute-start.17) | collective-permute-done | bytes 458784 | tf_op jit(solution)/shard_map/ppermute | solution.py:309
  69.2 6.6 %collective-permute-start.15 = (bf16[128,512]{1,0:T(8,128)(2,1)S(1)}, bf16[128,512]{1,0:T(8,128)(2,1)S(1)}, u32[]{:S(2)}, u32[]{:S(2)}) collective-permute-start(bf16[128,512]{1,0:T(8,128)(2,1)S(1)} %shard_map.124.refs_0_), channel_id=1, source_target_pairs={{0,128},{64,192},{128,0},{192,64},{1,129},{65,193},{129,1},{193,65... | collective-permute-start | bytes 393224 | tf_op jit(solution)/shard_map/ppermute | solution.py:298
  75.8 7.5 %shard_map.126.refs_4_ = bf16[128,512]{1,0:T(8,128)(2,1)S(1)} custom-call(s32[5]{0:T(128)S(1)} %stack.23.place_ref, bf16[32,7168]{1,0:T(8,128)(2,1)S(1)} %get-tuple-element.44.r0, bf16[32,7168]{1,0:T(8,128)(2,1)S(1)} %collective-permute-done.17.r1, bf16[32,7168]{1,0:T(8,128)(2,1)S(1)} %collective-permute-done.18.r2, ...), custom_call_target="tpu_custom_call" | custom-call | flops 1879048192 | bytes 16515072 | tf_op jit(solution)/shard_map/pallas_call | solution.py:176
  83.2 2.1 %collective-permute-start.20 = (bf16[128,512]{1,0:T(8,128)(2,1)S(1)}, bf16[128,512]{1,0:T(8,128)(2,1)S(1)}, u32[]{:S(2)}, u32[]{:S(2)}) collective-permute-start(bf16[128,512]{1,0:T(8,128)(2,1)S(1)} %shard_map.126.refs_4_), channel_id=1, source_target_pairs={{0,64},{64,128},{128,192},{192,0},{1,65},{65,129},{129,193},{193,1... | collective-permute-start | bytes 393224 | tf_op jit(solution)/shard_map/ppermute | solution.py:298
  85.3 1.8 %collective-permute-start.21 = (bf16[128,512]{1,0:T(8,128)(2,1)S(1)}, bf16[128,512]{1,0:T(8,128)(2,1)S(1)}, u32[]{:S(2)}, u32[]{:S(2)}) collective-permute-start(bf16[128,512]{1,0:T(8,128)(2,1)S(1)} %shard_map.126.refs_4_), channel_id=1, source_target_pairs={{0,128},{64,192},{128,0},{192,64},{1,129},{65,193},{129,1},{193,65... | collective-permute-start | bytes 393224 | tf_op jit(solution)/shard_map/ppermute | solution.py:298
  87.6 2.4 %collective-permute-done.20.refs_5_ = bf16[128,512]{1,0:T(8,128)(2,1)S(1)} collective-permute-done((bf16[128,512]{1,0:T(8,128)(2,1)S(1)}, bf16[128,512]{1,0:T(8,128)(2,1)S(1)}, u32[]{:S(2)}, u32[]{:S(2)}) %collective-permute-start.20) | collective-permute-done | bytes 131104 | tf_op jit(solution)/shard_map/ppermute | solution.py:298
  90.0 2.8 %collective-permute-done.21.refs_6_ = bf16[128,512]{1,0:T(8,128)(2,1)S(1)} collective-permute-done((bf16[128,512]{1,0:T(8,128)(2,1)S(1)}, bf16[128,512]{1,0:T(8,128)(2,1)S(1)}, u32[]{:S(2)}, u32[]{:S(2)}) %collective-permute-start.21) | collective-permute-done | bytes 131104 | tf_op jit(solution)/shard_map/ppermute | solution.py:298
  94.6 6.3 %shard_map.127 = bf16[256,1792]{1,0:T(8,128)(2,1)} custom-call(s32[5]{0:T(128)S(1)} %stack.23.place_ref, bf16[128,512]{1,0:T(8,128)(2,1)S(1)} %shard_map.124.refs_0_, bf16[128,512]{1,0:T(8,128)(2,1)S(1)} %collective-permute-done.14.refs_1_, bf16[128,512]{1,0:T(8,128)(2,1)S(1)} %collective-permute-done.15.refs_2_, ...), custom_call_target="tpu_custom_call" | custom-call | flops 1879048192 | bytes 8388608 | tf_op jit(solution)/shard_map/pallas_call | solution.py:225
  101.0 4.6 %all-to-all-start = ((bf16[16,16,1792]{2,1,0:T(8,128)(2,1)}), bf16[16,16,1792]{2,1,0:T(8,128)(2,1)S(1)}, u32[]{:S(2)}, u32[]{:S(2)}) async-start(bf16[16,16,1792]{2,1,0:T(8,128)(2,1)} %bitcast.54), calls=%async_computation | async-start | bytes 1835008 | tf_op jit(solution)/shard_map/all_to_all | solution.py:341
  105.7 2.4 %collective-permute-start.25 = (bf16[32,640]{1,0:T(8,128)(2,1)S(1)}, bf16[32,640]{1,0:T(8,128)(2,1)S(1)}, u32[]{:S(2)}, u32[]{:S(2)}) collective-permute-start(bf16[32,640]{1,0:T(8,128)(2,1)S(1)} %get-tuple-element.56), channel_id=1, source_target_pairs={{0,128},{64,192},{128,0},{192,64},{1,129},{65,193},{129,1},{193,65... | collective-permute-start | bytes 122888 | tf_op jit(solution)/shard_map/ppermute | solution.py:298
  110.7 1.4 %collective-permute-done.26 = bf16[32,640]{1,0:T(8,128)(2,1)S(1)} collective-permute-done((bf16[32,640]{1,0:T(8,128)(2,1)S(1)}, bf16[32,640]{1,0:T(8,128)(2,1)S(1)}, u32[]{:S(2)}, u32[]{:S(2)}) %collective-permute-start.26) | collective-permute-done | bytes 40992 | tf_op jit(solution)/shard_map/ppermute | solution.py:298
  112.3 5.4 %all-to-all-done = bf16[16,16,1792]{2,1,0:T(8,128)(2,1)S(1)} async-done(((bf16[16,16,1792]{2,1,0:T(8,128)(2,1)}), bf16[16,16,1792]{2,1,0:T(8,128)(2,1)S(1)}, u32[]{:S(2)}, u32[]{:S(2)}) %all-to-all-start) | async-done | bytes 917536 | tf_op jit(solution)/shard_map/all_to_all | solution.py:341
  117.7 1.9 %shard_map.128 = bf16[8,4,1792]{2,1,0:T(4,128)(2,1)} custom-call(s32[5]{0:T(128)S(1)} %stack.23.place_ref, bf16[256,1792]{1,0:T(8,128)(2,1)S(1)} %bitcast.50, bf16[16,128]{1,0:T(8,128)(2,1)S(1)} %slice.28.facts0, bf16[16,128]{1,0:T(8,128)(2,1)S(1)} %slice.29.facts1), custom_call_target="tpu_custom_call" | custom-call | flops 88080384 | bytes 1048576 | tf_op jit(solution)/shard_map/pallas_call | solution.py:265
  119.6 9.6 %all-to-all-start.1 = ((bf16[8,4,1792]{2,1,0:T(4,128)(2,1)}), bf16[8,4,1792]{2,1,0:T(4,128)(2,1)S(1)}, u32[]{:S(2)}, u32[]{:S(2)}) async-start(bf16[8,4,1792]{2,1,0:T(4,128)(2,1)} %shard_map.128), calls=%async_computation.1 | async-start | bytes 229376 | tf_op jit(solution)/shard_map/all_to_all | solution.py:350
  130.0 6.6 %all-to-all-done.1 = bf16[8,4,1792]{2,1,0:T(4,128)(2,1)S(1)} async-done(((bf16[8,4,1792]{2,1,0:T(4,128)(2,1)}), bf16[8,4,1792]{2,1,0:T(4,128)(2,1)S(1)}, u32[]{:S(2)}, u32[]{:S(2)}) %all-to-all-start.1) | async-done | bytes 114720 | tf_op jit(solution)/shard_map/all_to_all | solution.py:350
  (56 shorter events, 17.5 us)
Async XLA Ops:
  0.6 8.9 %copy-start = (bf16[1,1024,512]{2,1,0:T(8,128)(2,1)S(1)}, bf16[1,1024,512]{2,1,0:T(8,128)(2,1)}, u32[]{:S(2)}) copy-start(bf16[1,1024,512]{2,1,0:T(8,128)(2,1)} %param.13) | copy-start | bytes 3145732
  2.4 48.1 %collective-permute-start.10 = (bf16[2,7168,256]{2,1,0:T(8,128)(2,1)}, bf16[2,7168,256]{2,1,0:T(8,128)(2,1)}, u32[]{:S(2)}, u32[]{:S(2)}) collective-permute-start(bf16[2,7168,256]{2,1,0:T(8,128)(2,1)} %bitcast.51), channel_id=1, source_target_pairs={{0,32},{32,0},{1,33},{33,1},{2,34},{34,2},{3,35},{35,3},{4,36},{36... | collective-permute-start | bytes 22020104 | tf_op jit(solution)/shard_map/ppermute | solution.py:323
  2.4 9.3 %collective-permute-start = (bf16[4,7296]{1,0:T(4,128)(2,1)}, bf16[4,7296]{1,0:T(4,128)(2,1)S(1)}, u32[]{:S(2)}, u32[]{:S(2)}) collective-permute-start(bf16[4,7296]{1,0:T(4,128)(2,1)} %shard_map.122), channel_id=1, source_target_pairs={{0,64},{64,128},{128,192},{192,0},{1,65},{65,129},{129,193},{193,1... | collective-permute-start | bytes 175112 | tf_op jit(solution)/shard_map/ppermute | solution.py:298
  4.3 7.4 %collective-permute-start.1 = (bf16[4,7296]{1,0:T(4,128)(2,1)}, bf16[4,7296]{1,0:T(4,128)(2,1)S(1)}, u32[]{:S(2)}, u32[]{:S(2)}) collective-permute-start(bf16[4,7296]{1,0:T(4,128)(2,1)} %shard_map.122), channel_id=1, source_target_pairs={{0,128},{64,192},{128,0},{192,64},{1,129},{65,193},{129,1},{193,65... | collective-permute-start | bytes 175112 | tf_op jit(solution)/shard_map/ppermute | solution.py:298
  6.6 6.0 %collective-permute-start.2 = (bf16[4,7296]{1,0:T(4,128)(2,1)}, bf16[4,7296]{1,0:T(4,128)(2,1)S(1)}, u32[]{:S(2)}, u32[]{:S(2)}) collective-permute-start(bf16[4,7296]{1,0:T(4,128)(2,1)} %shard_map.122), channel_id=1, source_target_pairs={{0,192},{64,0},{128,64},{192,128},{1,193},{65,1},{129,65},{193,129... | collective-permute-start | bytes 175112 | tf_op jit(solution)/shard_map/ppermute | solution.py:298
  7.7 77.7 %collective-permute-start.23 = (bf16[4,2,256,896]{3,2,1,0:T(8,128)(2,1)}, bf16[4,2,256,896]{3,2,1,0:T(8,128)(2,1)}, u32[]{:S(2)}, u32[]{:S(2)}) collective-permute-start(bf16[4,2,256,896]{3,2,1,0:T(8,128)(2,1)} %bitcast.55), channel_id=1, source_target_pairs={{0,32},{32,0},{1,33},{33,1},{2,34},{34,2},{3,35},{35,3},{4,36},{36... | collective-permute-start | bytes 11010056 | tf_op jit(solution)/shard_map/ppermute | solution.py:324
  13.5 7.4 %collective-permute-start.3 = (bf16[16,7296]{1,0:T(8,128)(2,1)S(1)}, bf16[16,7296]{1,0:T(8,128)(2,1)S(1)}, u32[]{:S(2)}, u32[]{:S(2)}) collective-permute-start(bf16[16,7296]{1,0:T(8,128)(2,1)S(1)} %pad_maximum_fusion.t0), channel_id=1, source_target_pairs={{0,1},{1,2},{2,3},{3,0},{4,5},{5,6},{6,7},{7,4},{8,9},{9,10},{10,1... | collective-permute-start | bytes 700424 | tf_op jit(solution)/shard_map/ppermute | solution.py:309
  14.8 11.7 %collective-permute-start.4 = (bf16[16,7296]{1,0:T(8,128)(2,1)S(1)}, bf16[16,7296]{1,0:T(8,128)(2,1)S(1)}, u32[]{:S(2)}, u32[]{:S(2)}) collective-permute-start(bf16[16,7296]{1,0:T(8,128)(2,1)S(1)} %pad_maximum_fusion.t0), channel_id=1, source_target_pairs={{0,2},{1,3},{2,0},{3,1},{4,6},{5,7},{6,4},{7,5},{8,10},{9,11},{10,... | collective-permute-start | bytes 700424 | tf_op jit(solution)/shard_map/ppermute | solution.py:309
  17.8 8.8 %collective-permute-start.5 = (bf16[16,7296]{1,0:T(8,128)(2,1)S(1)}, bf16[16,7296]{1,0:T(8,128)(2,1)S(1)}, u32[]{:S(2)}, u32[]{:S(2)}) collective-permute-start(bf16[16,7296]{1,0:T(8,128)(2,1)S(1)} %pad_maximum_fusion.t0), channel_id=1, source_target_pairs={{0,3},{1,0},{2,1},{3,2},{4,7},{5,4},{6,5},{7,6},{8,11},{9,8},{10,9... | collective-permute-start | bytes 700424 | tf_op jit(solution)/shard_map/ppermute | solution.py:309
  20.9 15.6 %collective-permute-start.6 = (bf16[16,7296]{1,0:T(8,128)(2,1)S(1)}, bf16[16,7296]{1,0:T(8,128)(2,1)S(1)}, u32[]{:S(2)}, u32[]{:S(2)}) collective-permute-start(bf16[16,7296]{1,0:T(8,128)(2,1)S(1)} %pad_maximum_fusion.t0), channel_id=1, source_target_pairs={{0,16},{16,0},{1,17},{17,1},{2,18},{18,2},{3,19},{19,3},{4,20},{20... | collective-permute-start | bytes 700424 | tf_op jit(solution)/shard_map/ppermute | solution.py:330
  28.0 10.0 %collective-permute-start.7 = (bf16[32,7168]{1,0:T(8,128)(2,1)S(1)}, bf16[32,7168]{1,0:T(8,128)(2,1)S(1)}, u32[]{:S(2)}, u32[]{:S(2)}) collective-permute-start(bf16[32,7168]{1,0:T(8,128)(2,1)S(1)} %get-tuple-element.33), channel_id=1, source_target_pairs={{0,4},{1,5},{2,6},{3,7},{4,8},{5,9},{6,10},{7,11},{8,12},{9,13},{1... | collective-permute-start | bytes 1376264 | tf_op jit(solution)/shard_map/ppermute | solution.py:309
  29.6 15.9 %collective-permute-start.8 = (bf16[32,7168]{1,0:T(8,128)(2,1)S(1)}, bf16[32,7168]{1,0:T(8,128)(2,1)S(1)}, u32[]{:S(2)}, u32[]{:S(2)}) collective-permute-start(bf16[32,7168]{1,0:T(8,128)(2,1)S(1)} %get-tuple-element.35), channel_id=1, source_target_pairs={{0,8},{1,9},{2,10},{3,11},{4,12},{5,13},{6,14},{7,15},{8,0},{9,1},... | collective-permute-start | bytes 1376264 | tf_op jit(solution)/shard_map/ppermute | solution.py:309
  36.5 9.2 %collective-permute-start.9 = (bf16[32,7168]{1,0:T(8,128)(2,1)S(1)}, bf16[32,7168]{1,0:T(8,128)(2,1)S(1)}, u32[]{:S(2)}, u32[]{:S(2)}) collective-permute-start(bf16[32,7168]{1,0:T(8,128)(2,1)S(1)} %get-tuple-element.36), channel_id=1, source_target_pairs={{0,12},{1,13},{2,14},{3,15},{4,0},{5,1},{6,2},{7,3},{8,4},{9,5},{1... | collective-permute-start | bytes 1376264 | tf_op jit(solution)/shard_map/ppermute | solution.py:309
  38.0 20.0 %collective-permute-start.11 = (bf16[16,7296]{1,0:T(8,128)(2,1)S(1)}, bf16[16,7296]{1,0:T(8,128)(2,1)S(1)}, u32[]{:S(2)}, u32[]{:S(2)}) collective-permute-start(bf16[16,7296]{1,0:T(8,128)(2,1)S(1)} %collective-permute-done.6.t0), channel_id=1, source_target_pairs={{0,1},{1,2},{2,3},{3,0},{4,5},{5,6},{6,7},{7,4},{8,9},{9,10},{10,1... | collective-permute-start | bytes 700424 | tf_op jit(solution)/shard_map/ppermute | solution.py:309
  45.5 12.5 %collective-permute-start.12 = (bf16[16,7296]{1,0:T(8,128)(2,1)S(1)}, bf16[16,7296]{1,0:T(8,128)(2,1)S(1)}, u32[]{:S(2)}, u32[]{:S(2)}) collective-permute-start(bf16[16,7296]{1,0:T(8,128)(2,1)S(1)} %collective-permute-done.6.t0), channel_id=1, source_target_pairs={{0,2},{1,3},{2,0},{3,1},{4,6},{5,7},{6,4},{7,5},{8,10},{9,11},{10,... | collective-permute-start | bytes 700424 | tf_op jit(solution)/shard_map/ppermute | solution.py:309
  45.7 12.3 %collective-permute-start.13 = (bf16[16,7296]{1,0:T(8,128)(2,1)S(1)}, bf16[16,7296]{1,0:T(8,128)(2,1)S(1)}, u32[]{:S(2)}, u32[]{:S(2)}) collective-permute-start(bf16[16,7296]{1,0:T(8,128)(2,1)S(1)} %collective-permute-done.6.t0), channel_id=1, source_target_pairs={{0,3},{1,0},{2,1},{3,2},{4,7},{5,4},{6,5},{7,6},{8,11},{9,8},{10,9... | collective-permute-start | bytes 700424 | tf_op jit(solution)/shard_map/ppermute | solution.py:309
  59.4 9.8 %collective-permute-start.17 = (bf16[32,7168]{1,0:T(8,128)(2,1)S(1)}, bf16[32,7168]{1,0:T(8,128)(2,1)S(1)}, u32[]{:S(2)}, u32[]{:S(2)}) collective-permute-start(bf16[32,7168]{1,0:T(8,128)(2,1)S(1)} %get-tuple-element.45), channel_id=1, source_target_pairs={{0,4},{1,5},{2,6},{3,7},{4,8},{5,9},{6,10},{7,11},{8,12},{9,13},{1... | collective-permute-start | bytes 1376264 | tf_op jit(solution)/shard_map/ppermute | solution.py:309
  60.5 15.2 %collective-permute-start.18 = (bf16[32,7168]{1,0:T(8,128)(2,1)S(1)}, bf16[32,7168]{1,0:T(8,128)(2,1)S(1)}, u32[]{:S(2)}, u32[]{:S(2)}) collective-permute-start(bf16[32,7168]{1,0:T(8,128)(2,1)S(1)} %get-tuple-element.46), channel_id=1, source_target_pairs={{0,8},{1,9},{2,10},{3,11},{4,12},{5,13},{6,14},{7,15},{8,0},{9,1},... | collective-permute-start | bytes 1376264 | tf_op jit(solution)/shard_map/ppermute | solution.py:309
  63.7 12.0 %collective-permute-start.19 = (bf16[32,7168]{1,0:T(8,128)(2,1)S(1)}, bf16[32,7168]{1,0:T(8,128)(2,1)S(1)}, u32[]{:S(2)}, u32[]{:S(2)}) collective-permute-start(bf16[32,7168]{1,0:T(8,128)(2,1)S(1)} %get-tuple-element.47), channel_id=1, source_target_pairs={{0,12},{1,13},{2,14},{3,15},{4,0},{5,1},{6,2},{7,3},{8,4},{9,5},{1... | collective-permute-start | bytes 1376264 | tf_op jit(solution)/shard_map/ppermute | solution.py:309
  64.0 23.2 %collective-permute-start.14 = (bf16[128,512]{1,0:T(8,128)(2,1)S(1)}, bf16[128,512]{1,0:T(8,128)(2,1)S(1)}, u32[]{:S(2)}, u32[]{:S(2)}) collective-permute-start(bf16[128,512]{1,0:T(8,128)(2,1)S(1)} %shard_map.124.refs_0_), channel_id=1, source_target_pairs={{0,64},{64,128},{128,192},{192,0},{1,65},{65,129},{129,193},{193,1... | collective-permute-start | bytes 393224 | tf_op jit(solution)/shard_map/ppermute | solution.py:298
  69.2 18.4 %collective-permute-start.15 = (bf16[128,512]{1,0:T(8,128)(2,1)S(1)}, bf16[128,512]{1,0:T(8,128)(2,1)S(1)}, u32[]{:S(2)}, u32[]{:S(2)}) collective-permute-start(bf16[128,512]{1,0:T(8,128)(2,1)S(1)} %shard_map.124.refs_0_), channel_id=1, source_target_pairs={{0,128},{64,192},{128,0},{192,64},{1,129},{65,193},{129,1},{193,65... | collective-permute-start | bytes 393224 | tf_op jit(solution)/shard_map/ppermute | solution.py:298
  75.8 11.8 %collective-permute-start.16 = (bf16[128,512]{1,0:T(8,128)(2,1)S(1)}, bf16[128,512]{1,0:T(8,128)(2,1)S(1)}, u32[]{:S(2)}, u32[]{:S(2)}) collective-permute-start(bf16[128,512]{1,0:T(8,128)(2,1)S(1)} %shard_map.124.refs_0_), channel_id=1, source_target_pairs={{0,192},{64,0},{128,64},{192,128},{1,193},{65,1},{129,65},{193,129... | collective-permute-start | bytes 393224 | tf_op jit(solution)/shard_map/ppermute | solution.py:298
  83.2 6.7 %collective-permute-start.20 = (bf16[128,512]{1,0:T(8,128)(2,1)S(1)}, bf16[128,512]{1,0:T(8,128)(2,1)S(1)}, u32[]{:S(2)}, u32[]{:S(2)}) collective-permute-start(bf16[128,512]{1,0:T(8,128)(2,1)S(1)} %shard_map.126.refs_4_), channel_id=1, source_target_pairs={{0,64},{64,128},{128,192},{192,0},{1,65},{65,129},{129,193},{193,1... | collective-permute-start | bytes 393224 | tf_op jit(solution)/shard_map/ppermute | solution.py:298
  85.3 7.4 %collective-permute-start.21 = (bf16[128,512]{1,0:T(8,128)(2,1)S(1)}, bf16[128,512]{1,0:T(8,128)(2,1)S(1)}, u32[]{:S(2)}, u32[]{:S(2)}) collective-permute-start(bf16[128,512]{1,0:T(8,128)(2,1)S(1)} %shard_map.126.refs_4_), channel_id=1, source_target_pairs={{0,128},{64,192},{128,0},{192,64},{1,129},{65,193},{129,1},{193,65... | collective-permute-start | bytes 393224 | tf_op jit(solution)/shard_map/ppermute | solution.py:298
  87.1 6.8 %collective-permute-start.22 = (bf16[128,512]{1,0:T(8,128)(2,1)S(1)}, bf16[128,512]{1,0:T(8,128)(2,1)S(1)}, u32[]{:S(2)}, u32[]{:S(2)}) collective-permute-start(bf16[128,512]{1,0:T(8,128)(2,1)S(1)} %shard_map.126.refs_4_), channel_id=1, source_target_pairs={{0,192},{64,0},{128,64},{192,128},{1,193},{65,1},{129,65},{193,129... | collective-permute-start | bytes 393224 | tf_op jit(solution)/shard_map/ppermute | solution.py:298
  94.0 0.7 copy-start.1
  101.0 16.8 %all-to-all-start = ((bf16[16,16,1792]{2,1,0:T(8,128)(2,1)}), bf16[16,16,1792]{2,1,0:T(8,128)(2,1)S(1)}, u32[]{:S(2)}, u32[]{:S(2)}) async-start(bf16[16,16,1792]{2,1,0:T(8,128)(2,1)} %bitcast.54), calls=%async_computation | async-start | bytes 1835008 | tf_op jit(solution)/shard_map/all_to_all | solution.py:341
  105.6 4.1 %collective-permute-start.24 = (bf16[32,640]{1,0:T(8,128)(2,1)S(1)}, bf16[32,640]{1,0:T(8,128)(2,1)S(1)}, u32[]{:S(2)}, u32[]{:S(2)}) collective-permute-start(bf16[32,640]{1,0:T(8,128)(2,1)S(1)} %get-tuple-element.54), channel_id=1, source_target_pairs={{0,64},{64,128},{128,192},{192,0},{1,65},{65,129},{129,193},{193,1... | collective-permute-start | bytes 122888 | tf_op jit(solution)/shard_map/ppermute | solution.py:298
  105.7 5.0 %collective-permute-start.25 = (bf16[32,640]{1,0:T(8,128)(2,1)S(1)}, bf16[32,640]{1,0:T(8,128)(2,1)S(1)}, u32[]{:S(2)}, u32[]{:S(2)}) collective-permute-start(bf16[32,640]{1,0:T(8,128)(2,1)S(1)} %get-tuple-element.56), channel_id=1, source_target_pairs={{0,128},{64,192},{128,0},{192,64},{1,129},{65,193},{129,1},{193,65... | collective-permute-start | bytes 122888 | tf_op jit(solution)/shard_map/ppermute | solution.py:298
  108.1 4.0 %collective-permute-start.26 = (bf16[32,640]{1,0:T(8,128)(2,1)S(1)}, bf16[32,640]{1,0:T(8,128)(2,1)S(1)}, u32[]{:S(2)}, u32[]{:S(2)}) collective-permute-start(bf16[32,640]{1,0:T(8,128)(2,1)S(1)} %get-tuple-element.55), channel_id=1, source_target_pairs={{0,192},{64,0},{128,64},{192,128},{1,193},{65,1},{129,65},{193,129... | collective-permute-start | bytes 122888 | tf_op jit(solution)/shard_map/ppermute | solution.py:298
  119.6 16.9 %all-to-all-start.1 = ((bf16[8,4,1792]{2,1,0:T(4,128)(2,1)}), bf16[8,4,1792]{2,1,0:T(4,128)(2,1)S(1)}, u32[]{:S(2)}, u32[]{:S(2)}) async-start(bf16[8,4,1792]{2,1,0:T(4,128)(2,1)} %shard_map.128), calls=%async_computation.1 | async-start | bytes 229376 | tf_op jit(solution)/shard_map/all_to_all | solution.py:350

commit v8 on v7

--- a/solution.py
+++ b/solution.py
@@ -239,7 +239,7 @@
     )(place, *pieces, own, other)
 
 
-def mix_kernel(place_ref, back, facts0, facts1, out_ref):
+def weigh_kernel(place_ref, facts0, facts1, out_ref):
     ctx, half = place_ref[0], place_ref[2]
     lane = grid(128, 256, 1)
     spread = grid(128, 256, 0) == half * 32 + lane // 16 * SLOTS + lane % SLOTS
@@ -254,22 +254,36 @@
     )
     fits = (at // 8 == lane_ctx) & (at // 4 % 2 == jnp.where(chunk == 0, half, 1 - half))
     fits = fits & ((at % TOK).astype(f32) == token)
-    total = jnp.zeros((32, 1792), f32)
-    for part in (high, middle, low):
-        matrix = jnp.where(fits, part, 0.0).astype(bf16)
-        total += jnp.dot(matrix, back[...], preferred_element_type=f32)
+    for i, part in enumerate((high, middle, low)):
+        out_ref[32 * i : 32 * (i + 1)] = jnp.where(fits, part, 0.0).astype(bf16)
+
+
+def weigh(place, facts0, facts1):
+    return pl.pallas_call(
+        weigh_kernel,
+        out_shape=jax.ShapeDtypeStruct((96, 256), bf16),
+        in_specs=[SMEM] + [VMEM] * 2,
+        out_specs=VMEM,
+        compiler_params=room(6),
+        cost_estimate=pl.CostEstimate(flops=1 << 22, bytes_accessed=1 << 17, transcendentals=0),
+    )(place, facts0, facts1)
+
+
+def mix_kernel(gates, back, out_ref):
+    parts = jnp.dot(gates[...], back[...], preferred_element_type=f32)
+    total = parts[:32] + parts[32:64] + parts[64:]
     out_ref[...] = total.reshape(8, TOK, 1792).astype(bf16)
 
 
-def mix(place, back, facts0, facts1):
+def mix(gates, back):
     return pl.pallas_call(
         mix_kernel,
         out_shape=jax.ShapeDtypeStruct((8, TOK, 1792), bf16),
-        in_specs=[SMEM] + [VMEM] * 3,
+        in_specs=[VMEM] * 2,
         out_specs=VMEM,
         compiler_params=room(6),
-        cost_estimate=pl.CostEstimate(flops=2 * 32 * 256 * 1792 * 3, bytes_accessed=1 << 20, transcendentals=0),
-    )(place, back, facts0, facts1)
+        cost_estimate=pl.CostEstimate(flops=2 * 96 * 256 * 1792, bytes_accessed=1 << 20, transcendentals=0),
+    )(gates, back)
 
 
 def shards(
@@ -339,14 +353,15 @@
     pieces1 = hidden_of(got1)
     result = down(place, pieces0 + pieces1, weight_out, other_out)
     back = lax.all_to_all(result.reshape(16, 16, 1792), ("x", "y"), split_axis=0, concat_axis=0, tiled=True)
-    part, _ = lax.optimization_barrier((part, result))
+    part, facts0, facts1, _ = lax.optimization_barrier((part, facts0, facts1, result))
+    gates = weigh(place, facts0, facts1)
     parts = [lax.dynamic_index_in_dim(part, c, 0, keepdims=False)]
     for k in (1, 2, 3):
         sent = lax.dynamic_index_in_dim(part, (c + k) % 4, 0, keepdims=False)
         parts.append(hop(sent, k))
     attended = finish_attention(parts)
 
-    outgoing = mix(place, back.reshape(256, 1792), facts0, facts1)
+    outgoing = mix(gates, back.reshape(256, 1792))
     final = lax.all_to_all(outgoing, ("ctx", "zhi"), split_axis=0, concat_axis=0, tiled=True)
     final = final.reshape(4, 2, TOK, 1792).astype(f32)
     routed = (final[:, 0] + final[:, 1]).transpose(1, 0, 2).reshape(TOK, 4 * 1792)

time: 138 us -> 137 us (level)
  transfers between devices with their start and end apart: 29 -> 29, of which waited for: 13 -> 12; matrix products, arithmetic and copies ran while one was open for 4% -> 4% of each run, Pallas kernels for 13% -> 14%
where the time goes in v8:
time: 137 us; the launch traced here: 136 us
  starting transfers between devices  62.5 us (46%)
  waiting for transfers between devices  38.1 us (28%)
  Pallas kernels  27.4 us (20%)
  matrix products  2.97 us (2%)
  other arithmetic  2.63 us (2%)
  between operations  1.55 us (1%)
    ppermute x12, starting transfers between devices, along(): return lax.ppermute(value, ('att', 'x', 'y'), pairs)  22.6 us
    ppermute x12, starting transfers between devices, hop(): return lax.ppermute(value, 'ctx', [(i, (i + k) % 4) for i in range(4)])  20.1 us
    pallas_call x2, Pallas kernels, gate_up(): pl.pallas_call(gate_up_kernel, out_shape=jax.ShapeDtypeStruct((128, 512),...  14.9 us
    ppermute x12, waiting for transfers between devices, along(): return lax.ppermute(value, ('att', 'x', 'y'), pairs)  12.3 us
    all_to_all x1, starting transfers between devices, shards(): lax.all_to_all(outgoing, ('ctx', 'zhi'), split_axis=0, concat_axis=0, til...  9.62 us
    ppermute x12, waiting for transfers between devices, hop(): return lax.ppermute(value, 'ctx', [(i, (i + k) % 4) for i in range(4)])  9.58 us
    all_to_all x1, waiting for transfers between devices, shards(): lax.all_to_all(outgoing, ('ctx', 'zhi'), split_axis=0, concat_axis=0, til...  6.6 us
    pallas_call x1, Pallas kernels, down(): pl.pallas_call(down_kernel, out_shape=jax.ShapeDtypeStruct((256, 1792), b...  6.26 us
  transfers between devices with their start and end apart: 29, of which 12 were waited for; matrix products, arithmetic and copies ran while one was open for 4% of the time, Pallas kernels for 14%

profile of v8, /device:TPU:32, one launch (start us, length us, event | category | flops | bytes accessed | tf_op | source)
XLA Modules:
  0.0 136.2 jit_solution(209721098732392717)
XLA Ops:
  0.6 1.7 %shard_map.122 = bf16[4,7296]{1,0:T(4,128)(2,1)} custom-call(s32[4,8]{1,0:T(4,128)} %ids_ref.1, f32[4,8]{1,0:T(4,128)} %gates_ref.1, bf16[4,7168]{1,0:T(4,128)(2,1)} %rows_ref.1, bf16[7168]{0:T(1024)(128)(2,1)} %gain_ref.1), custom_call_target="tpu_custom_call" | custom-call | tf_op jit(solution)/shard_map/pallas_call | solution.py:80
  2.4 1.9 %collective-permute-start = (bf16[4,7296]{1,0:T(4,128)(2,1)}, bf16[4,7296]{1,0:T(4,128)(2,1)S(1)}, u32[]{:S(2)}, u32[]{:S(2)}) collective-permute-start(bf16[4,7296]{1,0:T(4,128)(2,1)} %shard_map.122), channel_id=1, source_target_pairs={{0,64},{64,128},{128,192},{192,0},{1,65},{65,129},{129,193},{193,1... | collective-permute-start | bytes 175112 | tf_op jit(solution)/shard_map/ppermute | solution.py:312
  4.3 2.3 %collective-permute-start.1 = (bf16[4,7296]{1,0:T(4,128)(2,1)}, bf16[4,7296]{1,0:T(4,128)(2,1)S(1)}, u32[]{:S(2)}, u32[]{:S(2)}) collective-permute-start(bf16[4,7296]{1,0:T(4,128)(2,1)} %shard_map.122), channel_id=1, source_target_pairs={{0,128},{64,192},{128,0},{192,64},{1,129},{65,193},{129,1},{193,65... | collective-permute-start | bytes 175112 | tf_op jit(solution)/shard_map/ppermute | solution.py:312
  9.5 1.5 %fusion.16 = (bf16[128,1024]{1,0:T(8,128)(2,1)S(1)}, f32[128]{0:T(128)S(1)}) fusion(f32[128,1024]{1,0:T(8,128)S(1)} %fusion.5, bf16[1,1024,512]{2,1,0:T(8,128)(2,1)S(1)} %copy-done, bf16[1,128,512]{2,1,0:T(8,128)(2,1)} %param.11, pred[1024]{0:T(1024)(128)(4,1)S(1)} %add_compare_fusion), kind=kOutput, calls=%fused_computation.30 | convolution fusion | flops 134872960 | bytes 1967616 | tf_op jit(solution)/shard_map/hr,tr->ht/dot_general | solution.py:20
  14.8 2.9 %collective-permute-start.5 = (bf16[16,7296]{1,0:T(8,128)(2,1)S(1)}, bf16[16,7296]{1,0:T(8,128)(2,1)S(1)}, u32[]{:S(2)}, u32[]{:S(2)}) collective-permute-start(bf16[16,7296]{1,0:T(8,128)(2,1)S(1)} %pad_maximum_fusion.t0), channel_id=1, source_target_pairs={{0,2},{1,3},{2,0},{3,1},{4,6},{5,7},{6,4},{7,5},{8,10},{9,11},{10,... | collective-permute-start | bytes 700424 | tf_op jit(solution)/shard_map/ppermute | solution.py:323
  19.1 1.8 %collective-permute-done.3.t1 = bf16[16,7296]{1,0:T(8,128)(2,1)S(1)} collective-permute-done((bf16[16,7296]{1,0:T(8,128)(2,1)S(1)}, bf16[16,7296]{1,0:T(8,128)(2,1)S(1)}, u32[]{:S(2)}, u32[]{:S(2)}) %collective-permute-start.3) | collective-permute-done | bytes 233504 | tf_op jit(solution)/shard_map/ppermute | solution.py:323
  20.9 5.6 %collective-permute-start.4 = (bf16[16,7296]{1,0:T(8,128)(2,1)S(1)}, bf16[16,7296]{1,0:T(8,128)(2,1)S(1)}, u32[]{:S(2)}, u32[]{:S(2)}) collective-permute-start(bf16[16,7296]{1,0:T(8,128)(2,1)S(1)} %pad_maximum_fusion.t0), channel_id=1, source_target_pairs={{0,16},{16,0},{1,17},{17,1},{2,18},{18,2},{3,19},{19,3},{4,20},{20... | collective-permute-start | bytes 700424 | tf_op jit(solution)/shard_map/ppermute | solution.py:344
  26.6 1.4 %shard_map.123 = (bf16[32,7168]{1,0:T(8,128)(2,1)S(1)}, bf16[32,7168]{1,0:T(8,128)(2,1)S(1)}, bf16[32,7168]{1,0:T(8,128)(2,1)S(1)}, bf16[32,7168]{1,0:T(8,128)(2,1)S(1)}) custom-call(s32[5]{0:T(128)S(1)} %stack.23.place_ref, bf16[16,7296]{1,0:T(8,128)(2,1)S(1)} %pad_maximum_fusion.t0, bf16[16,7296]{1,0:T(8,128)(2,1)S(1)} %collective-permute-done.3.t1, ...), custom_call_target="tpu_custom_call" | custom-call | flops 117440512 | bytes 2752512 | tf_op jit(solution)/shard_map/pallas_call | solution.py:120
  28.0 1.6 %collective-permute-start.7 = (bf16[32,7168]{1,0:T(8,128)(2,1)S(1)}, bf16[32,7168]{1,0:T(8,128)(2,1)S(1)}, u32[]{:S(2)}, u32[]{:S(2)}) collective-permute-start(bf16[32,7168]{1,0:T(8,128)(2,1)S(1)} %get-tuple-element.35), channel_id=1, source_target_pairs={{0,4},{1,5},{2,6},{3,7},{4,8},{5,9},{6,10},{7,11},{8,12},{9,13},{1... | collective-permute-start | bytes 1376264 | tf_op jit(solution)/shard_map/ppermute | solution.py:323
  29.6 2.7 %collective-permute-start.8 = (bf16[32,7168]{1,0:T(8,128)(2,1)S(1)}, bf16[32,7168]{1,0:T(8,128)(2,1)S(1)}, u32[]{:S(2)}, u32[]{:S(2)}) collective-permute-start(bf16[32,7168]{1,0:T(8,128)(2,1)S(1)} %get-tuple-element.39), channel_id=1, source_target_pairs={{0,8},{1,9},{2,10},{3,11},{4,12},{5,13},{6,14},{7,15},{8,0},{9,1},... | collective-permute-start | bytes 1376264 | tf_op jit(solution)/shard_map/ppermute | solution.py:323
  32.3 4.2 %collective-permute-done.4.t0 = bf16[16,7296]{1,0:T(8,128)(2,1)S(1)} collective-permute-done((bf16[16,7296]{1,0:T(8,128)(2,1)S(1)}, bf16[16,7296]{1,0:T(8,128)(2,1)S(1)}, u32[]{:S(2)}, u32[]{:S(2)}) %collective-permute-start.4) | collective-permute-done | bytes 233504 | tf_op jit(solution)/shard_map/ppermute | solution.py:344
  36.5 1.5 %collective-permute-start.9 = (bf16[32,7168]{1,0:T(8,128)(2,1)S(1)}, bf16[32,7168]{1,0:T(8,128)(2,1)S(1)}, u32[]{:S(2)}, u32[]{:S(2)}) collective-permute-start(bf16[32,7168]{1,0:T(8,128)(2,1)S(1)} %get-tuple-element.40), channel_id=1, source_target_pairs={{0,12},{1,13},{2,14},{3,15},{4,0},{5,1},{6,2},{7,3},{8,4},{9,5},{1... | collective-permute-start | bytes 1376264 | tf_op jit(solution)/shard_map/ppermute | solution.py:323
  38.0 1.6 %collective-permute-start.11 = (bf16[16,7296]{1,0:T(8,128)(2,1)S(1)}, bf16[16,7296]{1,0:T(8,128)(2,1)S(1)}, u32[]{:S(2)}, u32[]{:S(2)}) collective-permute-start(bf16[16,7296]{1,0:T(8,128)(2,1)S(1)} %collective-permute-done.4.t0), channel_id=1, source_target_pairs={{0,1},{1,2},{2,3},{3,0},{4,5},{5,6},{6,7},{7,4},{8,9},{9,10},{10,1... | collective-permute-start | bytes 700424 | tf_op jit(solution)/shard_map/ppermute | solution.py:323
  39.6 5.8 %collective-permute-done.8.r2 = bf16[32,7168]{1,0:T(8,128)(2,1)S(1)} collective-permute-done((bf16[32,7168]{1,0:T(8,128)(2,1)S(1)}, bf16[32,7168]{1,0:T(8,128)(2,1)S(1)}, u32[]{:S(2)}, u32[]{:S(2)}) %collective-permute-start.8) | collective-permute-done | bytes 458784 | tf_op jit(solution)/shard_map/ppermute | solution.py:323
  45.8 4.7 %collective-permute-start.13 = (bf16[16,7296]{1,0:T(8,128)(2,1)S(1)}, bf16[16,7296]{1,0:T(8,128)(2,1)S(1)}, u32[]{:S(2)}, u32[]{:S(2)}) collective-permute-start(bf16[16,7296]{1,0:T(8,128)(2,1)S(1)} %collective-permute-done.4.t0), channel_id=1, source_target_pairs={{0,3},{1,0},{2,1},{3,2},{4,7},{5,4},{6,5},{7,6},{8,11},{9,8},{10,9... | collective-permute-start | bytes 700424 | tf_op jit(solution)/shard_map/ppermute | solution.py:323
  50.5 7.5 %shard_map.124.refs_0_ = bf16[128,512]{1,0:T(8,128)(2,1)S(1)} custom-call(s32[5]{0:T(128)S(1)} %stack.23.place_ref, bf16[32,7168]{1,0:T(8,128)(2,1)S(1)} %get-tuple-element.37.r0, bf16[32,7168]{1,0:T(8,128)(2,1)S(1)} %collective-permute-done.7.r1, bf16[32,7168]{1,0:T(8,128)(2,1)S(1)} %collective-permute-done.8.r2, ...), custom_call_target="tpu_custom_call" | custom-call | flops 1879048192 | bytes 16515072 | tf_op jit(solution)/shard_map/pallas_call | solution.py:176
  58.0 1.4 %shard_map.125 = (bf16[32,7168]{1,0:T(8,128)(2,1)S(1)}, bf16[32,7168]{1,0:T(8,128)(2,1)S(1)}, bf16[32,7168]{1,0:T(8,128)(2,1)S(1)}, bf16[32,7168]{1,0:T(8,128)(2,1)S(1)}) custom-call(s32[5]{0:T(128)S(1)} %stack.23.place_ref, bf16[16,7296]{1,0:T(8,128)(2,1)S(1)} %collective-permute-done.4.t0, bf16[16,7296]{1,0:T(8,128)(2,1)S(1)} %collective-permute-done.11.t1, ...), custom_call_target="tpu_custom_call" | custom-call | flops 117440512 | bytes 2752512 | tf_op jit(solution)/shard_map/pallas_call | solution.py:120
  60.5 3.2 %collective-permute-start.18 = (bf16[32,7168]{1,0:T(8,128)(2,1)S(1)}, bf16[32,7168]{1,0:T(8,128)(2,1)S(1)}, u32[]{:S(2)}, u32[]{:S(2)}) collective-permute-start(bf16[32,7168]{1,0:T(8,128)(2,1)S(1)} %get-tuple-element.50), channel_id=1, source_target_pairs={{0,8},{1,9},{2,10},{3,11},{4,12},{5,13},{6,14},{7,15},{8,0},{9,1},... | collective-permute-start | bytes 1376264 | tf_op jit(solution)/shard_map/ppermute | solution.py:323
  64.5 4.7 %collective-permute-done.17.r1 = bf16[32,7168]{1,0:T(8,128)(2,1)S(1)} collective-permute-done((bf16[32,7168]{1,0:T(8,128)(2,1)S(1)}, bf16[32,7168]{1,0:T(8,128)(2,1)S(1)}, u32[]{:S(2)}, u32[]{:S(2)}) %collective-permute-start.17) | collective-permute-done | bytes 458784 | tf_op jit(solution)/shard_map/ppermute | solution.py:323
  69.2 6.6 %collective-permute-start.15 = (bf16[128,512]{1,0:T(8,128)(2,1)S(1)}, bf16[128,512]{1,0:T(8,128)(2,1)S(1)}, u32[]{:S(2)}, u32[]{:S(2)}) collective-permute-start(bf16[128,512]{1,0:T(8,128)(2,1)S(1)} %shard_map.124.refs_0_), channel_id=1, source_target_pairs={{0,128},{64,192},{128,0},{192,64},{1,129},{65,193},{129,1},{193,65... | collective-permute-start | bytes 393224 | tf_op jit(solution)/shard_map/ppermute | solution.py:312
  75.8 7.5 %shard_map.126.refs_4_ = bf16[128,512]{1,0:T(8,128)(2,1)S(1)} custom-call(s32[5]{0:T(128)S(1)} %stack.23.place_ref, bf16[32,7168]{1,0:T(8,128)(2,1)S(1)} %get-tuple-element.48.r0, bf16[32,7168]{1,0:T(8,128)(2,1)S(1)} %collective-permute-done.17.r1, bf16[32,7168]{1,0:T(8,128)(2,1)S(1)} %collective-permute-done.18.r2, ...), custom_call_target="tpu_custom_call" | custom-call | flops 1879048192 | bytes 16515072 | tf_op jit(solution)/shard_map/pallas_call | solution.py:176
  83.2 2.1 %collective-permute-start.20 = (bf16[128,512]{1,0:T(8,128)(2,1)S(1)}, bf16[128,512]{1,0:T(8,128)(2,1)S(1)}, u32[]{:S(2)}, u32[]{:S(2)}) collective-permute-start(bf16[128,512]{1,0:T(8,128)(2,1)S(1)} %shard_map.126.refs_4_), channel_id=1, source_target_pairs={{0,64},{64,128},{128,192},{192,0},{1,65},{65,129},{129,193},{193,1... | collective-permute-start | bytes 393224 | tf_op jit(solution)/shard_map/ppermute | solution.py:312
  85.3 1.8 %collective-permute-start.21 = (bf16[128,512]{1,0:T(8,128)(2,1)S(1)}, bf16[128,512]{1,0:T(8,128)(2,1)S(1)}, u32[]{:S(2)}, u32[]{:S(2)}) collective-permute-start(bf16[128,512]{1,0:T(8,128)(2,1)S(1)} %shard_map.126.refs_4_), channel_id=1, source_target_pairs={{0,128},{64,192},{128,0},{192,64},{1,129},{65,193},{129,1},{193,65... | collective-permute-start | bytes 393224 | tf_op jit(solution)/shard_map/ppermute | solution.py:312
  87.6 2.4 %collective-permute-done.20.refs_5_ = bf16[128,512]{1,0:T(8,128)(2,1)S(1)} collective-permute-done((bf16[128,512]{1,0:T(8,128)(2,1)S(1)}, bf16[128,512]{1,0:T(8,128)(2,1)S(1)}, u32[]{:S(2)}, u32[]{:S(2)}) %collective-permute-start.20) | collective-permute-done | bytes 131104 | tf_op jit(solution)/shard_map/ppermute | solution.py:312
  90.0 2.8 %collective-permute-done.21.refs_6_ = bf16[128,512]{1,0:T(8,128)(2,1)S(1)} collective-permute-done((bf16[128,512]{1,0:T(8,128)(2,1)S(1)}, bf16[128,512]{1,0:T(8,128)(2,1)S(1)}, u32[]{:S(2)}, u32[]{:S(2)}) %collective-permute-start.21) | collective-permute-done | bytes 131104 | tf_op jit(solution)/shard_map/ppermute | solution.py:312
  94.6 6.3 %shard_map.127 = bf16[256,1792]{1,0:T(8,128)(2,1)} custom-call(s32[5]{0:T(128)S(1)} %stack.23.place_ref, bf16[128,512]{1,0:T(8,128)(2,1)S(1)} %shard_map.124.refs_0_, bf16[128,512]{1,0:T(8,128)(2,1)S(1)} %collective-permute-done.14.refs_1_, bf16[128,512]{1,0:T(8,128)(2,1)S(1)} %collective-permute-done.15.refs_2_, ...), custom_call_target="tpu_custom_call" | custom-call | flops 1879048192 | bytes 8388608 | tf_op jit(solution)/shard_map/pallas_call | solution.py:225
  100.9 4.6 %all-to-all-start = ((bf16[16,16,1792]{2,1,0:T(8,128)(2,1)}), bf16[16,16,1792]{2,1,0:T(8,128)(2,1)S(1)}, u32[]{:S(2)}, u32[]{:S(2)}) async-start(bf16[16,16,1792]{2,1,0:T(8,128)(2,1)} %bitcast.54), calls=%async_computation | async-start | bytes 1835008 | tf_op jit(solution)/shard_map/all_to_all | solution.py:355
  105.6 2.4 %collective-permute-start.25 = (bf16[32,640]{1,0:T(8,128)(2,1)S(1)}, bf16[32,640]{1,0:T(8,128)(2,1)S(1)}, u32[]{:S(2)}, u32[]{:S(2)}) collective-permute-start(bf16[32,640]{1,0:T(8,128)(2,1)S(1)} %get-tuple-element.60), channel_id=1, source_target_pairs={{0,128},{64,192},{128,0},{192,64},{1,129},{65,193},{129,1},{193,65... | collective-permute-start | bytes 122888 | tf_op jit(solution)/shard_map/ppermute | solution.py:312
  110.6 1.4 %collective-permute-done.26 = bf16[32,640]{1,0:T(8,128)(2,1)S(1)} collective-permute-done((bf16[32,640]{1,0:T(8,128)(2,1)S(1)}, bf16[32,640]{1,0:T(8,128)(2,1)S(1)}, u32[]{:S(2)}, u32[]{:S(2)}) %collective-permute-start.26) | collective-permute-done | bytes 40992 | tf_op jit(solution)/shard_map/ppermute | solution.py:312
  112.2 5.4 %all-to-all-done = bf16[16,16,1792]{2,1,0:T(8,128)(2,1)S(1)} async-done(((bf16[16,16,1792]{2,1,0:T(8,128)(2,1)}), bf16[16,16,1792]{2,1,0:T(8,128)(2,1)S(1)}, u32[]{:S(2)}, u32[]{:S(2)}) %all-to-all-start) | async-done | bytes 917536 | tf_op jit(solution)/shard_map/all_to_all | solution.py:355
  118.6 9.6 %all-to-all-start.1 = ((bf16[8,4,1792]{2,1,0:T(4,128)(2,1)}), bf16[8,4,1792]{2,1,0:T(4,128)(2,1)S(1)}, u32[]{:S(2)}, u32[]{:S(2)}) async-start(bf16[8,4,1792]{2,1,0:T(4,128)(2,1)} %shard_map.129), calls=%async_computation.1 | async-start | bytes 229376 | tf_op jit(solution)/shard_map/all_to_all | solution.py:365
  128.9 6.6 %all-to-all-done.1 = bf16[8,4,1792]{2,1,0:T(4,128)(2,1)S(1)} async-done(((bf16[8,4,1792]{2,1,0:T(4,128)(2,1)}), bf16[8,4,1792]{2,1,0:T(4,128)(2,1)S(1)}, u32[]{:S(2)}, u32[]{:S(2)}) %all-to-all-start.1) | async-done | bytes 114720 | tf_op jit(solution)/shard_map/all_to_all | solution.py:365
  (57 shorter events, 17.2 us)
Async XLA Ops:
  0.6 8.9 %copy-start = (bf16[1,1024,512]{2,1,0:T(8,128)(2,1)S(1)}, bf16[1,1024,512]{2,1,0:T(8,128)(2,1)}, u32[]{:S(2)}) copy-start(bf16[1,1024,512]{2,1,0:T(8,128)(2,1)} %param.13) | copy-start | bytes 3145732
  2.4 48.1 %collective-permute-start.10 = (bf16[2,7168,256]{2,1,0:T(8,128)(2,1)}, bf16[2,7168,256]{2,1,0:T(8,128)(2,1)}, u32[]{:S(2)}, u32[]{:S(2)}) collective-permute-start(bf16[2,7168,256]{2,1,0:T(8,128)(2,1)} %bitcast.51), channel_id=1, source_target_pairs={{0,32},{32,0},{1,33},{33,1},{2,34},{34,2},{3,35},{35,3},{4,36},{36... | collective-permute-start | bytes 22020104 | tf_op jit(solution)/shard_map/ppermute | solution.py:337
  2.4 9.3 %collective-permute-start = (bf16[4,7296]{1,0:T(4,128)(2,1)}, bf16[4,7296]{1,0:T(4,128)(2,1)S(1)}, u32[]{:S(2)}, u32[]{:S(2)}) collective-permute-start(bf16[4,7296]{1,0:T(4,128)(2,1)} %shard_map.122), channel_id=1, source_target_pairs={{0,64},{64,128},{128,192},{192,0},{1,65},{65,129},{129,193},{193,1... | collective-permute-start | bytes 175112 | tf_op jit(solution)/shard_map/ppermute | solution.py:312
  4.3 7.4 %collective-permute-start.1 = (bf16[4,7296]{1,0:T(4,128)(2,1)}, bf16[4,7296]{1,0:T(4,128)(2,1)S(1)}, u32[]{:S(2)}, u32[]{:S(2)}) collective-permute-start(bf16[4,7296]{1,0:T(4,128)(2,1)} %shard_map.122), channel_id=1, source_target_pairs={{0,128},{64,192},{128,0},{192,64},{1,129},{65,193},{129,1},{193,65... | collective-permute-start | bytes 175112 | tf_op jit(solution)/shard_map/ppermute | solution.py:312
  6.6 6.0 %collective-permute-start.2 = (bf16[4,7296]{1,0:T(4,128)(2,1)}, bf16[4,7296]{1,0:T(4,128)(2,1)S(1)}, u32[]{:S(2)}, u32[]{:S(2)}) collective-permute-start(bf16[4,7296]{1,0:T(4,128)(2,1)} %shard_map.122), channel_id=1, source_target_pairs={{0,192},{64,0},{128,64},{192,128},{1,193},{65,1},{129,65},{193,129... | collective-permute-start | bytes 175112 | tf_op jit(solution)/shard_map/ppermute | solution.py:312
  7.7 77.6 %collective-permute-start.23 = (bf16[4,2,256,896]{3,2,1,0:T(8,128)(2,1)}, bf16[4,2,256,896]{3,2,1,0:T(8,128)(2,1)}, u32[]{:S(2)}, u32[]{:S(2)}) collective-permute-start(bf16[4,2,256,896]{3,2,1,0:T(8,128)(2,1)} %bitcast.55), channel_id=1, source_target_pairs={{0,32},{32,0},{1,33},{33,1},{2,34},{34,2},{3,35},{35,3},{4,36},{36... | collective-permute-start | bytes 11010056 | tf_op jit(solution)/shard_map/ppermute | solution.py:338
  13.5 7.4 %collective-permute-start.3 = (bf16[16,7296]{1,0:T(8,128)(2,1)S(1)}, bf16[16,7296]{1,0:T(8,128)(2,1)S(1)}, u32[]{:S(2)}, u32[]{:S(2)}) collective-permute-start(bf16[16,7296]{1,0:T(8,128)(2,1)S(1)} %pad_maximum_fusion.t0), channel_id=1, source_target_pairs={{0,1},{1,2},{2,3},{3,0},{4,5},{5,6},{6,7},{7,4},{8,9},{9,10},{10,1... | collective-permute-start | bytes 700424 | tf_op jit(solution)/shard_map/ppermute | solution.py:323
  14.8 11.7 %collective-permute-start.5 = (bf16[16,7296]{1,0:T(8,128)(2,1)S(1)}, bf16[16,7296]{1,0:T(8,128)(2,1)S(1)}, u32[]{:S(2)}, u32[]{:S(2)}) collective-permute-start(bf16[16,7296]{1,0:T(8,128)(2,1)S(1)} %pad_maximum_fusion.t0), channel_id=1, source_target_pairs={{0,2},{1,3},{2,0},{3,1},{4,6},{5,7},{6,4},{7,5},{8,10},{9,11},{10,... | collective-permute-start | bytes 700424 | tf_op jit(solution)/shard_map/ppermute | solution.py:323
  17.7 8.8 %collective-permute-start.6 = (bf16[16,7296]{1,0:T(8,128)(2,1)S(1)}, bf16[16,7296]{1,0:T(8,128)(2,1)S(1)}, u32[]{:S(2)}, u32[]{:S(2)}) collective-permute-start(bf16[16,7296]{1,0:T(8,128)(2,1)S(1)} %pad_maximum_fusion.t0), channel_id=1, source_target_pairs={{0,3},{1,0},{2,1},{3,2},{4,7},{5,4},{6,5},{7,6},{8,11},{9,8},{10,9... | collective-permute-start | bytes 700424 | tf_op jit(solution)/shard_map/ppermute | solution.py:323
  20.9 15.6 %collective-permute-start.4 = (bf16[16,7296]{1,0:T(8,128)(2,1)S(1)}, bf16[16,7296]{1,0:T(8,128)(2,1)S(1)}, u32[]{:S(2)}, u32[]{:S(2)}) collective-permute-start(bf16[16,7296]{1,0:T(8,128)(2,1)S(1)} %pad_maximum_fusion.t0), channel_id=1, source_target_pairs={{0,16},{16,0},{1,17},{17,1},{2,18},{18,2},{3,19},{19,3},{4,20},{20... | collective-permute-start | bytes 700424 | tf_op jit(solution)/shard_map/ppermute | solution.py:344
  28.0 10.0 %collective-permute-start.7 = (bf16[32,7168]{1,0:T(8,128)(2,1)S(1)}, bf16[32,7168]{1,0:T(8,128)(2,1)S(1)}, u32[]{:S(2)}, u32[]{:S(2)}) collective-permute-start(bf16[32,7168]{1,0:T(8,128)(2,1)S(1)} %get-tuple-element.35), channel_id=1, source_target_pairs={{0,4},{1,5},{2,6},{3,7},{4,8},{5,9},{6,10},{7,11},{8,12},{9,13},{1... | collective-permute-start | bytes 1376264 | tf_op jit(solution)/shard_map/ppermute | solution.py:323
  29.6 15.9 %collective-permute-start.8 = (bf16[32,7168]{1,0:T(8,128)(2,1)S(1)}, bf16[32,7168]{1,0:T(8,128)(2,1)S(1)}, u32[]{:S(2)}, u32[]{:S(2)}) collective-permute-start(bf16[32,7168]{1,0:T(8,128)(2,1)S(1)} %get-tuple-element.39), channel_id=1, source_target_pairs={{0,8},{1,9},{2,10},{3,11},{4,12},{5,13},{6,14},{7,15},{8,0},{9,1},... | collective-permute-start | bytes 1376264 | tf_op jit(solution)/shard_map/ppermute | solution.py:323
  36.5 9.3 %collective-permute-start.9 = (bf16[32,7168]{1,0:T(8,128)(2,1)S(1)}, bf16[32,7168]{1,0:T(8,128)(2,1)S(1)}, u32[]{:S(2)}, u32[]{:S(2)}) collective-permute-start(bf16[32,7168]{1,0:T(8,128)(2,1)S(1)} %get-tuple-element.40), channel_id=1, source_target_pairs={{0,12},{1,13},{2,14},{3,15},{4,0},{5,1},{6,2},{7,3},{8,4},{9,5},{1... | collective-permute-start | bytes 1376264 | tf_op jit(solution)/shard_map/ppermute | solution.py:323
  38.0 20.0 %collective-permute-start.11 = (bf16[16,7296]{1,0:T(8,128)(2,1)S(1)}, bf16[16,7296]{1,0:T(8,128)(2,1)S(1)}, u32[]{:S(2)}, u32[]{:S(2)}) collective-permute-start(bf16[16,7296]{1,0:T(8,128)(2,1)S(1)} %collective-permute-done.4.t0), channel_id=1, source_target_pairs={{0,1},{1,2},{2,3},{3,0},{4,5},{5,6},{6,7},{7,4},{8,9},{9,10},{10,1... | collective-permute-start | bytes 700424 | tf_op jit(solution)/shard_map/ppermute | solution.py:323
  45.5 12.5 %collective-permute-start.12 = (bf16[16,7296]{1,0:T(8,128)(2,1)S(1)}, bf16[16,7296]{1,0:T(8,128)(2,1)S(1)}, u32[]{:S(2)}, u32[]{:S(2)}) collective-permute-start(bf16[16,7296]{1,0:T(8,128)(2,1)S(1)} %collective-permute-done.4.t0), channel_id=1, source_target_pairs={{0,2},{1,3},{2,0},{3,1},{4,6},{5,7},{6,4},{7,5},{8,10},{9,11},{10,... | collective-permute-start | bytes 700424 | tf_op jit(solution)/shard_map/ppermute | solution.py:323
  45.8 12.2 %collective-permute-start.13 = (bf16[16,7296]{1,0:T(8,128)(2,1)S(1)}, bf16[16,7296]{1,0:T(8,128)(2,1)S(1)}, u32[]{:S(2)}, u32[]{:S(2)}) collective-permute-start(bf16[16,7296]{1,0:T(8,128)(2,1)S(1)} %collective-permute-done.4.t0), channel_id=1, source_target_pairs={{0,3},{1,0},{2,1},{3,2},{4,7},{5,4},{6,5},{7,6},{8,11},{9,8},{10,9... | collective-permute-start | bytes 700424 | tf_op jit(solution)/shard_map/ppermute | solution.py:323
  59.4 9.8 %collective-permute-start.17 = (bf16[32,7168]{1,0:T(8,128)(2,1)S(1)}, bf16[32,7168]{1,0:T(8,128)(2,1)S(1)}, u32[]{:S(2)}, u32[]{:S(2)}) collective-permute-start(bf16[32,7168]{1,0:T(8,128)(2,1)S(1)} %get-tuple-element.49), channel_id=1, source_target_pairs={{0,4},{1,5},{2,6},{3,7},{4,8},{5,9},{6,10},{7,11},{8,12},{9,13},{1... | collective-permute-start | bytes 1376264 | tf_op jit(solution)/shard_map/ppermute | solution.py:323
  60.5 15.2 %collective-permute-start.18 = (bf16[32,7168]{1,0:T(8,128)(2,1)S(1)}, bf16[32,7168]{1,0:T(8,128)(2,1)S(1)}, u32[]{:S(2)}, u32[]{:S(2)}) collective-permute-start(bf16[32,7168]{1,0:T(8,128)(2,1)S(1)} %get-tuple-element.50), channel_id=1, source_target_pairs={{0,8},{1,9},{2,10},{3,11},{4,12},{5,13},{6,14},{7,15},{8,0},{9,1},... | collective-permute-start | bytes 1376264 | tf_op jit(solution)/shard_map/ppermute | solution.py:323
  63.7 12.0 %collective-permute-start.19 = (bf16[32,7168]{1,0:T(8,128)(2,1)S(1)}, bf16[32,7168]{1,0:T(8,128)(2,1)S(1)}, u32[]{:S(2)}, u32[]{:S(2)}) collective-permute-start(bf16[32,7168]{1,0:T(8,128)(2,1)S(1)} %get-tuple-element.51), channel_id=1, source_target_pairs={{0,12},{1,13},{2,14},{3,15},{4,0},{5,1},{6,2},{7,3},{8,4},{9,5},{1... | collective-permute-start | bytes 1376264 | tf_op jit(solution)/shard_map/ppermute | solution.py:323
  63.9 23.2 %collective-permute-start.14 = (bf16[128,512]{1,0:T(8,128)(2,1)S(1)}, bf16[128,512]{1,0:T(8,128)(2,1)S(1)}, u32[]{:S(2)}, u32[]{:S(2)}) collective-permute-start(bf16[128,512]{1,0:T(8,128)(2,1)S(1)} %shard_map.124.refs_0_), channel_id=1, source_target_pairs={{0,64},{64,128},{128,192},{192,0},{1,65},{65,129},{129,193},{193,1... | collective-permute-start | bytes 393224 | tf_op jit(solution)/shard_map/ppermute | solution.py:312
  69.2 18.4 %collective-permute-start.15 = (bf16[128,512]{1,0:T(8,128)(2,1)S(1)}, bf16[128,512]{1,0:T(8,128)(2,1)S(1)}, u32[]{:S(2)}, u32[]{:S(2)}) collective-permute-start(bf16[128,512]{1,0:T(8,128)(2,1)S(1)} %shard_map.124.refs_0_), channel_id=1, source_target_pairs={{0,128},{64,192},{128,0},{192,64},{1,129},{65,193},{129,1},{193,65... | collective-permute-start | bytes 393224 | tf_op jit(solution)/shard_map/ppermute | solution.py:312
  75.7 11.8 %collective-permute-start.16 = (bf16[128,512]{1,0:T(8,128)(2,1)S(1)}, bf16[128,512]{1,0:T(8,128)(2,1)S(1)}, u32[]{:S(2)}, u32[]{:S(2)}) collective-permute-start(bf16[128,512]{1,0:T(8,128)(2,1)S(1)} %shard_map.124.refs_0_), channel_id=1, source_target_pairs={{0,192},{64,0},{128,64},{192,128},{1,193},{65,1},{129,65},{193,129... | collective-permute-start | bytes 393224 | tf_op jit(solution)/shard_map/ppermute | solution.py:312
  83.2 6.8 %collective-permute-start.20 = (bf16[128,512]{1,0:T(8,128)(2,1)S(1)}, bf16[128,512]{1,0:T(8,128)(2,1)S(1)}, u32[]{:S(2)}, u32[]{:S(2)}) collective-permute-start(bf16[128,512]{1,0:T(8,128)(2,1)S(1)} %shard_map.126.refs_4_), channel_id=1, source_target_pairs={{0,64},{64,128},{128,192},{192,0},{1,65},{65,129},{129,193},{193,1... | collective-permute-start | bytes 393224 | tf_op jit(solution)/shard_map/ppermute | solution.py:312
  85.3 7.4 %collective-permute-start.21 = (bf16[128,512]{1,0:T(8,128)(2,1)S(1)}, bf16[128,512]{1,0:T(8,128)(2,1)S(1)}, u32[]{:S(2)}, u32[]{:S(2)}) collective-permute-start(bf16[128,512]{1,0:T(8,128)(2,1)S(1)} %shard_map.126.refs_4_), channel_id=1, source_target_pairs={{0,128},{64,192},{128,0},{192,64},{1,129},{65,193},{129,1},{193,65... | collective-permute-start | bytes 393224 | tf_op jit(solution)/shard_map/ppermute | solution.py:312
  87.1 6.8 %collective-permute-start.22 = (bf16[128,512]{1,0:T(8,128)(2,1)S(1)}, bf16[128,512]{1,0:T(8,128)(2,1)S(1)}, u32[]{:S(2)}, u32[]{:S(2)}) collective-permute-start(bf16[128,512]{1,0:T(8,128)(2,1)S(1)} %shard_map.126.refs_4_), channel_id=1, source_target_pairs={{0,192},{64,0},{128,64},{192,128},{1,193},{65,1},{129,65},{193,129... | collective-permute-start | bytes 393224 | tf_op jit(solution)/shard_map/ppermute | solution.py:312
  93.9 0.7 copy-start.1
  100.9 16.8 %all-to-all-start = ((bf16[16,16,1792]{2,1,0:T(8,128)(2,1)}), bf16[16,16,1792]{2,1,0:T(8,128)(2,1)S(1)}, u32[]{:S(2)}, u32[]{:S(2)}) async-start(bf16[16,16,1792]{2,1,0:T(8,128)(2,1)} %bitcast.54), calls=%async_computation | async-start | bytes 1835008 | tf_op jit(solution)/shard_map/all_to_all | solution.py:355
  105.5 4.1 %collective-permute-start.24 = (bf16[32,640]{1,0:T(8,128)(2,1)S(1)}, bf16[32,640]{1,0:T(8,128)(2,1)S(1)}, u32[]{:S(2)}, u32[]{:S(2)}) collective-permute-start(bf16[32,640]{1,0:T(8,128)(2,1)S(1)} %get-tuple-element.58), channel_id=1, source_target_pairs={{0,64},{64,128},{128,192},{192,0},{1,65},{65,129},{129,193},{193,1... | collective-permute-start | bytes 122888 | tf_op jit(solution)/shard_map/ppermute | solution.py:312
  105.6 5.0 %collective-permute-start.25 = (bf16[32,640]{1,0:T(8,128)(2,1)S(1)}, bf16[32,640]{1,0:T(8,128)(2,1)S(1)}, u32[]{:S(2)}, u32[]{:S(2)}) collective-permute-start(bf16[32,640]{1,0:T(8,128)(2,1)S(1)} %get-tuple-element.60), channel_id=1, source_target_pairs={{0,128},{64,192},{128,0},{192,64},{1,129},{65,193},{129,1},{193,65... | collective-permute-start | bytes 122888 | tf_op jit(solution)/shard_map/ppermute | solution.py:312
  108.0 4.0 %collective-permute-start.26 = (bf16[32,640]{1,0:T(8,128)(2,1)S(1)}, bf16[32,640]{1,0:T(8,128)(2,1)S(1)}, u32[]{:S(2)}, u32[]{:S(2)}) collective-permute-start(bf16[32,640]{1,0:T(8,128)(2,1)S(1)} %get-tuple-element.59), channel_id=1, source_target_pairs={{0,192},{64,0},{128,64},{192,128},{1,193},{65,1},{129,65},{193,129... | collective-permute-start | bytes 122888 | tf_op jit(solution)/shard_map/ppermute | solution.py:312
  118.6 16.9 %all-to-all-start.1 = ((bf16[8,4,1792]{2,1,0:T(4,128)(2,1)}), bf16[8,4,1792]{2,1,0:T(4,128)(2,1)S(1)}, u32[]{:S(2)}, u32[]{:S(2)}) async-start(bf16[8,4,1792]{2,1,0:T(4,128)(2,1)} %shard_map.129), calls=%async_computation.1 | async-start | bytes 229376 | tf_op jit(solution)/shard_map/all_to_all | solution.py:365

commit v9 on v8

--- a/solution.py
+++ b/solution.py
@@ -232,7 +232,7 @@
             pltpu.VMEM((2, 4, 2, 256, 896), bf16),
             pltpu.SemaphoreType.DMA((4, 4)),
         ],
-        compiler_params=room(53),
+        compiler_params=room(51),
         cost_estimate=pl.CostEstimate(
             flops=2 * 256 * 2048 * 1792, bytes_accessed=2 * 2048 * 1792 + 2 * 256 * 2048, transcendentals=0
         ),

time: 137 us -> 136 us (level)
  no operation moved by 1% of the time
where the time goes in v9:
time: 136 us
  starting transfers between devices  62.5 us (46%)
  waiting for transfers between devices  38.1 us (28%)
  Pallas kernels  27.4 us (20%)
  matrix products  2.98 us (2%)
  other arithmetic  2.63 us (2%)
  between operations  1.54 us (1%)
    ppermute x12, starting transfers between devices, along(): return lax.ppermute(value, ('att', 'x', 'y'), pairs)  22.6 us
    ppermute x12, starting transfers between devices, hop(): return lax.ppermute(value, 'ctx', [(i, (i + k) % 4) for i in range(4)])  20.1 us
    pallas_call x2, Pallas kernels, gate_up(): pl.pallas_call(gate_up_kernel, out_shape=jax.ShapeDtypeStruct((128, 512),...  14.9 us
    ppermute x12, waiting for transfers between devices, along(): return lax.ppermute(value, ('att', 'x', 'y'), pairs)  12.4 us
    all_to_all x1, starting transfers between devices, shards(): lax.all_to_all(outgoing, ('ctx', 'zhi'), split_axis=0, concat_axis=0, til...  9.63 us
    ppermute x12, waiting for transfers between devices, hop(): return lax.ppermute(value, 'ctx', [(i, (i + k) % 4) for i in range(4)])  9.57 us
    all_to_all x1, waiting for transfers between devices, shards(): lax.all_to_all(outgoing, ('ctx', 'zhi'), split_axis=0, concat_axis=0, til...  6.6 us
    pallas_call x1, Pallas kernels, down(): pl.pallas_call(down_kernel, out_shape=jax.ShapeDtypeStruct((256, 1792), b...  6.26 us
  transfers between devices with their start and end apart: 29, of which 12 were waited for; matrix products, arithmetic and copies ran while one was open for 4% of the time, Pallas kernels for 14%

profile of v9, /device:TPU:32, one launch (start us, length us, event | category | flops | bytes accessed | tf_op | source)
XLA Modules:
  0.0 135.5 jit_solution(8389272300713536027)
XLA Ops:
  0.6 1.7 %shard_map.122 = bf16[4,7296]{1,0:T(4,128)(2,1)} custom-call(s32[4,8]{1,0:T(4,128)} %ids_ref.1, f32[4,8]{1,0:T(4,128)} %gates_ref.1, bf16[4,7168]{1,0:T(4,128)(2,1)} %rows_ref.1, bf16[7168]{0:T(1024)(128)(2,1)} %gain_ref.1), custom_call_target="tpu_custom_call" | custom-call | tf_op jit(solution)/shard_map/pallas_call | solution.py:80
  2.4 1.9 %collective-permute-start = (bf16[4,7296]{1,0:T(4,128)(2,1)}, bf16[4,7296]{1,0:T(4,128)(2,1)S(1)}, u32[]{:S(2)}, u32[]{:S(2)}) collective-permute-start(bf16[4,7296]{1,0:T(4,128)(2,1)} %shard_map.122), channel_id=1, source_target_pairs={{0,64},{64,128},{128,192},{192,0},{1,65},{65,129},{129,193},{193,1... | collective-permute-start | bytes 175112 | tf_op jit(solution)/shard_map/ppermute | solution.py:312
  4.3 2.3 %collective-permute-start.1 = (bf16[4,7296]{1,0:T(4,128)(2,1)}, bf16[4,7296]{1,0:T(4,128)(2,1)S(1)}, u32[]{:S(2)}, u32[]{:S(2)}) collective-permute-start(bf16[4,7296]{1,0:T(4,128)(2,1)} %shard_map.122), channel_id=1, source_target_pairs={{0,128},{64,192},{128,0},{192,64},{1,129},{65,193},{129,1},{193,65... | collective-permute-start | bytes 175112 | tf_op jit(solution)/shard_map/ppermute | solution.py:312
  9.5 1.5 %fusion.16 = (bf16[128,1024]{1,0:T(8,128)(2,1)S(1)}, f32[128]{0:T(128)S(1)}) fusion(f32[128,1024]{1,0:T(8,128)S(1)} %fusion.5, bf16[1,1024,512]{2,1,0:T(8,128)(2,1)S(1)} %copy-done, bf16[1,128,512]{2,1,0:T(8,128)(2,1)} %param.11, pred[1024]{0:T(1024)(128)(4,1)S(1)} %add_compare_fusion), kind=kOutput, calls=%fused_computation.30 | convolution fusion | flops 134872960 | bytes 1967616 | tf_op jit(solution)/shard_map/hr,tr->ht/dot_general | solution.py:20
  14.8 2.9 %collective-permute-start.5 = (bf16[16,7296]{1,0:T(8,128)(2,1)S(1)}, bf16[16,7296]{1,0:T(8,128)(2,1)S(1)}, u32[]{:S(2)}, u32[]{:S(2)}) collective-permute-start(bf16[16,7296]{1,0:T(8,128)(2,1)S(1)} %pad_maximum_fusion.t0), channel_id=1, source_target_pairs={{0,2},{1,3},{2,0},{3,1},{4,6},{5,7},{6,4},{7,5},{8,10},{9,11},{10,... | collective-permute-start | bytes 700424 | tf_op jit(solution)/shard_map/ppermute | solution.py:323
  19.1 1.8 %collective-permute-done.3.t1 = bf16[16,7296]{1,0:T(8,128)(2,1)S(1)} collective-permute-done((bf16[16,7296]{1,0:T(8,128)(2,1)S(1)}, bf16[16,7296]{1,0:T(8,128)(2,1)S(1)}, u32[]{:S(2)}, u32[]{:S(2)}) %collective-permute-start.3) | collective-permute-done | bytes 233504 | tf_op jit(solution)/shard_map/ppermute | solution.py:323
  20.8 5.6 %collective-permute-start.4 = (bf16[16,7296]{1,0:T(8,128)(2,1)S(1)}, bf16[16,7296]{1,0:T(8,128)(2,1)S(1)}, u32[]{:S(2)}, u32[]{:S(2)}) collective-permute-start(bf16[16,7296]{1,0:T(8,128)(2,1)S(1)} %pad_maximum_fusion.t0), channel_id=1, source_target_pairs={{0,16},{16,0},{1,17},{17,1},{2,18},{18,2},{3,19},{19,3},{4,20},{20... | collective-permute-start | bytes 700424 | tf_op jit(solution)/shard_map/ppermute | solution.py:344
  26.6 1.4 %shard_map.123 = (bf16[32,7168]{1,0:T(8,128)(2,1)S(1)}, bf16[32,7168]{1,0:T(8,128)(2,1)S(1)}, bf16[32,7168]{1,0:T(8,128)(2,1)S(1)}, bf16[32,7168]{1,0:T(8,128)(2,1)S(1)}) custom-call(s32[5]{0:T(128)S(1)} %stack.23.place_ref, bf16[16,7296]{1,0:T(8,128)(2,1)S(1)} %pad_maximum_fusion.t0, bf16[16,7296]{1,0:T(8,128)(2,1)S(1)} %collective-permute-done.3.t1, ...), custom_call_target="tpu_custom_call" | custom-call | flops 117440512 | bytes 2752512 | tf_op jit(solution)/shard_map/pallas_call | solution.py:120
  28.0 1.6 %collective-permute-start.7 = (bf16[32,7168]{1,0:T(8,128)(2,1)S(1)}, bf16[32,7168]{1,0:T(8,128)(2,1)S(1)}, u32[]{:S(2)}, u32[]{:S(2)}) collective-permute-start(bf16[32,7168]{1,0:T(8,128)(2,1)S(1)} %get-tuple-element.35), channel_id=1, source_target_pairs={{0,4},{1,5},{2,6},{3,7},{4,8},{5,9},{6,10},{7,11},{8,12},{9,13},{1... | collective-permute-start | bytes 1376264 | tf_op jit(solution)/shard_map/ppermute | solution.py:323
  29.6 2.7 %collective-permute-start.8 = (bf16[32,7168]{1,0:T(8,128)(2,1)S(1)}, bf16[32,7168]{1,0:T(8,128)(2,1)S(1)}, u32[]{:S(2)}, u32[]{:S(2)}) collective-permute-start(bf16[32,7168]{1,0:T(8,128)(2,1)S(1)} %get-tuple-element.39), channel_id=1, source_target_pairs={{0,8},{1,9},{2,10},{3,11},{4,12},{5,13},{6,14},{7,15},{8,0},{9,1},... | collective-permute-start | bytes 1376264 | tf_op jit(solution)/shard_map/ppermute | solution.py:323
  32.3 4.2 %collective-permute-done.4.t0 = bf16[16,7296]{1,0:T(8,128)(2,1)S(1)} collective-permute-done((bf16[16,7296]{1,0:T(8,128)(2,1)S(1)}, bf16[16,7296]{1,0:T(8,128)(2,1)S(1)}, u32[]{:S(2)}, u32[]{:S(2)}) %collective-permute-start.4) | collective-permute-done | bytes 233504 | tf_op jit(solution)/shard_map/ppermute | solution.py:344
  36.5 1.5 %collective-permute-start.9 = (bf16[32,7168]{1,0:T(8,128)(2,1)S(1)}, bf16[32,7168]{1,0:T(8,128)(2,1)S(1)}, u32[]{:S(2)}, u32[]{:S(2)}) collective-permute-start(bf16[32,7168]{1,0:T(8,128)(2,1)S(1)} %get-tuple-element.40), channel_id=1, source_target_pairs={{0,12},{1,13},{2,14},{3,15},{4,0},{5,1},{6,2},{7,3},{8,4},{9,5},{1... | collective-permute-start | bytes 1376264 | tf_op jit(solution)/shard_map/ppermute | solution.py:323
  38.0 1.6 %collective-permute-start.11 = (bf16[16,7296]{1,0:T(8,128)(2,1)S(1)}, bf16[16,7296]{1,0:T(8,128)(2,1)S(1)}, u32[]{:S(2)}, u32[]{:S(2)}) collective-permute-start(bf16[16,7296]{1,0:T(8,128)(2,1)S(1)} %collective-permute-done.4.t0), channel_id=1, source_target_pairs={{0,1},{1,2},{2,3},{3,0},{4,5},{5,6},{6,7},{7,4},{8,9},{9,10},{10,1... | collective-permute-start | bytes 700424 | tf_op jit(solution)/shard_map/ppermute | solution.py:323
  39.6 5.8 %collective-permute-done.8.r2 = bf16[32,7168]{1,0:T(8,128)(2,1)S(1)} collective-permute-done((bf16[32,7168]{1,0:T(8,128)(2,1)S(1)}, bf16[32,7168]{1,0:T(8,128)(2,1)S(1)}, u32[]{:S(2)}, u32[]{:S(2)}) %collective-permute-start.8) | collective-permute-done | bytes 458784 | tf_op jit(solution)/shard_map/ppermute | solution.py:323
  45.7 4.8 %collective-permute-start.13 = (bf16[16,7296]{1,0:T(8,128)(2,1)S(1)}, bf16[16,7296]{1,0:T(8,128)(2,1)S(1)}, u32[]{:S(2)}, u32[]{:S(2)}) collective-permute-start(bf16[16,7296]{1,0:T(8,128)(2,1)S(1)} %collective-permute-done.4.t0), channel_id=1, source_target_pairs={{0,3},{1,0},{2,1},{3,2},{4,7},{5,4},{6,5},{7,6},{8,11},{9,8},{10,9... | collective-permute-start | bytes 700424 | tf_op jit(solution)/shard_map/ppermute | solution.py:323
  50.5 7.5 %shard_map.124.refs_0_ = bf16[128,512]{1,0:T(8,128)(2,1)S(1)} custom-call(s32[5]{0:T(128)S(1)} %stack.23.place_ref, bf16[32,7168]{1,0:T(8,128)(2,1)S(1)} %get-tuple-element.37.r0, bf16[32,7168]{1,0:T(8,128)(2,1)S(1)} %collective-permute-done.7.r1, bf16[32,7168]{1,0:T(8,128)(2,1)S(1)} %collective-permute-done.8.r2, ...), custom_call_target="tpu_custom_call" | custom-call | flops 1879048192 | bytes 16515072 | tf_op jit(solution)/shard_map/pallas_call | solution.py:176
  58.0 1.4 %shard_map.125 = (bf16[32,7168]{1,0:T(8,128)(2,1)S(1)}, bf16[32,7168]{1,0:T(8,128)(2,1)S(1)}, bf16[32,7168]{1,0:T(8,128)(2,1)S(1)}, bf16[32,7168]{1,0:T(8,128)(2,1)S(1)}) custom-call(s32[5]{0:T(128)S(1)} %stack.23.place_ref, bf16[16,7296]{1,0:T(8,128)(2,1)S(1)} %collective-permute-done.4.t0, bf16[16,7296]{1,0:T(8,128)(2,1)S(1)} %collective-permute-done.11.t1, ...), custom_call_target="tpu_custom_call" | custom-call | flops 117440512 | bytes 2752512 | tf_op jit(solution)/shard_map/pallas_call | solution.py:120
  60.5 3.2 %collective-permute-start.18 = (bf16[32,7168]{1,0:T(8,128)(2,1)S(1)}, bf16[32,7168]{1,0:T(8,128)(2,1)S(1)}, u32[]{:S(2)}, u32[]{:S(2)}) collective-permute-start(bf16[32,7168]{1,0:T(8,128)(2,1)S(1)} %get-tuple-element.50), channel_id=1, source_target_pairs={{0,8},{1,9},{2,10},{3,11},{4,12},{5,13},{6,14},{7,15},{8,0},{9,1},... | collective-permute-start | bytes 1376264 | tf_op jit(solution)/shard_map/ppermute | solution.py:323
  64.4 4.7 %collective-permute-done.17.r1 = bf16[32,7168]{1,0:T(8,128)(2,1)S(1)} collective-permute-done((bf16[32,7168]{1,0:T(8,128)(2,1)S(1)}, bf16[32,7168]{1,0:T(8,128)(2,1)S(1)}, u32[]{:S(2)}, u32[]{:S(2)}) %collective-permute-start.17) | collective-permute-done | bytes 458784 | tf_op jit(solution)/shard_map/ppermute | solution.py:323
  69.2 6.6 %collective-permute-start.15 = (bf16[128,512]{1,0:T(8,128)(2,1)S(1)}, bf16[128,512]{1,0:T(8,128)(2,1)S(1)}, u32[]{:S(2)}, u32[]{:S(2)}) collective-permute-start(bf16[128,512]{1,0:T(8,128)(2,1)S(1)} %shard_map.124.refs_0_), channel_id=1, source_target_pairs={{0,128},{64,192},{128,0},{192,64},{1,129},{65,193},{129,1},{193,65... | collective-permute-start | bytes 393224 | tf_op jit(solution)/shard_map/ppermute | solution.py:312
  75.7 7.5 %shard_map.126.refs_4_ = bf16[128,512]{1,0:T(8,128)(2,1)S(1)} custom-call(s32[5]{0:T(128)S(1)} %stack.23.place_ref, bf16[32,7168]{1,0:T(8,128)(2,1)S(1)} %get-tuple-element.48.r0, bf16[32,7168]{1,0:T(8,128)(2,1)S(1)} %collective-permute-done.17.r1, bf16[32,7168]{1,0:T(8,128)(2,1)S(1)} %collective-permute-done.18.r2, ...), custom_call_target="tpu_custom_call" | custom-call | flops 1879048192 | bytes 16515072 | tf_op jit(solution)/shard_map/pallas_call | solution.py:176
  83.2 2.1 %collective-permute-start.20 = (bf16[128,512]{1,0:T(8,128)(2,1)S(1)}, bf16[128,512]{1,0:T(8,128)(2,1)S(1)}, u32[]{:S(2)}, u32[]{:S(2)}) collective-permute-start(bf16[128,512]{1,0:T(8,128)(2,1)S(1)} %shard_map.126.refs_4_), channel_id=1, source_target_pairs={{0,64},{64,128},{128,192},{192,0},{1,65},{65,129},{129,193},{193,1... | collective-permute-start | bytes 393224 | tf_op jit(solution)/shard_map/ppermute | solution.py:312
  85.3 1.8 %collective-permute-start.21 = (bf16[128,512]{1,0:T(8,128)(2,1)S(1)}, bf16[128,512]{1,0:T(8,128)(2,1)S(1)}, u32[]{:S(2)}, u32[]{:S(2)}) collective-permute-start(bf16[128,512]{1,0:T(8,128)(2,1)S(1)} %shard_map.126.refs_4_), channel_id=1, source_target_pairs={{0,128},{64,192},{128,0},{192,64},{1,129},{65,193},{129,1},{193,65... | collective-permute-start | bytes 393224 | tf_op jit(solution)/shard_map/ppermute | solution.py:312
  87.6 2.4 %collective-permute-done.20.refs_5_ = bf16[128,512]{1,0:T(8,128)(2,1)S(1)} collective-permute-done((bf16[128,512]{1,0:T(8,128)(2,1)S(1)}, bf16[128,512]{1,0:T(8,128)(2,1)S(1)}, u32[]{:S(2)}, u32[]{:S(2)}) %collective-permute-start.20) | collective-permute-done | bytes 131104 | tf_op jit(solution)/shard_map/ppermute | solution.py:312
  90.0 2.8 %collective-permute-done.21.refs_6_ = bf16[128,512]{1,0:T(8,128)(2,1)S(1)} collective-permute-done((bf16[128,512]{1,0:T(8,128)(2,1)S(1)}, bf16[128,512]{1,0:T(8,128)(2,1)S(1)}, u32[]{:S(2)}, u32[]{:S(2)}) %collective-permute-start.21) | collective-permute-done | bytes 131104 | tf_op jit(solution)/shard_map/ppermute | solution.py:312
  93.9 6.3 %shard_map.127 = bf16[256,1792]{1,0:T(8,128)(2,1)} custom-call(s32[5]{0:T(128)S(1)} %stack.23.place_ref, bf16[128,512]{1,0:T(8,128)(2,1)S(1)} %shard_map.124.refs_0_, bf16[128,512]{1,0:T(8,128)(2,1)S(1)} %collective-permute-done.14.refs_1_, bf16[128,512]{1,0:T(8,128)(2,1)S(1)} %collective-permute-done.15.refs_2_, ...), custom_call_target="tpu_custom_call" | custom-call | flops 1879048192 | bytes 8388608 | tf_op jit(solution)/shard_map/pallas_call | solution.py:225
  100.2 4.6 %all-to-all-start = ((bf16[16,16,1792]{2,1,0:T(8,128)(2,1)}), bf16[16,16,1792]{2,1,0:T(8,128)(2,1)S(1)}, u32[]{:S(2)}, u32[]{:S(2)}) async-start(bf16[16,16,1792]{2,1,0:T(8,128)(2,1)} %bitcast.19), calls=%async_computation | async-start | bytes 1835008 | tf_op jit(solution)/shard_map/all_to_all | solution.py:355
  104.9 2.4 %collective-permute-start.25 = (bf16[32,640]{1,0:T(8,128)(2,1)S(1)}, bf16[32,640]{1,0:T(8,128)(2,1)S(1)}, u32[]{:S(2)}, u32[]{:S(2)}) collective-permute-start(bf16[32,640]{1,0:T(8,128)(2,1)S(1)} %get-tuple-element.60), channel_id=1, source_target_pairs={{0,128},{64,192},{128,0},{192,64},{1,129},{65,193},{129,1},{193,65... | collective-permute-start | bytes 122888 | tf_op jit(solution)/shard_map/ppermute | solution.py:312
  109.9 1.4 %collective-permute-done.26 = bf16[32,640]{1,0:T(8,128)(2,1)S(1)} collective-permute-done((bf16[32,640]{1,0:T(8,128)(2,1)S(1)}, bf16[32,640]{1,0:T(8,128)(2,1)S(1)}, u32[]{:S(2)}, u32[]{:S(2)}) %collective-permute-start.26) | collective-permute-done | bytes 40992 | tf_op jit(solution)/shard_map/ppermute | solution.py:312
  111.5 5.4 %all-to-all-done = bf16[16,16,1792]{2,1,0:T(8,128)(2,1)S(1)} async-done(((bf16[16,16,1792]{2,1,0:T(8,128)(2,1)}), bf16[16,16,1792]{2,1,0:T(8,128)(2,1)S(1)}, u32[]{:S(2)}, u32[]{:S(2)}) %all-to-all-start) | async-done | bytes 917536 | tf_op jit(solution)/shard_map/all_to_all | solution.py:355
  117.9 9.6 %all-to-all-start.1 = ((bf16[8,4,1792]{2,1,0:T(4,128)(2,1)}), bf16[8,4,1792]{2,1,0:T(4,128)(2,1)S(1)}, u32[]{:S(2)}, u32[]{:S(2)}) async-start(bf16[8,4,1792]{2,1,0:T(4,128)(2,1)} %shard_map.129), calls=%async_computation.1 | async-start | bytes 229376 | tf_op jit(solution)/shard_map/all_to_all | solution.py:365
  128.2 6.6 %all-to-all-done.1 = bf16[8,4,1792]{2,1,0:T(4,128)(2,1)S(1)} async-done(((bf16[8,4,1792]{2,1,0:T(4,128)(2,1)}), bf16[8,4,1792]{2,1,0:T(4,128)(2,1)S(1)}, u32[]{:S(2)}, u32[]{:S(2)}) %all-to-all-start.1) | async-done | bytes 114720 | tf_op jit(solution)/shard_map/all_to_all | solution.py:365
  (55 shorter events, 16.4 us)
Async XLA Ops:
  0.6 8.9 %copy-start = (bf16[1,1024,512]{2,1,0:T(8,128)(2,1)S(1)}, bf16[1,1024,512]{2,1,0:T(8,128)(2,1)}, u32[]{:S(2)}) copy-start(bf16[1,1024,512]{2,1,0:T(8,128)(2,1)} %param.13) | copy-start | bytes 3145732
  2.4 48.1 %collective-permute-start.10 = (bf16[2,7168,256]{2,1,0:T(8,128)(2,1)}, bf16[2,7168,256]{2,1,0:T(8,128)(2,1)}, u32[]{:S(2)}, u32[]{:S(2)}) collective-permute-start(bf16[2,7168,256]{2,1,0:T(8,128)(2,1)} %bitcast.51), channel_id=1, source_target_pairs={{0,32},{32,0},{1,33},{33,1},{2,34},{34,2},{3,35},{35,3},{4,36},{36... | collective-permute-start | bytes 22020104 | tf_op jit(solution)/shard_map/ppermute | solution.py:337
  2.4 9.3 %collective-permute-start = (bf16[4,7296]{1,0:T(4,128)(2,1)}, bf16[4,7296]{1,0:T(4,128)(2,1)S(1)}, u32[]{:S(2)}, u32[]{:S(2)}) collective-permute-start(bf16[4,7296]{1,0:T(4,128)(2,1)} %shard_map.122), channel_id=1, source_target_pairs={{0,64},{64,128},{128,192},{192,0},{1,65},{65,129},{129,193},{193,1... | collective-permute-start | bytes 175112 | tf_op jit(solution)/shard_map/ppermute | solution.py:312
  4.3 7.4 %collective-permute-start.1 = (bf16[4,7296]{1,0:T(4,128)(2,1)}, bf16[4,7296]{1,0:T(4,128)(2,1)S(1)}, u32[]{:S(2)}, u32[]{:S(2)}) collective-permute-start(bf16[4,7296]{1,0:T(4,128)(2,1)} %shard_map.122), channel_id=1, source_target_pairs={{0,128},{64,192},{128,0},{192,64},{1,129},{65,193},{129,1},{193,65... | collective-permute-start | bytes 175112 | tf_op jit(solution)/shard_map/ppermute | solution.py:312
  6.6 6.0 %collective-permute-start.2 = (bf16[4,7296]{1,0:T(4,128)(2,1)}, bf16[4,7296]{1,0:T(4,128)(2,1)S(1)}, u32[]{:S(2)}, u32[]{:S(2)}) collective-permute-start(bf16[4,7296]{1,0:T(4,128)(2,1)} %shard_map.122), channel_id=1, source_target_pairs={{0,192},{64,0},{128,64},{192,128},{1,193},{65,1},{129,65},{193,129... | collective-permute-start | bytes 175112 | tf_op jit(solution)/shard_map/ppermute | solution.py:312
  7.7 77.6 %collective-permute-start.23 = (bf16[4,2,256,896]{3,2,1,0:T(8,128)(2,1)}, bf16[4,2,256,896]{3,2,1,0:T(8,128)(2,1)}, u32[]{:S(2)}, u32[]{:S(2)}) collective-permute-start(bf16[4,2,256,896]{3,2,1,0:T(8,128)(2,1)} %bitcast.54), channel_id=1, source_target_pairs={{0,32},{32,0},{1,33},{33,1},{2,34},{34,2},{3,35},{35,3},{4,36},{36... | collective-permute-start | bytes 11010056 | tf_op jit(solution)/shard_map/ppermute | solution.py:338
  13.5 7.4 %collective-permute-start.3 = (bf16[16,7296]{1,0:T(8,128)(2,1)S(1)}, bf16[16,7296]{1,0:T(8,128)(2,1)S(1)}, u32[]{:S(2)}, u32[]{:S(2)}) collective-permute-start(bf16[16,7296]{1,0:T(8,128)(2,1)S(1)} %pad_maximum_fusion.t0), channel_id=1, source_target_pairs={{0,1},{1,2},{2,3},{3,0},{4,5},{5,6},{6,7},{7,4},{8,9},{9,10},{10,1... | collective-permute-start | bytes 700424 | tf_op jit(solution)/shard_map/ppermute | solution.py:323
  14.8 11.7 %collective-permute-start.5 = (bf16[16,7296]{1,0:T(8,128)(2,1)S(1)}, bf16[16,7296]{1,0:T(8,128)(2,1)S(1)}, u32[]{:S(2)}, u32[]{:S(2)}) collective-permute-start(bf16[16,7296]{1,0:T(8,128)(2,1)S(1)} %pad_maximum_fusion.t0), channel_id=1, source_target_pairs={{0,2},{1,3},{2,0},{3,1},{4,6},{5,7},{6,4},{7,5},{8,10},{9,11},{10,... | collective-permute-start | bytes 700424 | tf_op jit(solution)/shard_map/ppermute | solution.py:323
  17.7 8.8 %collective-permute-start.6 = (bf16[16,7296]{1,0:T(8,128)(2,1)S(1)}, bf16[16,7296]{1,0:T(8,128)(2,1)S(1)}, u32[]{:S(2)}, u32[]{:S(2)}) collective-permute-start(bf16[16,7296]{1,0:T(8,128)(2,1)S(1)} %pad_maximum_fusion.t0), channel_id=1, source_target_pairs={{0,3},{1,0},{2,1},{3,2},{4,7},{5,4},{6,5},{7,6},{8,11},{9,8},{10,9... | collective-permute-start | bytes 700424 | tf_op jit(solution)/shard_map/ppermute | solution.py:323
  20.8 15.6 %collective-permute-start.4 = (bf16[16,7296]{1,0:T(8,128)(2,1)S(1)}, bf16[16,7296]{1,0:T(8,128)(2,1)S(1)}, u32[]{:S(2)}, u32[]{:S(2)}) collective-permute-start(bf16[16,7296]{1,0:T(8,128)(2,1)S(1)} %pad_maximum_fusion.t0), channel_id=1, source_target_pairs={{0,16},{16,0},{1,17},{17,1},{2,18},{18,2},{3,19},{19,3},{4,20},{20... | collective-permute-start | bytes 700424 | tf_op jit(solution)/shard_map/ppermute | solution.py:344
  28.0 10.0 %collective-permute-start.7 = (bf16[32,7168]{1,0:T(8,128)(2,1)S(1)}, bf16[32,7168]{1,0:T(8,128)(2,1)S(1)}, u32[]{:S(2)}, u32[]{:S(2)}) collective-permute-start(bf16[32,7168]{1,0:T(8,128)(2,1)S(1)} %get-tuple-element.35), channel_id=1, source_target_pairs={{0,4},{1,5},{2,6},{3,7},{4,8},{5,9},{6,10},{7,11},{8,12},{9,13},{1... | collective-permute-start | bytes 1376264 | tf_op jit(solution)/shard_map/ppermute | solution.py:323
  29.6 15.9 %collective-permute-start.8 = (bf16[32,7168]{1,0:T(8,128)(2,1)S(1)}, bf16[32,7168]{1,0:T(8,128)(2,1)S(1)}, u32[]{:S(2)}, u32[]{:S(2)}) collective-permute-start(bf16[32,7168]{1,0:T(8,128)(2,1)S(1)} %get-tuple-element.39), channel_id=1, source_target_pairs={{0,8},{1,9},{2,10},{3,11},{4,12},{5,13},{6,14},{7,15},{8,0},{9,1},... | collective-permute-start | bytes 1376264 | tf_op jit(solution)/shard_map/ppermute | solution.py:323
  36.5 9.2 %collective-permute-start.9 = (bf16[32,7168]{1,0:T(8,128)(2,1)S(1)}, bf16[32,7168]{1,0:T(8,128)(2,1)S(1)}, u32[]{:S(2)}, u32[]{:S(2)}) collective-permute-start(bf16[32,7168]{1,0:T(8,128)(2,1)S(1)} %get-tuple-element.40), channel_id=1, source_target_pairs={{0,12},{1,13},{2,14},{3,15},{4,0},{5,1},{6,2},{7,3},{8,4},{9,5},{1... | collective-permute-start | bytes 1376264 | tf_op jit(solution)/shard_map/ppermute | solution.py:323
  38.0 20.0 %collective-permute-start.11 = (bf16[16,7296]{1,0:T(8,128)(2,1)S(1)}, bf16[16,7296]{1,0:T(8,128)(2,1)S(1)}, u32[]{:S(2)}, u32[]{:S(2)}) collective-permute-start(bf16[16,7296]{1,0:T(8,128)(2,1)S(1)} %collective-permute-done.4.t0), channel_id=1, source_target_pairs={{0,1},{1,2},{2,3},{3,0},{4,5},{5,6},{6,7},{7,4},{8,9},{9,10},{10,1... | collective-permute-start | bytes 700424 | tf_op jit(solution)/shard_map/ppermute | solution.py:323
  45.5 12.5 %collective-permute-start.12 = (bf16[16,7296]{1,0:T(8,128)(2,1)S(1)}, bf16[16,7296]{1,0:T(8,128)(2,1)S(1)}, u32[]{:S(2)}, u32[]{:S(2)}) collective-permute-start(bf16[16,7296]{1,0:T(8,128)(2,1)S(1)} %collective-permute-done.4.t0), channel_id=1, source_target_pairs={{0,2},{1,3},{2,0},{3,1},{4,6},{5,7},{6,4},{7,5},{8,10},{9,11},{10,... | collective-permute-start | bytes 700424 | tf_op jit(solution)/shard_map/ppermute | solution.py:323
  45.7 12.3 %collective-permute-start.13 = (bf16[16,7296]{1,0:T(8,128)(2,1)S(1)}, bf16[16,7296]{1,0:T(8,128)(2,1)S(1)}, u32[]{:S(2)}, u32[]{:S(2)}) collective-permute-start(bf16[16,7296]{1,0:T(8,128)(2,1)S(1)} %collective-permute-done.4.t0), channel_id=1, source_target_pairs={{0,3},{1,0},{2,1},{3,2},{4,7},{5,4},{6,5},{7,6},{8,11},{9,8},{10,9... | collective-permute-start | bytes 700424 | tf_op jit(solution)/shard_map/ppermute | solution.py:323
  59.4 9.8 %collective-permute-start.17 = (bf16[32,7168]{1,0:T(8,128)(2,1)S(1)}, bf16[32,7168]{1,0:T(8,128)(2,1)S(1)}, u32[]{:S(2)}, u32[]{:S(2)}) collective-permute-start(bf16[32,7168]{1,0:T(8,128)(2,1)S(1)} %get-tuple-element.49), channel_id=1, source_target_pairs={{0,4},{1,5},{2,6},{3,7},{4,8},{5,9},{6,10},{7,11},{8,12},{9,13},{1... | collective-permute-start | bytes 1376264 | tf_op jit(solution)/shard_map/ppermute | solution.py:323
  60.5 15.2 %collective-permute-start.18 = (bf16[32,7168]{1,0:T(8,128)(2,1)S(1)}, bf16[32,7168]{1,0:T(8,128)(2,1)S(1)}, u32[]{:S(2)}, u32[]{:S(2)}) collective-permute-start(bf16[32,7168]{1,0:T(8,128)(2,1)S(1)} %get-tuple-element.50), channel_id=1, source_target_pairs={{0,8},{1,9},{2,10},{3,11},{4,12},{5,13},{6,14},{7,15},{8,0},{9,1},... | collective-permute-start | bytes 1376264 | tf_op jit(solution)/shard_map/ppermute | solution.py:323
  63.7 12.0 %collective-permute-start.19 = (bf16[32,7168]{1,0:T(8,128)(2,1)S(1)}, bf16[32,7168]{1,0:T(8,128)(2,1)S(1)}, u32[]{:S(2)}, u32[]{:S(2)}) collective-permute-start(bf16[32,7168]{1,0:T(8,128)(2,1)S(1)} %get-tuple-element.51), channel_id=1, source_target_pairs={{0,12},{1,13},{2,14},{3,15},{4,0},{5,1},{6,2},{7,3},{8,4},{9,5},{1... | collective-permute-start | bytes 1376264 | tf_op jit(solution)/shard_map/ppermute | solution.py:323
  63.9 23.2 %collective-permute-start.14 = (bf16[128,512]{1,0:T(8,128)(2,1)S(1)}, bf16[128,512]{1,0:T(8,128)(2,1)S(1)}, u32[]{:S(2)}, u32[]{:S(2)}) collective-permute-start(bf16[128,512]{1,0:T(8,128)(2,1)S(1)} %shard_map.124.refs_0_), channel_id=1, source_target_pairs={{0,64},{64,128},{128,192},{192,0},{1,65},{65,129},{129,193},{193,1... | collective-permute-start | bytes 393224 | tf_op jit(solution)/shard_map/ppermute | solution.py:312
  69.2 18.4 %collective-permute-start.15 = (bf16[128,512]{1,0:T(8,128)(2,1)S(1)}, bf16[128,512]{1,0:T(8,128)(2,1)S(1)}, u32[]{:S(2)}, u32[]{:S(2)}) collective-permute-start(bf16[128,512]{1,0:T(8,128)(2,1)S(1)} %shard_map.124.refs_0_), channel_id=1, source_target_pairs={{0,128},{64,192},{128,0},{192,64},{1,129},{65,193},{129,1},{193,65... | collective-permute-start | bytes 393224 | tf_op jit(solution)/shard_map/ppermute | solution.py:312
  75.7 11.8 %collective-permute-start.16 = (bf16[128,512]{1,0:T(8,128)(2,1)S(1)}, bf16[128,512]{1,0:T(8,128)(2,1)S(1)}, u32[]{:S(2)}, u32[]{:S(2)}) collective-permute-start(bf16[128,512]{1,0:T(8,128)(2,1)S(1)} %shard_map.124.refs_0_), channel_id=1, source_target_pairs={{0,192},{64,0},{128,64},{192,128},{1,193},{65,1},{129,65},{193,129... | collective-permute-start | bytes 393224 | tf_op jit(solution)/shard_map/ppermute | solution.py:312
  83.2 6.8 %collective-permute-start.20 = (bf16[128,512]{1,0:T(8,128)(2,1)S(1)}, bf16[128,512]{1,0:T(8,128)(2,1)S(1)}, u32[]{:S(2)}, u32[]{:S(2)}) collective-permute-start(bf16[128,512]{1,0:T(8,128)(2,1)S(1)} %shard_map.126.refs_4_), channel_id=1, source_target_pairs={{0,64},{64,128},{128,192},{192,0},{1,65},{65,129},{129,193},{193,1... | collective-permute-start | bytes 393224 | tf_op jit(solution)/shard_map/ppermute | solution.py:312
  85.3 7.4 %collective-permute-start.21 = (bf16[128,512]{1,0:T(8,128)(2,1)S(1)}, bf16[128,512]{1,0:T(8,128)(2,1)S(1)}, u32[]{:S(2)}, u32[]{:S(2)}) collective-permute-start(bf16[128,512]{1,0:T(8,128)(2,1)S(1)} %shard_map.126.refs_4_), channel_id=1, source_target_pairs={{0,128},{64,192},{128,0},{192,64},{1,129},{65,193},{129,1},{193,65... | collective-permute-start | bytes 393224 | tf_op jit(solution)/shard_map/ppermute | solution.py:312
  87.1 6.8 %collective-permute-start.22 = (bf16[128,512]{1,0:T(8,128)(2,1)S(1)}, bf16[128,512]{1,0:T(8,128)(2,1)S(1)}, u32[]{:S(2)}, u32[]{:S(2)}) collective-permute-start(bf16[128,512]{1,0:T(8,128)(2,1)S(1)} %shard_map.126.refs_4_), channel_id=1, source_target_pairs={{0,192},{64,0},{128,64},{192,128},{1,193},{65,1},{129,65},{193,129... | collective-permute-start | bytes 393224 | tf_op jit(solution)/shard_map/ppermute | solution.py:312
  100.2 16.8 %all-to-all-start = ((bf16[16,16,1792]{2,1,0:T(8,128)(2,1)}), bf16[16,16,1792]{2,1,0:T(8,128)(2,1)S(1)}, u32[]{:S(2)}, u32[]{:S(2)}) async-start(bf16[16,16,1792]{2,1,0:T(8,128)(2,1)} %bitcast.19), calls=%async_computation | async-start | bytes 1835008 | tf_op jit(solution)/shard_map/all_to_all | solution.py:355
  104.8 4.1 %collective-permute-start.24 = (bf16[32,640]{1,0:T(8,128)(2,1)S(1)}, bf16[32,640]{1,0:T(8,128)(2,1)S(1)}, u32[]{:S(2)}, u32[]{:S(2)}) collective-permute-start(bf16[32,640]{1,0:T(8,128)(2,1)S(1)} %get-tuple-element.58), channel_id=1, source_target_pairs={{0,64},{64,128},{128,192},{192,0},{1,65},{65,129},{129,193},{193,1... | collective-permute-start | bytes 122888 | tf_op jit(solution)/shard_map/ppermute | solution.py:312
  104.9 5.0 %collective-permute-start.25 = (bf16[32,640]{1,0:T(8,128)(2,1)S(1)}, bf16[32,640]{1,0:T(8,128)(2,1)S(1)}, u32[]{:S(2)}, u32[]{:S(2)}) collective-permute-start(bf16[32,640]{1,0:T(8,128)(2,1)S(1)} %get-tuple-element.60), channel_id=1, source_target_pairs={{0,128},{64,192},{128,0},{192,64},{1,129},{65,193},{129,1},{193,65... | collective-permute-start | bytes 122888 | tf_op jit(solution)/shard_map/ppermute | solution.py:312
  107.3 4.0 %collective-permute-start.26 = (bf16[32,640]{1,0:T(8,128)(2,1)S(1)}, bf16[32,640]{1,0:T(8,128)(2,1)S(1)}, u32[]{:S(2)}, u32[]{:S(2)}) collective-permute-start(bf16[32,640]{1,0:T(8,128)(2,1)S(1)} %get-tuple-element.59), channel_id=1, source_target_pairs={{0,192},{64,0},{128,64},{192,128},{1,193},{65,1},{129,65},{193,129... | collective-permute-start | bytes 122888 | tf_op jit(solution)/shard_map/ppermute | solution.py:312
  117.9 16.9 %all-to-all-start.1 = ((bf16[8,4,1792]{2,1,0:T(4,128)(2,1)}), bf16[8,4,1792]{2,1,0:T(4,128)(2,1)S(1)}, u32[]{:S(2)}, u32[]{:S(2)}) async-start(bf16[8,4,1792]{2,1,0:T(4,128)(2,1)} %shard_map.129), calls=%async_computation.1 | async-start | bytes 229376 | tf_op jit(solution)/shard_map/all_to_all | solution.py:365
